TPU v7x, 32 devices: a whole 2x2x4 slice. The times are simulated.
32 devices in a mesh: row: 4 (over y, x), col: 4 (over z), lag: 2 (over core).
Axes of the slice: x: 2, y: 2, z: 4, core: 2. Of those that a mesh axis runs over, the one named last changes fastest.
Arguments:
- history: bfloat16 [8, 4, 128, 8192], P('lag', 'col', None, 'row'), may hold values from -6 to 6
- kernel_tiles: bfloat16 [4, 4, 8, 12, 256, 256], P('row', 'col', 'lag'), may hold values from -0.09375 to 0.09375
- tile_rows: int32 [4, 4, 8, 12], P('row', 'col', 'lag'), may hold values from 0 to 31
- tile_cols: int32 [4, 4, 8, 12], P('row', 'col', 'lag'), may hold values from 0 to 31
- tile_count: int32 [4, 4, 8], P('row', 'col', 'lag'), may hold values from 3 to 12, as said below
- base_stress: float32 [128, 32768], P(None, ('row', 'col', 'lag')), may hold values from -6 to 6
- prev_rate: float32 [128, 32768], P(None, ('row', 'col', 'lag')), may hold values from -6 to 6
- direct_effect: float32 [128, 32768], P(None, ('row', 'col', 'lag')), may hold values from 0.5 to 2
- state_var: float32 [128, 32768], P(None, ('row', 'col', 'lag')), may hold values from -2 to 2
Outputs:
- stress_change: float32 [128, 32768], P(None, ('row', 'col', 'lag'))
- new_rate: float32 [128, 32768], P(None, ('row', 'col', 'lag'))
Inputs may be any that keep to these rules, and one draw needn't show every extreme that they name: `tile_count`: every draw has some device and lag with all 12 slots live.
All inputs are finite; a program needn't handle non-finite values.
Results may differ from a plain program's by a relative error of at most 0.0003.
Values may be sent and summed in bfloat16 or wider, within the bound.
No kernel may reach another device: no remote copies, remote signals or barrier semaphores. Data moves between devices by JAX's collectives and lax.ppermute only.
A program may use at most 64 MiB of HBM per device.

v0:
```python
import jax
import jax.numpy as jnp
from jax import lax
from jax.sharding import PartitionSpec as P

NEWTON = 4


def inverse_sinh(value):
    magnitude = jnp.abs(value)
    return jnp.sign(value) * jnp.log(magnitude + jnp.sqrt(1.0 + magnitude * magnitude))


def local(
    history,
    kernel_tiles,
    tile_rows,
    tile_cols,
    tile_count,
    base_stress,
    prev_rate,
    direct_effect,
    state_var,
):
    gathered = lax.all_gather(history, "row", axis=3, tiled=True)
    lag_local = gathered.shape[0]
    sims_count = gathered.shape[2]
    tile_side = kernel_tiles.shape[4]
    slots = kernel_tiles.shape[3]
    col_blocks = gathered.shape[3] // tile_side
    blocks = gathered.reshape(lag_local, sims_count, col_blocks, tile_side)
    choose = jax.nn.one_hot(tile_cols[0, 0], col_blocks, dtype=jnp.bfloat16)
    picked = jnp.einsum(
        "lkb,lsbj->lksj", choose, blocks, preferred_element_type=jnp.float32
    ).astype(jnp.bfloat16)
    contrib = jnp.einsum(
        "lksj,lkij->slki", picked, kernel_tiles[0, 0], preferred_element_type=jnp.float32
    )
    rec_local = base_stress.shape[1] * lax.axis_size(("col", "lag"))
    row_blocks = rec_local // tile_side
    alive_mask = (jnp.arange(slots)[None, :] < tile_count[0, 0][:, None]).astype(jnp.float32)
    masked = (contrib * alive_mask[None, :, :, None]).reshape(
        sims_count, lag_local * slots, tile_side
    )
    targets = tile_rows[0, 0].reshape(lag_local * slots)
    placed = (
        jnp.zeros((sims_count, row_blocks, tile_side), jnp.float32).at[:, targets, :].add(masked)
    )
    partial_stress = placed.reshape(sims_count, rec_local)
    owned = base_stress.shape[1]
    summed = lax.psum(partial_stress, ("col", "lag"))
    offset = lax.axis_index(("col", "lag")) * owned
    stress_change = lax.dynamic_slice_in_dim(summed, offset, owned, 1)
    driving = base_stress + stress_change
    factor = jnp.exp(state_var) / 2.0
    velocity = prev_rate
    for step in range(NEWTON):
        scaled = velocity * factor
        misfit = direct_effect * inverse_sinh(scaled) + 0.5 * velocity - driving
        slope = direct_effect * factor / jnp.sqrt(1.0 + scaled * scaled) + 0.5
        velocity = velocity - misfit / slope
    return (stress_change, velocity)


def solution(mesh):
    return jax.shard_map(
        local,
        mesh=mesh,
        in_specs=(
            P("lag", "col", None, "row"),
            P("row", "col", "lag", None, None, None),
            P("row", "col", "lag", None),
            P("row", "col", "lag", None),
            P("row", "col", "lag"),
            P(None, ("row", "col", "lag")),
            P(None, ("row", "col", "lag")),
            P(None, ("row", "col", "lag")),
            P(None, ("row", "col", "lag")),
        ),
        out_specs=(P(None, ("row", "col", "lag")), P(None, ("row", "col", "lag"))),
        check_vma=False,
    )
```

profile of v0, /device:TPU:0, one launch (start us, length us, event | category | flops | bytes accessed | tf_op | source)
XLA Modules:
  0.0 251.7 jit_solution(15460717152722409937)
XLA Ops:
  7.2 0.0 all-gather.2.cloned.1.call-start
  7.2 0.7 all-gather.2.cloned.1.call-update
  7.9 0.0 all-reduce.2.cloned.1.call-start
  7.9 0.8 reshape_squeeze.3
  8.7 0.7 fusion.12
  9.4 90.7 %all-gather.2.cloned.1.call-done = bf16[4,1,128,8192]{3,2,1,0:T(8,128)(2,1)} async-done(((bf16[4,1,128,2048]{3,2,1,0:T(8,128)(2,1)}), bf16[4,1,128,8192]{3,2,1,0:T(8,128)(2,1)}) %all-gather.2.cloned.1.call-update) | async-done | bytes 8388624 | tf_op jit(solution)/shard_map/all_gather | solution.py:25
  100.2 0.0 copy-start.4
  100.2 9.6 %copy.26 = bf16[64,8,32,256]{3,2,1,0:T(8,128)(2,1)} copy(bf16[64,8,32,256]{3,1,2,0:T(8,128)(2,1)} %bitcast.34) | data formatting | bytes 16777216
  109.8 0.0 slice-start
  109.8 0.0 copy-done.4
  109.8 0.0 slice-start.1
  109.8 4.8 %fusion = bf16[4,12,128,256]{3,1,2,0:T(8,128)(2,1)S(1)} fusion(s32[4,12]{1,0:T(4,128)S(1)} %bitcast.35, bf16[4,128,32,256]{3,2,1,0:T(8,128)(2,1)} %bitcast.30), kind=kOutput, calls=%fused_computation.1 | convolution fusion | flops 100664832 | bytes 11534528 | tf_op jit(solution)/shard_map/lkb,lsbj->lksj/dot_general | solution.py:33
  114.6 0.0 slice-done
  114.6 0.4 slice-done.1
  115.0 4.8 %broadcast_multiply_fusion = f32[4,12,128,256]{3,2,1,0:T(8,128)} fusion(f32[4,12]{1,0:T(4,128)S(1)} %fusion.12, bf16[1,1,4,12,256,256]{5,4,3,2,1,0:T(8,128)(2,1)S(1)} %bitcast.33, bf16[4,12,128,256]{3,1,2,0:T(8,128)(2,1)S(1)} %fusion), kind=kOutput, calls=%fused_computation.6 | convolution fusion | flops 806879232 | bytes 15728832 | tf_op jit(solution)/shard_map/lksj,lkij->slki/dot_general | solution.py:36
  119.8 2.5 broadcast_in_dim.4
  122.3 14.6 %scatter_fusion = f32[128,32,256]{2,0,1:T(8,128)} fusion(f32[128,32,256]{2,0,1:T(8,128)} %broadcast_in_dim.4, s32[48]{0:T(128)S(1)} %fusion.13, f32[48,128,256]{2,1,0:T(8,128)} %bitcast.29), kind=kCustom, calls=%fused_computation | custom fusion | flops 1572864 | bytes 18874560 | tf_op jit(solution)/shard_map/scatter-add | solution.py:47
  137.0 0.0 copy-start
  137.0 5.7 %copy.11 = f32[128,32,256]{0,2,1:T(8,128)} copy(f32[128,32,256]{2,0,1:T(8,128)} %scatter_fusion) | data formatting | bytes 8388608 | tf_op jit(solution)/shard_map/scatter-add | solution.py:47
  142.7 0.0 all-reduce.2.cloned.1.call-update
  142.7 0.0 copy-done
  142.8 0.2 copy.12
  142.9 0.0 copy-done.1
  143.0 0.2 copy.14
  143.2 0.0 copy-done.2
  143.2 0.2 copy.16
  143.4 0.0 copy-done.3
  143.4 0.2 copy.18
  143.6 96.0 %all-reduce.2.cloned.1.call-done = f32[128,8192]{0,1:T(8,128)} async-done(((f32[128,8192]{0,1:T(8,128)}), f32[128,8192]{0,1:T(8,128)}) %all-reduce.2.cloned.1.call-update) | async-done | bytes 4194320 | tf_op jit(solution)/shard_map/psum | solution.py:51
  239.6 3.3 %divide_subtract_fusion = (f32[128,1024]{0,1:T(8,128)S(1)}, f32[128,1024]{0,1:T(8,128)S(1)}) fusion(f32[128,1024]{0,1:T(8,128)S(1)} %copy.14, f32[128,1024]{0,1:T(8,128)S(1)} %copy.18, f32[128,1024]{0,1:T(8,128)S(1)} %copy.16, f32[128,1024]{0,1:T(8,128)S(1)} %copy.12, f32[128,8192]{0,1:T(8,128)} %all-reduce.2.cloned.1.call-done, s32[]{:T(128)S(6)} %select_n.14), kind=kLoop, calls=%fused_computation.7 | loop fusion | flops 8257536 | bytes 3670020 | tf_op jit(solution)/shard_map/sub | solution.py:61
  242.9 1.0 copy.22
  243.9 1.0 copy.23
  (5 shorter events, 0.0 us)
Async XLA Ops:
  7.2 93.0 %all-gather.2.cloned.1.call-start = ((), (), s32[]{:S(2)}) async-start(), calls=%async_computation | async-start | bytes 10485760 | tf_op jit(solution)/shard_map/all_gather | solution.py:25
  7.9 231.7 %all-reduce.2.cloned.1.call-start = ((), (), s32[]{:S(2)}) async-start(), calls=%async_computation.1 | async-start | bytes 8388608 | tf_op jit(solution)/shard_map/psum | solution.py:51
  100.2 9.6 %copy-start.4 = (s32[1,1,4,12]{3,2,1,0:T(4,128)S(1)}, s32[1,1,4,12]{3,2,1,0:T(4,128)}, u32[]{:S(2)}) copy-start(s32[1,1,4,12]{3,2,1,0:T(4,128)} %param.12) | copy-start | bytes 580
  109.8 4.8 %slice-start = ((s8[6291456]{0:T(1024)(128)(4,1)}), s8[4194304]{0:T(1024)(128)(4,1)S(1)}, s32[]{:S(2)}) async-start(s8[6291456]{0:T(1024)(128)(4,1)} %bitcast.32), calls=%async_computation.2 | async-start | bytes 8388608
  109.8 5.2 %slice-start.1 = ((s8[6291456]{0:T(1024)(128)(4,1)}), s8[2097152]{0:T(1024)(128)(4,1)S(1)}, s32[]{:S(2)}) async-start(s8[6291456]{0:T(1024)(128)(4,1)} %bitcast.32), calls=%async_computation.3 | async-start | bytes 4194304
  137.0 5.8 %copy-start = (f32[128,1024]{1,0:T(8,128)S(1)}, f32[128,1024]{1,0:T(8,128)}, u32[]{:S(2)}) copy-start(f32[128,1024]{1,0:T(8,128)} %param.17) | copy-start | bytes 1572868
  137.0 6.0 %copy-start.1 = (f32[128,1024]{1,0:T(8,128)S(1)}, f32[128,1024]{1,0:T(8,128)}, u32[]{:S(2)}) copy-start(f32[128,1024]{1,0:T(8,128)} %param.16) | copy-start | bytes 1572868
  137.0 6.2 %copy-start.2 = (f32[128,1024]{1,0:T(8,128)S(1)}, f32[128,1024]{1,0:T(8,128)}, u32[]{:S(2)}) copy-start(f32[128,1024]{1,0:T(8,128)} %param.14) | copy-start | bytes 1572868
  137.0 6.4 %copy-start.3 = (f32[128,1024]{1,0:T(8,128)S(1)}, f32[128,1024]{1,0:T(8,128)}, u32[]{:S(2)}) copy-start(f32[128,1024]{1,0:T(8,128)} %param.15) | copy-start | bytes 1572868
Sparse Core Ops, SparseCore 0:
  9.8 90.2 all-gather.1
  142.9 96.6 all-reduce.1
where the time goes:
time: 252 us
  waiting for transfers between devices  187 us (74%)
  local copies, waits for them, and re-layouts  21.8 us (9%)
  other arithmetic  18.7 us (7%)
  between operations  14.1 us (6%)
  matrix products  9.66 us (4%)
    psum x1, waiting for transfers between devices, local(): summed = lax.psum(partial_stress, ('col', 'lag'))  96 us
    all_gather x1, waiting for transfers between devices, local(): gathered = lax.all_gather(history, 'row', axis=3, tiled=True)  90.7 us
    scatter-add x1, other arithmetic, local(): jnp.zeros((sims_count, row_blocks, tile_side), jnp.float32)  14.6 us
    unnamed x21, local copies, waits for them, and re-layouts  12.7 us
    scatter-add x1, local copies, waits for them, and re-layouts, local(): jnp.zeros((sims_count, row_blocks, tile_side), jnp.float32)  5.75 us
  transfers between devices with their start and end apart: 2, of which 2 were waited for; matrix products, arithmetic and copies ran while one was open for 1% of the time, Pallas kernels for 0%

commit v1 on v0

v1 whole, which is shorter than its diff:
```python
import functools

import jax
import jax.numpy as jnp
from jax import lax
from jax.experimental import pallas as pl
from jax.experimental.pallas import tpu as pltpu
from jax.sharding import PartitionSpec as P

NEWTON = 4
CAP = 16
PAD = 16
VMEM_LIMIT = 48 * 1024 * 1024
ANY = pl.BlockSpec(memory_space=pl.ANY)
SMEM = pl.BlockSpec(memory_space=pltpu.SMEM)


def inverse_sinh(value):
    magnitude = jnp.abs(value)
    length = jnp.log(magnitude + jnp.sqrt(1.0 + magnitude * magnitude))
    return jnp.where(value < 0.0, -length, length)


def friction(stress, base, velocity, direct, state):
    driving = base + stress
    factor = jnp.exp(state) / 2.0
    gain = direct * factor
    for step in range(NEWTON):
        scaled = velocity * factor
        misfit = direct * inverse_sinh(scaled) + 0.5 * velocity - driving
        slope = gain / jnp.sqrt(1.0 + scaled * scaled) + 0.5
        velocity = velocity - misfit / slope
    return velocity


def partners(size, step):
    return [(index, index ^ step) for index in range(size)]


def pack_kernel(cap, row_ref, *refs):
    peers = (len(refs) - 2) // 2
    needs, history, packed, sems = refs[:peers], refs[peers], refs[peers + 1 : -1], refs[-1]
    lags, _, sims, width = history.shape
    side = packed[0].shape[2]
    local_blocks = width // side
    total = needs[0].shape[0] // lags
    first = row_ref[0] * local_blocks
    counts = []
    for peer in range(peers):

        def visit(step, position, peer=peer):
            lag = step // local_blocks
            block = step % local_blocks
            wanted = jnp.logical_and(
                needs[peer][lag * total + first + block] > 0, position < cap
            )

            @pl.when(wanted)
            def _():
                pltpu.make_async_copy(
                    history.at[lag, 0, :, pl.ds(pl.multiple_of(block * side, side), side)],
                    packed[peer].at[position],
                    sems.at[peer, position],
                ).start()

            return position + wanted.astype(jnp.int32)

        counts.append(lax.fori_loop(0, lags * local_blocks, visit, jnp.int32(0)))
    for peer in range(peers):

        def settle(position, carry, peer=peer):
            pltpu.make_async_copy(
                history.at[0, 0, :, pl.ds(0, side)], packed[peer].at[position], sems.at[peer, position]
            ).wait()
            return carry

        lax.fori_loop(0, counts[peer], settle, 0)


def pack(row, needs, history, side, cap):
    sims = history.shape[2]
    return pl.pallas_call(
        functools.partial(pack_kernel, cap),
        out_shape=[jax.ShapeDtypeStruct((cap, sims, side), history.dtype)] * len(needs),
        in_specs=[SMEM] * (1 + len(needs)) + [ANY],
        out_specs=[ANY] * len(needs),
        scratch_shapes=[pltpu.SemaphoreType.DMA((len(needs), cap))],
        compiler_params=pltpu.CompilerParams(vmem_limit_bytes=VMEM_LIMIT),
        name="pack_history",
    )(row, *needs, history)


def tiles_kernel(cap, where_ref, cols, rows, counts, places, *refs):
    kept, given, blocks, weights, sums, block_sems, weight_sems, out_sems = refs[-8:]
    tiles, history, received = refs[0], refs[1], refs[2:-8]
    _, _, lags, slots, side, _ = tiles.shape
    local_blocks = history.shape[3] // side
    total = places.shape[0] // lags
    _, col_size, per_owner, sims, _ = sums.shape
    row, core = where_ref[0], where_ref[1]

    def copies(lag, slot):
        index = lag * slots + slot
        col = cols[index]
        relative = lax.bitwise_xor(col // local_blocks, row)
        place = jnp.minimum(places[lag * total + col], cap - 1)
        local = pl.multiple_of((col % local_blocks) * side, side)
        return index, relative, place, local

    for lag in range(lags):

        def begin(slot, carry, lag=lag):
            index, relative, place, local = copies(lag, slot)
            pltpu.make_async_copy(
                tiles.at[0, 0, lag, slot], weights.at[index], weight_sems.at[index]
            ).start()

            @pl.when(relative == 0)
            def _():
                pltpu.make_async_copy(
                    history.at[lag, 0, :, pl.ds(local, side)], blocks.at[index], block_sems.at[index]
                ).start()

            for peer in range(len(received)):

                @pl.when(relative == peer + 1)
                def _(peer=peer):
                    pltpu.make_async_copy(
                        received[peer].at[place], blocks.at[index], block_sems.at[index]
                    ).start()

            return carry

        lax.fori_loop(0, counts[lag], begin, 0)
    sums[...] = jnp.zeros_like(sums)
    for lag in range(lags):

        def multiply(slot, carry, lag=lag):
            index = lag * slots + slot
            pltpu.make_async_copy(
                tiles.at[0, 0, lag, slot], weights.at[index], weight_sems.at[index]
            ).wait()
            pltpu.make_async_copy(
                history.at[lag, 0, :, pl.ds(0, side)], blocks.at[index], block_sems.at[index]
            ).wait()
            owner = rows[index] // per_owner
            other = lax.bitwise_xor(owner % 2, core)
            spot = (other, owner // 2, rows[index] % per_owner)
            sums[spot] += lax.dot_general(
                blocks[index],
                weights[index],
                (((1,), (1,)), ((), ())),
                preferred_element_type=jnp.float32,
            )
            return carry

        lax.fori_loop(0, counts[lag], multiply, 0)
    to_give = pltpu.make_async_copy(sums.at[1], given, out_sems.at[0])
    to_keep = pltpu.make_async_copy(sums.at[0], kept, out_sems.at[1])
    to_give.start()
    to_keep.start()
    to_give.wait()
    to_keep.wait()


def multiply_tiles(where, cols, rows, counts, places, tiles, history, received, col_size, per_owner, cap):
    _, _, lags, slots, side, _ = tiles.shape
    sims = history.shape[2]
    half = jax.ShapeDtypeStruct((col_size, per_owner, sims, side), jnp.float32)
    count = lags * slots
    return pl.pallas_call(
        functools.partial(tiles_kernel, cap),
        out_shape=[half, half],
        in_specs=[SMEM] * 5 + [ANY] * (2 + len(received)),
        out_specs=[ANY, ANY],
        scratch_shapes=[
            pltpu.VMEM((count, sims, side), history.dtype),
            pltpu.VMEM((count, side, side), tiles.dtype),
            pltpu.VMEM((2,) + half.shape, jnp.float32),
            pltpu.SemaphoreType.DMA((count,)),
            pltpu.SemaphoreType.DMA((count,)),
            pltpu.SemaphoreType.DMA((2,)),
        ],
        compiler_params=pltpu.CompilerParams(vmem_limit_bytes=VMEM_LIMIT),
        name="multiply_tiles",
    )(where, cols, rows, counts, places, tiles, history, *received)


def code_kernel(col_ref, kept, got, *refs):
    left, right, staged, total, in_sems, out_sems, own_sem = refs[-7:]
    own, coded = refs[0], refs[1:-7]
    col_size, per_owner, sims, side = kept.shape
    col = col_ref[0]
    reads = []
    for step in list(range(1, col_size)) + [0]:
        chunk = lax.bitwise_xor(col, step)
        pair = (
            pltpu.make_async_copy(kept.at[chunk], left.at[step], in_sems.at[0, step]),
            pltpu.make_async_copy(got.at[chunk], right.at[step], in_sems.at[1, step]),
        )
        for copy in pair:
            copy.start()
        reads.append((step, pair))
    writes = []
    for step, pair in reads:
        for copy in pair:
            copy.wait()
        if step == 0:
            total[...] = left[0] + right[0]
            writes.append(pltpu.make_async_copy(total, own, own_sem))
        else:
            slot = step - 1
            exponents = []
            for block in range(per_owner):
                value = left[step, block] + right[step, block]
                largest = jnp.maximum(jnp.max(jnp.abs(value), axis=0, keepdims=True), 1e-30)
                exponent = jnp.ceil(jnp.log2(largest))
                grid = jnp.clip(jnp.round(value * jnp.exp2(15.0 - exponent)), -32767.0, 32767.0)
                staged[slot, pl.ds(block * sims, sims), :] = grid.astype(jnp.int32).astype(jnp.int16)
                exponents.append(exponent)
            if per_owner < PAD:
                exponents.append(jnp.zeros((PAD - per_owner, side), jnp.float32))
            rows = jnp.concatenate(exponents, axis=0)
            staged[slot, pl.ds(per_owner * sims, PAD), :] = rows.astype(jnp.int32).astype(jnp.int16)
            writes.append(pltpu.make_async_copy(staged.at[slot], coded[slot], out_sems.at[slot]))
        writes[-1].start()
    for copy in writes:
        copy.wait()


def code(col, kept, got):
    col_size, per_owner, sims, side = kept.shape
    rows = per_owner * sims + PAD
    chunk = jax.ShapeDtypeStruct((rows, side), jnp.int16)
    return pl.pallas_call(
        code_kernel,
        out_shape=[jax.ShapeDtypeStruct(kept.shape[1:], jnp.float32)] + [chunk] * (col_size - 1),
        in_specs=[SMEM, ANY, ANY],
        out_specs=[ANY] * col_size,
        scratch_shapes=[
            pltpu.VMEM(kept.shape, jnp.float32),
            pltpu.VMEM(kept.shape, jnp.float32),
            pltpu.VMEM((col_size - 1, rows, side), jnp.int16),
            pltpu.VMEM(kept.shape[1:], jnp.float32),
            pltpu.SemaphoreType.DMA((2, col_size)),
            pltpu.SemaphoreType.DMA((col_size - 1,)),
            pltpu.SemaphoreType.DMA,
        ],
        compiler_params=pltpu.CompilerParams(vmem_limit_bytes=VMEM_LIMIT),
        name="add_and_code",
    )(col, kept, got)


def solve_kernel(per_owner, *refs):
    base, rate, direct, state, own = refs[:5]
    stress_out, rate_out = refs[-2:]
    codes = refs[5:-2]
    block = pl.program_id(0)
    stress = own[0]
    for index in range(len(codes) // 2):
        values, exponents = codes[2 * index], codes[2 * index + 1]
        powers = exponents[...].astype(jnp.int32).astype(jnp.float32)
        chosen = lax.broadcasted_iota(jnp.int32, powers.shape, 0) == block
        power = jnp.sum(jnp.where(chosen, powers, 0.0), axis=0, keepdims=True)
        stress = stress + values[...].astype(jnp.int32).astype(jnp.float32) * jnp.exp2(power - 15.0)
    stress_out[...] = stress
    rate_out[...] = friction(stress, base[...], rate[...], direct[...], state[...])


def solve(base, rate, direct, state, own, coded):
    per_owner, sims, side = own.shape
    wide = pl.BlockSpec((sims, side), lambda block: (0, block))
    specs = [wide] * 4 + [pl.BlockSpec((1, sims, side), lambda block: (block, 0, 0))]
    operands = [base, rate, direct, state, own]
    behind = per_owner * sims // PAD
    for chunk in coded:
        specs += [
            pl.BlockSpec((sims, side), lambda block: (block, 0)),
            pl.BlockSpec((PAD, side), lambda block: (behind, 0)),
        ]
        operands += [chunk, chunk]
    return pl.pallas_call(
        functools.partial(solve_kernel, per_owner),
        grid=(per_owner,),
        out_shape=[jax.ShapeDtypeStruct(base.shape, jnp.float32)] * 2,
        in_specs=specs,
        out_specs=[wide, wide],
        compiler_params=pltpu.CompilerParams(vmem_limit_bytes=VMEM_LIMIT),
        name="friction_solve",
    )(*operands)


def general(history, kernel_tiles, tile_rows, tile_cols, tile_count, base_stress, prev_rate, direct_effect, state_var):
    gathered = lax.all_gather(history, "row", axis=3, tiled=True)
    lag_local = gathered.shape[0]
    sims_count = gathered.shape[2]
    tile_side = kernel_tiles.shape[4]
    slots = kernel_tiles.shape[3]
    col_blocks = gathered.shape[3] // tile_side
    blocks = gathered.reshape(lag_local, sims_count, col_blocks, tile_side)
    choose = jax.nn.one_hot(tile_cols[0, 0], col_blocks, dtype=jnp.bfloat16)
    picked = jnp.einsum(
        "lkb,lsbj->lksj", choose, blocks, preferred_element_type=jnp.float32
    ).astype(jnp.bfloat16)
    contrib = jnp.einsum(
        "lksj,lkij->slki", picked, kernel_tiles[0, 0], preferred_element_type=jnp.float32
    )
    owned = base_stress.shape[1]
    rec_local = owned * lax.axis_size(("col", "lag"))
    row_blocks = rec_local // tile_side
    alive_mask = (jnp.arange(slots)[None, :] < tile_count[0, 0][:, None]).astype(jnp.float32)
    masked = (contrib * alive_mask[None, :, :, None]).reshape(
        sims_count, lag_local * slots, tile_side
    )
    targets = tile_rows[0, 0].reshape(lag_local * slots)
    placed = (
        jnp.zeros((sims_count, row_blocks, tile_side), jnp.float32).at[:, targets, :].add(masked)
    )
    summed = lax.psum(placed.reshape(sims_count, rec_local), ("col", "lag"))
    offset = lax.axis_index(("col", "lag")) * owned
    stress = lax.dynamic_slice_in_dim(summed, offset, owned, 1)
    return stress, friction(stress, base_stress, prev_rate, direct_effect, state_var)


def local(history, kernel_tiles, tile_rows, tile_cols, tile_count, base_stress, prev_rate, direct_effect, state_var):
    _, _, lags, slots, side, _ = kernel_tiles.shape
    row_size, col_size, core_size = (lax.axis_size(axis) for axis in ("row", "col", "lag"))
    row, col, core = (lax.axis_index(axis).astype(jnp.int32) for axis in ("row", "col", "lag"))
    local_blocks = history.shape[3] // side
    total = row_size * local_blocks
    per_owner = base_stress.shape[1] // side
    cap = min(CAP, lags * local_blocks)

    live = jnp.arange(slots)[None, :] < tile_count[0, 0][:, None]
    hits = (tile_cols[0, 0][:, :, None] == jnp.arange(total)[None, None, :]) & live[:, :, None]
    need = jnp.any(hits, axis=1).astype(jnp.int32)
    request = need.reshape(lags * total)
    requests = [lax.ppermute(request, "row", partners(row_size, step)) for step in range(1, row_size)]
    packed = pack(row[None], requests, history, side, cap)
    received = [
        lax.ppermute(packed[step - 1], "row", partners(row_size, step)) for step in range(1, row_size)
    ]

    by_owner = need.reshape(lags, row_size, local_blocks).transpose(1, 0, 2).reshape(row_size, -1)
    before = jnp.arange(lags * local_blocks)
    places = jnp.sum(
        jnp.where(before[None, None, :] < before[None, :, None], by_owner[:, None, :], 0), axis=2
    )
    places = places.reshape(row_size, lags, local_blocks).transpose(1, 0, 2).reshape(lags * total)
    elsewhere = jnp.arange(row_size) != row
    over = jnp.any((jnp.sum(by_owner, axis=1) > cap) & elsewhere)
    overflow = lax.pmax(over.astype(jnp.float32), ("row", "col", "lag"))

    kept, given = multiply_tiles(
        jnp.stack([row, core]),
        tile_cols.reshape(-1),
        tile_rows.reshape(-1),
        tile_count.reshape(-1),
        places,
        kernel_tiles,
        history,
        received,
        col_size,
        per_owner,
        cap,
    )
    got = lax.ppermute(given, "lag", partners(core_size, 1))
    own, *coded = code(col[None], kept, got)
    arrived = [
        lax.ppermute(coded[step - 1], "col", partners(col_size, step)) for step in range(1, col_size)
    ]
    stress, rate = solve(base_stress, prev_rate, direct_effect, state_var, own, arrived)
    return lax.cond(
        overflow > 0.0,
        lambda: general(
            history, kernel_tiles, tile_rows, tile_cols, tile_count, base_stress, prev_rate, direct_effect, state_var
        ),
        lambda: (stress, rate),
    )


def solution(mesh):
    return jax.shard_map(
        local,
        mesh=mesh,
        in_specs=(
            P("lag", "col", None, "row"),
            P("row", "col", "lag", None, None, None),
            P("row", "col", "lag", None),
            P("row", "col", "lag", None),
            P("row", "col", "lag"),
            P(None, ("row", "col", "lag")),
            P(None, ("row", "col", "lag")),
            P(None, ("row", "col", "lag")),
            P(None, ("row", "col", "lag")),
        ),
        out_specs=(P(None, ("row", "col", "lag")), P(None, ("row", "col", "lag"))),
        check_vma=False,
    )
```

time: 252 us -> 200 us (0.79)
  waiting for transfers between devices: 187 us -> 50.8 us
  Pallas kernels: 0 us -> 60.5 us
  blocking collectives: 0 us -> 45.1 us
  starting transfers between devices: 0.08 us -> 18.7 us
  other arithmetic: 18.7 us -> 1.78 us
  local copies, waits for them, and re-layouts: 21.8 us -> 8.84 us
  matrix products: 9.66 us -> 0 us
    psum x1 -> x0, waiting for transfers between devices: 96 us -> none  [local(): summed = lax.psum(partial_stress, ('col', 'lag'))]
    all_gather x1 -> x0, waiting for transfers between devices: 90.7 us -> none  [local(): gathered = lax.all_gather(history, 'row', axis=3, tiled=True)]
    pallas_call x0 -> x4, Pallas kernels: none -> 60.5 us  [the longest x1 41.9 us: pack(): pl.pallas_call(functools.partial(pack_kernel, cap), out_shape=[jax.ShapeD...]
    ppermute x0 -> x10, waiting for transfers between devices: none -> 50.8 us  [the longest x3 41.9 us: local(): lax.ppermute(packed[step - 1], 'row', partners(row_size, step))]
    pmax x0 -> x1, blocking collectives: none -> 45.1 us  [local(): overflow = lax.pmax(over.astype(jnp.float32), ('row', 'col', 'lag'))]
    ppermute x0 -> x10, starting transfers between devices: none -> 18.7 us  [the longest x3 10.6 us: local(): lax.ppermute(coded[step - 1], 'col', partners(col_size, step))]
    scatter-add x1 -> x0, other arithmetic: 14.6 us -> none  [local(): jnp.zeros((sims_count, row_blocks, tile_side), jnp.float32)]
    dot_general x2 -> x0, matrix products: 9.66 us -> none  [the longest x1 4.83 us: local(): jnp.einsum('lksj,lkij->slki', picked, kernel_tiles[0, 0], preferred_eleme...]
  transfers between devices with their start and end apart: 2 -> 10, of which waited for: 2 -> 6; matrix products, arithmetic and copies ran while one was open for 1% -> 1% of each run, Pallas kernels for 0% -> 0%
where the time goes in v1:
time: 200 us; the launch traced here: 201 us
  Pallas kernels  60.5 us (30%)
  waiting for transfers between devices  50.8 us (25%)
  blocking collectives  45.1 us (23%)
  starting transfers between devices  18.7 us (9%)
  between operations  15.5 us (8%)
  local copies, waits for them, and re-layouts  8.84 us (4%)
    pmax x1, blocking collectives, local(): overflow = lax.pmax(over.astype(jnp.float32), ('row', 'col', 'lag'))  45.1 us
    pallas_call x1, Pallas kernels, pack(): pl.pallas_call(functools.partial(pack_kernel, cap), out_shape=[jax.ShapeD...  41.9 us
    ppermute x3, waiting for transfers between devices, local(): lax.ppermute(packed[step - 1], 'row', partners(row_size, step))  41.9 us
    pallas_call x1, Pallas kernels, multiply_tiles(): pl.pallas_call(functools.partial(tiles_kernel, cap), out_shape=[half, hal...  12 us
    ppermute x3, starting transfers between devices, local(): lax.ppermute(coded[step - 1], 'col', partners(col_size, step))  10.6 us
    unnamed x18, local copies, waits for them, and re-layouts  6.01 us
    pallas_call x1, Pallas kernels, solve(): pl.pallas_call(functools.partial(solve_kernel, per_owner), grid=(per_owne...  4.83 us
    ppermute x3, starting transfers between devices, local(): lax.ppermute(request, 'row', partners(row_size, step))  4.48 us
  transfers between devices with their start and end apart: 10, of which 6 were waited for; matrix products, arithmetic and copies ran while one was open for 1% of the time, Pallas kernels for 0%

profile of v1, /device:TPU:0, one launch (start us, length us, event | category | flops | bytes accessed | tf_op | source)
XLA Modules:
  0.0 201.3 jit_solution(1109388952633799718)
XLA Ops:
  7.2 0.7 iota_compare_fusion.4
  7.8 0.8 copy.30
  8.8 2.9 %collective-permute-start = (s32[128]{0:T(128)S(1)}, s32[128]{0:T(128)S(1)}, u32[]{:S(2)}, u32[]{:S(2)}) collective-permute-start(s32[128]{0:T(128)S(1)} %reshape.133), channel_id=1, source_target_pairs={{0,8},{8,0},{16,24},{24,16},{1,9},{9,1},{17,25},{25,17},{2,10},{10... | collective-permute-start | bytes 1544 | tf_op jit(solution)/shard_map/ppermute | solution.py:338
  11.7 1.5 collective-permute-start.1
  13.3 2.0 collective-permute-done.1.refs_1_
  15.3 2.4 %collective-permute-done.2.refs_2_ = s32[128]{0:T(128)S(1)} collective-permute-done((s32[128]{0:T(128)S(1)}, s32[128]{0:T(128)S(1)}, u32[]{:S(2)}, u32[]{:S(2)}) %collective-permute-start.2) | collective-permute-done | bytes 544 | tf_op jit(solution)/shard_map/ppermute | solution.py:338
  17.7 41.9 %pack_history.1 = (bf16[16,128,256]{2,1,0:T(8,128)(2,1)}, bf16[16,128,256]{2,1,0:T(8,128)(2,1)}, bf16[16,128,256]{2,1,0:T(8,128)(2,1)}) custom-call(s32[1]{0:T(128)} %bitcast.14.row_ref, s32[128]{0:T(128)S(1)} %collective-permute-done.refs_0_, s32[128]{0:T(128)S(1)} %collective-permute-done.1.refs_1_, s32[128]{0:T(128)S(1)} %collective-permute-done.2.refs_2_, ...), custom_call_target="tpu_custom_call" | custom-call | tf_op jit(solution)/shard_map/pack_history/pallas_call | solution.py:82
  59.7 0.6 collective-permute-start.4
  60.3 2.8 %collective-permute-start.5 = (bf16[16,128,256]{2,1,0:T(8,128)(2,1)}, bf16[16,128,256]{2,1,0:T(8,128)(2,1)S(1)}, u32[]{:S(2)}, u32[]{:S(2)}) collective-permute-start(bf16[16,128,256]{2,1,0:T(8,128)(2,1)} %get-tuple-element.44), channel_id=1, source_target_pairs={{0,24},{8,16},{16,8},{24,0},{1,25},{9,17},{17,9},{25,1},{2,26},{10... | collective-permute-start | bytes 3145736 | tf_op jit(solution)/shard_map/ppermute | solution.py:341
  63.2 0.8 reshape.128.cols
  64.1 0.1 select_reduce_fusion
  64.3 0.1 reshape.131.places
  64.4 0.8 reshape.129.rows
  65.3 19.6 %collective-permute-done.3.refs_2_ = bf16[16,128,256]{2,1,0:T(8,128)(2,1)S(1)} collective-permute-done((bf16[16,128,256]{2,1,0:T(8,128)(2,1)}, bf16[16,128,256]{2,1,0:T(8,128)(2,1)S(1)}, u32[]{:S(2)}, u32[]{:S(2)}) %collective-permute-start.3) | collective-permute-done | bytes 1048608 | tf_op jit(solution)/shard_map/ppermute | solution.py:341
  84.9 1.0 copy-done
  85.9 22.2 %collective-permute-done.5.refs_4_ = bf16[16,128,256]{2,1,0:T(8,128)(2,1)S(1)} collective-permute-done((bf16[16,128,256]{2,1,0:T(8,128)(2,1)}, bf16[16,128,256]{2,1,0:T(8,128)(2,1)S(1)}, u32[]{:S(2)}, u32[]{:S(2)}) %collective-permute-start.5) | collective-permute-done | bytes 1048608 | tf_op jit(solution)/shard_map/ppermute | solution.py:341
  108.1 1.0 copy-done.2
  109.1 1.2 copy-done.1
  110.3 1.2 copy-done.3
  111.5 12.0 %multiply_tiles.1 = (f32[4,4,128,256]{3,2,1,0:T(8,128)S(1)}, f32[4,4,128,256]{3,2,1,0:T(8,128)}) custom-call(s32[2]{0:T(128)S(1)} %pad_add_fusion.where_ref, s32[48]{0:T(128)S(1)} %reshape.128.cols, s32[48]{0:T(128)S(1)} %reshape.129.rows, s32[4]{0:T(128)} %bitcast.52, s32[128]{0:T(128)S(1)} %reshape.131.places, bf16[1,1,4,12,256,256]{5,4,3,2,1,0:T(8,128)(2,1)} %refs_0_.2, ...), custom_call_target="tpu_custom_call" | custom-call | tf_op jit(solution)/shard_map/multiply_tiles/pallas_call | solution.py:171
  123.7 4.5 %collective-permute-done.6.got = f32[4,4,128,256]{3,2,1,0:T(8,128)} collective-permute-done((f32[4,4,128,256]{3,2,1,0:T(8,128)}, f32[4,4,128,256]{3,2,1,0:T(8,128)}, u32[]{:S(2)}, u32[]{:S(2)}) %collective-permute-start.6) | collective-permute-done | bytes 2097184 | tf_op jit(solution)/shard_map/ppermute | solution.py:367
  128.1 1.8 add_and_code.1
  129.9 1.9 collective-permute-start.7
  131.9 7.2 %collective-permute-start.8 = (s16[528,256]{1,0:T(8,128)(2,1)S(1)}, s16[528,256]{1,0:T(8,128)(2,1)S(1)}, u32[]{:S(2)}, u32[]{:S(2)}) collective-permute-start(s16[528,256]{1,0:T(8,128)(2,1)S(1)} %get-tuple-element.49), channel_id=1, source_target_pairs={{0,4},{2,6},{4,0},{6,2},{1,5},{3,7},{5,1},{7,3},{8,12},{10,14},{12... | collective-permute-start | bytes 811016 | tf_op jit(solution)/shard_map/ppermute | solution.py:370
  139.1 1.4 collective-permute-start.9
  140.6 0.1 reduce_sum.27
  140.7 0.6 and_reduce_fusion
  142.0 45.1 %pmax.7 = f32[]{:T(128)} all-reduce(f32[]{:T(128)S(6)} %convert_element_type.33), channel_id=1, replica_groups=mesh['row'=4,'col'=4,'lag'=2] {'row','col','lag'}, use_global_device_ids=true, to_apply=%region_4.5 | all-reduce | flops 1 | bytes 8 | tf_op jit(solution)/shard_map/pmax | solution.py:352
  187.8 4.8 %friction_solve.1 = (f32[128,1024]{1,0:T(8,128)S(1)}, f32[128,1024]{1,0:T(8,128)S(1)}) custom-call(f32[128,1024]{1,0:T(8,128)} %refs_0_.3, f32[128,1024]{1,0:T(8,128)} %refs_1_.3, f32[128,1024]{1,0:T(8,128)} %refs_2_.1, f32[128,1024]{1,0:T(8,128)} %refs_3_.3, f32[4,128,256]{2,1,0:T(8,128)S(1)} %get-tuple-element.47.refs_4_, ...), custom_call_target="tpu_custom_call" | custom-call | tf_op jit(solution)/shard_map/friction_solve/pallas_call | solution.py:282
  192.7 0.2 conditional.1
  192.9 0.8 copy-done.11
  193.7 0.8 copy-done.12
  (32 shorter events, 0.9 us)
Async XLA Ops:
  8.8 4.5 %collective-permute-start = (s32[128]{0:T(128)S(1)}, s32[128]{0:T(128)S(1)}, u32[]{:S(2)}, u32[]{:S(2)}) collective-permute-start(s32[128]{0:T(128)S(1)} %reshape.133), channel_id=1, source_target_pairs={{0,8},{8,0},{16,24},{24,16},{1,9},{9,1},{17,25},{25,17},{2,10},{10... | collective-permute-start | bytes 1544 | tf_op jit(solution)/shard_map/ppermute | solution.py:338
  11.7 3.5 %collective-permute-start.1 = (s32[128]{0:T(128)S(1)}, s32[128]{0:T(128)S(1)}, u32[]{:S(2)}, u32[]{:S(2)}) collective-permute-start(s32[128]{0:T(128)S(1)} %reshape.133), channel_id=1, source_target_pairs={{0,16},{8,24},{16,0},{24,8},{1,17},{9,25},{17,1},{25,9},{2,18},{10... | collective-permute-start | bytes 1544 | tf_op jit(solution)/shard_map/ppermute | solution.py:338
  13.3 4.4 %collective-permute-start.2 = (s32[128]{0:T(128)S(1)}, s32[128]{0:T(128)S(1)}, u32[]{:S(2)}, u32[]{:S(2)}) collective-permute-start(s32[128]{0:T(128)S(1)} %reshape.133), channel_id=1, source_target_pairs={{0,24},{8,16},{16,8},{24,0},{1,25},{9,17},{17,9},{25,1},{2,26},{10... | collective-permute-start | bytes 1544 | tf_op jit(solution)/shard_map/ppermute | solution.py:338
  59.6 25.2 %collective-permute-start.3 = (bf16[16,128,256]{2,1,0:T(8,128)(2,1)}, bf16[16,128,256]{2,1,0:T(8,128)(2,1)S(1)}, u32[]{:S(2)}, u32[]{:S(2)}) collective-permute-start(bf16[16,128,256]{2,1,0:T(8,128)(2,1)} %get-tuple-element.42), channel_id=1, source_target_pairs={{0,8},{8,0},{16,24},{24,16},{1,9},{9,1},{17,25},{25,17},{2,10},{10... | collective-permute-start | bytes 3145736 | tf_op jit(solution)/shard_map/ppermute | solution.py:341
  59.7 25.2 %collective-permute-start.4 = (bf16[16,128,256]{2,1,0:T(8,128)(2,1)}, bf16[16,128,256]{2,1,0:T(8,128)(2,1)S(1)}, u32[]{:S(2)}, u32[]{:S(2)}) collective-permute-start(bf16[16,128,256]{2,1,0:T(8,128)(2,1)} %get-tuple-element.43), channel_id=1, source_target_pairs={{0,16},{8,24},{16,0},{24,8},{1,17},{9,25},{17,1},{25,9},{2,18},{10... | collective-permute-start | bytes 3145736 | tf_op jit(solution)/shard_map/ppermute | solution.py:341
  60.3 47.8 %collective-permute-start.5 = (bf16[16,128,256]{2,1,0:T(8,128)(2,1)}, bf16[16,128,256]{2,1,0:T(8,128)(2,1)S(1)}, u32[]{:S(2)}, u32[]{:S(2)}) collective-permute-start(bf16[16,128,256]{2,1,0:T(8,128)(2,1)} %get-tuple-element.44), channel_id=1, source_target_pairs={{0,24},{8,16},{16,8},{24,0},{1,25},{9,17},{17,9},{25,1},{2,26},{10... | collective-permute-start | bytes 3145736 | tf_op jit(solution)/shard_map/ppermute | solution.py:341
  84.9 1.0 copy-start
  108.1 1.0 copy-start.2
  109.1 1.2 copy-start.1
  110.3 1.2 copy-start.3
  123.5 64.3 %copy-start.8 = (s32[1,1,4,12]{3,2,1,0:T(4,128)S(1)}, s32[1,1,4,12]{3,2,1,0:T(4,128)}, u32[]{:S(2)}) copy-start(s32[1,1,4,12]{3,2,1,0:T(4,128)} %param.14) | copy-start | bytes 580
  123.6 64.3 %copy-start.9 = (s32[1,1,4,12]{3,2,1,0:T(4,128)S(1)}, s32[1,1,4,12]{3,2,1,0:T(4,128)}, u32[]{:S(2)}) copy-start(s32[1,1,4,12]{3,2,1,0:T(4,128)} %param.13) | copy-start | bytes 580
  123.6 64.3 %copy-start.10 = (s32[1,1,4]{2,1,0:T(1,128)S(1)}, s32[1,1,4]{2,1,0:T(1,128)}, u32[]{:S(2)}) copy-start(s32[1,1,4]{2,1,0:T(1,128)} %param.15) | copy-start | bytes 52
  123.6 4.6 %collective-permute-start.6 = (f32[4,4,128,256]{3,2,1,0:T(8,128)}, f32[4,4,128,256]{3,2,1,0:T(8,128)}, u32[]{:S(2)}, u32[]{:S(2)}) collective-permute-start(f32[4,4,128,256]{3,2,1,0:T(8,128)} %get-tuple-element.46), channel_id=1, source_target_pairs={{0,1},{1,0},{2,3},{3,2},{4,5},{5,4},{6,7},{7,6},{8,9},{9,8},{10,11... | collective-permute-start | bytes 6291464 | tf_op jit(solution)/shard_map/ppermute | solution.py:367
  129.9 57.8 %collective-permute-start.7 = (s16[528,256]{1,0:T(8,128)(2,1)S(1)}, s16[528,256]{1,0:T(8,128)(2,1)S(1)}, u32[]{:S(2)}, u32[]{:S(2)}) collective-permute-start(s16[528,256]{1,0:T(8,128)(2,1)S(1)} %get-tuple-element.48), channel_id=1, source_target_pairs={{0,2},{2,0},{4,6},{6,4},{1,3},{3,1},{5,7},{7,5},{8,10},{10,8},{12,... | collective-permute-start | bytes 811016 | tf_op jit(solution)/shard_map/ppermute | solution.py:370
  131.9 55.9 %collective-permute-start.8 = (s16[528,256]{1,0:T(8,128)(2,1)S(1)}, s16[528,256]{1,0:T(8,128)(2,1)S(1)}, u32[]{:S(2)}, u32[]{:S(2)}) collective-permute-start(s16[528,256]{1,0:T(8,128)(2,1)S(1)} %get-tuple-element.49), channel_id=1, source_target_pairs={{0,4},{2,6},{4,0},{6,2},{1,5},{3,7},{5,1},{7,3},{8,12},{10,14},{12... | collective-permute-start | bytes 811016 | tf_op jit(solution)/shard_map/ppermute | solution.py:370
  139.1 48.7 %collective-permute-start.9 = (s16[528,256]{1,0:T(8,128)(2,1)S(1)}, s16[528,256]{1,0:T(8,128)(2,1)S(1)}, u32[]{:S(2)}, u32[]{:S(2)}) collective-permute-start(s16[528,256]{1,0:T(8,128)(2,1)S(1)} %get-tuple-element.50), channel_id=1, source_target_pairs={{0,6},{2,4},{4,2},{6,0},{1,7},{3,5},{5,3},{7,1},{8,14},{10,12},{12... | collective-permute-start | bytes 811016 | tf_op jit(solution)/shard_map/ppermute | solution.py:370
  192.9 0.8 copy-start.11
  193.7 0.8 copy-start.12

commit v2 on v0

v2 whole, which is shorter than its diff:
```python
import functools
import math

import jax
import jax.numpy as jnp
from jax import lax
from jax.experimental import pallas as pl
from jax.experimental.pallas import tpu as pltpu
from jax.sharding import PartitionSpec as P

NEWTON = 4
CAP = 16
FIRST = 4
PAD = 16
LANES = 128
GROUP = 4
ANY = pl.BlockSpec(memory_space=pl.ANY)
SMEM = pl.BlockSpec(memory_space=pltpu.SMEM)
VMEM = pl.BlockSpec(memory_space=pltpu.VMEM)


def params(*shapes):
    held = sum(math.prod(s.shape) * jnp.dtype(s.dtype).itemsize for s in shapes)
    return pltpu.CompilerParams(vmem_limit_bytes=held + 8 * 1024 * 1024)


def partners(size, step):
    return [(index, index ^ step) for index in range(size)]


def inverse_sinh(value, root):
    length = jnp.log(jnp.abs(value) + root)
    return jnp.where(value < 0.0, -length, length)


def friction(stress, base, velocity, direct, state):
    driving = base + stress
    factor = jnp.exp(state) / 2.0
    gain = direct * factor
    for step in range(NEWTON):
        scaled = velocity * factor
        root = jnp.sqrt(1.0 + scaled * scaled)
        misfit = direct * inverse_sinh(scaled, root) + 0.5 * velocity - driving
        velocity = velocity - misfit / (gain / root + 0.5)
    return velocity


def request_kernel(cols, counts, need):
    lags, total = need.shape
    slots = cols.shape[3]
    names = lax.broadcasted_iota(jnp.int32, (1, total), 1)
    for lag in range(lags):
        marks = jnp.zeros((1, total), jnp.int32)
        for slot in range(slots):
            marks = jnp.where(
                (names == cols[0, 0, lag, slot]) & (slot < counts[0, 0, lag]), 1, marks
            )
        need[lag : lag + 1, :] = marks


def make_request(cols, counts, total):
    return pl.pallas_call(
        request_kernel,
        out_shape=jax.ShapeDtypeStruct((cols.shape[2], total), jnp.int32),
        in_specs=[SMEM, SMEM],
        out_specs=VMEM,
        name="mark_blocks",
    )(cols, counts)


def load_kernel(history, held, sem):
    copy = pltpu.make_async_copy(history, held, sem)
    copy.start()
    copy.wait()


def load(history):
    return pl.pallas_call(
        load_kernel,
        out_shape=history,
        in_specs=[ANY],
        out_specs=VMEM,
        scratch_shapes=[pltpu.SemaphoreType.DMA],
        compiler_params=params(history),
        name="load_history",
    )(history)


def pack_kernel(cap, pieces, side, where, *refs):
    peers = (len(refs) - 1) // (len(pieces) + 1)
    needs, history, packed = refs[:peers], refs[peers], refs[peers + 1 :]
    lags, sims, width = history.shape
    local_blocks = width // side
    first = where[0] * local_blocks
    for peer in range(peers):
        position = jnp.int32(0)
        for lag in range(lags):
            for block in range(local_blocks):
                wanted = needs[peer][lag, first + block]

                @pl.when((wanted > 0) & (position < cap))
                def _(peer=peer, lag=lag, block=block, position=position):
                    for piece, (begin, part) in enumerate(pieces):
                        packed[piece * peers + peer][position] = history[
                            lag, begin : begin + part, block * side : (block + 1) * side
                        ]

                position = position + wanted


def pack(where, needs, history, side, cap, pieces):
    outs = []
    for _, part in pieces:
        outs += [jax.ShapeDtypeStruct((cap, part, side), history.dtype)] * len(needs)
    return pl.pallas_call(
        functools.partial(pack_kernel, cap, pieces, side),
        out_shape=outs,
        in_specs=[SMEM] * (1 + len(needs)) + [VMEM],
        out_specs=[VMEM] * len(outs),
        compiler_params=params(history, *outs),
        name="pack_history",
    )(where, *needs, history)


def plan_kernel(cap, col_size, per_owner, where, cols, rows, counts, *refs):
    needs, tiles, (table, size, over, held, places, sem) = refs[:-7], refs[-7], refs[-6:]
    lags, total = needs[0].shape
    row, core = where[0], where[2]
    members = len(needs)
    started = jnp.int32(0)
    for lag in range(lags):

        def begin(slot, started, lag=lag):
            pltpu.make_async_copy(tiles.at[lag, slot], held.at[started], sem.at[started]).start()
            return started + 1

        started = lax.fori_loop(0, counts[0, 0, lag], begin, started)
    local_blocks = total // members
    for owner in range(members):
        position = jnp.int32(0)
        for lag in range(lags):
            for block in range(owner * local_blocks, (owner + 1) * local_blocks):
                places[lag, block] = position
                position = position + needs[0][lag, block]
    above = jnp.int32(0)
    for member in range(members):
        for owner in range(members):

            def count(block, wanted, member=member, owner=owner):
                for lag in range(lags):
                    wanted = wanted + needs[member][lag, owner * local_blocks + block]
                return wanted

            wanted = lax.fori_loop(0, local_blocks, count, jnp.int32(0))
            foreign = lax.bitwise_xor(row, member) != owner
            above = jnp.where(foreign & (wanted > cap), 1, above)
    over[0] = above
    filled = jnp.int32(0)
    for lag in range(lags):

        def note(slot, filled, lag=lag):
            col = cols[0, 0, lag, slot]
            target = rows[0, 0, lag, slot]
            owner = target // per_owner
            half = lax.bitwise_xor(owner % 2, core) * col_size + owner // 2
            table[0, filled] = lag
            table[1, filled] = lax.bitwise_xor(col // local_blocks, row)
            table[2, filled] = col % local_blocks
            table[3, filled] = jnp.minimum(places[lag, col], cap - 1)
            table[4, filled] = half * per_owner + target % per_owner
            return filled + 1

        filled = lax.fori_loop(0, counts[0, 0, lag], note, filled)
    size[0] = filled

    def settle(index, carry):
        pltpu.make_async_copy(tiles.at[0, 0], held.at[index], sem.at[index]).wait()
        return carry

    lax.fori_loop(0, filled, settle, 0)


def make_plan(where, cols, rows, counts, needs, tiles, cap, col_size, per_owner):
    lags, total = needs[0].shape
    count = lags * cols.shape[3]
    held = jax.ShapeDtypeStruct((count,) + tiles.shape[2:], tiles.dtype)
    return pl.pallas_call(
        functools.partial(plan_kernel, cap, col_size, per_owner),
        out_shape=[
            jax.ShapeDtypeStruct((5, count), jnp.int32),
            jax.ShapeDtypeStruct((1,), jnp.int32),
            jax.ShapeDtypeStruct((1,), jnp.int32),
            held,
        ],
        in_specs=[SMEM] * (4 + len(needs)) + [ANY],
        out_specs=[SMEM] * 3 + [VMEM],
        scratch_shapes=[pltpu.SMEM((lags, total), jnp.int32), pltpu.SemaphoreType.DMA((count,))],
        compiler_params=params(held),
        name="plan_tiles",
    )(where, cols, rows, counts, *needs, tiles)


def tiles_kernel(first, whole, extra, over, table, size, tiles, history, *refs):
    received, (kept, given, blocks, sums) = refs[: len(refs) - 4 - extra], refs[-4:]
    side = tiles.shape[2]
    halves, part, _ = sums.shape
    live = size[0]
    sums[...] = jnp.zeros_like(sums)

    def fetch(index, carry):
        lag, relative = table[0, index], table[1, index]
        lanes = pl.ds(pl.multiple_of(table[2, index] * side, side), side)

        @pl.when(relative == 0)
        def _():
            blocks[index] = history[lag, pl.ds(first, part), lanes]

        for peer in range(len(received)):

            @pl.when(relative == peer + 1)
            def _(peer=peer):
                if whole:
                    blocks[index] = received[peer][lag, pl.ds(first, part), lanes]
                else:
                    blocks[index] = received[peer][table[3, index]]

        return carry

    lax.fori_loop(0, live, fetch, 0)

    def multiply(group, carry):
        products = []
        for offset in range(GROUP):
            index = jnp.minimum(group * GROUP + offset, live - 1)
            products.append(
                lax.dot_general(
                    blocks[index], tiles[index], (((1,), (1,)), ((), ())), preferred_element_type=jnp.float32
                )
            )
        for offset, product in enumerate(products):
            index = group * GROUP + offset
            spot = table[4, jnp.minimum(index, live - 1)]
            sums[spot] += product if offset == 0 else jnp.where(index < live, product, 0.0)
        return carry

    lax.fori_loop(0, (live + GROUP - 1) // GROUP, multiply, 0)
    kept[...] = sums[: halves // 2]
    given[: halves // 2] = sums[halves // 2 :]
    given[halves // 2] = jnp.full((part, side), 1.0, jnp.float32) * over[0].astype(jnp.float32)


def multiply_tiles(first, part, whole, over, table, size, tiles, history, received, chunks, after):
    side = tiles.shape[2]
    half = jax.ShapeDtypeStruct((chunks, part, side), jnp.float32)
    more = jax.ShapeDtypeStruct((chunks + 1, part, side), jnp.float32)
    blocks = pltpu.VMEM((table.shape[1], part, side), history.dtype)
    sums = pltpu.VMEM((2 * chunks, part, side), jnp.float32)
    return pl.pallas_call(
        functools.partial(tiles_kernel, first, whole, len(after)),
        out_shape=[half, more],
        in_specs=[SMEM] * 3 + [VMEM] * (2 + len(received)) + [ANY] * len(after),
        out_specs=[VMEM, VMEM],
        scratch_shapes=[blocks, sums],
        compiler_params=params(tiles, history, *received, half, half, blocks, sums),
        name="multiply_tiles",
    )(over, table, size, tiles, history, *received, *after)


def code_kernel(per_owner, where, over, kept, got, own, *coded):
    chunks, part, side = kept.shape
    col = where[1]
    flag = jnp.maximum(over[0].astype(jnp.float32), got[chunks][:1, :LANES])
    for step in list(range(1, chunks // per_owner)) + [0]:
        chunk = lax.bitwise_xor(col, step) * per_owner
        exponents = []
        for block in range(per_owner):
            value = kept[chunk + block] + got[chunk + block]
            if step == 0:
                own[block] = value
                continue
            out = coded[step - 1]
            largest = jnp.maximum(jnp.max(jnp.abs(value), axis=0, keepdims=True), 1e-30)
            exponent = jnp.ceil(jnp.log2(largest))
            grid = jnp.clip(jnp.round(value * jnp.exp2(15.0 - exponent)), -32767.0, 32767.0)
            grid = grid.astype(jnp.int32).astype(jnp.int16)
            for lane in range(side // LANES):
                at = len(exponents)
                out[pl.ds(at * part, part), :] = grid[:, lane * LANES : (lane + 1) * LANES]
                exponents.append(exponent[:, lane * LANES : (lane + 1) * LANES])
        if step > 0:
            at = len(exponents)
            exponents.append(jnp.zeros((PAD - 1 - at, LANES), jnp.float32))
            exponents.append(flag)
            tail = jnp.concatenate(exponents, axis=0)
            out[pl.ds(at * part, PAD), :] = tail.astype(jnp.int32).astype(jnp.int16)


def code(where, over, kept, got, per_owner):
    chunks, part, side = kept.shape
    chunk = jax.ShapeDtypeStruct((per_owner * part * (side // LANES) + PAD, LANES), jnp.int16)
    own = jax.ShapeDtypeStruct((per_owner, part, side), jnp.float32)
    outs = [own] + [chunk] * (chunks // per_owner - 1)
    return pl.pallas_call(
        functools.partial(code_kernel, per_owner),
        out_shape=outs,
        in_specs=[SMEM] * 2 + [VMEM, VMEM],
        out_specs=[VMEM] * len(outs),
        compiler_params=params(kept, got, *outs),
        name="add_and_code",
    )(where, over, kept, got)


def solve_kernel(first, fresh, over, *refs):
    refs = refs if fresh else refs[2:]
    base, rate, direct, state, own = refs[:5]
    codes, (stress_out, rate_out, flag_out, stress_held, rate_held, sems) = refs[5:-6], refs[-6:]
    per_owner, part, side = own.shape
    rows = pl.ds(first, part)
    tails = []
    flag = over[0].astype(jnp.float32)
    for chunk in codes:
        tail = chunk[pl.ds(chunk.shape[0] - PAD, PAD), :].astype(jnp.int32).astype(jnp.float32)
        flag = jnp.maximum(flag, jnp.max(tail[PAD - 1 :, :]))
        tails.append(tail)
    flag_out[0] = flag.astype(jnp.int32)
    for at in range(per_owner * (side // LANES)):
        block, lane = at // (side // LANES), at % (side // LANES)
        stress = own[block, :, pl.ds(lane * LANES, LANES)]
        for chunk, tail in zip(codes, tails):
            values = chunk[pl.ds(at * part, part), :].astype(jnp.int32).astype(jnp.float32)
            stress = stress + values * jnp.exp2(tail[at : at + 1, :] - 15.0)
        lanes = pl.ds(at * LANES, LANES)
        stress_held[:, lanes] = stress
        rate_held[:, lanes] = friction(
            stress, base[rows, lanes], rate[rows, lanes], direct[rows, lanes], state[rows, lanes]
        )
    copies = (
        pltpu.make_async_copy(stress_held, stress_out.at[rows], sems.at[0]),
        pltpu.make_async_copy(rate_held, rate_out.at[rows], sems.at[1]),
    )
    for copy in copies:
        copy.start()
    for copy in copies:
        copy.wait()


def solve(first, over, fields, own, coded, before):
    sims, owned = fields[0].shape
    part = own.shape[1]
    fresh = before is None
    carried = [] if fresh else list(before)
    held = pltpu.VMEM((part, owned), jnp.float32)
    return pl.pallas_call(
        functools.partial(solve_kernel, first, fresh),
        out_shape=[jax.ShapeDtypeStruct(fields[0].shape, jnp.float32)] * 2
        + [jax.ShapeDtypeStruct((1,), jnp.int32)],
        in_specs=[SMEM] + [ANY] * len(carried) + [VMEM] * (5 + len(coded)),
        out_specs=[ANY, ANY, SMEM],
        input_output_aliases={} if fresh else {1: 0, 2: 1},
        scratch_shapes=[held, held, pltpu.SemaphoreType.DMA((2,))],
        compiler_params=params(*fields, own, held, held, *coded),
        name="friction_solve",
    )(over, *carried, *fields, own, *coded)


def reduce(first, where, over, fields, kept, given, before):
    per_owner = fields[0].shape[1] // kept.shape[2]
    col_size = lax.axis_size("col")
    got = lax.ppermute(given, "lag", partners(lax.axis_size("lag"), 1))
    own, *coded = code(where, over, kept, got, per_owner)
    arrived = [None] * (col_size - 1)
    for step in range(col_size - 1, 0, -1):
        arrived[step - 1] = lax.ppermute(coded[step - 1], "col", partners(col_size, step))
    return solve(first, over, fields, own, arrived, before)


def local(history, kernel_tiles, tile_rows, tile_cols, tile_count, base_stress, prev_rate, direct_effect, state_var):
    _, _, lags, slots, side, _ = kernel_tiles.shape
    row_size, col_size = (lax.axis_size(axis) for axis in ("row", "col"))
    where = jnp.stack([lax.axis_index(axis).astype(jnp.int32) for axis in ("row", "col", "lag")])
    history = history[:, 0]
    tiles = kernel_tiles[0, 0]
    sims = history.shape[1]
    cut = sims * FIRST // 8
    pieces = ((0, cut), (cut, sims - cut))
    local_blocks = history.shape[2] // side
    total = row_size * local_blocks
    per_owner = base_stress.shape[1] // side
    chunks = col_size * per_owner
    cap = min(CAP, lags * local_blocks)
    fields = (base_stress, prev_rate, direct_effect, state_var)

    need = make_request(tile_cols, tile_count, total)
    requests = [lax.ppermute(need, "row", partners(row_size, step)) for step in range(1, row_size)]
    held = load(history)
    packed = list(pack(where, requests, held, side, cap, pieces))
    received = [
        [lax.ppermute(packed.pop(0), "row", partners(row_size, step)) for step in range(1, row_size)]
        for _ in pieces
    ]
    table, size, over, live_tiles = make_plan(
        where, tile_cols, tile_rows, tile_count, [need, *requests], tiles, cap, col_size, per_owner
    )

    after = ()
    result = None
    for (first, part), blocks in zip(pieces, received):
        kept, given = multiply_tiles(
            first, part, False, over, table, size, live_tiles, held, blocks, chunks, after
        )
        *result, flag = reduce(first, where, over, fields, kept, given, result)
        after = (flag,)

    def general():
        everything = [lax.ppermute(history, "row", partners(row_size, step)) for step in range(1, row_size)]
        kept, given = multiply_tiles(
            0, sims, True, over, table, size, live_tiles, history, everything, chunks, ()
        )
        return tuple(reduce(0, where, over, fields, kept, given, None)[:2])

    return lax.cond(flag[0] > 0, general, lambda: tuple(result))


def solution(mesh):
    return jax.shard_map(
        local,
        mesh=mesh,
        in_specs=(
            P("lag", "col", None, "row"),
            P("row", "col", "lag", None, None, None),
            P("row", "col", "lag", None),
            P("row", "col", "lag", None),
            P("row", "col", "lag"),
            P(None, ("row", "col", "lag")),
            P(None, ("row", "col", "lag")),
            P(None, ("row", "col", "lag")),
            P(None, ("row", "col", "lag")),
        ),
        out_specs=(P(None, ("row", "col", "lag")), P(None, ("row", "col", "lag"))),
        check_vma=False,
    )
```

time: 252 us -> 98 us (0.39)
  waiting for transfers between devices: 187 us -> 38.3 us
  Pallas kernels: 0 us -> 31.6 us
  starting transfers between devices: 0.08 us -> 25.9 us
  local copies, waits for them, and re-layouts: 21.8 us -> 0.06 us
  other arithmetic: 18.7 us -> 0.08 us
  between operations: 14.1 us -> 1.67 us
  matrix products: 9.66 us -> 0 us
    psum x1 -> x0, waiting for transfers between devices: 96 us -> none  [local(): summed = lax.psum(partial_stress, ('col', 'lag'))]
    all_gather x1 -> x0, waiting for transfers between devices: 90.7 us -> none  [local(): gathered = lax.all_gather(history, 'row', axis=3, tiled=True)]
    ppermute x0 -> x17, waiting for transfers between devices: none -> 38.3 us  [the longest x6 17.1 us: local(): lax.ppermute(packed.pop(0), 'row', partners(row_size, step))]
    pallas_call x0 -> x10, Pallas kernels: none -> 31.6 us  [the longest x2 9.84 us: multiply_tiles(): pl.pallas_call(functools.partial(tiles_kernel, first, whole, len(after)),...]
    ppermute x0 -> x17, starting transfers between devices: none -> 25.9 us  [the longest x6 14 us: reduce(): lax.ppermute(coded[step - 1], 'col', partners(col_size, step))]
    scatter-add x1 -> x0, other arithmetic: 14.6 us -> none  [local(): jnp.zeros((sims_count, row_blocks, tile_side), jnp.float32)]
    unnamed x21 -> x20, local copies, waits for them, and re-layouts: 12.7 us -> 0.06 us
    dot_general x2 -> x0, matrix products: 9.66 us -> none  [the longest x1 4.83 us: local(): jnp.einsum('lksj,lkij->slki', picked, kernel_tiles[0, 0], preferred_eleme...]
  transfers between devices with their start and end apart: 2 -> 17, of which waited for: 2 -> 11; matrix products, arithmetic and copies ran while one was open for 1% -> 0% of each run, Pallas kernels for 0% -> 15%
where the time goes in v2:
time: 98 us; the launch traced here: 97.8 us
  waiting for transfers between devices  38.3 us (39%)
  Pallas kernels  31.6 us (32%)
  starting transfers between devices  25.9 us (26%)
  between operations  1.67 us (2%)
    ppermute x6, waiting for transfers between devices, local(): lax.ppermute(packed.pop(0), 'row', partners(row_size, step))  17.1 us
    ppermute x6, waiting for transfers between devices, reduce(): lax.ppermute(coded[step - 1], 'col', partners(col_size, step))  16.6 us
    ppermute x6, starting transfers between devices, reduce(): lax.ppermute(coded[step - 1], 'col', partners(col_size, step))  14 us
    pallas_call x2, Pallas kernels, multiply_tiles(): pl.pallas_call(functools.partial(tiles_kernel, first, whole, len(after)),...  9.84 us
    pallas_call x1, Pallas kernels, make_plan(): pl.pallas_call(functools.partial(plan_kernel, cap, col_size, per_owner),...  8.04 us
    ppermute x6, starting transfers between devices, local(): lax.ppermute(packed.pop(0), 'row', partners(row_size, step))  7.27 us
    pallas_call x2, Pallas kernels, solve(): pl.pallas_call(functools.partial(solve_kernel, first, fresh), out_shape=[...  6.14 us
    ppermute x3, starting transfers between devices, local(): lax.ppermute(need, 'row', partners(row_size, step))  4.46 us
  transfers between devices with their start and end apart: 17, of which 11 were waited for; matrix products, arithmetic and copies ran while one was open for 0% of the time, Pallas kernels for 15%

profile of v2, /device:TPU:0, one launch (start us, length us, event | category | flops | bytes accessed | tf_op | source)
XLA Modules:
  0.0 97.8 jit_solution(17515232239397143246)
XLA Ops:
  0.6 1.3 %mark_blocks.1.refs_0_ = s32[4,32]{1,0:T(4,128)} custom-call(s32[1,1,4,12]{3,2,1,0:T(4,128)} %cols.3, s32[1,1,4]{2,1,0:T(1,128)} %counts.3), custom_call_target="tpu_custom_call" | custom-call | tf_op jit(solution)/shard_map/mark_blocks/pallas_call | solution.py:62
  2.0 3.9 %collective-permute-start.9 = (s32[4,32]{1,0:T(4,128)}, s32[4,32]{1,0:T(4,128)S(1)}, u32[]{:S(2)}, u32[]{:S(2)}) collective-permute-start(s32[4,32]{1,0:T(4,128)} %mark_blocks.1.refs_0_), channel_id=1, source_target_pairs={{0,24},{8,16},{16,8},{24,0},{1,25},{9,17},{17,9},{25,1},{2,26},{10... | collective-permute-start | bytes 1544 | tf_op jit(solution)/shard_map/ppermute | solution.py:394
  5.9 0.5 collective-permute-start.8
  6.5 1.8 %load_history.1.refs_3_.history = bf16[4,128,2048]{2,1,0:T(8,128)(2,1)S(1)} custom-call(bf16[4,128,2048]{2,1,0:T(8,128)(2,1)} %bitcast.7), custom_call_target="tpu_custom_call" | custom-call | tf_op jit(solution)/shard_map/load_history/pallas_call | solution.py:78
  8.3 1.3 %collective-permute-done.8.refs_2_.refs_1_ = s32[4,32]{1,0:T(4,128)S(1)} collective-permute-done((s32[4,32]{1,0:T(4,128)}, s32[4,32]{1,0:T(4,128)S(1)}, u32[]{:S(2)}, u32[]{:S(2)}) %collective-permute-start.8) | collective-permute-done | bytes 544 | tf_op jit(solution)/shard_map/ppermute | solution.py:394
  9.7 0.5 collective-permute-done.7.refs_1_.refs_0_
  10.2 1.8 %pack_history.1 = (bf16[16,64,256]{2,1,0:T(8,128)(2,1)S(1)}, bf16[16,64,256]{2,1,0:T(8,128)(2,1)S(1)}, bf16[16,64,256]{2,1,0:T(8,128)(2,1)S(1)}, bf16[16,64,256]...) custom-call(s32[3]{0:T(128)S(1)} %pad_add_fusion.where, ...), custom_call_target="tpu_custom_call" | custom-call | tf_op jit(solution)/shard_map/pack_history/pallas_call | solution.py:115
  12.2 1.9 %collective-permute-start.11 = (bf16[16,64,256]{2,1,0:T(8,128)(2,1)S(1)}, bf16[16,64,256]{2,1,0:T(8,128)(2,1)S(1)}, u32[]{:S(2)}, u32[]{:S(2)}) collective-permute-start(bf16[16,64,256]{2,1,0:T(8,128)(2,1)S(1)} %get-tuple-element.77), channel_id=1, source_target_pairs={{0,16},{8,24},{16,0},{24,8},{1,17},{9,25},{17,1},{25,9},{2,18},{10... | collective-permute-start | bytes 1572872 | tf_op jit(solution)/shard_map/ppermute | solution.py:398
  14.1 1.5 %collective-permute-start.12 = (bf16[16,64,256]{2,1,0:T(8,128)(2,1)S(1)}, bf16[16,64,256]{2,1,0:T(8,128)(2,1)S(1)}, u32[]{:S(2)}, u32[]{:S(2)}) collective-permute-start(bf16[16,64,256]{2,1,0:T(8,128)(2,1)S(1)} %get-tuple-element.78), channel_id=1, source_target_pairs={{0,24},{8,16},{16,8},{24,0},{1,25},{9,17},{17,9},{25,1},{2,26},{10... | collective-permute-start | bytes 1572872 | tf_op jit(solution)/shard_map/ppermute | solution.py:398
  15.6 8.0 %plan_tiles.1 = (s32[5,48]{1,0:T(8,128)S(1)}, s32[1]{0:T(128)}, s32[1]{0:T(128)}, bf16[48,256,256]{2,1,0:T(8,128)(2,1)S(1)}) custom-call(s32[3]{0:T(128)S(1)} %pad_add_fusion.where, s32[1,1,4,12]{3,2,1,0:T(4,128)S(1)} %copy-done.1, s32[1,1,4,12]{3,2,1,0:T(4,128)S(1)} %copy-done.3, s32[1,1,4]{2,1,0:T(1,128)S(1)} %copy-done.4, s32[4,32]{1,0:T(4,128)S(1)} %copy-done.2, ...), custom_call_target="tpu_custom_call" | custom-call | tf_op jit(solution)/shard_map/plan_tiles/pallas_call | solution.py:187
  23.6 3.3 %collective-permute-done.10.refs_0_ = bf16[16,64,256]{2,1,0:T(8,128)(2,1)S(1)} collective-permute-done((bf16[16,64,256]{2,1,0:T(8,128)(2,1)S(1)}, bf16[16,64,256]{2,1,0:T(8,128)(2,1)S(1)}, u32[]{:S(2)}, u32[]{:S(2)}) %collective-permute-start.10) | collective-permute-done | bytes 524320 | tf_op jit(solution)/shard_map/ppermute | solution.py:398
  26.9 8.1 %collective-permute-done.11.refs_1_ = bf16[16,64,256]{2,1,0:T(8,128)(2,1)S(1)} collective-permute-done((bf16[16,64,256]{2,1,0:T(8,128)(2,1)S(1)}, bf16[16,64,256]{2,1,0:T(8,128)(2,1)S(1)}, u32[]{:S(2)}, u32[]{:S(2)}) %collective-permute-start.11) | collective-permute-done | bytes 524320 | tf_op jit(solution)/shard_map/ppermute | solution.py:398
  35.0 1.2 %collective-permute-done.12.refs_2_ = bf16[16,64,256]{2,1,0:T(8,128)(2,1)S(1)} collective-permute-done((bf16[16,64,256]{2,1,0:T(8,128)(2,1)S(1)}, bf16[16,64,256]{2,1,0:T(8,128)(2,1)S(1)}, u32[]{:S(2)}, u32[]{:S(2)}) %collective-permute-start.12) | collective-permute-done | bytes 524320 | tf_op jit(solution)/shard_map/ppermute | solution.py:398
  36.2 4.6 %multiply_tiles.4 = (f32[16,64,256]{2,1,0:T(8,128)S(1)}, f32[17,64,256]{2,1,0:T(8,128)S(1)}) custom-call(s32[1]{0:T(128)} %get-tuple-element.72.over, s32[5,48]{1,0:T(8,128)S(1)} %get-tuple-element.73.table, s32[1]{0:T(128)} %get-tuple-element.74.size, bf16[48,256,256]{2,1,0:T(8,128)(2,1)S(1)} %get-tuple-element.75.tiles, ...), custom_call_target="tpu_custom_call" | custom-call | tf_op jit(solution)/shard_map/multiply_tiles/pallas_call | solution.py:258
  40.9 2.0 %collective-permute-start.17 = (bf16[16,64,256]{2,1,0:T(8,128)(2,1)S(1)}, bf16[16,64,256]{2,1,0:T(8,128)(2,1)S(1)}, u32[]{:S(2)}, u32[]{:S(2)}) collective-permute-start(bf16[16,64,256]{2,1,0:T(8,128)(2,1)S(1)} %get-tuple-element.87), channel_id=1, source_target_pairs={{0,8},{8,0},{16,24},{24,16},{1,9},{9,1},{17,25},{25,17},{2,10},{10... | collective-permute-start | bytes 1572872 | tf_op jit(solution)/shard_map/ppermute | solution.py:398
  42.9 1.7 %collective-permute-start.18 = (bf16[16,64,256]{2,1,0:T(8,128)(2,1)S(1)}, bf16[16,64,256]{2,1,0:T(8,128)(2,1)S(1)}, u32[]{:S(2)}, u32[]{:S(2)}) collective-permute-start(bf16[16,64,256]{2,1,0:T(8,128)(2,1)S(1)} %get-tuple-element.88), channel_id=1, source_target_pairs={{0,16},{8,24},{16,0},{24,8},{1,17},{9,25},{17,1},{25,9},{2,18},{10... | collective-permute-start | bytes 1572872 | tf_op jit(solution)/shard_map/ppermute | solution.py:398
  44.6 1.4 %add_and_code.4 = (f32[4,64,256]{2,1,0:T(8,128)S(1)}, s16[528,128]{1,0:T(8,128)(2,1)S(1)}, s16[528,128]{1,0:T(8,128)(2,1)S(1)}, s16[528,128]{1,0:T(8,128)(2,1)S(1)}) custom-call(s32[3]{0:T(128)S(1)} %pad_add_fusion.where, s32[1]{0:T(128)} %get-tuple-element.72.over, f32[16,64,256]{2,1,0:T(8,128)S(1)} %get-tuple-element.79.kept, ...), custom_call_target="tpu_custom_call" | custom-call | tf_op jit(solution)/shard_map/add_and_code/pallas_call | solution.py:303
  46.0 2.4 %collective-permute-start.14 = (s16[528,128]{1,0:T(8,128)(2,1)S(1)}, s16[528,128]{1,0:T(8,128)(2,1)S(1)}, u32[]{:S(2)}, u32[]{:S(2)}) collective-permute-start(s16[528,128]{1,0:T(8,128)(2,1)S(1)} %get-tuple-element.82), channel_id=1, source_target_pairs={{0,2},{2,0},{4,6},{6,4},{1,3},{3,1},{5,7},{7,5},{8,10},{10,8},{12,... | collective-permute-start | bytes 405512 | tf_op jit(solution)/shard_map/ppermute | solution.py:373
  48.4 2.6 %collective-permute-start.15 = (s16[528,128]{1,0:T(8,128)(2,1)S(1)}, s16[528,128]{1,0:T(8,128)(2,1)S(1)}, u32[]{:S(2)}, u32[]{:S(2)}) collective-permute-start(s16[528,128]{1,0:T(8,128)(2,1)S(1)} %get-tuple-element.83), channel_id=1, source_target_pairs={{0,4},{2,6},{4,0},{6,2},{1,5},{3,7},{5,1},{7,3},{8,12},{10,14},{12... | collective-permute-start | bytes 405512 | tf_op jit(solution)/shard_map/ppermute | solution.py:373
  51.0 2.5 %collective-permute-done.14.refs_5_ = s16[528,128]{1,0:T(8,128)(2,1)S(1)} collective-permute-done((s16[528,128]{1,0:T(8,128)(2,1)S(1)}, s16[528,128]{1,0:T(8,128)(2,1)S(1)}, u32[]{:S(2)}, u32[]{:S(2)}) %collective-permute-start.14) | collective-permute-done | bytes 135200 | tf_op jit(solution)/shard_map/ppermute | solution.py:373
  53.5 3.6 %collective-permute-start.16 = (s16[528,128]{1,0:T(8,128)(2,1)S(1)}, s16[528,128]{1,0:T(8,128)(2,1)S(1)}, u32[]{:S(2)}, u32[]{:S(2)}) collective-permute-start(s16[528,128]{1,0:T(8,128)(2,1)S(1)} %get-tuple-element.84), channel_id=1, source_target_pairs={{0,6},{2,4},{4,2},{6,0},{1,7},{3,5},{5,3},{7,1},{8,14},{10,12},{12... | collective-permute-start | bytes 405512 | tf_op jit(solution)/shard_map/ppermute | solution.py:373
  57.1 3.3 %collective-permute-done.15.refs_6_ = s16[528,128]{1,0:T(8,128)(2,1)S(1)} collective-permute-done((s16[528,128]{1,0:T(8,128)(2,1)S(1)}, s16[528,128]{1,0:T(8,128)(2,1)S(1)}, u32[]{:S(2)}, u32[]{:S(2)}) %collective-permute-start.15) | collective-permute-done | bytes 135200 | tf_op jit(solution)/shard_map/ppermute | solution.py:373
  60.5 3.1 %friction_solve.4 = (f32[128,1024]{1,0:T(8,128)}, f32[128,1024]{1,0:T(8,128)}, s32[1]{0:T(128)}) custom-call(s32[1]{0:T(128)} %get-tuple-element.72.over, f32[128,1024]{1,0:T(8,128)S(1)} %copy-done.7, f32[128,1024]{1,0:T(8,128)S(1)} %copy-done.8, f32[128,1024]{1,0:T(8,128)S(1)} %copy-done.9, f32[128,1024]{1,0:T(8,128)S(1)} %copy-done.12, ...), custom_call_target="tpu_custom_call" | custom-call | tf_op jit(solution)/shard_map/friction_solve/pallas_call | solution.py:353
  63.6 4.6 %collective-permute-done.18.refs_1_ = bf16[16,64,256]{2,1,0:T(8,128)(2,1)S(1)} collective-permute-done((bf16[16,64,256]{2,1,0:T(8,128)(2,1)S(1)}, bf16[16,64,256]{2,1,0:T(8,128)(2,1)S(1)}, u32[]{:S(2)}, u32[]{:S(2)}) %collective-permute-start.18) | collective-permute-done | bytes 524320 | tf_op jit(solution)/shard_map/ppermute | solution.py:398
  68.1 5.2 %multiply_tiles.5 = (f32[16,64,256]{2,1,0:T(8,128)S(1)}, f32[17,64,256]{2,1,0:T(8,128)S(1)}) custom-call(s32[1]{0:T(128)} %get-tuple-element.72.over, s32[5,48]{1,0:T(8,128)S(1)} %get-tuple-element.73.table, s32[1]{0:T(128)} %get-tuple-element.74.size, bf16[48,256,256]{2,1,0:T(8,128)(2,1)S(1)} %get-tuple-element.75.tiles, ...), custom_call_target="tpu_custom_call" | custom-call | tf_op jit(solution)/shard_map/multiply_tiles/pallas_call | solution.py:258
  73.5 2.7 %collective-permute-done.20.got = f32[17,64,256]{2,1,0:T(8,128)S(1)} collective-permute-done((f32[17,64,256]{2,1,0:T(8,128)S(1)}, f32[17,64,256]{2,1,0:T(8,128)S(1)}, u32[]{:S(2)}, u32[]{:S(2)}) %collective-permute-start.20) | collective-permute-done | bytes 1114144 | tf_op jit(solution)/shard_map/ppermute | solution.py:369
  76.2 1.4 %add_and_code.5 = (f32[4,64,256]{2,1,0:T(8,128)S(1)}, s16[528,128]{1,0:T(8,128)(2,1)S(1)}, s16[528,128]{1,0:T(8,128)(2,1)S(1)}, s16[528,128]{1,0:T(8,128)(2,1)S(1)}) custom-call(s32[3]{0:T(128)S(1)} %pad_add_fusion.where, s32[1]{0:T(128)} %get-tuple-element.72.over, f32[16,64,256]{2,1,0:T(8,128)S(1)} %get-tuple-element.91.kept, ...), custom_call_target="tpu_custom_call" | custom-call | tf_op jit(solution)/shard_map/add_and_code/pallas_call | solution.py:303
  77.6 2.9 %collective-permute-start.21 = (s16[528,128]{1,0:T(8,128)(2,1)S(1)}, s16[528,128]{1,0:T(8,128)(2,1)S(1)}, u32[]{:S(2)}, u32[]{:S(2)}) collective-permute-start(s16[528,128]{1,0:T(8,128)(2,1)S(1)} %get-tuple-element.94), channel_id=1, source_target_pairs={{0,2},{2,0},{4,6},{6,4},{1,3},{3,1},{5,7},{7,5},{8,10},{10,8},{12,... | collective-permute-start | bytes 405512 | tf_op jit(solution)/shard_map/ppermute | solution.py:373
  80.5 2.2 %collective-permute-start.22 = (s16[528,128]{1,0:T(8,128)(2,1)S(1)}, s16[528,128]{1,0:T(8,128)(2,1)S(1)}, u32[]{:S(2)}, u32[]{:S(2)}) collective-permute-start(s16[528,128]{1,0:T(8,128)(2,1)S(1)} %get-tuple-element.95), channel_id=1, source_target_pairs={{0,4},{2,6},{4,0},{6,2},{1,5},{3,7},{5,1},{7,3},{8,12},{10,14},{12... | collective-permute-start | bytes 405512 | tf_op jit(solution)/shard_map/ppermute | solution.py:373
  83.0 3.4 %collective-permute-done.21.refs_7_ = s16[528,128]{1,0:T(8,128)(2,1)S(1)} collective-permute-done((s16[528,128]{1,0:T(8,128)(2,1)S(1)}, s16[528,128]{1,0:T(8,128)(2,1)S(1)}, u32[]{:S(2)}, u32[]{:S(2)}) %collective-permute-start.21) | collective-permute-done | bytes 135200 | tf_op jit(solution)/shard_map/ppermute | solution.py:373
  86.3 7.4 %collective-permute-done.22.refs_8_ = s16[528,128]{1,0:T(8,128)(2,1)S(1)} collective-permute-done((s16[528,128]{1,0:T(8,128)(2,1)S(1)}, s16[528,128]{1,0:T(8,128)(2,1)S(1)}, u32[]{:S(2)}, u32[]{:S(2)}) %collective-permute-start.22) | collective-permute-done | bytes 135200 | tf_op jit(solution)/shard_map/ppermute | solution.py:373
  93.7 3.1 %friction_solve.5 = (f32[128,1024]{1,0:T(8,128)}, f32[128,1024]{1,0:T(8,128)}, s32[1]{0:T(128)}) custom-call(s32[1]{0:T(128)} %get-tuple-element.72.over, f32[128,1024]{1,0:T(8,128)} %get-tuple-element.85.refs_0_, f32[128,1024]{1,0:T(8,128)} %get-tuple-element.86.refs_1_, f32[128,1024]{1,0:T(8,128)S(1)} %copy-done.7, ...), custom_call_target="tpu_custom_call", output_to_operand_aliasing={{0}: (1, {}), {1}: (2, {})} | custom-call | tf_op jit(solution)/shard_map/friction_solve/pallas_call | solution.py:353
  (34 shorter events, 1.1 us)
Async XLA Ops:
  2.0 6.3 %collective-permute-start.9 = (s32[4,32]{1,0:T(4,128)}, s32[4,32]{1,0:T(4,128)S(1)}, u32[]{:S(2)}, u32[]{:S(2)}) collective-permute-start(s32[4,32]{1,0:T(4,128)} %mark_blocks.1.refs_0_), channel_id=1, source_target_pairs={{0,24},{8,16},{16,8},{24,0},{1,25},{9,17},{17,9},{25,1},{2,26},{10... | collective-permute-start | bytes 1544 | tf_op jit(solution)/shard_map/ppermute | solution.py:394
  5.9 3.8 %collective-permute-start.8 = (s32[4,32]{1,0:T(4,128)}, s32[4,32]{1,0:T(4,128)S(1)}, u32[]{:S(2)}, u32[]{:S(2)}) collective-permute-start(s32[4,32]{1,0:T(4,128)} %mark_blocks.1.refs_0_), channel_id=1, source_target_pairs={{0,16},{8,24},{16,0},{24,8},{1,17},{9,25},{17,1},{25,9},{2,18},{10... | collective-permute-start | bytes 1544 | tf_op jit(solution)/shard_map/ppermute | solution.py:394
  6.4 3.8 %collective-permute-start.7 = (s32[4,32]{1,0:T(4,128)}, s32[4,32]{1,0:T(4,128)S(1)}, u32[]{:S(2)}, u32[]{:S(2)}) collective-permute-start(s32[4,32]{1,0:T(4,128)} %mark_blocks.1.refs_0_), channel_id=1, source_target_pairs={{0,8},{8,0},{16,24},{24,16},{1,9},{9,1},{17,25},{25,17},{2,10},{10... | collective-permute-start | bytes 1544 | tf_op jit(solution)/shard_map/ppermute | solution.py:394
  6.5 9.0 %copy-start = (bf16[1,1,4,12,256,256]{5,4,3,2,1,0:T(8,128)(2,1)S(1)}, bf16[1,1,4,12,256,256]{5,4,3,2,1,0:T(8,128)(2,1)}, u32[]{:S(2)}) copy-start(bf16[1,1,4,12,256,256]{5,4,3,2,1,0:T(8,128)(2,1)} %param.12) | copy-start | bytes 18874372
  8.3 7.3 %copy-start.1 = (s32[1,1,4,12]{3,2,1,0:T(4,128)S(1)}, s32[1,1,4,12]{3,2,1,0:T(4,128)}, u32[]{:S(2)}) copy-start(s32[1,1,4,12]{3,2,1,0:T(4,128)} %cols.3) | copy-start | bytes 580
  8.3 7.3 %copy-start.2 = (s32[4,32]{1,0:T(4,128)S(1)}, s32[4,32]{1,0:T(4,128)}, u32[]{:S(2)}) copy-start(s32[4,32]{1,0:T(4,128)} %mark_blocks.1.refs_0_) | copy-start | bytes 1540
  8.3 7.3 %copy-start.3 = (s32[1,1,4,12]{3,2,1,0:T(4,128)S(1)}, s32[1,1,4,12]{3,2,1,0:T(4,128)}, u32[]{:S(2)}) copy-start(s32[1,1,4,12]{3,2,1,0:T(4,128)} %rows.1) | copy-start | bytes 580
  8.3 7.3 %copy-start.4 = (s32[1,1,4]{2,1,0:T(1,128)S(1)}, s32[1,1,4]{2,1,0:T(1,128)}, u32[]{:S(2)}) copy-start(s32[1,1,4]{2,1,0:T(1,128)} %counts.3) | copy-start | bytes 52
  12.0 14.9 %collective-permute-start.10 = (bf16[16,64,256]{2,1,0:T(8,128)(2,1)S(1)}, bf16[16,64,256]{2,1,0:T(8,128)(2,1)S(1)}, u32[]{:S(2)}, u32[]{:S(2)}) collective-permute-start(bf16[16,64,256]{2,1,0:T(8,128)(2,1)S(1)} %get-tuple-element.76), channel_id=1, source_target_pairs={{0,8},{8,0},{16,24},{24,16},{1,9},{9,1},{17,25},{25,17},{2,10},{10... | collective-permute-start | bytes 1572872 | tf_op jit(solution)/shard_map/ppermute | solution.py:398
  12.2 22.8 %collective-permute-start.11 = (bf16[16,64,256]{2,1,0:T(8,128)(2,1)S(1)}, bf16[16,64,256]{2,1,0:T(8,128)(2,1)S(1)}, u32[]{:S(2)}, u32[]{:S(2)}) collective-permute-start(bf16[16,64,256]{2,1,0:T(8,128)(2,1)S(1)} %get-tuple-element.77), channel_id=1, source_target_pairs={{0,16},{8,24},{16,0},{24,8},{1,17},{9,25},{17,1},{25,9},{2,18},{10... | collective-permute-start | bytes 1572872 | tf_op jit(solution)/shard_map/ppermute | solution.py:398
  14.1 22.1 %collective-permute-start.12 = (bf16[16,64,256]{2,1,0:T(8,128)(2,1)S(1)}, bf16[16,64,256]{2,1,0:T(8,128)(2,1)S(1)}, u32[]{:S(2)}, u32[]{:S(2)}) collective-permute-start(bf16[16,64,256]{2,1,0:T(8,128)(2,1)S(1)} %get-tuple-element.78), channel_id=1, source_target_pairs={{0,24},{8,16},{16,8},{24,0},{1,25},{9,17},{17,9},{25,1},{2,26},{10... | collective-permute-start | bytes 1572872 | tf_op jit(solution)/shard_map/ppermute | solution.py:398
  40.8 19.7 %copy-start.7 = (f32[128,1024]{1,0:T(8,128)S(1)}, f32[128,1024]{1,0:T(8,128)}, u32[]{:S(2)}) copy-start(f32[128,1024]{1,0:T(8,128)} %refs_2_.3) | copy-start | bytes 1572868
  40.8 19.7 %copy-start.8 = (f32[128,1024]{1,0:T(8,128)S(1)}, f32[128,1024]{1,0:T(8,128)}, u32[]{:S(2)}) copy-start(f32[128,1024]{1,0:T(8,128)} %refs_3_.3) | copy-start | bytes 1572868
  40.8 19.6 %copy-start.9 = (f32[128,1024]{1,0:T(8,128)S(1)}, f32[128,1024]{1,0:T(8,128)}, u32[]{:S(2)}) copy-start(f32[128,1024]{1,0:T(8,128)} %refs_4_.1) | copy-start | bytes 1572868
  40.8 19.6 %copy-start.12 = (f32[128,1024]{1,0:T(8,128)S(1)}, f32[128,1024]{1,0:T(8,128)}, u32[]{:S(2)}) copy-start(f32[128,1024]{1,0:T(8,128)} %refs_5_.1) | copy-start | bytes 1572868
  40.8 3.8 %collective-permute-start.13 = (f32[17,64,256]{2,1,0:T(8,128)S(1)}, f32[17,64,256]{2,1,0:T(8,128)S(1)}, u32[]{:S(2)}, u32[]{:S(2)}) collective-permute-start(f32[17,64,256]{2,1,0:T(8,128)S(1)} %get-tuple-element.80), channel_id=1, source_target_pairs={{0,1},{1,0},{2,3},{3,2},{4,5},{5,4},{6,7},{7,6},{8,9},{9,8},{10,11... | collective-permute-start | bytes 3342344 | tf_op jit(solution)/shard_map/ppermute | solution.py:369
  40.9 22.6 %collective-permute-start.17 = (bf16[16,64,256]{2,1,0:T(8,128)(2,1)S(1)}, bf16[16,64,256]{2,1,0:T(8,128)(2,1)S(1)}, u32[]{:S(2)}, u32[]{:S(2)}) collective-permute-start(bf16[16,64,256]{2,1,0:T(8,128)(2,1)S(1)} %get-tuple-element.87), channel_id=1, source_target_pairs={{0,8},{8,0},{16,24},{24,16},{1,9},{9,1},{17,25},{25,17},{2,10},{10... | collective-permute-start | bytes 1572872 | tf_op jit(solution)/shard_map/ppermute | solution.py:398
  42.9 25.2 %collective-permute-start.18 = (bf16[16,64,256]{2,1,0:T(8,128)(2,1)S(1)}, bf16[16,64,256]{2,1,0:T(8,128)(2,1)S(1)}, u32[]{:S(2)}, u32[]{:S(2)}) collective-permute-start(bf16[16,64,256]{2,1,0:T(8,128)(2,1)S(1)} %get-tuple-element.88), channel_id=1, source_target_pairs={{0,16},{8,24},{16,0},{24,8},{1,17},{9,25},{17,1},{25,9},{2,18},{10... | collective-permute-start | bytes 1572872 | tf_op jit(solution)/shard_map/ppermute | solution.py:398
  44.6 23.5 %collective-permute-start.19 = (bf16[16,64,256]{2,1,0:T(8,128)(2,1)S(1)}, bf16[16,64,256]{2,1,0:T(8,128)(2,1)S(1)}, u32[]{:S(2)}, u32[]{:S(2)}) collective-permute-start(bf16[16,64,256]{2,1,0:T(8,128)(2,1)S(1)} %get-tuple-element.89), channel_id=1, source_target_pairs={{0,24},{8,16},{16,8},{24,0},{1,25},{9,17},{17,9},{25,1},{2,26},{10... | collective-permute-start | bytes 1572872 | tf_op jit(solution)/shard_map/ppermute | solution.py:398
  46.0 7.5 %collective-permute-start.14 = (s16[528,128]{1,0:T(8,128)(2,1)S(1)}, s16[528,128]{1,0:T(8,128)(2,1)S(1)}, u32[]{:S(2)}, u32[]{:S(2)}) collective-permute-start(s16[528,128]{1,0:T(8,128)(2,1)S(1)} %get-tuple-element.82), channel_id=1, source_target_pairs={{0,2},{2,0},{4,6},{6,4},{1,3},{3,1},{5,7},{7,5},{8,10},{10,8},{12,... | collective-permute-start | bytes 405512 | tf_op jit(solution)/shard_map/ppermute | solution.py:373
  48.4 12.1 %collective-permute-start.15 = (s16[528,128]{1,0:T(8,128)(2,1)S(1)}, s16[528,128]{1,0:T(8,128)(2,1)S(1)}, u32[]{:S(2)}, u32[]{:S(2)}) collective-permute-start(s16[528,128]{1,0:T(8,128)(2,1)S(1)} %get-tuple-element.83), channel_id=1, source_target_pairs={{0,4},{2,6},{4,0},{6,2},{1,5},{3,7},{5,1},{7,3},{8,12},{10,14},{12... | collective-permute-start | bytes 405512 | tf_op jit(solution)/shard_map/ppermute | solution.py:373
  53.5 6.9 %collective-permute-start.16 = (s16[528,128]{1,0:T(8,128)(2,1)S(1)}, s16[528,128]{1,0:T(8,128)(2,1)S(1)}, u32[]{:S(2)}, u32[]{:S(2)}) collective-permute-start(s16[528,128]{1,0:T(8,128)(2,1)S(1)} %get-tuple-element.84), channel_id=1, source_target_pairs={{0,6},{2,4},{4,2},{6,0},{1,7},{3,5},{5,3},{7,1},{8,14},{10,12},{12... | collective-permute-start | bytes 405512 | tf_op jit(solution)/shard_map/ppermute | solution.py:373
  73.4 2.8 %collective-permute-start.20 = (f32[17,64,256]{2,1,0:T(8,128)S(1)}, f32[17,64,256]{2,1,0:T(8,128)S(1)}, u32[]{:S(2)}, u32[]{:S(2)}) collective-permute-start(f32[17,64,256]{2,1,0:T(8,128)S(1)} %get-tuple-element.92), channel_id=1, source_target_pairs={{0,1},{1,0},{2,3},{3,2},{4,5},{5,4},{6,7},{7,6},{8,9},{9,8},{10,11... | collective-permute-start | bytes 3342344 | tf_op jit(solution)/shard_map/ppermute | solution.py:369
  77.6 19.8 %copy-start.6 = (bf16[4,1,128,2048]{3,2,1,0:T(8,128)(2,1)S(1)}, bf16[4,1,128,2048]{3,2,1,0:T(8,128)(2,1)}, u32[]{:S(2)}) copy-start(bf16[4,1,128,2048]{3,2,1,0:T(8,128)(2,1)} %param.11) | copy-start | bytes 6291460
  77.6 8.7 %collective-permute-start.21 = (s16[528,128]{1,0:T(8,128)(2,1)S(1)}, s16[528,128]{1,0:T(8,128)(2,1)S(1)}, u32[]{:S(2)}, u32[]{:S(2)}) collective-permute-start(s16[528,128]{1,0:T(8,128)(2,1)S(1)} %get-tuple-element.94), channel_id=1, source_target_pairs={{0,2},{2,0},{4,6},{6,4},{1,3},{3,1},{5,7},{7,5},{8,10},{10,8},{12,... | collective-permute-start | bytes 405512 | tf_op jit(solution)/shard_map/ppermute | solution.py:373
  80.5 13.2 %collective-permute-start.22 = (s16[528,128]{1,0:T(8,128)(2,1)S(1)}, s16[528,128]{1,0:T(8,128)(2,1)S(1)}, u32[]{:S(2)}, u32[]{:S(2)}) collective-permute-start(s16[528,128]{1,0:T(8,128)(2,1)S(1)} %get-tuple-element.95), channel_id=1, source_target_pairs={{0,4},{2,6},{4,0},{6,2},{1,5},{3,7},{5,1},{7,3},{8,12},{10,14},{12... | collective-permute-start | bytes 405512 | tf_op jit(solution)/shard_map/ppermute | solution.py:373
  82.7 11.0 %collective-permute-start.23 = (s16[528,128]{1,0:T(8,128)(2,1)S(1)}, s16[528,128]{1,0:T(8,128)(2,1)S(1)}, u32[]{:S(2)}, u32[]{:S(2)}) collective-permute-start(s16[528,128]{1,0:T(8,128)(2,1)S(1)} %get-tuple-element.96), channel_id=1, source_target_pairs={{0,6},{2,4},{4,2},{6,0},{1,7},{3,5},{5,3},{7,1},{8,14},{10,12},{12... | collective-permute-start | bytes 405512 | tf_op jit(solution)/shard_map/ppermute | solution.py:373

commit v3 on v2

--- a/solution.py
+++ b/solution.py
@@ -10,9 +10,10 @@
 
 NEWTON = 4
 CAP = 16
-FIRST = 4
+FIRST = 3
 PAD = 16
 LANES = 128
+SPLIT = 2
 GROUP = 4
 ANY = pl.BlockSpec(memory_space=pl.ANY)
 SMEM = pl.BlockSpec(memory_space=pltpu.SMEM)
@@ -123,18 +124,10 @@
 
 
 def plan_kernel(cap, col_size, per_owner, where, cols, rows, counts, *refs):
-    needs, tiles, (table, size, over, held, places, sem) = refs[:-7], refs[-7], refs[-6:]
+    needs, tiles, (table, size, over, held, places) = refs[:-6], refs[-6], refs[-5:]
     lags, total = needs[0].shape
     row, core = where[0], where[2]
     members = len(needs)
-    started = jnp.int32(0)
-    for lag in range(lags):
-
-        def begin(slot, started, lag=lag):
-            pltpu.make_async_copy(tiles.at[lag, slot], held.at[started], sem.at[started]).start()
-            return started + 1
-
-        started = lax.fori_loop(0, counts[0, 0, lag], begin, started)
     local_blocks = total // members
     for owner in range(members):
         position = jnp.int32(0)
@@ -145,13 +138,10 @@
     above = jnp.int32(0)
     for member in range(members):
         for owner in range(members):
-
-            def count(block, wanted, member=member, owner=owner):
-                for lag in range(lags):
+            wanted = jnp.int32(0)
+            for lag in range(lags):
+                for block in range(local_blocks):
                     wanted = wanted + needs[member][lag, owner * local_blocks + block]
-                return wanted
-
-            wanted = lax.fori_loop(0, local_blocks, count, jnp.int32(0))
             foreign = lax.bitwise_xor(row, member) != owner
             above = jnp.where(foreign & (wanted > cap), 1, above)
     over[0] = above
@@ -168,16 +158,11 @@
             table[2, filled] = col % local_blocks
             table[3, filled] = jnp.minimum(places[lag, col], cap - 1)
             table[4, filled] = half * per_owner + target % per_owner
+            held[filled] = tiles[lag, slot]
             return filled + 1
 
         filled = lax.fori_loop(0, counts[0, 0, lag], note, filled)
     size[0] = filled
-
-    def settle(index, carry):
-        pltpu.make_async_copy(tiles.at[0, 0], held.at[index], sem.at[index]).wait()
-        return carry
-
-    lax.fori_loop(0, filled, settle, 0)
 
 
 def make_plan(where, cols, rows, counts, needs, tiles, cap, col_size, per_owner):
@@ -192,16 +177,17 @@
             jax.ShapeDtypeStruct((1,), jnp.int32),
             held,
         ],
-        in_specs=[SMEM] * (4 + len(needs)) + [ANY],
+        in_specs=[SMEM] * (4 + len(needs)) + [VMEM],
         out_specs=[SMEM] * 3 + [VMEM],
-        scratch_shapes=[pltpu.SMEM((lags, total), jnp.int32), pltpu.SemaphoreType.DMA((count,))],
-        compiler_params=params(held),
+        scratch_shapes=[pltpu.SMEM((lags, total), jnp.int32)],
+        compiler_params=params(tiles, held),
         name="plan_tiles",
     )(where, cols, rows, counts, *needs, tiles)
 
 
 def tiles_kernel(first, whole, extra, over, table, size, tiles, history, *refs):
-    received, (kept, given, blocks, sums) = refs[: len(refs) - 4 - extra], refs[-4:]
+    received, given = refs[: len(refs) - 3 - SPLIT - extra], refs[-2 - SPLIT : -2]
+    kept, (blocks, sums) = refs[-3 - SPLIT], refs[-2:]
     side = tiles.shape[2]
     halves, part, _ = sums.shape
     live = size[0]
@@ -245,36 +231,45 @@
 
     lax.fori_loop(0, (live + GROUP - 1) // GROUP, multiply, 0)
     kept[...] = sums[: halves // 2]
-    given[: halves // 2] = sums[halves // 2 :]
-    given[halves // 2] = jnp.full((part, side), 1.0, jnp.float32) * over[0].astype(jnp.float32)
+    half = halves // 2
+    for index, target in enumerate(given):
+        size = half // SPLIT
+        target[:size] = sums[half + index * size : half + (index + 1) * size]
+    given[0][half // SPLIT] = jnp.full((part, side), 1.0, jnp.float32) * over[0].astype(jnp.float32)
 
 
 def multiply_tiles(first, part, whole, over, table, size, tiles, history, received, chunks, after):
     side = tiles.shape[2]
     half = jax.ShapeDtypeStruct((chunks, part, side), jnp.float32)
-    more = jax.ShapeDtypeStruct((chunks + 1, part, side), jnp.float32)
+    more = [
+        jax.ShapeDtypeStruct((chunks // SPLIT + (index == 0), part, side), jnp.float32) for index in range(SPLIT)
+    ]
     blocks = pltpu.VMEM((table.shape[1], part, side), history.dtype)
     sums = pltpu.VMEM((2 * chunks, part, side), jnp.float32)
     return pl.pallas_call(
         functools.partial(tiles_kernel, first, whole, len(after)),
-        out_shape=[half, more],
+        out_shape=[half, *more],
         in_specs=[SMEM] * 3 + [VMEM] * (2 + len(received)) + [ANY] * len(after),
-        out_specs=[VMEM, VMEM],
+        out_specs=[VMEM] * (1 + SPLIT),
         scratch_shapes=[blocks, sums],
         compiler_params=params(tiles, history, *received, half, half, blocks, sums),
         name="multiply_tiles",
     )(over, table, size, tiles, history, *received, *after)
 
 
-def code_kernel(per_owner, where, over, kept, got, own, *coded):
+def code_kernel(per_owner, where, over, kept, *refs):
+    got, own, coded, theirs = refs[:SPLIT], refs[SPLIT], refs[SPLIT + 1 : -1], refs[-1]
     chunks, part, side = kept.shape
+    size = chunks // SPLIT
+    for index, source in enumerate(got):
+        theirs[index * size : (index + 1) * size] = source[:size]
     col = where[1]
-    flag = jnp.maximum(over[0].astype(jnp.float32), got[chunks][:1, :LANES])
+    flag = jnp.maximum(over[0].astype(jnp.float32), got[0][size][:1, :LANES])
     for step in list(range(1, chunks // per_owner)) + [0]:
         chunk = lax.bitwise_xor(col, step) * per_owner
         exponents = []
         for block in range(per_owner):
-            value = kept[chunk + block] + got[chunk + block]
+            value = kept[chunk + block] + theirs[chunk + block]
             if step == 0:
                 own[block] = value
                 continue
@@ -303,11 +298,12 @@
     return pl.pallas_call(
         functools.partial(code_kernel, per_owner),
         out_shape=outs,
-        in_specs=[SMEM] * 2 + [VMEM, VMEM],
+        in_specs=[SMEM] * 2 + [VMEM] * (1 + len(got)),
         out_specs=[VMEM] * len(outs),
-        compiler_params=params(kept, got, *outs),
+        scratch_shapes=[pltpu.VMEM(kept.shape, jnp.float32)],
+        compiler_params=params(kept, kept, *got, *outs),
         name="add_and_code",
-    )(where, over, kept, got)
+    )(where, over, kept, *got)
 
 
 def solve_kernel(first, fresh, over, *refs):
@@ -366,7 +362,7 @@
 def reduce(first, where, over, fields, kept, given, before):
     per_owner = fields[0].shape[1] // kept.shape[2]
     col_size = lax.axis_size("col")
-    got = lax.ppermute(given, "lag", partners(lax.axis_size("lag"), 1))
+    got = [lax.ppermute(array, "lag", partners(lax.axis_size("lag"), 1)) for array in given]
     own, *coded = code(where, over, kept, got, per_owner)
     arrived = [None] * (col_size - 1)
     for step in range(col_size - 1, 0, -1):
@@ -405,7 +401,7 @@
     after = ()
     result = None
     for (first, part), blocks in zip(pieces, received):
-        kept, given = multiply_tiles(
+        kept, *given = multiply_tiles(
             first, part, False, over, table, size, live_tiles, held, blocks, chunks, after
         )
         *result, flag = reduce(first, where, over, fields, kept, given, result)
@@ -413,7 +409,7 @@
 
     def general():
         everything = [lax.ppermute(history, "row", partners(row_size, step)) for step in range(1, row_size)]
-        kept, given = multiply_tiles(
+        kept, *given = multiply_tiles(
             0, sims, True, over, table, size, live_tiles, history, everything, chunks, ()
         )
         return tuple(reduce(0, where, over, fields, kept, given, None)[:2])

time: 98 us -> 92.8 us (0.947); the launches traced: 97.8 us -> 91.5 us
  waiting for transfers between devices: 38.3 us -> 34 us
  Pallas kernels: 31.6 us -> 28.4 us
  starting transfers between devices: 25.9 us -> 27.1 us
    ppermute x6, waiting for transfers between devices: 17.1 us -> 11.9 us  [local(): lax.ppermute(packed.pop(0), 'row', partners(row_size, step))]
    pallas_call x1, Pallas kernels: 8.04 us -> 2.89 us  [make_plan(): pl.pallas_call(functools.partial(plan_kernel, cap, col_size, per_owner),...]
    ppermute x2 -> x4, waiting for transfers between devices: 2.71 us -> 4.49 us  [reduce(): lax.ppermute(array, 'lag', partners(lax.axis_size('lag'), 1))]
    pallas_call x2, Pallas kernels: 9.84 us -> 11.6 us  [multiply_tiles(): pl.pallas_call(functools.partial(tiles_kernel, first, whole, len(after)),...]
  transfers between devices with their start and end apart: 17 -> 19, of which waited for: 11 -> 12; matrix products, arithmetic and copies ran while one was open for 0% -> 0% of each run, Pallas kernels for 15% -> 15%
where the time goes in v3:
time: 92.8 us; the launch traced here: 91.5 us
  waiting for transfers between devices  34 us (37%)
  Pallas kernels  28.4 us (31%)
  starting transfers between devices  27.1 us (29%)
  between operations  1.69 us (2%)
    ppermute x6, waiting for transfers between devices, reduce(): lax.ppermute(coded[step - 1], 'col', partners(col_size, step))  15.7 us
    ppermute x6, starting transfers between devices, reduce(): lax.ppermute(coded[step - 1], 'col', partners(col_size, step))  14.4 us
    ppermute x6, waiting for transfers between devices, local(): lax.ppermute(packed.pop(0), 'row', partners(row_size, step))  11.9 us
    pallas_call x2, Pallas kernels, multiply_tiles(): pl.pallas_call(functools.partial(tiles_kernel, first, whole, len(after)),...  11.6 us
    ppermute x6, starting transfers between devices, local(): lax.ppermute(packed.pop(0), 'row', partners(row_size, step))  7.04 us
    pallas_call x2, Pallas kernels, solve(): pl.pallas_call(functools.partial(solve_kernel, first, fresh), out_shape=[...  6.2 us
    ppermute x4, waiting for transfers between devices, reduce(): lax.ppermute(array, 'lag', partners(lax.axis_size('lag'), 1))  4.49 us
    ppermute x3, starting transfers between devices, local(): lax.ppermute(need, 'row', partners(row_size, step))  4.46 us
  transfers between devices with their start and end apart: 19, of which 12 were waited for; matrix products, arithmetic and copies ran while one was open for 0% of the time, Pallas kernels for 15%

profile of v3, /device:TPU:0, one launch (start us, length us, event | category | flops | bytes accessed | tf_op | source)
XLA Modules:
  0.0 91.5 jit_solution(15190454062425274853)
XLA Ops:
  0.6 1.3 %mark_blocks.1.refs_0_ = s32[4,32]{1,0:T(4,128)} custom-call(s32[1,1,4,12]{3,2,1,0:T(4,128)} %cols.3, s32[1,1,4]{2,1,0:T(1,128)} %counts.3), custom_call_target="tpu_custom_call" | custom-call | tf_op jit(solution)/shard_map/mark_blocks/pallas_call | solution.py:63
  2.0 3.9 %collective-permute-start.10 = (s32[4,32]{1,0:T(4,128)}, s32[4,32]{1,0:T(4,128)S(1)}, u32[]{:S(2)}, u32[]{:S(2)}) collective-permute-start(s32[4,32]{1,0:T(4,128)} %mark_blocks.1.refs_0_), channel_id=1, source_target_pairs={{0,24},{8,16},{16,8},{24,0},{1,25},{9,17},{17,9},{25,1},{2,26},{10... | collective-permute-start | bytes 1544 | tf_op jit(solution)/shard_map/ppermute | solution.py:390
  5.9 0.5 collective-permute-start.9
  6.5 1.8 %load_history.1.refs_3_.history = bf16[4,128,2048]{2,1,0:T(8,128)(2,1)S(1)} custom-call(bf16[4,128,2048]{2,1,0:T(8,128)(2,1)} %bitcast.7), custom_call_target="tpu_custom_call" | custom-call | tf_op jit(solution)/shard_map/load_history/pallas_call | solution.py:79
  8.3 1.3 %collective-permute-done.9.refs_2_.refs_1_ = s32[4,32]{1,0:T(4,128)S(1)} collective-permute-done((s32[4,32]{1,0:T(4,128)}, s32[4,32]{1,0:T(4,128)S(1)}, u32[]{:S(2)}, u32[]{:S(2)}) %collective-permute-start.9) | collective-permute-done | bytes 544 | tf_op jit(solution)/shard_map/ppermute | solution.py:390
  9.7 0.5 collective-permute-done.8.refs_1_.refs_0_
  10.2 1.9 %pack_history.1 = (bf16[16,48,256]{2,1,0:T(8,128)(2,1)S(1)}, bf16[16,48,256]{2,1,0:T(8,128)(2,1)S(1)}, bf16[16,48,256]{2,1,0:T(8,128)(2,1)S(1)}, bf16[16,80,256]...) custom-call(s32[3]{0:T(128)S(1)} %pad_add_fusion.where, ...), custom_call_target="tpu_custom_call" | custom-call | tf_op jit(solution)/shard_map/pack_history/pallas_call | solution.py:116
  12.2 1.9 %collective-permute-start.12 = (bf16[16,48,256]{2,1,0:T(8,128)(2,1)S(1)}, bf16[16,48,256]{2,1,0:T(8,128)(2,1)S(1)}, u32[]{:S(2)}, u32[]{:S(2)}) collective-permute-start(bf16[16,48,256]{2,1,0:T(8,128)(2,1)S(1)} %get-tuple-element.80), channel_id=1, source_target_pairs={{0,16},{8,24},{16,0},{24,8},{1,17},{9,25},{17,1},{25,9},{2,18},{10... | collective-permute-start | bytes 1179656 | tf_op jit(solution)/shard_map/ppermute | solution.py:394
  14.1 1.5 %collective-permute-start.13 = (bf16[16,48,256]{2,1,0:T(8,128)(2,1)S(1)}, bf16[16,48,256]{2,1,0:T(8,128)(2,1)S(1)}, u32[]{:S(2)}, u32[]{:S(2)}) collective-permute-start(bf16[16,48,256]{2,1,0:T(8,128)(2,1)S(1)} %get-tuple-element.81), channel_id=1, source_target_pairs={{0,24},{8,16},{16,8},{24,0},{1,25},{9,17},{17,9},{25,1},{2,26},{10... | collective-permute-start | bytes 1179656 | tf_op jit(solution)/shard_map/ppermute | solution.py:394
  15.7 1.9 %collective-permute-start.20 = (bf16[16,80,256]{2,1,0:T(8,128)(2,1)S(1)}, bf16[16,80,256]{2,1,0:T(8,128)(2,1)S(1)}, u32[]{:S(2)}, u32[]{:S(2)}) collective-permute-start(bf16[16,80,256]{2,1,0:T(8,128)(2,1)S(1)} %get-tuple-element.92), channel_id=1, source_target_pairs={{0,16},{8,24},{16,0},{24,8},{1,17},{9,25},{17,1},{25,9},{2,18},{10... | collective-permute-start | bytes 1966088 | tf_op jit(solution)/shard_map/ppermute | solution.py:394
  17.6 6.5 %collective-permute-done.11.refs_0_ = bf16[16,48,256]{2,1,0:T(8,128)(2,1)S(1)} collective-permute-done((bf16[16,48,256]{2,1,0:T(8,128)(2,1)S(1)}, bf16[16,48,256]{2,1,0:T(8,128)(2,1)S(1)}, u32[]{:S(2)}, u32[]{:S(2)}) %collective-permute-start.11) | collective-permute-done | bytes 393248 | tf_op jit(solution)/shard_map/ppermute | solution.py:394
  24.1 1.5 %collective-permute-start.21 = (bf16[16,80,256]{2,1,0:T(8,128)(2,1)S(1)}, bf16[16,80,256]{2,1,0:T(8,128)(2,1)S(1)}, u32[]{:S(2)}, u32[]{:S(2)}) collective-permute-start(bf16[16,80,256]{2,1,0:T(8,128)(2,1)S(1)} %get-tuple-element.93), channel_id=1, source_target_pairs={{0,24},{8,16},{16,8},{24,0},{1,25},{9,17},{17,9},{25,1},{2,26},{10... | collective-permute-start | bytes 1966088 | tf_op jit(solution)/shard_map/ppermute | solution.py:394
  25.6 2.9 %plan_tiles.1 = (s32[5,48]{1,0:T(8,128)S(1)}, s32[1]{0:T(128)}, s32[1]{0:T(128)}, bf16[48,256,256]{2,1,0:T(8,128)(2,1)S(1)}) custom-call(s32[3]{0:T(128)S(1)} %pad_add_fusion.where, s32[1,1,4,12]{3,2,1,0:T(4,128)S(1)} %copy-done.1, s32[1,1,4,12]{3,2,1,0:T(4,128)S(1)} %copy-done.3, s32[1,1,4]{2,1,0:T(1,128)S(1)} %copy-done.4, s32[4,32]{1,0:T(4,128)S(1)} %copy-done.2, ...), custom_call_target="tpu_custom_call" | custom-call | tf_op jit(solution)/shard_map/plan_tiles/pallas_call | solution.py:172
  28.5 3.4 %collective-permute-done.12.refs_1_ = bf16[16,48,256]{2,1,0:T(8,128)(2,1)S(1)} collective-permute-done((bf16[16,48,256]{2,1,0:T(8,128)(2,1)S(1)}, bf16[16,48,256]{2,1,0:T(8,128)(2,1)S(1)}, u32[]{:S(2)}, u32[]{:S(2)}) %collective-permute-start.12) | collective-permute-done | bytes 393248 | tf_op jit(solution)/shard_map/ppermute | solution.py:394
  32.0 1.6 %collective-permute-done.13.refs_2_ = bf16[16,48,256]{2,1,0:T(8,128)(2,1)S(1)} collective-permute-done((bf16[16,48,256]{2,1,0:T(8,128)(2,1)S(1)}, bf16[16,48,256]{2,1,0:T(8,128)(2,1)S(1)}, u32[]{:S(2)}, u32[]{:S(2)}) %collective-permute-start.13) | collective-permute-done | bytes 393248 | tf_op jit(solution)/shard_map/ppermute | solution.py:394
  33.5 5.4 %multiply_tiles.4 = (f32[16,48,256]{2,1,0:T(8,128)S(1)}, f32[9,48,256]{2,1,0:T(8,128)S(1)}, f32[8,48,256]{2,1,0:T(8,128)S(1)}) custom-call(s32[1]{0:T(128)} %get-tuple-element.75.over, s32[5,48]{1,0:T(8,128)S(1)} %get-tuple-element.76.table, s32[1]{0:T(128)} %get-tuple-element.77.size, bf16[48,256,256]{2,1,0:T(8,128)(2,1)S(1)} %get-tuple-element.78.tiles, ...), custom_call_target="tpu_custom_call" | custom-call | tf_op jit(solution)/shard_map/multiply_tiles/pallas_call | solution.py:249
  39.0 0.5 collective-permute-start.15
  39.5 1.8 %collective-permute-done.15.refs_1_ = f32[8,48,256]{2,1,0:T(8,128)S(1)} collective-permute-done((f32[8,48,256]{2,1,0:T(8,128)S(1)}, f32[8,48,256]{2,1,0:T(8,128)S(1)}, u32[]{:S(2)}, u32[]{:S(2)}) %collective-permute-start.15) | collective-permute-done | bytes 393248 | tf_op jit(solution)/shard_map/ppermute | solution.py:365
  41.3 1.3 %add_and_code.4 = (f32[4,48,256]{2,1,0:T(8,128)S(1)}, s16[400,128]{1,0:T(8,128)(2,1)S(1)}, s16[400,128]{1,0:T(8,128)(2,1)S(1)}, s16[400,128]{1,0:T(8,128)(2,1)S(1)}) custom-call(s32[3]{0:T(128)S(1)} %pad_add_fusion.where, s32[1]{0:T(128)} %get-tuple-element.75.over, f32[16,48,256]{2,1,0:T(8,128)S(1)} %get-tuple-element.82.kept, ...), custom_call_target="tpu_custom_call" | custom-call | tf_op jit(solution)/shard_map/add_and_code/pallas_call | solution.py:298
  42.7 0.8 collective-permute-start.16
  43.5 3.8 %collective-permute-start.17 = (s16[400,128]{1,0:T(8,128)(2,1)S(1)}, s16[400,128]{1,0:T(8,128)(2,1)S(1)}, u32[]{:S(2)}, u32[]{:S(2)}) collective-permute-start(s16[400,128]{1,0:T(8,128)(2,1)S(1)} %get-tuple-element.87), channel_id=1, source_target_pairs={{0,4},{2,6},{4,0},{6,2},{1,5},{3,7},{5,1},{7,3},{8,12},{10,14},{12... | collective-permute-start | bytes 307208 | tf_op jit(solution)/shard_map/ppermute | solution.py:369
  47.7 5.2 %collective-permute-start.18 = (s16[400,128]{1,0:T(8,128)(2,1)S(1)}, s16[400,128]{1,0:T(8,128)(2,1)S(1)}, u32[]{:S(2)}, u32[]{:S(2)}) collective-permute-start(s16[400,128]{1,0:T(8,128)(2,1)S(1)} %get-tuple-element.88), channel_id=1, source_target_pairs={{0,6},{2,4},{4,2},{6,0},{1,7},{3,5},{5,3},{7,1},{8,14},{10,12},{12... | collective-permute-start | bytes 307208 | tf_op jit(solution)/shard_map/ppermute | solution.py:369
  52.8 2.7 %collective-permute-done.18.refs_7_ = s16[400,128]{1,0:T(8,128)(2,1)S(1)} collective-permute-done((s16[400,128]{1,0:T(8,128)(2,1)S(1)}, s16[400,128]{1,0:T(8,128)(2,1)S(1)}, u32[]{:S(2)}, u32[]{:S(2)}) %collective-permute-start.18) | collective-permute-done | bytes 102432 | tf_op jit(solution)/shard_map/ppermute | solution.py:369
  55.6 2.7 %friction_solve.4 = (f32[128,1024]{1,0:T(8,128)}, f32[128,1024]{1,0:T(8,128)}, s32[1]{0:T(128)}) custom-call(s32[1]{0:T(128)} %get-tuple-element.75.over, f32[128,1024]{1,0:T(8,128)S(1)} %copy-done.7, f32[128,1024]{1,0:T(8,128)S(1)} %copy-done.8, f32[128,1024]{1,0:T(8,128)S(1)} %copy-done.9, f32[128,1024]{1,0:T(8,128)S(1)} %copy-done.12, ...), custom_call_target="tpu_custom_call" | custom-call | tf_op jit(solution)/shard_map/friction_solve/pallas_call | solution.py:349
  58.7 6.2 %multiply_tiles.5 = (f32[16,80,256]{2,1,0:T(8,128)S(1)}, f32[9,80,256]{2,1,0:T(8,128)S(1)}, f32[8,80,256]{2,1,0:T(8,128)S(1)}) custom-call(s32[1]{0:T(128)} %get-tuple-element.75.over, s32[5,48]{1,0:T(8,128)S(1)} %get-tuple-element.76.table, s32[1]{0:T(128)} %get-tuple-element.77.size, bf16[48,256,256]{2,1,0:T(8,128)(2,1)S(1)} %get-tuple-element.78.tiles, ...), custom_call_target="tpu_custom_call" | custom-call | tf_op jit(solution)/shard_map/multiply_tiles/pallas_call | solution.py:249
  65.5 2.6 %collective-permute-done.23.refs_1_ = f32[8,80,256]{2,1,0:T(8,128)S(1)} collective-permute-done((f32[8,80,256]{2,1,0:T(8,128)S(1)}, f32[8,80,256]{2,1,0:T(8,128)S(1)}, u32[]{:S(2)}, u32[]{:S(2)}) %collective-permute-start.23) | collective-permute-done | bytes 655392 | tf_op jit(solution)/shard_map/ppermute | solution.py:365
  68.2 1.5 %add_and_code.5 = (f32[4,80,256]{2,1,0:T(8,128)S(1)}, s16[656,128]{1,0:T(8,128)(2,1)S(1)}, s16[656,128]{1,0:T(8,128)(2,1)S(1)}, s16[656,128]{1,0:T(8,128)(2,1)S(1)}) custom-call(s32[3]{0:T(128)S(1)} %pad_add_fusion.where, s32[1]{0:T(128)} %get-tuple-element.75.over, f32[16,80,256]{2,1,0:T(8,128)S(1)} %get-tuple-element.95.kept, ...), custom_call_target="tpu_custom_call" | custom-call | tf_op jit(solution)/shard_map/add_and_code/pallas_call | solution.py:298
  69.7 2.0 %collective-permute-start.24 = (s16[656,128]{1,0:T(8,128)(2,1)S(1)}, s16[656,128]{1,0:T(8,128)(2,1)S(1)}, u32[]{:S(2)}, u32[]{:S(2)}) collective-permute-start(s16[656,128]{1,0:T(8,128)(2,1)S(1)} %get-tuple-element.99), channel_id=1, source_target_pairs={{0,2},{2,0},{4,6},{6,4},{1,3},{3,1},{5,7},{7,5},{8,10},{10,8},{12,... | collective-permute-start | bytes 503816 | tf_op jit(solution)/shard_map/ppermute | solution.py:369
  71.7 2.6 %collective-permute-start.25 = (s16[656,128]{1,0:T(8,128)(2,1)S(1)}, s16[656,128]{1,0:T(8,128)(2,1)S(1)}, u32[]{:S(2)}, u32[]{:S(2)}) collective-permute-start(s16[656,128]{1,0:T(8,128)(2,1)S(1)} %get-tuple-element.100), channel_id=1, source_target_pairs={{0,4},{2,6},{4,0},{6,2},{1,5},{3,7},{5,1},{7,3},{8,12},{10,14},{12... | collective-permute-start | bytes 503816 | tf_op jit(solution)/shard_map/ppermute | solution.py:369
  74.3 5.1 %collective-permute-done.24.refs_7_ = s16[656,128]{1,0:T(8,128)(2,1)S(1)} collective-permute-done((s16[656,128]{1,0:T(8,128)(2,1)S(1)}, s16[656,128]{1,0:T(8,128)(2,1)S(1)}, u32[]{:S(2)}, u32[]{:S(2)}) %collective-permute-start.24) | collective-permute-done | bytes 167968 | tf_op jit(solution)/shard_map/ppermute | solution.py:369
  79.4 7.5 %collective-permute-done.25.refs_8_ = s16[656,128]{1,0:T(8,128)(2,1)S(1)} collective-permute-done((s16[656,128]{1,0:T(8,128)(2,1)S(1)}, s16[656,128]{1,0:T(8,128)(2,1)S(1)}, u32[]{:S(2)}, u32[]{:S(2)}) %collective-permute-start.25) | collective-permute-done | bytes 167968 | tf_op jit(solution)/shard_map/ppermute | solution.py:369
  86.9 3.5 %friction_solve.5 = (f32[128,1024]{1,0:T(8,128)}, f32[128,1024]{1,0:T(8,128)}, s32[1]{0:T(128)}) custom-call(s32[1]{0:T(128)} %get-tuple-element.75.over, f32[128,1024]{1,0:T(8,128)} %get-tuple-element.89.refs_0_, f32[128,1024]{1,0:T(8,128)} %get-tuple-element.90.refs_1_, f32[128,1024]{1,0:T(8,128)S(1)} %copy-done.7, ...), custom_call_target="tpu_custom_call", output_to_operand_aliasing={{0}: (1, {}), {1}: (2, {})} | custom-call | tf_op jit(solution)/shard_map/friction_solve/pallas_call | solution.py:349
  (38 shorter events, 2.2 us)
Async XLA Ops:
  2.0 6.3 %collective-permute-start.10 = (s32[4,32]{1,0:T(4,128)}, s32[4,32]{1,0:T(4,128)S(1)}, u32[]{:S(2)}, u32[]{:S(2)}) collective-permute-start(s32[4,32]{1,0:T(4,128)} %mark_blocks.1.refs_0_), channel_id=1, source_target_pairs={{0,24},{8,16},{16,8},{24,0},{1,25},{9,17},{17,9},{25,1},{2,26},{10... | collective-permute-start | bytes 1544 | tf_op jit(solution)/shard_map/ppermute | solution.py:390
  5.9 3.8 %collective-permute-start.9 = (s32[4,32]{1,0:T(4,128)}, s32[4,32]{1,0:T(4,128)S(1)}, u32[]{:S(2)}, u32[]{:S(2)}) collective-permute-start(s32[4,32]{1,0:T(4,128)} %mark_blocks.1.refs_0_), channel_id=1, source_target_pairs={{0,16},{8,24},{16,0},{24,8},{1,17},{9,25},{17,1},{25,9},{2,18},{10... | collective-permute-start | bytes 1544 | tf_op jit(solution)/shard_map/ppermute | solution.py:390
  6.4 3.8 %collective-permute-start.8 = (s32[4,32]{1,0:T(4,128)}, s32[4,32]{1,0:T(4,128)S(1)}, u32[]{:S(2)}, u32[]{:S(2)}) collective-permute-start(s32[4,32]{1,0:T(4,128)} %mark_blocks.1.refs_0_), channel_id=1, source_target_pairs={{0,8},{8,0},{16,24},{24,16},{1,9},{9,1},{17,25},{25,17},{2,10},{10... | collective-permute-start | bytes 1544 | tf_op jit(solution)/shard_map/ppermute | solution.py:390
  6.5 19.1 %copy-start = (bf16[1,1,4,12,256,256]{5,4,3,2,1,0:T(8,128)(2,1)S(1)}, bf16[1,1,4,12,256,256]{5,4,3,2,1,0:T(8,128)(2,1)}, u32[]{:S(2)}) copy-start(bf16[1,1,4,12,256,256]{5,4,3,2,1,0:T(8,128)(2,1)} %param.12) | copy-start | bytes 18874372
  8.3 17.3 %copy-start.1 = (s32[1,1,4,12]{3,2,1,0:T(4,128)S(1)}, s32[1,1,4,12]{3,2,1,0:T(4,128)}, u32[]{:S(2)}) copy-start(s32[1,1,4,12]{3,2,1,0:T(4,128)} %cols.3) | copy-start | bytes 580
  8.3 17.3 %copy-start.2 = (s32[4,32]{1,0:T(4,128)S(1)}, s32[4,32]{1,0:T(4,128)}, u32[]{:S(2)}) copy-start(s32[4,32]{1,0:T(4,128)} %mark_blocks.1.refs_0_) | copy-start | bytes 1540
  8.3 17.3 %copy-start.3 = (s32[1,1,4,12]{3,2,1,0:T(4,128)S(1)}, s32[1,1,4,12]{3,2,1,0:T(4,128)}, u32[]{:S(2)}) copy-start(s32[1,1,4,12]{3,2,1,0:T(4,128)} %rows.1) | copy-start | bytes 580
  8.3 17.3 %copy-start.4 = (s32[1,1,4]{2,1,0:T(1,128)S(1)}, s32[1,1,4]{2,1,0:T(1,128)}, u32[]{:S(2)}) copy-start(s32[1,1,4]{2,1,0:T(1,128)} %counts.3) | copy-start | bytes 52
  12.0 12.1 %collective-permute-start.11 = (bf16[16,48,256]{2,1,0:T(8,128)(2,1)S(1)}, bf16[16,48,256]{2,1,0:T(8,128)(2,1)S(1)}, u32[]{:S(2)}, u32[]{:S(2)}) collective-permute-start(bf16[16,48,256]{2,1,0:T(8,128)(2,1)S(1)} %get-tuple-element.79), channel_id=1, source_target_pairs={{0,8},{8,0},{16,24},{24,16},{1,9},{9,1},{17,25},{25,17},{2,10},{10... | collective-permute-start | bytes 1179656 | tf_op jit(solution)/shard_map/ppermute | solution.py:394
  12.2 19.7 %collective-permute-start.12 = (bf16[16,48,256]{2,1,0:T(8,128)(2,1)S(1)}, bf16[16,48,256]{2,1,0:T(8,128)(2,1)S(1)}, u32[]{:S(2)}, u32[]{:S(2)}) collective-permute-start(bf16[16,48,256]{2,1,0:T(8,128)(2,1)S(1)} %get-tuple-element.80), channel_id=1, source_target_pairs={{0,16},{8,24},{16,0},{24,8},{1,17},{9,25},{17,1},{25,9},{2,18},{10... | collective-permute-start | bytes 1179656 | tf_op jit(solution)/shard_map/ppermute | solution.py:394
  14.1 19.4 %collective-permute-start.13 = (bf16[16,48,256]{2,1,0:T(8,128)(2,1)S(1)}, bf16[16,48,256]{2,1,0:T(8,128)(2,1)S(1)}, u32[]{:S(2)}, u32[]{:S(2)}) collective-permute-start(bf16[16,48,256]{2,1,0:T(8,128)(2,1)S(1)} %get-tuple-element.81), channel_id=1, source_target_pairs={{0,24},{8,16},{16,8},{24,0},{1,25},{9,17},{17,9},{25,1},{2,26},{10... | collective-permute-start | bytes 1179656 | tf_op jit(solution)/shard_map/ppermute | solution.py:394
  15.6 42.7 %collective-permute-start.19 = (bf16[16,80,256]{2,1,0:T(8,128)(2,1)S(1)}, bf16[16,80,256]{2,1,0:T(8,128)(2,1)S(1)}, u32[]{:S(2)}, u32[]{:S(2)}) collective-permute-start(bf16[16,80,256]{2,1,0:T(8,128)(2,1)S(1)} %get-tuple-element.91), channel_id=1, source_target_pairs={{0,8},{8,0},{16,24},{24,16},{1,9},{9,1},{17,25},{25,17},{2,10},{10... | collective-permute-start | bytes 1966088 | tf_op jit(solution)/shard_map/ppermute | solution.py:394
  15.7 42.6 %collective-permute-start.20 = (bf16[16,80,256]{2,1,0:T(8,128)(2,1)S(1)}, bf16[16,80,256]{2,1,0:T(8,128)(2,1)S(1)}, u32[]{:S(2)}, u32[]{:S(2)}) collective-permute-start(bf16[16,80,256]{2,1,0:T(8,128)(2,1)S(1)} %get-tuple-element.92), channel_id=1, source_target_pairs={{0,16},{8,24},{16,0},{24,8},{1,17},{9,25},{17,1},{25,9},{2,18},{10... | collective-permute-start | bytes 1966088 | tf_op jit(solution)/shard_map/ppermute | solution.py:394
  24.1 34.6 %collective-permute-start.21 = (bf16[16,80,256]{2,1,0:T(8,128)(2,1)S(1)}, bf16[16,80,256]{2,1,0:T(8,128)(2,1)S(1)}, u32[]{:S(2)}, u32[]{:S(2)}) collective-permute-start(bf16[16,80,256]{2,1,0:T(8,128)(2,1)S(1)} %get-tuple-element.93), channel_id=1, source_target_pairs={{0,24},{8,16},{16,8},{24,0},{1,25},{9,17},{17,9},{25,1},{2,26},{10... | collective-permute-start | bytes 1966088 | tf_op jit(solution)/shard_map/ppermute | solution.py:394
  33.5 22.0 %copy-start.7 = (f32[128,1024]{1,0:T(8,128)S(1)}, f32[128,1024]{1,0:T(8,128)}, u32[]{:S(2)}) copy-start(f32[128,1024]{1,0:T(8,128)} %refs_2_.3) | copy-start | bytes 1572868
  33.5 22.0 %copy-start.8 = (f32[128,1024]{1,0:T(8,128)S(1)}, f32[128,1024]{1,0:T(8,128)}, u32[]{:S(2)}) copy-start(f32[128,1024]{1,0:T(8,128)} %refs_3_.3) | copy-start | bytes 1572868
  33.5 22.0 %copy-start.9 = (f32[128,1024]{1,0:T(8,128)S(1)}, f32[128,1024]{1,0:T(8,128)}, u32[]{:S(2)}) copy-start(f32[128,1024]{1,0:T(8,128)} %refs_4_.1) | copy-start | bytes 1572868
  33.5 22.0 %copy-start.12 = (f32[128,1024]{1,0:T(8,128)S(1)}, f32[128,1024]{1,0:T(8,128)}, u32[]{:S(2)}) copy-start(f32[128,1024]{1,0:T(8,128)} %refs_5_.1) | copy-start | bytes 1572868
  38.9 2.4 %collective-permute-start.14 = (f32[9,48,256]{2,1,0:T(8,128)S(1)}, f32[9,48,256]{2,1,0:T(8,128)S(1)}, u32[]{:S(2)}, u32[]{:S(2)}) collective-permute-start(f32[9,48,256]{2,1,0:T(8,128)S(1)} %get-tuple-element.83), channel_id=1, source_target_pairs={{0,1},{1,0},{2,3},{3,2},{4,5},{5,4},{6,7},{7,6},{8,9},{9,8},{10,11... | collective-permute-start | bytes 1327112 | tf_op jit(solution)/shard_map/ppermute | solution.py:365
  39.0 2.3 %collective-permute-start.15 = (f32[8,48,256]{2,1,0:T(8,128)S(1)}, f32[8,48,256]{2,1,0:T(8,128)S(1)}, u32[]{:S(2)}, u32[]{:S(2)}) collective-permute-start(f32[8,48,256]{2,1,0:T(8,128)S(1)} %get-tuple-element.84), channel_id=1, source_target_pairs={{0,1},{1,0},{2,3},{3,2},{4,5},{5,4},{6,7},{7,6},{8,9},{9,8},{10,11... | collective-permute-start | bytes 1179656 | tf_op jit(solution)/shard_map/ppermute | solution.py:365
  42.7 5.0 %collective-permute-start.16 = (s16[400,128]{1,0:T(8,128)(2,1)S(1)}, s16[400,128]{1,0:T(8,128)(2,1)S(1)}, u32[]{:S(2)}, u32[]{:S(2)}) collective-permute-start(s16[400,128]{1,0:T(8,128)(2,1)S(1)} %get-tuple-element.86), channel_id=1, source_target_pairs={{0,2},{2,0},{4,6},{6,4},{1,3},{3,1},{5,7},{7,5},{8,10},{10,8},{12,... | collective-permute-start | bytes 307208 | tf_op jit(solution)/shard_map/ppermute | solution.py:369
  43.5 9.3 %collective-permute-start.17 = (s16[400,128]{1,0:T(8,128)(2,1)S(1)}, s16[400,128]{1,0:T(8,128)(2,1)S(1)}, u32[]{:S(2)}, u32[]{:S(2)}) collective-permute-start(s16[400,128]{1,0:T(8,128)(2,1)S(1)} %get-tuple-element.87), channel_id=1, source_target_pairs={{0,4},{2,6},{4,0},{6,2},{1,5},{3,7},{5,1},{7,3},{8,12},{10,14},{12... | collective-permute-start | bytes 307208 | tf_op jit(solution)/shard_map/ppermute | solution.py:369
  47.7 7.9 %collective-permute-start.18 = (s16[400,128]{1,0:T(8,128)(2,1)S(1)}, s16[400,128]{1,0:T(8,128)(2,1)S(1)}, u32[]{:S(2)}, u32[]{:S(2)}) collective-permute-start(s16[400,128]{1,0:T(8,128)(2,1)S(1)} %get-tuple-element.88), channel_id=1, source_target_pairs={{0,6},{2,4},{4,2},{6,0},{1,7},{3,5},{5,3},{7,1},{8,14},{10,12},{12... | collective-permute-start | bytes 307208 | tf_op jit(solution)/shard_map/ppermute | solution.py:369
  64.9 3.2 %collective-permute-start.22 = (f32[9,80,256]{2,1,0:T(8,128)S(1)}, f32[9,80,256]{2,1,0:T(8,128)S(1)}, u32[]{:S(2)}, u32[]{:S(2)}) collective-permute-start(f32[9,80,256]{2,1,0:T(8,128)S(1)} %get-tuple-element.96), channel_id=1, source_target_pairs={{0,1},{1,0},{2,3},{3,2},{4,5},{5,4},{6,7},{7,6},{8,9},{9,8},{10,11... | collective-permute-start | bytes 2211848 | tf_op jit(solution)/shard_map/ppermute | solution.py:365
  65.0 3.1 %collective-permute-start.23 = (f32[8,80,256]{2,1,0:T(8,128)S(1)}, f32[8,80,256]{2,1,0:T(8,128)S(1)}, u32[]{:S(2)}, u32[]{:S(2)}) collective-permute-start(f32[8,80,256]{2,1,0:T(8,128)S(1)} %get-tuple-element.97), channel_id=1, source_target_pairs={{0,1},{1,0},{2,3},{3,2},{4,5},{5,4},{6,7},{7,6},{8,9},{9,8},{10,11... | collective-permute-start | bytes 1966088 | tf_op jit(solution)/shard_map/ppermute | solution.py:365
  69.6 21.4 %copy-start.6 = (bf16[4,1,128,2048]{3,2,1,0:T(8,128)(2,1)S(1)}, bf16[4,1,128,2048]{3,2,1,0:T(8,128)(2,1)}, u32[]{:S(2)}) copy-start(bf16[4,1,128,2048]{3,2,1,0:T(8,128)(2,1)} %param.11) | copy-start | bytes 6291460
  69.7 9.7 %collective-permute-start.24 = (s16[656,128]{1,0:T(8,128)(2,1)S(1)}, s16[656,128]{1,0:T(8,128)(2,1)S(1)}, u32[]{:S(2)}, u32[]{:S(2)}) collective-permute-start(s16[656,128]{1,0:T(8,128)(2,1)S(1)} %get-tuple-element.99), channel_id=1, source_target_pairs={{0,2},{2,0},{4,6},{6,4},{1,3},{3,1},{5,7},{7,5},{8,10},{10,8},{12,... | collective-permute-start | bytes 503816 | tf_op jit(solution)/shard_map/ppermute | solution.py:369
  71.7 15.3 %collective-permute-start.25 = (s16[656,128]{1,0:T(8,128)(2,1)S(1)}, s16[656,128]{1,0:T(8,128)(2,1)S(1)}, u32[]{:S(2)}, u32[]{:S(2)}) collective-permute-start(s16[656,128]{1,0:T(8,128)(2,1)S(1)} %get-tuple-element.100), channel_id=1, source_target_pairs={{0,4},{2,6},{4,0},{6,2},{1,5},{3,7},{5,1},{7,3},{8,12},{10,14},{12... | collective-permute-start | bytes 503816 | tf_op jit(solution)/shard_map/ppermute | solution.py:369
  74.3 12.7 %collective-permute-start.26 = (s16[656,128]{1,0:T(8,128)(2,1)S(1)}, s16[656,128]{1,0:T(8,128)(2,1)S(1)}, u32[]{:S(2)}, u32[]{:S(2)}) collective-permute-start(s16[656,128]{1,0:T(8,128)(2,1)S(1)} %get-tuple-element.101), channel_id=1, source_target_pairs={{0,6},{2,4},{4,2},{6,0},{1,7},{3,5},{5,3},{7,1},{8,14},{10,12},{12... | collective-permute-start | bytes 503816 | tf_op jit(solution)/shard_map/ppermute | solution.py:369

commit v4 on v3

--- a/solution.py
+++ b/solution.py
@@ -10,11 +10,12 @@
 
 NEWTON = 4
 CAP = 16
-FIRST = 3
+PIECES = (4, 4)
 PAD = 16
 LANES = 128
 SPLIT = 2
-GROUP = 4
+WAIT = 1
+GROUP = 8
 ANY = pl.BlockSpec(memory_space=pl.ANY)
 SMEM = pl.BlockSpec(memory_space=pltpu.SMEM)
 VMEM = pl.BlockSpec(memory_space=pltpu.VMEM)
@@ -27,11 +28,6 @@
 
 def partners(size, step):
     return [(index, index ^ step) for index in range(size)]
-
-
-def inverse_sinh(value, root):
-    length = jnp.log(jnp.abs(value) + root)
-    return jnp.where(value < 0.0, -length, length)
 
 
 def friction(stress, base, velocity, direct, state):
@@ -40,9 +36,11 @@
     gain = direct * factor
     for step in range(NEWTON):
         scaled = velocity * factor
-        root = jnp.sqrt(1.0 + scaled * scaled)
-        misfit = direct * inverse_sinh(scaled, root) + 0.5 * velocity - driving
-        velocity = velocity - misfit / (gain / root + 0.5)
+        square = 1.0 + scaled * scaled
+        inverse = lax.rsqrt(square)
+        length = jnp.log(jnp.abs(scaled) + square * inverse)
+        misfit = direct * jnp.where(scaled < 0.0, -length, length) + 0.5 * velocity - driving
+        velocity = velocity - misfit / (gain * inverse + 0.5)
     return velocity
 
 
@@ -87,9 +85,10 @@
     )(history)
 
 
-def pack_kernel(cap, pieces, side, where, *refs):
-    peers = (len(refs) - 1) // (len(pieces) + 1)
-    needs, history, packed = refs[:peers], refs[peers], refs[peers + 1 :]
+def pack_kernel(cap, piece, side, extra, where, *refs):
+    begin, part = piece
+    peers = (len(refs) - 1 - extra) // 2
+    needs, history, packed = refs[:peers], refs[peers], refs[peers + 1 + extra :]
     lags, sims, width = history.shape
     local_blocks = width // side
     first = where[0] * local_blocks
@@ -101,30 +100,27 @@
 
                 @pl.when((wanted > 0) & (position < cap))
                 def _(peer=peer, lag=lag, block=block, position=position):
-                    for piece, (begin, part) in enumerate(pieces):
-                        packed[piece * peers + peer][position] = history[
-                            lag, begin : begin + part, block * side : (block + 1) * side
-                        ]
+                    packed[peer][position] = history[
+                        lag, begin : begin + part, block * side : (block + 1) * side
+                    ]
 
                 position = position + wanted
 
 
-def pack(where, needs, history, side, cap, pieces):
-    outs = []
-    for _, part in pieces:
-        outs += [jax.ShapeDtypeStruct((cap, part, side), history.dtype)] * len(needs)
-    return pl.pallas_call(
-        functools.partial(pack_kernel, cap, pieces, side),
+def pack(where, needs, history, side, cap, piece, after):
+    outs = [jax.ShapeDtypeStruct((cap, piece[1], side), history.dtype)] * len(needs)
+    return pl.pallas_call(
+        functools.partial(pack_kernel, cap, piece, side, len(after)),
         out_shape=outs,
-        in_specs=[SMEM] * (1 + len(needs)) + [VMEM],
+        in_specs=[SMEM] * (1 + len(needs)) + [VMEM] + [ANY] * len(after),
         out_specs=[VMEM] * len(outs),
         compiler_params=params(history, *outs),
         name="pack_history",
-    )(where, *needs, history)
+    )(where, *needs, history, *after)
 
 
 def plan_kernel(cap, col_size, per_owner, where, cols, rows, counts, *refs):
-    needs, tiles, (table, size, over, held, places) = refs[:-6], refs[-6], refs[-5:]
+    needs, tiles, (table, size, over, held, places, ends) = refs[:-7], refs[-7], refs[-6:]
     lags, total = needs[0].shape
     row, core = where[0], where[2]
     members = len(needs)
@@ -145,24 +141,38 @@
             foreign = lax.bitwise_xor(row, member) != owner
             above = jnp.where(foreign & (wanted > cap), 1, above)
     over[0] = above
-    filled = jnp.int32(0)
+    tally = [jnp.int32(0)] * members
     for lag in range(lags):
 
-        def note(slot, filled, lag=lag):
+        def tell(slot, tally, lag=lag):
+            source = lax.bitwise_xor(cols[0, 0, lag, slot] // local_blocks, row)
+            return tuple(count + (source == index).astype(jnp.int32) for index, count in enumerate(tally))
+
+        tally = lax.fori_loop(0, counts[0, 0, lag], tell, tuple(tally))
+    begin = jnp.int32(0)
+    for member in range(members):
+        size[member] = begin
+        ends[member] = begin
+        begin = begin + tally[member]
+    size[members] = begin
+    for lag in range(lags):
+
+        def note(slot, carry, lag=lag):
             col = cols[0, 0, lag, slot]
             target = rows[0, 0, lag, slot]
             owner = target // per_owner
             half = lax.bitwise_xor(owner % 2, core) * col_size + owner // 2
+            source = lax.bitwise_xor(col // local_blocks, row)
+            filled = ends[source]
+            ends[source] = filled + 1
             table[0, filled] = lag
-            table[1, filled] = lax.bitwise_xor(col // local_blocks, row)
+            table[1, filled] = half * per_owner + target % per_owner
             table[2, filled] = col % local_blocks
             table[3, filled] = jnp.minimum(places[lag, col], cap - 1)
-            table[4, filled] = half * per_owner + target % per_owner
             held[filled] = tiles[lag, slot]
-            return filled + 1
-
-        filled = lax.fori_loop(0, counts[0, 0, lag], note, filled)
-    size[0] = filled
+            return carry
+
+        lax.fori_loop(0, counts[0, 0, lag], note, 0)
 
 
 def make_plan(where, cols, rows, counts, needs, tiles, cap, col_size, per_owner):
@@ -172,47 +182,41 @@
     return pl.pallas_call(
         functools.partial(plan_kernel, cap, col_size, per_owner),
         out_shape=[
-            jax.ShapeDtypeStruct((5, count), jnp.int32),
-            jax.ShapeDtypeStruct((1,), jnp.int32),
+            jax.ShapeDtypeStruct((4, count), jnp.int32),
+            jax.ShapeDtypeStruct((len(needs) + 1,), jnp.int32),
             jax.ShapeDtypeStruct((1,), jnp.int32),
             held,
         ],
         in_specs=[SMEM] * (4 + len(needs)) + [VMEM],
         out_specs=[SMEM] * 3 + [VMEM],
-        scratch_shapes=[pltpu.SMEM((lags, total), jnp.int32)],
+        scratch_shapes=[pltpu.SMEM((lags, total), jnp.int32), pltpu.SMEM((len(needs),), jnp.int32)],
         compiler_params=params(tiles, held),
         name="plan_tiles",
     )(where, cols, rows, counts, *needs, tiles)
 
 
 def tiles_kernel(first, whole, extra, over, table, size, tiles, history, *refs):
-    received, given = refs[: len(refs) - 3 - SPLIT - extra], refs[-2 - SPLIT : -2]
-    kept, (blocks, sums) = refs[-3 - SPLIT], refs[-2:]
+    received, (sums, *given), blocks = refs[: len(refs) - 2 - SPLIT - extra], refs[-2 - SPLIT : -1], refs[-1]
     side = tiles.shape[2]
     halves, part, _ = sums.shape
-    live = size[0]
+    live = size[len(received) + 1]
     sums[...] = jnp.zeros_like(sums)
 
-    def fetch(index, carry):
-        lag, relative = table[0, index], table[1, index]
-        lanes = pl.ds(pl.multiple_of(table[2, index] * side, side), side)
-
-        @pl.when(relative == 0)
-        def _():
-            blocks[index] = history[lag, pl.ds(first, part), lanes]
-
-        for peer in range(len(received)):
-
-            @pl.when(relative == peer + 1)
-            def _(peer=peer):
-                if whole:
-                    blocks[index] = received[peer][lag, pl.ds(first, part), lanes]
-                else:
-                    blocks[index] = received[peer][table[3, index]]
-
-        return carry
-
-    lax.fori_loop(0, live, fetch, 0)
+    def fetch(source):
+        def one(index, carry):
+            lanes = pl.ds(pl.multiple_of(table[2, index] * side, side), side)
+            if source == 0:
+                blocks[index] = history[table[0, index], pl.ds(first, part), lanes]
+            elif whole:
+                blocks[index] = received[source - 1][table[0, index], pl.ds(first, part), lanes]
+            else:
+                blocks[index] = received[source - 1][table[3, index]]
+            return carry
+
+        return one
+
+    for source in range(len(received) + 1):
+        lax.fori_loop(size[source], size[source + 1], fetch(source), 0)
 
     def multiply(group, carry):
         products = []
@@ -225,46 +229,66 @@
             )
         for offset, product in enumerate(products):
             index = group * GROUP + offset
-            spot = table[4, jnp.minimum(index, live - 1)]
+            spot = table[1, jnp.minimum(index, live - 1)]
             sums[spot] += product if offset == 0 else jnp.where(index < live, product, 0.0)
         return carry
 
     lax.fori_loop(0, (live + GROUP - 1) // GROUP, multiply, 0)
-    kept[...] = sums[: halves // 2]
     half = halves // 2
+    size = half // SPLIT
+    flag = jnp.full((1, side), 1.0, jnp.float32) * over[0].astype(jnp.float32)
     for index, target in enumerate(given):
-        size = half // SPLIT
-        target[:size] = sums[half + index * size : half + (index + 1) * size]
-    given[0][half // SPLIT] = jnp.full((part, side), 1.0, jnp.float32) * over[0].astype(jnp.float32)
+        exponents = []
+        for chunk in range(size):
+            grid, exponent = to_fixed(sums[half + index * size + chunk])
+            target[chunk * part : (chunk + 1) * part] = grid
+            exponents.append(exponent)
+        exponents += [jnp.zeros((PAD - 1 - size, side), jnp.float32), flag]
+        tail = jnp.concatenate(exponents, axis=0)
+        target[size * part :] = tail.astype(jnp.int32).astype(jnp.int16)
 
 
 def multiply_tiles(first, part, whole, over, table, size, tiles, history, received, chunks, after):
     side = tiles.shape[2]
-    half = jax.ShapeDtypeStruct((chunks, part, side), jnp.float32)
-    more = [
-        jax.ShapeDtypeStruct((chunks // SPLIT + (index == 0), part, side), jnp.float32) for index in range(SPLIT)
-    ]
+    more = [jax.ShapeDtypeStruct((chunks // SPLIT * part + PAD, side), jnp.int16)] * SPLIT
     blocks = pltpu.VMEM((table.shape[1], part, side), history.dtype)
-    sums = pltpu.VMEM((2 * chunks, part, side), jnp.float32)
+    sums = jax.ShapeDtypeStruct((2 * chunks, part, side), jnp.float32)
     return pl.pallas_call(
         functools.partial(tiles_kernel, first, whole, len(after)),
-        out_shape=[half, *more],
+        out_shape=[sums, *more],
         in_specs=[SMEM] * 3 + [VMEM] * (2 + len(received)) + [ANY] * len(after),
         out_specs=[VMEM] * (1 + SPLIT),
-        scratch_shapes=[blocks, sums],
-        compiler_params=params(tiles, history, *received, half, half, blocks, sums),
+        scratch_shapes=[blocks],
+        compiler_params=params(tiles, history, *received, *more, blocks, sums),
         name="multiply_tiles",
     )(over, table, size, tiles, history, *received, *after)
 
 
-def code_kernel(per_owner, where, over, kept, *refs):
-    got, own, coded, theirs = refs[:SPLIT], refs[SPLIT], refs[SPLIT + 1 : -1], refs[-1]
-    chunks, part, side = kept.shape
+def to_fixed(value):
+    largest = jnp.maximum(jnp.max(jnp.abs(value), axis=0, keepdims=True), 1e-30)
+    exponent = jnp.ceil(jnp.log2(largest))
+    grid = jnp.clip(jnp.round(value * jnp.exp2(15.0 - exponent)), -32767.0, 32767.0)
+    return grid.astype(jnp.int32).astype(jnp.int16), exponent
+
+
+def from_fixed(grid, exponent):
+    return grid.astype(jnp.int32).astype(jnp.float32) * jnp.exp2(exponent - 15.0)
+
+
+def code_kernel(per_owner, extra, where, over, kept, *refs):
+    got, own, coded = refs[:SPLIT], refs[SPLIT + extra], refs[SPLIT + extra + 1 : -1]
+    theirs = refs[-1]
+    chunks, part, side = theirs.shape
     size = chunks // SPLIT
+    flag = over[0].astype(jnp.float32)
     for index, source in enumerate(got):
-        theirs[index * size : (index + 1) * size] = source[:size]
+        tail = source[size * part :, :].astype(jnp.int32).astype(jnp.float32)
+        flag = jnp.maximum(flag, tail[PAD - 1 :, :LANES])
+        for chunk in range(size):
+            theirs[index * size + chunk] = from_fixed(
+                source[chunk * part : (chunk + 1) * part, :], tail[chunk : chunk + 1, :]
+            )
     col = where[1]
-    flag = jnp.maximum(over[0].astype(jnp.float32), got[0][size][:1, :LANES])
     for step in list(range(1, chunks // per_owner)) + [0]:
         chunk = lax.bitwise_xor(col, step) * per_owner
         exponents = []
@@ -274,10 +298,7 @@
                 own[block] = value
                 continue
             out = coded[step - 1]
-            largest = jnp.maximum(jnp.max(jnp.abs(value), axis=0, keepdims=True), 1e-30)
-            exponent = jnp.ceil(jnp.log2(largest))
-            grid = jnp.clip(jnp.round(value * jnp.exp2(15.0 - exponent)), -32767.0, 32767.0)
-            grid = grid.astype(jnp.int32).astype(jnp.int16)
+            grid, exponent = to_fixed(value)
             for lane in range(side // LANES):
                 at = len(exponents)
                 out[pl.ds(at * part, part), :] = grid[:, lane * LANES : (lane + 1) * LANES]
@@ -290,20 +311,21 @@
             out[pl.ds(at * part, PAD), :] = tail.astype(jnp.int32).astype(jnp.int16)
 
 
-def code(where, over, kept, got, per_owner):
+def code(where, over, kept, got, per_owner, after):
     chunks, part, side = kept.shape
+    chunks = chunks // 2
     chunk = jax.ShapeDtypeStruct((per_owner * part * (side // LANES) + PAD, LANES), jnp.int16)
     own = jax.ShapeDtypeStruct((per_owner, part, side), jnp.float32)
     outs = [own] + [chunk] * (chunks // per_owner - 1)
     return pl.pallas_call(
-        functools.partial(code_kernel, per_owner),
+        functools.partial(code_kernel, per_owner, len(after)),
         out_shape=outs,
-        in_specs=[SMEM] * 2 + [VMEM] * (1 + len(got)),
+        in_specs=[SMEM] * 2 + [VMEM] * (1 + len(got)) + [ANY] * len(after),
         out_specs=[VMEM] * len(outs),
-        scratch_shapes=[pltpu.VMEM(kept.shape, jnp.float32)],
+        scratch_shapes=[pltpu.VMEM((chunks, part, side), jnp.float32)],
         compiler_params=params(kept, kept, *got, *outs),
         name="add_and_code",
-    )(where, over, kept, *got)
+    )(where, over, kept, *got, *after)
 
 
 def solve_kernel(first, fresh, over, *refs):
@@ -323,8 +345,7 @@
         block, lane = at // (side // LANES), at % (side // LANES)
         stress = own[block, :, pl.ds(lane * LANES, LANES)]
         for chunk, tail in zip(codes, tails):
-            values = chunk[pl.ds(at * part, part), :].astype(jnp.int32).astype(jnp.float32)
-            stress = stress + values * jnp.exp2(tail[at : at + 1, :] - 15.0)
+            stress = stress + from_fixed(chunk[pl.ds(at * part, part), :], tail[at : at + 1, :])
         lanes = pl.ds(at * LANES, LANES)
         stress_held[:, lanes] = stress
         rate_held[:, lanes] = friction(
@@ -359,15 +380,15 @@
     )(over, *carried, *fields, own, *coded)
 
 
-def reduce(first, where, over, fields, kept, given, before):
+def reduce(first, where, over, fields, kept, given, before, after):
     per_owner = fields[0].shape[1] // kept.shape[2]
     col_size = lax.axis_size("col")
     got = [lax.ppermute(array, "lag", partners(lax.axis_size("lag"), 1)) for array in given]
-    own, *coded = code(where, over, kept, got, per_owner)
-    arrived = [None] * (col_size - 1)
-    for step in range(col_size - 1, 0, -1):
-        arrived[step - 1] = lax.ppermute(coded[step - 1], "col", partners(col_size, step))
-    return solve(first, over, fields, own, arrived, before)
+    own, *coded = code(where, over, kept, got, per_owner, after)
+    arrived = [
+        lax.ppermute(coded[step - 1], "col", partners(col_size, step)) for step in [*range(2, col_size), 1]
+    ]
+    return solve(first, over, fields, own, arrived, before), (arrived[0], arrived[1]), tuple(arrived)
 
 
 def local(history, kernel_tiles, tile_rows, tile_cols, tile_count, base_stress, prev_rate, direct_effect, state_var):
@@ -377,8 +398,9 @@
     history = history[:, 0]
     tiles = kernel_tiles[0, 0]
     sims = history.shape[1]
-    cut = sims * FIRST // 8
-    pieces = ((0, cut), (cut, sims - cut))
+    pieces = []
+    for eighths in PIECES:
+        pieces.append((sum(part for _, part in pieces), sims * eighths // 8))
     local_blocks = history.shape[2] // side
     total = row_size * local_blocks
     per_owner = base_stress.shape[1] // side
@@ -389,11 +411,12 @@
     need = make_request(tile_cols, tile_count, total)
     requests = [lax.ppermute(need, "row", partners(row_size, step)) for step in range(1, row_size)]
     held = load(history)
-    packed = list(pack(where, requests, held, side, cap, pieces))
-    received = [
-        [lax.ppermute(packed.pop(0), "row", partners(row_size, step)) for step in range(1, row_size)]
-        for _ in pieces
-    ]
+    received = []
+    for piece in pieces:
+        packed = pack(where, requests, held, side, cap, piece, received[-1][:WAIT] if received else ())
+        received.append(
+            [lax.ppermute(packed[step - 1], "row", partners(row_size, step)) for step in range(1, row_size)]
+        )
     table, size, over, live_tiles = make_plan(
         where, tile_cols, tile_rows, tile_count, [need, *requests], tiles, cap, col_size, per_owner
     )
@@ -404,15 +427,14 @@
         kept, *given = multiply_tiles(
             first, part, False, over, table, size, live_tiles, held, blocks, chunks, after
         )
-        *result, flag = reduce(first, where, over, fields, kept, given, result)
-        after = (flag,)
+        (*result, flag), after, _ = reduce(first, where, over, fields, kept, given, result, ())
 
     def general():
         everything = [lax.ppermute(history, "row", partners(row_size, step)) for step in range(1, row_size)]
         kept, *given = multiply_tiles(
             0, sims, True, over, table, size, live_tiles, history, everything, chunks, ()
         )
-        return tuple(reduce(0, where, over, fields, kept, given, None)[:2])
+        return tuple(reduce(0, where, over, fields, kept, given, None, ())[0][:2])
 
     return lax.cond(flag[0] > 0, general, lambda: tuple(result))
 

time: 92.8 us -> 85.9 us (0.926); the launches traced: 91.5 us -> 85.7 us
  starting transfers between devices: 27.1 us -> 22.2 us
  Pallas kernels: 28.4 us -> 27 us
    ppermute x6, starting transfers between devices: 14.4 us -> 9.53 us  [reduce(): lax.ppermute(coded[step - 1], 'col', partners(col_size, step))]
    pallas_call x2, Pallas kernels: 11.6 us -> 8.21 us  [multiply_tiles(): pl.pallas_call(functools.partial(tiles_kernel, first, whole, len(after)),...]
    ppermute x4, waiting for transfers between devices: 4.49 us -> 1.43 us  [reduce(): lax.ppermute(array, 'lag', partners(lax.axis_size('lag'), 1))]
    ppermute x6, waiting for transfers between devices: 11.9 us -> 14.5 us  [local(): lax.ppermute(packed[step - 1], 'row', partners(row_size, step))]
    pallas_call x3 -> x4, Pallas kernels: 4.67 us -> 6.46 us  [the longest x2 3.48 us: pack(): pl.pallas_call(functools.partial(pack_kernel, cap, piece, side, len(after...]
  transfers between devices with their start and end apart: 19 -> 19, of which waited for: 12 -> 9; matrix products, arithmetic and copies ran while one was open for 0% -> 0% of each run, Pallas kernels for 15% -> 20%
where the time goes in v4:
time: 85.9 us; the launch traced here: 85.7 us
  waiting for transfers between devices  34.4 us (40%)
  Pallas kernels  27 us (31%)
  starting transfers between devices  22.2 us (26%)
  between operations  1.66 us (2%)
    ppermute x6, waiting for transfers between devices, reduce(): lax.ppermute(coded[step - 1], 'col', partners(col_size, step))  16.6 us
    ppermute x6, waiting for transfers between devices, local(): lax.ppermute(packed[step - 1], 'row', partners(row_size, step))  14.5 us
    ppermute x6, starting transfers between devices, reduce(): lax.ppermute(coded[step - 1], 'col', partners(col_size, step))  9.53 us
    pallas_call x2, Pallas kernels, multiply_tiles(): pl.pallas_call(functools.partial(tiles_kernel, first, whole, len(after)),...  8.21 us
    ppermute x6, starting transfers between devices, local(): lax.ppermute(packed[step - 1], 'row', partners(row_size, step))  7.11 us
    pallas_call x2, Pallas kernels, solve(): pl.pallas_call(functools.partial(solve_kernel, first, fresh), out_shape=[...  5.55 us
    ppermute x3, starting transfers between devices, local(): lax.ppermute(need, 'row', partners(row_size, step))  4.46 us
    pallas_call x1, Pallas kernels, make_plan(): pl.pallas_call(functools.partial(plan_kernel, cap, col_size, per_owner),...  3.73 us
  transfers between devices with their start and end apart: 19, of which 9 were waited for; matrix products, arithmetic and copies ran while one was open for 0% of the time, Pallas kernels for 20%

profile of v4, /device:TPU:0, one launch (start us, length us, event | category | flops | bytes accessed | tf_op | source)
XLA Modules:
  0.0 85.7 jit_solution(12712391735307878474)
XLA Ops:
  0.6 1.3 %mark_blocks.1.refs_0_ = s32[4,32]{1,0:T(4,128)} custom-call(s32[1,1,4,12]{3,2,1,0:T(4,128)} %cols.3, s32[1,1,4]{2,1,0:T(1,128)} %counts.3), custom_call_target="tpu_custom_call" | custom-call | tf_op jit(solution)/shard_map/mark_blocks/pallas_call | solution.py:61
  2.0 3.9 %collective-permute-start.10 = (s32[4,32]{1,0:T(4,128)}, s32[4,32]{1,0:T(4,128)S(1)}, u32[]{:S(2)}, u32[]{:S(2)}) collective-permute-start(s32[4,32]{1,0:T(4,128)} %mark_blocks.1.refs_0_), channel_id=1, source_target_pairs={{0,24},{8,16},{16,8},{24,0},{1,25},{9,17},{17,9},{25,1},{2,26},{10... | collective-permute-start | bytes 1544 | tf_op jit(solution)/shard_map/ppermute | solution.py:412
  5.9 0.5 collective-permute-start.9
  6.5 1.8 %load_history.1.refs_3_.history = bf16[4,128,2048]{2,1,0:T(8,128)(2,1)S(1)} custom-call(bf16[4,128,2048]{2,1,0:T(8,128)(2,1)} %bitcast.7), custom_call_target="tpu_custom_call" | custom-call | tf_op jit(solution)/shard_map/load_history/pallas_call | solution.py:77
  8.3 1.3 %collective-permute-done.9.refs_2_.refs_1_ = s32[4,32]{1,0:T(4,128)S(1)} collective-permute-done((s32[4,32]{1,0:T(4,128)}, s32[4,32]{1,0:T(4,128)S(1)}, u32[]{:S(2)}, u32[]{:S(2)}) %collective-permute-start.9) | collective-permute-done | bytes 544 | tf_op jit(solution)/shard_map/ppermute | solution.py:412
  9.7 0.5 collective-permute-done.8.refs_1_.refs_0_
  10.2 1.7 %pack_history.2 = (bf16[16,64,256]{2,1,0:T(8,128)(2,1)S(1)}, bf16[16,64,256]{2,1,0:T(8,128)(2,1)S(1)}, bf16[16,64,256]{2,1,0:T(8,128)(2,1)S(1)}) custom-call(s32[3]{0:T(128)S(1)} %pad_add_fusion.where, s32[4,32]{1,0:T(4,128)S(1)} %collective-permute-done.8.refs_1_.refs_0_, s32[4,32]{1,0:T(4,128)S(1)} %collective-permute-done.9.refs_2_.refs_1_, ...), custom_call_target="tpu_custom_call" | custom-call | tf_op jit(solution)/shard_map/pack_history/pallas_call | solution.py:112
  12.1 1.9 %collective-permute-start.12 = (bf16[16,64,256]{2,1,0:T(8,128)(2,1)S(1)}, bf16[16,64,256]{2,1,0:T(8,128)(2,1)S(1)}, u32[]{:S(2)}, u32[]{:S(2)}) collective-permute-start(bf16[16,64,256]{2,1,0:T(8,128)(2,1)S(1)} %get-tuple-element.79), channel_id=1, source_target_pairs={{0,16},{8,24},{16,0},{24,8},{1,17},{9,25},{17,1},{25,9},{2,18},{10... | collective-permute-start | bytes 1572872 | tf_op jit(solution)/shard_map/ppermute | solution.py:418
  14.0 1.4 %collective-permute-start.13 = (bf16[16,64,256]{2,1,0:T(8,128)(2,1)S(1)}, bf16[16,64,256]{2,1,0:T(8,128)(2,1)S(1)}, u32[]{:S(2)}, u32[]{:S(2)}) collective-permute-start(bf16[16,64,256]{2,1,0:T(8,128)(2,1)S(1)} %get-tuple-element.80), channel_id=1, source_target_pairs={{0,24},{8,16},{16,8},{24,0},{1,25},{9,17},{17,9},{25,1},{2,26},{10... | collective-permute-start | bytes 1572872 | tf_op jit(solution)/shard_map/ppermute | solution.py:418
  15.5 11.4 %collective-permute-done.11.refs_0_.refs_4_ = bf16[16,64,256]{2,1,0:T(8,128)(2,1)S(1)} collective-permute-done((bf16[16,64,256]{2,1,0:T(8,128)(2,1)S(1)}, bf16[16,64,256]{2,1,0:T(8,128)(2,1)S(1)}, u32[]{:S(2)}, u32[]{:S(2)}) %collective-permute-start.11) | collective-permute-done | bytes 524320 | tf_op jit(solution)/shard_map/ppermute | solution.py:418
  26.8 1.7 %pack_history.3 = (bf16[16,64,256]{2,1,0:T(8,128)(2,1)S(1)}, bf16[16,64,256]{2,1,0:T(8,128)(2,1)S(1)}, bf16[16,64,256]{2,1,0:T(8,128)(2,1)S(1)}) custom-call(s32[3]{0:T(128)S(1)} %pad_add_fusion.where, s32[4,32]{1,0:T(4,128)S(1)} %collective-permute-done.8.refs_1_.refs_0_, s32[4,32]{1,0:T(4,128)S(1)} %collective-permute-done.9.refs_2_.refs_1_, ...), custom_call_target="tpu_custom_call" | custom-call | tf_op jit(solution)/shard_map/pack_history/pallas_call | solution.py:112
  28.8 1.9 %collective-permute-start.20 = (bf16[16,64,256]{2,1,0:T(8,128)(2,1)S(1)}, bf16[16,64,256]{2,1,0:T(8,128)(2,1)S(1)}, u32[]{:S(2)}, u32[]{:S(2)}) collective-permute-start(bf16[16,64,256]{2,1,0:T(8,128)(2,1)S(1)} %get-tuple-element.91), channel_id=1, source_target_pairs={{0,16},{8,24},{16,0},{24,8},{1,17},{9,25},{17,1},{25,9},{2,18},{10... | collective-permute-start | bytes 1572872 | tf_op jit(solution)/shard_map/ppermute | solution.py:418
  30.7 1.4 %collective-permute-start.21 = (bf16[16,64,256]{2,1,0:T(8,128)(2,1)S(1)}, bf16[16,64,256]{2,1,0:T(8,128)(2,1)S(1)}, u32[]{:S(2)}, u32[]{:S(2)}) collective-permute-start(bf16[16,64,256]{2,1,0:T(8,128)(2,1)S(1)} %get-tuple-element.92), channel_id=1, source_target_pairs={{0,24},{8,16},{16,8},{24,0},{1,25},{9,17},{17,9},{25,1},{2,26},{10... | collective-permute-start | bytes 1572872 | tf_op jit(solution)/shard_map/ppermute | solution.py:418
  32.2 3.7 %plan_tiles.1 = (s32[4,48]{1,0:T(4,128)S(1)}, s32[5]{0:T(128)S(1)}, s32[1]{0:T(128)}, bf16[48,256,256]{2,1,0:T(8,128)(2,1)S(1)}) custom-call(s32[3]{0:T(128)S(1)} %pad_add_fusion.where, s32[1,1,4,12]{3,2,1,0:T(4,128)S(1)} %copy-done.1, s32[1,1,4,12]{3,2,1,0:T(4,128)S(1)} %copy-done.3, s32[1,1,4]{2,1,0:T(1,128)S(1)} %copy-done.4, s32[4,32]{1,0:T(4,128)S(1)} %copy-done.2, ...), custom_call_target="tpu_custom_call" | custom-call | tf_op jit(solution)/shard_map/plan_tiles/pallas_call | solution.py:182
  35.9 3.2 %collective-permute-done.13.refs_2_ = bf16[16,64,256]{2,1,0:T(8,128)(2,1)S(1)} collective-permute-done((bf16[16,64,256]{2,1,0:T(8,128)(2,1)S(1)}, bf16[16,64,256]{2,1,0:T(8,128)(2,1)S(1)}, u32[]{:S(2)}, u32[]{:S(2)}) %collective-permute-start.13) | collective-permute-done | bytes 524320 | tf_op jit(solution)/shard_map/ppermute | solution.py:418
  39.1 4.1 %multiply_tiles.4 = (f32[32,64,256]{2,1,0:T(8,128)S(1)}, s16[528,256]{1,0:T(8,128)(2,1)S(1)}, s16[528,256]{1,0:T(8,128)(2,1)S(1)}) custom-call(s32[1]{0:T(128)} %get-tuple-element.74.over, s32[4,48]{1,0:T(4,128)S(1)} %get-tuple-element.75.table, s32[5]{0:T(128)S(1)} %get-tuple-element.76.size, bf16[48,256,256]{2,1,0:T(8,128)(2,1)S(1)} %get-tuple-element.77.tiles, ...), custom_call_target="tpu_custom_call" | custom-call | tf_op jit(solution)/shard_map/multiply_tiles/pallas_call | solution.py:256
  43.3 0.5 collective-permute-start.15
  43.8 1.0 %collective-permute-done.14.refs_0_ = s16[528,256]{1,0:T(8,128)(2,1)S(1)} collective-permute-done((s16[528,256]{1,0:T(8,128)(2,1)S(1)}, s16[528,256]{1,0:T(8,128)(2,1)S(1)}, u32[]{:S(2)}, u32[]{:S(2)}) %collective-permute-start.14) | collective-permute-done | bytes 270368 | tf_op jit(solution)/shard_map/ppermute | solution.py:386
  44.8 0.4 collective-permute-done.15.refs_1_
  45.2 1.5 %add_and_code.4 = (f32[4,64,256]{2,1,0:T(8,128)S(1)}, s16[528,128]{1,0:T(8,128)(2,1)S(1)}, s16[528,128]{1,0:T(8,128)(2,1)S(1)}, s16[528,128]{1,0:T(8,128)(2,1)S(1)}) custom-call(s32[3]{0:T(128)S(1)} %pad_add_fusion.where, s32[1]{0:T(128)} %get-tuple-element.74.over, f32[32,64,256]{2,1,0:T(8,128)S(1)} %get-tuple-element.81.kept, ...), custom_call_target="tpu_custom_call" | custom-call | tf_op jit(solution)/shard_map/add_and_code/pallas_call | solution.py:320
  46.7 2.2 %collective-permute-start.16 = (s16[528,128]{1,0:T(8,128)(2,1)S(1)}, s16[528,128]{1,0:T(8,128)(2,1)S(1)}, u32[]{:S(2)}, u32[]{:S(2)}) collective-permute-start(s16[528,128]{1,0:T(8,128)(2,1)S(1)} %get-tuple-element.85), channel_id=1, source_target_pairs={{0,4},{2,6},{4,0},{6,2},{1,5},{3,7},{5,1},{7,3},{8,12},{10,14},{12... | collective-permute-start | bytes 405512 | tf_op jit(solution)/shard_map/ppermute | solution.py:389
  48.8 1.1 %collective-permute-start.17 = (s16[528,128]{1,0:T(8,128)(2,1)S(1)}, s16[528,128]{1,0:T(8,128)(2,1)S(1)}, u32[]{:S(2)}, u32[]{:S(2)}) collective-permute-start(s16[528,128]{1,0:T(8,128)(2,1)S(1)} %get-tuple-element.86), channel_id=1, source_target_pairs={{0,6},{2,4},{4,2},{6,0},{1,7},{3,5},{5,3},{7,1},{8,14},{10,12},{12... | collective-permute-start | bytes 405512 | tf_op jit(solution)/shard_map/ppermute | solution.py:389
  49.9 9.7 %collective-permute-done.16.refs_5_.refs_3_ = s16[528,128]{1,0:T(8,128)(2,1)S(1)} collective-permute-done((s16[528,128]{1,0:T(8,128)(2,1)S(1)}, s16[528,128]{1,0:T(8,128)(2,1)S(1)}, u32[]{:S(2)}, u32[]{:S(2)}) %collective-permute-start.16) | collective-permute-done | bytes 135200 | tf_op jit(solution)/shard_map/ppermute | solution.py:389
  59.6 4.1 %multiply_tiles.5 = (f32[32,64,256]{2,1,0:T(8,128)S(1)}, s16[528,256]{1,0:T(8,128)(2,1)S(1)}, s16[528,256]{1,0:T(8,128)(2,1)S(1)}) custom-call(s32[1]{0:T(128)} %get-tuple-element.74.over, s32[4,48]{1,0:T(4,128)S(1)} %get-tuple-element.75.table, s32[5]{0:T(128)S(1)} %get-tuple-element.76.size, bf16[48,256,256]{2,1,0:T(8,128)(2,1)S(1)} %get-tuple-element.77.tiles, ...), custom_call_target="tpu_custom_call" | custom-call | tf_op jit(solution)/shard_map/multiply_tiles/pallas_call | solution.py:256
  63.9 0.5 collective-permute-start.23
  64.4 2.1 %collective-permute-start.18 = (s16[528,128]{1,0:T(8,128)(2,1)S(1)}, s16[528,128]{1,0:T(8,128)(2,1)S(1)}, u32[]{:S(2)}, u32[]{:S(2)}) collective-permute-start(s16[528,128]{1,0:T(8,128)(2,1)S(1)} %get-tuple-element.87), channel_id=1, source_target_pairs={{0,2},{2,0},{4,6},{6,4},{1,3},{3,1},{5,7},{7,5},{8,10},{10,8},{12,... | collective-permute-start | bytes 405512 | tf_op jit(solution)/shard_map/ppermute | solution.py:389
  66.5 1.5 %add_and_code.5 = (f32[4,64,256]{2,1,0:T(8,128)S(1)}, s16[528,128]{1,0:T(8,128)(2,1)S(1)}, s16[528,128]{1,0:T(8,128)(2,1)S(1)}, s16[528,128]{1,0:T(8,128)(2,1)S(1)}) custom-call(s32[3]{0:T(128)S(1)} %pad_add_fusion.where, s32[1]{0:T(128)} %get-tuple-element.74.over, f32[32,64,256]{2,1,0:T(8,128)S(1)} %get-tuple-element.93.kept, ...), custom_call_target="tpu_custom_call" | custom-call | tf_op jit(solution)/shard_map/add_and_code/pallas_call | solution.py:320
  68.0 3.5 %collective-permute-start.24 = (s16[528,128]{1,0:T(8,128)(2,1)S(1)}, s16[528,128]{1,0:T(8,128)(2,1)S(1)}, u32[]{:S(2)}, u32[]{:S(2)}) collective-permute-start(s16[528,128]{1,0:T(8,128)(2,1)S(1)} %get-tuple-element.97), channel_id=1, source_target_pairs={{0,4},{2,6},{4,0},{6,2},{1,5},{3,7},{5,1},{7,3},{8,12},{10,14},{12... | collective-permute-start | bytes 405512 | tf_op jit(solution)/shard_map/ppermute | solution.py:389
  71.5 0.4 collective-permute-start.25
  72.2 2.8 %friction_solve.4 = (f32[128,1024]{1,0:T(8,128)}, f32[128,1024]{1,0:T(8,128)}, s32[1]{0:T(128)}) custom-call(s32[1]{0:T(128)} %get-tuple-element.74.over, f32[128,1024]{1,0:T(8,128)S(1)} %copy-done.7, f32[128,1024]{1,0:T(8,128)S(1)} %copy-done.8, f32[128,1024]{1,0:T(8,128)S(1)} %copy-done.9, f32[128,1024]{1,0:T(8,128)S(1)} %copy-done.12, ...), custom_call_target="tpu_custom_call" | custom-call | tf_op jit(solution)/shard_map/friction_solve/pallas_call | solution.py:370
  75.0 6.8 %collective-permute-done.24.refs_7_ = s16[528,128]{1,0:T(8,128)(2,1)S(1)} collective-permute-done((s16[528,128]{1,0:T(8,128)(2,1)S(1)}, s16[528,128]{1,0:T(8,128)(2,1)S(1)}, u32[]{:S(2)}, u32[]{:S(2)}) %collective-permute-start.24) | collective-permute-done | bytes 135200 | tf_op jit(solution)/shard_map/ppermute | solution.py:389
  81.9 2.8 %friction_solve.5 = (f32[128,1024]{1,0:T(8,128)}, f32[128,1024]{1,0:T(8,128)}, s32[1]{0:T(128)}) custom-call(s32[1]{0:T(128)} %get-tuple-element.74.over, f32[128,1024]{1,0:T(8,128)} %get-tuple-element.88.refs_0_, f32[128,1024]{1,0:T(8,128)} %get-tuple-element.89.refs_1_, f32[128,1024]{1,0:T(8,128)S(1)} %copy-done.7, ...), custom_call_target="tpu_custom_call", output_to_operand_aliasing={{0}: (1, {}), {1}: (2, {})} | custom-call | tf_op jit(solution)/shard_map/friction_solve/pallas_call | solution.py:370
  (39 shorter events, 1.3 us)
Async XLA Ops:
  2.0 6.3 %collective-permute-start.10 = (s32[4,32]{1,0:T(4,128)}, s32[4,32]{1,0:T(4,128)S(1)}, u32[]{:S(2)}, u32[]{:S(2)}) collective-permute-start(s32[4,32]{1,0:T(4,128)} %mark_blocks.1.refs_0_), channel_id=1, source_target_pairs={{0,24},{8,16},{16,8},{24,0},{1,25},{9,17},{17,9},{25,1},{2,26},{10... | collective-permute-start | bytes 1544 | tf_op jit(solution)/shard_map/ppermute | solution.py:412
  5.9 3.8 %collective-permute-start.9 = (s32[4,32]{1,0:T(4,128)}, s32[4,32]{1,0:T(4,128)S(1)}, u32[]{:S(2)}, u32[]{:S(2)}) collective-permute-start(s32[4,32]{1,0:T(4,128)} %mark_blocks.1.refs_0_), channel_id=1, source_target_pairs={{0,16},{8,24},{16,0},{24,8},{1,17},{9,25},{17,1},{25,9},{2,18},{10... | collective-permute-start | bytes 1544 | tf_op jit(solution)/shard_map/ppermute | solution.py:412
  6.4 3.8 %collective-permute-start.8 = (s32[4,32]{1,0:T(4,128)}, s32[4,32]{1,0:T(4,128)S(1)}, u32[]{:S(2)}, u32[]{:S(2)}) collective-permute-start(s32[4,32]{1,0:T(4,128)} %mark_blocks.1.refs_0_), channel_id=1, source_target_pairs={{0,8},{8,0},{16,24},{24,16},{1,9},{9,1},{17,25},{25,17},{2,10},{10... | collective-permute-start | bytes 1544 | tf_op jit(solution)/shard_map/ppermute | solution.py:412
  6.5 25.6 %copy-start = (bf16[1,1,4,12,256,256]{5,4,3,2,1,0:T(8,128)(2,1)S(1)}, bf16[1,1,4,12,256,256]{5,4,3,2,1,0:T(8,128)(2,1)}, u32[]{:S(2)}) copy-start(bf16[1,1,4,12,256,256]{5,4,3,2,1,0:T(8,128)(2,1)} %param.12) | copy-start | bytes 18874372
  8.3 23.9 %copy-start.1 = (s32[1,1,4,12]{3,2,1,0:T(4,128)S(1)}, s32[1,1,4,12]{3,2,1,0:T(4,128)}, u32[]{:S(2)}) copy-start(s32[1,1,4,12]{3,2,1,0:T(4,128)} %cols.3) | copy-start | bytes 580
  8.3 23.9 %copy-start.2 = (s32[4,32]{1,0:T(4,128)S(1)}, s32[4,32]{1,0:T(4,128)}, u32[]{:S(2)}) copy-start(s32[4,32]{1,0:T(4,128)} %mark_blocks.1.refs_0_) | copy-start | bytes 1540
  8.3 23.9 %copy-start.3 = (s32[1,1,4,12]{3,2,1,0:T(4,128)S(1)}, s32[1,1,4,12]{3,2,1,0:T(4,128)}, u32[]{:S(2)}) copy-start(s32[1,1,4,12]{3,2,1,0:T(4,128)} %rows.1) | copy-start | bytes 580
  8.3 23.9 %copy-start.4 = (s32[1,1,4]{2,1,0:T(1,128)S(1)}, s32[1,1,4]{2,1,0:T(1,128)}, u32[]{:S(2)}) copy-start(s32[1,1,4]{2,1,0:T(1,128)} %counts.3) | copy-start | bytes 52
  11.9 14.9 %collective-permute-start.11 = (bf16[16,64,256]{2,1,0:T(8,128)(2,1)S(1)}, bf16[16,64,256]{2,1,0:T(8,128)(2,1)S(1)}, u32[]{:S(2)}, u32[]{:S(2)}) collective-permute-start(bf16[16,64,256]{2,1,0:T(8,128)(2,1)S(1)} %get-tuple-element.78), channel_id=1, source_target_pairs={{0,8},{8,0},{16,24},{24,16},{1,9},{9,1},{17,25},{25,17},{2,10},{10... | collective-permute-start | bytes 1572872 | tf_op jit(solution)/shard_map/ppermute | solution.py:418
  12.1 23.8 %collective-permute-start.12 = (bf16[16,64,256]{2,1,0:T(8,128)(2,1)S(1)}, bf16[16,64,256]{2,1,0:T(8,128)(2,1)S(1)}, u32[]{:S(2)}, u32[]{:S(2)}) collective-permute-start(bf16[16,64,256]{2,1,0:T(8,128)(2,1)S(1)} %get-tuple-element.79), channel_id=1, source_target_pairs={{0,16},{8,24},{16,0},{24,8},{1,17},{9,25},{17,1},{25,9},{2,18},{10... | collective-permute-start | bytes 1572872 | tf_op jit(solution)/shard_map/ppermute | solution.py:418
  14.0 25.0 %collective-permute-start.13 = (bf16[16,64,256]{2,1,0:T(8,128)(2,1)S(1)}, bf16[16,64,256]{2,1,0:T(8,128)(2,1)S(1)}, u32[]{:S(2)}, u32[]{:S(2)}) collective-permute-start(bf16[16,64,256]{2,1,0:T(8,128)(2,1)S(1)} %get-tuple-element.80), channel_id=1, source_target_pairs={{0,24},{8,16},{16,8},{24,0},{1,25},{9,17},{17,9},{25,1},{2,26},{10... | collective-permute-start | bytes 1572872 | tf_op jit(solution)/shard_map/ppermute | solution.py:418
  28.6 31.0 %collective-permute-start.19 = (bf16[16,64,256]{2,1,0:T(8,128)(2,1)S(1)}, bf16[16,64,256]{2,1,0:T(8,128)(2,1)S(1)}, u32[]{:S(2)}, u32[]{:S(2)}) collective-permute-start(bf16[16,64,256]{2,1,0:T(8,128)(2,1)S(1)} %get-tuple-element.90), channel_id=1, source_target_pairs={{0,8},{8,0},{16,24},{24,16},{1,9},{9,1},{17,25},{25,17},{2,10},{10... | collective-permute-start | bytes 1572872 | tf_op jit(solution)/shard_map/ppermute | solution.py:418
  28.8 30.8 %collective-permute-start.20 = (bf16[16,64,256]{2,1,0:T(8,128)(2,1)S(1)}, bf16[16,64,256]{2,1,0:T(8,128)(2,1)S(1)}, u32[]{:S(2)}, u32[]{:S(2)}) collective-permute-start(bf16[16,64,256]{2,1,0:T(8,128)(2,1)S(1)} %get-tuple-element.91), channel_id=1, source_target_pairs={{0,16},{8,24},{16,0},{24,8},{1,17},{9,25},{17,1},{25,9},{2,18},{10... | collective-permute-start | bytes 1572872 | tf_op jit(solution)/shard_map/ppermute | solution.py:418
  30.7 28.9 %collective-permute-start.21 = (bf16[16,64,256]{2,1,0:T(8,128)(2,1)S(1)}, bf16[16,64,256]{2,1,0:T(8,128)(2,1)S(1)}, u32[]{:S(2)}, u32[]{:S(2)}) collective-permute-start(bf16[16,64,256]{2,1,0:T(8,128)(2,1)S(1)} %get-tuple-element.92), channel_id=1, source_target_pairs={{0,24},{8,16},{16,8},{24,0},{1,25},{9,17},{17,9},{25,1},{2,26},{10... | collective-permute-start | bytes 1572872 | tf_op jit(solution)/shard_map/ppermute | solution.py:418
  43.2 1.6 %collective-permute-start.14 = (s16[528,256]{1,0:T(8,128)(2,1)S(1)}, s16[528,256]{1,0:T(8,128)(2,1)S(1)}, u32[]{:S(2)}, u32[]{:S(2)}) collective-permute-start(s16[528,256]{1,0:T(8,128)(2,1)S(1)} %get-tuple-element.82), channel_id=1, source_target_pairs={{0,1},{1,0},{2,3},{3,2},{4,5},{5,4},{6,7},{7,6},{8,9},{9,8},{10,11... | collective-permute-start | bytes 811016 | tf_op jit(solution)/shard_map/ppermute | solution.py:386
  43.3 1.9 %collective-permute-start.15 = (s16[528,256]{1,0:T(8,128)(2,1)S(1)}, s16[528,256]{1,0:T(8,128)(2,1)S(1)}, u32[]{:S(2)}, u32[]{:S(2)}) collective-permute-start(s16[528,256]{1,0:T(8,128)(2,1)S(1)} %get-tuple-element.83), channel_id=1, source_target_pairs={{0,1},{1,0},{2,3},{3,2},{4,5},{5,4},{6,7},{7,6},{8,9},{9,8},{10,11... | collective-permute-start | bytes 811016 | tf_op jit(solution)/shard_map/ppermute | solution.py:386
  46.7 12.9 %collective-permute-start.16 = (s16[528,128]{1,0:T(8,128)(2,1)S(1)}, s16[528,128]{1,0:T(8,128)(2,1)S(1)}, u32[]{:S(2)}, u32[]{:S(2)}) collective-permute-start(s16[528,128]{1,0:T(8,128)(2,1)S(1)} %get-tuple-element.85), channel_id=1, source_target_pairs={{0,4},{2,6},{4,0},{6,2},{1,5},{3,7},{5,1},{7,3},{8,12},{10,14},{12... | collective-permute-start | bytes 405512 | tf_op jit(solution)/shard_map/ppermute | solution.py:389
  48.8 10.8 %collective-permute-start.17 = (s16[528,128]{1,0:T(8,128)(2,1)S(1)}, s16[528,128]{1,0:T(8,128)(2,1)S(1)}, u32[]{:S(2)}, u32[]{:S(2)}) collective-permute-start(s16[528,128]{1,0:T(8,128)(2,1)S(1)} %get-tuple-element.86), channel_id=1, source_target_pairs={{0,6},{2,4},{4,2},{6,0},{1,7},{3,5},{5,3},{7,1},{8,14},{10,12},{12... | collective-permute-start | bytes 405512 | tf_op jit(solution)/shard_map/ppermute | solution.py:389
  63.7 8.4 %copy-start.7 = (f32[128,1024]{1,0:T(8,128)S(1)}, f32[128,1024]{1,0:T(8,128)}, u32[]{:S(2)}) copy-start(f32[128,1024]{1,0:T(8,128)} %refs_2_.3) | copy-start | bytes 1572868
  63.8 8.4 %copy-start.8 = (f32[128,1024]{1,0:T(8,128)S(1)}, f32[128,1024]{1,0:T(8,128)}, u32[]{:S(2)}) copy-start(f32[128,1024]{1,0:T(8,128)} %refs_3_.3) | copy-start | bytes 1572868
  63.8 8.4 %copy-start.9 = (f32[128,1024]{1,0:T(8,128)S(1)}, f32[128,1024]{1,0:T(8,128)}, u32[]{:S(2)}) copy-start(f32[128,1024]{1,0:T(8,128)} %refs_4_.1) | copy-start | bytes 1572868
  63.8 8.4 %copy-start.12 = (f32[128,1024]{1,0:T(8,128)S(1)}, f32[128,1024]{1,0:T(8,128)}, u32[]{:S(2)}) copy-start(f32[128,1024]{1,0:T(8,128)} %refs_5_.1) | copy-start | bytes 1572868
  63.8 2.7 %collective-permute-start.22 = (s16[528,256]{1,0:T(8,128)(2,1)S(1)}, s16[528,256]{1,0:T(8,128)(2,1)S(1)}, u32[]{:S(2)}, u32[]{:S(2)}) collective-permute-start(s16[528,256]{1,0:T(8,128)(2,1)S(1)} %get-tuple-element.94), channel_id=1, source_target_pairs={{0,1},{1,0},{2,3},{3,2},{4,5},{5,4},{6,7},{7,6},{8,9},{9,8},{10,11... | collective-permute-start | bytes 811016 | tf_op jit(solution)/shard_map/ppermute | solution.py:386
  63.9 2.6 %collective-permute-start.23 = (s16[528,256]{1,0:T(8,128)(2,1)S(1)}, s16[528,256]{1,0:T(8,128)(2,1)S(1)}, u32[]{:S(2)}, u32[]{:S(2)}) collective-permute-start(s16[528,256]{1,0:T(8,128)(2,1)S(1)} %get-tuple-element.95), channel_id=1, source_target_pairs={{0,1},{1,0},{2,3},{3,2},{4,5},{5,4},{6,7},{7,6},{8,9},{9,8},{10,11... | collective-permute-start | bytes 811016 | tf_op jit(solution)/shard_map/ppermute | solution.py:386
  64.4 7.8 %collective-permute-start.18 = (s16[528,128]{1,0:T(8,128)(2,1)S(1)}, s16[528,128]{1,0:T(8,128)(2,1)S(1)}, u32[]{:S(2)}, u32[]{:S(2)}) collective-permute-start(s16[528,128]{1,0:T(8,128)(2,1)S(1)} %get-tuple-element.87), channel_id=1, source_target_pairs={{0,2},{2,0},{4,6},{6,4},{1,3},{3,1},{5,7},{7,5},{8,10},{10,8},{12,... | collective-permute-start | bytes 405512 | tf_op jit(solution)/shard_map/ppermute | solution.py:389
  68.0 13.7 %collective-permute-start.24 = (s16[528,128]{1,0:T(8,128)(2,1)S(1)}, s16[528,128]{1,0:T(8,128)(2,1)S(1)}, u32[]{:S(2)}, u32[]{:S(2)}) collective-permute-start(s16[528,128]{1,0:T(8,128)(2,1)S(1)} %get-tuple-element.97), channel_id=1, source_target_pairs={{0,4},{2,6},{4,0},{6,2},{1,5},{3,7},{5,1},{7,3},{8,12},{10,14},{12... | collective-permute-start | bytes 405512 | tf_op jit(solution)/shard_map/ppermute | solution.py:389
  71.5 10.3 %collective-permute-start.25 = (s16[528,128]{1,0:T(8,128)(2,1)S(1)}, s16[528,128]{1,0:T(8,128)(2,1)S(1)}, u32[]{:S(2)}, u32[]{:S(2)}) collective-permute-start(s16[528,128]{1,0:T(8,128)(2,1)S(1)} %get-tuple-element.98), channel_id=1, source_target_pairs={{0,6},{2,4},{4,2},{6,0},{1,7},{3,5},{5,3},{7,1},{8,14},{10,12},{12... | collective-permute-start | bytes 405512 | tf_op jit(solution)/shard_map/ppermute | solution.py:389
  71.9 9.9 %collective-permute-start.26 = (s16[528,128]{1,0:T(8,128)(2,1)S(1)}, s16[528,128]{1,0:T(8,128)(2,1)S(1)}, u32[]{:S(2)}, u32[]{:S(2)}) collective-permute-start(s16[528,128]{1,0:T(8,128)(2,1)S(1)} %get-tuple-element.99), channel_id=1, source_target_pairs={{0,2},{2,0},{4,6},{6,4},{1,3},{3,1},{5,7},{7,5},{8,10},{10,8},{12,... | collective-permute-start | bytes 405512 | tf_op jit(solution)/shard_map/ppermute | solution.py:389
  74.9 10.3 %copy-start.6 = (bf16[4,1,128,2048]{3,2,1,0:T(8,128)(2,1)S(1)}, bf16[4,1,128,2048]{3,2,1,0:T(8,128)(2,1)}, u32[]{:S(2)}) copy-start(bf16[4,1,128,2048]{3,2,1,0:T(8,128)(2,1)} %param.11) | copy-start | bytes 6291460

commit v5 on v4

--- a/solution.py
+++ b/solution.py
@@ -13,6 +13,7 @@
 PIECES = (4, 4)
 PAD = 16
 LANES = 128
+OVER = 16
 SPLIT = 2
 WAIT = 1
 GROUP = 8
@@ -85,13 +86,13 @@
     )(history)
 
 
-def pack_kernel(cap, piece, side, extra, where, *refs):
+def pack_kernel(cap, piece, side, extra, *refs):
     begin, part = piece
     peers = (len(refs) - 1 - extra) // 2
     needs, history, packed = refs[:peers], refs[peers], refs[peers + 1 + extra :]
     lags, sims, width = history.shape
     local_blocks = width // side
-    first = where[0] * local_blocks
+    first = lax.axis_index("row") * local_blocks
     for peer in range(peers):
         position = jnp.int32(0)
         for lag in range(lags):
@@ -107,22 +108,22 @@
                 position = position + wanted
 
 
-def pack(where, needs, history, side, cap, piece, after):
+def pack(needs, history, side, cap, piece, after):
     outs = [jax.ShapeDtypeStruct((cap, piece[1], side), history.dtype)] * len(needs)
     return pl.pallas_call(
         functools.partial(pack_kernel, cap, piece, side, len(after)),
         out_shape=outs,
-        in_specs=[SMEM] * (1 + len(needs)) + [VMEM] + [ANY] * len(after),
+        in_specs=[SMEM] * len(needs) + [VMEM] + [ANY] * len(after),
         out_specs=[VMEM] * len(outs),
         compiler_params=params(history, *outs),
         name="pack_history",
-    )(where, *needs, history, *after)
-
-
-def plan_kernel(cap, col_size, per_owner, where, cols, rows, counts, *refs):
-    needs, tiles, (table, size, over, held, places, ends) = refs[:-7], refs[-7], refs[-6:]
+    )(*needs, history, *after)
+
+
+def plan_kernel(cap, col_size, per_owner, cols, rows, counts, *refs):
+    needs, tiles, (table, held, places, ends) = refs[:-5], refs[-5], refs[-4:]
     lags, total = needs[0].shape
-    row, core = where[0], where[2]
+    row, core = lax.axis_index("row"), lax.axis_index("lag")
     members = len(needs)
     local_blocks = total // members
     for owner in range(members):
@@ -140,7 +141,7 @@
                     wanted = wanted + needs[member][lag, owner * local_blocks + block]
             foreign = lax.bitwise_xor(row, member) != owner
             above = jnp.where(foreign & (wanted > cap), 1, above)
-    over[0] = above
+    table[4, OVER] = above
     tally = [jnp.int32(0)] * members
     for lag in range(lags):
 
@@ -151,10 +152,10 @@
         tally = lax.fori_loop(0, counts[0, 0, lag], tell, tuple(tally))
     begin = jnp.int32(0)
     for member in range(members):
-        size[member] = begin
+        table[4, member] = begin
         ends[member] = begin
         begin = begin + tally[member]
-    size[members] = begin
+    table[4, members] = begin
     for lag in range(lags):
 
         def note(slot, carry, lag=lag):
@@ -175,31 +176,29 @@
         lax.fori_loop(0, counts[0, 0, lag], note, 0)
 
 
-def make_plan(where, cols, rows, counts, needs, tiles, cap, col_size, per_owner):
+def make_plan(cols, rows, counts, needs, tiles, cap, col_size, per_owner):
     lags, total = needs[0].shape
     count = lags * cols.shape[3]
     held = jax.ShapeDtypeStruct((count,) + tiles.shape[2:], tiles.dtype)
     return pl.pallas_call(
         functools.partial(plan_kernel, cap, col_size, per_owner),
         out_shape=[
-            jax.ShapeDtypeStruct((4, count), jnp.int32),
-            jax.ShapeDtypeStruct((len(needs) + 1,), jnp.int32),
-            jax.ShapeDtypeStruct((1,), jnp.int32),
+            jax.ShapeDtypeStruct((5, count), jnp.int32),
             held,
         ],
-        in_specs=[SMEM] * (4 + len(needs)) + [VMEM],
-        out_specs=[SMEM] * 3 + [VMEM],
+        in_specs=[SMEM] * (3 + len(needs)) + [VMEM],
+        out_specs=[SMEM, VMEM],
         scratch_shapes=[pltpu.SMEM((lags, total), jnp.int32), pltpu.SMEM((len(needs),), jnp.int32)],
         compiler_params=params(tiles, held),
         name="plan_tiles",
-    )(where, cols, rows, counts, *needs, tiles)
-
-
-def tiles_kernel(first, whole, extra, over, table, size, tiles, history, *refs):
+    )(cols, rows, counts, *needs, tiles)
+
+
+def tiles_kernel(first, whole, extra, table, tiles, history, *refs):
     received, (sums, *given), blocks = refs[: len(refs) - 2 - SPLIT - extra], refs[-2 - SPLIT : -1], refs[-1]
     side = tiles.shape[2]
     halves, part, _ = sums.shape
-    live = size[len(received) + 1]
+    live = table[4, len(received) + 1]
     sums[...] = jnp.zeros_like(sums)
 
     def fetch(source):
@@ -216,7 +215,7 @@
         return one
 
     for source in range(len(received) + 1):
-        lax.fori_loop(size[source], size[source + 1], fetch(source), 0)
+        lax.fori_loop(table[4, source], table[4, source + 1], fetch(source), 0)
 
     def multiply(group, carry):
         products = []
@@ -236,7 +235,7 @@
     lax.fori_loop(0, (live + GROUP - 1) // GROUP, multiply, 0)
     half = halves // 2
     size = half // SPLIT
-    flag = jnp.full((1, side), 1.0, jnp.float32) * over[0].astype(jnp.float32)
+    flag = jnp.full((1, side), 1.0, jnp.float32) * table[4, OVER].astype(jnp.float32)
     for index, target in enumerate(given):
         exponents = []
         for chunk in range(size):
@@ -248,7 +247,7 @@
         target[size * part :] = tail.astype(jnp.int32).astype(jnp.int16)
 
 
-def multiply_tiles(first, part, whole, over, table, size, tiles, history, received, chunks, after):
+def multiply_tiles(first, part, whole, table, tiles, history, received, chunks, after):
     side = tiles.shape[2]
     more = [jax.ShapeDtypeStruct((chunks // SPLIT * part + PAD, side), jnp.int16)] * SPLIT
     blocks = pltpu.VMEM((table.shape[1], part, side), history.dtype)
@@ -256,12 +255,12 @@
     return pl.pallas_call(
         functools.partial(tiles_kernel, first, whole, len(after)),
         out_shape=[sums, *more],
-        in_specs=[SMEM] * 3 + [VMEM] * (2 + len(received)) + [ANY] * len(after),
+        in_specs=[SMEM] + [VMEM] * (2 + len(received)) + [ANY] * len(after),
         out_specs=[VMEM] * (1 + SPLIT),
         scratch_shapes=[blocks],
         compiler_params=params(tiles, history, *received, *more, blocks, sums),
         name="multiply_tiles",
-    )(over, table, size, tiles, history, *received, *after)
+    )(table, tiles, history, *received, *after)
 
 
 def to_fixed(value):
@@ -275,12 +274,12 @@
     return grid.astype(jnp.int32).astype(jnp.float32) * jnp.exp2(exponent - 15.0)
 
 
-def code_kernel(per_owner, extra, where, over, kept, *refs):
+def code_kernel(per_owner, extra, table, kept, *refs):
     got, own, coded = refs[:SPLIT], refs[SPLIT + extra], refs[SPLIT + extra + 1 : -1]
     theirs = refs[-1]
     chunks, part, side = theirs.shape
     size = chunks // SPLIT
-    flag = over[0].astype(jnp.float32)
+    flag = table[4, OVER].astype(jnp.float32)
     for index, source in enumerate(got):
         tail = source[size * part :, :].astype(jnp.int32).astype(jnp.float32)
         flag = jnp.maximum(flag, tail[PAD - 1 :, :LANES])
@@ -288,7 +287,7 @@
             theirs[index * size + chunk] = from_fixed(
                 source[chunk * part : (chunk + 1) * part, :], tail[chunk : chunk + 1, :]
             )
-    col = where[1]
+    col = lax.axis_index("col")
     for step in list(range(1, chunks // per_owner)) + [0]:
         chunk = lax.bitwise_xor(col, step) * per_owner
         exponents = []
@@ -311,7 +310,7 @@
             out[pl.ds(at * part, PAD), :] = tail.astype(jnp.int32).astype(jnp.int16)
 
 
-def code(where, over, kept, got, per_owner, after):
+def code(table, kept, got, per_owner, after):
     chunks, part, side = kept.shape
     chunks = chunks // 2
     chunk = jax.ShapeDtypeStruct((per_owner * part * (side // LANES) + PAD, LANES), jnp.int16)
@@ -320,81 +319,84 @@
     return pl.pallas_call(
         functools.partial(code_kernel, per_owner, len(after)),
         out_shape=outs,
-        in_specs=[SMEM] * 2 + [VMEM] * (1 + len(got)) + [ANY] * len(after),
+        in_specs=[SMEM] + [VMEM] * (1 + len(got)) + [ANY] * len(after),
         out_specs=[VMEM] * len(outs),
         scratch_shapes=[pltpu.VMEM((chunks, part, side), jnp.float32)],
         compiler_params=params(kept, kept, *got, *outs),
         name="add_and_code",
-    )(where, over, kept, *got, *after)
-
-
-def solve_kernel(first, fresh, over, *refs):
-    refs = refs if fresh else refs[2:]
-    base, rate, direct, state, own = refs[:5]
-    codes, (stress_out, rate_out, flag_out, stress_held, rate_held, sems) = refs[5:-6], refs[-6:]
+    )(table, kept, *got, *after)
+
+
+def solve_kernel(first, fresh, *refs):
+    refs, (stress_out, rate_out, stress_held, rate_held, sems) = refs[:-5], refs[-5:]
+    if fresh:
+        table, *refs, flag_out = refs
+    else:
+        refs = refs[2:]
+    base, rate, direct, state, own, *codes = refs
     per_owner, part, side = own.shape
     rows = pl.ds(first, part)
-    tails = []
-    flag = over[0].astype(jnp.float32)
-    for chunk in codes:
-        tail = chunk[pl.ds(chunk.shape[0] - PAD, PAD), :].astype(jnp.int32).astype(jnp.float32)
-        flag = jnp.maximum(flag, jnp.max(tail[PAD - 1 :, :]))
-        tails.append(tail)
-    flag_out[0] = flag.astype(jnp.int32)
-    for at in range(per_owner * (side // LANES)):
+    tails = [chunk[pl.ds(chunk.shape[0] - PAD, PAD), :].astype(jnp.int32).astype(jnp.float32) for chunk in codes]
+    if fresh:
+        flag = table[4, OVER].astype(jnp.float32)
+        for tail in tails:
+            flag = jnp.maximum(flag, jnp.max(tail[PAD - 1 :, :]))
+        flag_out[0] = flag.astype(jnp.int32)
+    count = per_owner * (side // LANES)
+    copies = []
+    for at in range(count):
         block, lane = at // (side // LANES), at % (side // LANES)
         stress = own[block, :, pl.ds(lane * LANES, LANES)]
         for chunk, tail in zip(codes, tails):
             stress = stress + from_fixed(chunk[pl.ds(at * part, part), :], tail[at : at + 1, :])
+        stress_held[:, pl.ds(at * LANES, LANES)] = stress
+    copies.append(pltpu.make_async_copy(stress_held, stress_out.at[rows], sems.at[0]))
+    copies[-1].start()
+    for at in range(count):
         lanes = pl.ds(at * LANES, LANES)
-        stress_held[:, lanes] = stress
         rate_held[:, lanes] = friction(
-            stress, base[rows, lanes], rate[rows, lanes], direct[rows, lanes], state[rows, lanes]
+            stress_held[:, lanes], base[rows, lanes], rate[rows, lanes], direct[rows, lanes], state[rows, lanes]
         )
-    copies = (
-        pltpu.make_async_copy(stress_held, stress_out.at[rows], sems.at[0]),
-        pltpu.make_async_copy(rate_held, rate_out.at[rows], sems.at[1]),
-    )
-    for copy in copies:
-        copy.start()
+    copies.append(pltpu.make_async_copy(rate_held, rate_out.at[rows], sems.at[1]))
+    copies[-1].start()
     for copy in copies:
         copy.wait()
 
 
-def solve(first, over, fields, own, coded, before):
+def solve(first, table, fields, own, coded, before):
     sims, owned = fields[0].shape
     part = own.shape[1]
     fresh = before is None
-    carried = [] if fresh else list(before)
+    field = jax.ShapeDtypeStruct(fields[0].shape, jnp.float32)
     held = pltpu.VMEM((part, owned), jnp.float32)
-    return pl.pallas_call(
+    flag = [jax.ShapeDtypeStruct((1,), jnp.int32)] if fresh else []
+    results = pl.pallas_call(
         functools.partial(solve_kernel, first, fresh),
-        out_shape=[jax.ShapeDtypeStruct(fields[0].shape, jnp.float32)] * 2
-        + [jax.ShapeDtypeStruct((1,), jnp.int32)],
-        in_specs=[SMEM] + [ANY] * len(carried) + [VMEM] * (5 + len(coded)),
-        out_specs=[ANY, ANY, SMEM],
-        input_output_aliases={} if fresh else {1: 0, 2: 1},
+        out_shape=flag + [field, field],
+        in_specs=([SMEM] if fresh else [ANY, ANY]) + [VMEM] * (5 + len(coded)),
+        out_specs=[SMEM] * len(flag) + [ANY, ANY],
+        input_output_aliases={} if fresh else {0: 0, 1: 1},
         scratch_shapes=[held, held, pltpu.SemaphoreType.DMA((2,))],
         compiler_params=params(*fields, own, held, held, *coded),
         name="friction_solve",
-    )(over, *carried, *fields, own, *coded)
-
-
-def reduce(first, where, over, fields, kept, given, before, after):
+    )(*([table] if fresh else before), *fields, own, *coded)
+    return results[:-2], results[-2:]
+
+
+def reduce(first, table, fields, kept, given, before, after):
     per_owner = fields[0].shape[1] // kept.shape[2]
     col_size = lax.axis_size("col")
     got = [lax.ppermute(array, "lag", partners(lax.axis_size("lag"), 1)) for array in given]
-    own, *coded = code(where, over, kept, got, per_owner, after)
+    own, *coded = code(table, kept, got, per_owner, after)
     arrived = [
         lax.ppermute(coded[step - 1], "col", partners(col_size, step)) for step in [*range(2, col_size), 1]
     ]
-    return solve(first, over, fields, own, arrived, before), (arrived[0], arrived[1]), tuple(arrived)
+    return solve(first, table, fields, own, arrived, before), (arrived[0], arrived[1]), tuple(arrived)
 
 
 def local(history, kernel_tiles, tile_rows, tile_cols, tile_count, base_stress, prev_rate, direct_effect, state_var):
     _, _, lags, slots, side, _ = kernel_tiles.shape
     row_size, col_size = (lax.axis_size(axis) for axis in ("row", "col"))
-    where = jnp.stack([lax.axis_index(axis).astype(jnp.int32) for axis in ("row", "col", "lag")])
     history = history[:, 0]
     tiles = kernel_tiles[0, 0]
     sims = history.shape[1]
@@ -413,30 +415,31 @@
     held = load(history)
     received = []
     for piece in pieces:
-        packed = pack(where, requests, held, side, cap, piece, received[-1][:WAIT] if received else ())
+        packed = pack(requests, held, side, cap, piece, received[-1][:WAIT] if received else ())
         received.append(
             [lax.ppermute(packed[step - 1], "row", partners(row_size, step)) for step in range(1, row_size)]
         )
-    table, size, over, live_tiles = make_plan(
-        where, tile_cols, tile_rows, tile_count, [need, *requests], tiles, cap, col_size, per_owner
+    table, live_tiles = make_plan(
+        tile_cols, tile_rows, tile_count, [need, *requests], tiles, cap, col_size, per_owner
     )
 
     after = ()
-    result = None
+    flags = result = None
     for (first, part), blocks in zip(pieces, received):
         kept, *given = multiply_tiles(
-            first, part, False, over, table, size, live_tiles, held, blocks, chunks, after
+            first, part, False, table, live_tiles, held, blocks, chunks, after
         )
-        (*result, flag), after, _ = reduce(first, where, over, fields, kept, given, result, ())
+        (flag, result), after, _ = reduce(first, table, fields, kept, given, result, ())
+        flags = flags or flag
 
     def general():
         everything = [lax.ppermute(history, "row", partners(row_size, step)) for step in range(1, row_size)]
         kept, *given = multiply_tiles(
-            0, sims, True, over, table, size, live_tiles, history, everything, chunks, ()
+            0, sims, True, table, live_tiles, history, everything, chunks, ()
         )
-        return tuple(reduce(0, where, over, fields, kept, given, None, ())[0][:2])
-
-    return lax.cond(flag[0] > 0, general, lambda: tuple(result))
+        return tuple(reduce(0, table, fields, kept, given, None, ())[0][1])
+
+    return lax.cond(flags[0][0] > 0, general, lambda: tuple(result))
 
 
 def solution(mesh):

time: 85.9 us -> 82.3 us (0.958)
  Pallas kernels: 27 us -> 22.7 us
  starting transfers between devices: 22.2 us -> 23.8 us
  waiting for transfers between devices: 34.4 us -> 33.5 us
    pallas_call x2, Pallas kernels: 8.21 us -> 6.16 us  [multiply_tiles(): pl.pallas_call(functools.partial(tiles_kernel, first, whole, len(after)),...]
    ppermute x6, starting transfers between devices: 9.53 us -> 11.1 us  [reduce(): lax.ppermute(coded[step - 1], 'col', partners(col_size, step))]
    ppermute x6, waiting for transfers between devices: 16.6 us -> 15.2 us  [reduce(): lax.ppermute(coded[step - 1], 'col', partners(col_size, step))]
    pallas_call x2, Pallas kernels: 5.55 us -> 4.49 us  [solve(): pl.pallas_call(functools.partial(solve_kernel, first, fresh), out_shape=f...]
    pallas_call x2, Pallas kernels: 2.97 us -> 1.98 us  [code(): pl.pallas_call(functools.partial(code_kernel, per_owner, len(after)), out...]
  transfers between devices with their start and end apart: 19 -> 19, of which waited for: 9 -> 9; matrix products, arithmetic and copies ran while one was open for 0% -> 0% of each run, Pallas kernels for 20% -> 18%
where the time goes in v5:
time: 82.3 us; the launch traced here: 82.2 us
  waiting for transfers between devices  33.5 us (41%)
  starting transfers between devices  23.8 us (29%)
  Pallas kernels  22.7 us (28%)
  between operations  1.88 us (2%)
    ppermute x6, waiting for transfers between devices, reduce(): lax.ppermute(coded[step - 1], 'col', partners(col_size, step))  15.2 us
    ppermute x6, waiting for transfers between devices, local(): lax.ppermute(packed[step - 1], 'row', partners(row_size, step))  14.9 us
    ppermute x6, starting transfers between devices, reduce(): lax.ppermute(coded[step - 1], 'col', partners(col_size, step))  11.1 us
    ppermute x6, starting transfers between devices, local(): lax.ppermute(packed[step - 1], 'row', partners(row_size, step))  7.11 us
    pallas_call x2, Pallas kernels, multiply_tiles(): pl.pallas_call(functools.partial(tiles_kernel, first, whole, len(after)),...  6.16 us
    pallas_call x2, Pallas kernels, solve(): pl.pallas_call(functools.partial(solve_kernel, first, fresh), out_shape=f...  4.49 us
    ppermute x3, starting transfers between devices, local(): lax.ppermute(need, 'row', partners(row_size, step))  4.46 us
    pallas_call x1, Pallas kernels, make_plan(): pl.pallas_call(functools.partial(plan_kernel, cap, col_size, per_owner),...  3.52 us
  transfers between devices with their start and end apart: 19, of which 9 were waited for; matrix products, arithmetic and copies ran while one was open for 0% of the time, Pallas kernels for 18%

profile of v5, /device:TPU:0, one launch (start us, length us, event | category | flops | bytes accessed | tf_op | source)
XLA Modules:
  0.0 82.2 jit_solution(18339490294682650694)
XLA Ops:
  0.6 1.3 %mark_blocks.1.refs_0_ = s32[4,32]{1,0:T(4,128)} custom-call(s32[1,1,4,12]{3,2,1,0:T(4,128)} %cols.3, s32[1,1,4]{2,1,0:T(1,128)} %counts.3), custom_call_target="tpu_custom_call" | custom-call | tf_op jit(solution)/shard_map/mark_blocks/pallas_call | solution.py:62
  2.0 3.9 %collective-permute-start.10 = (s32[4,32]{1,0:T(4,128)}, s32[4,32]{1,0:T(4,128)S(1)}, u32[]{:S(2)}, u32[]{:S(2)}) collective-permute-start(s32[4,32]{1,0:T(4,128)} %mark_blocks.1.refs_0_), channel_id=1, source_target_pairs={{0,24},{8,16},{16,8},{24,0},{1,25},{9,17},{17,9},{25,1},{2,26},{10... | collective-permute-start | bytes 1544 | tf_op jit(solution)/shard_map/ppermute | solution.py:414
  5.9 0.5 collective-permute-start.9
  6.4 1.7 %load_history.1.refs_3_.history = bf16[4,128,2048]{2,1,0:T(8,128)(2,1)S(1)} custom-call(bf16[4,128,2048]{2,1,0:T(8,128)(2,1)} %bitcast.4), custom_call_target="tpu_custom_call" | custom-call | tf_op jit(solution)/shard_map/load_history/pallas_call | solution.py:78
  8.2 1.4 %collective-permute-done.9.refs_2_.refs_1_ = s32[4,32]{1,0:T(4,128)S(1)} collective-permute-done((s32[4,32]{1,0:T(4,128)}, s32[4,32]{1,0:T(4,128)S(1)}, u32[]{:S(2)}, u32[]{:S(2)}) %collective-permute-start.9) | collective-permute-done | bytes 544 | tf_op jit(solution)/shard_map/ppermute | solution.py:414
  9.7 0.5 collective-permute-done.8.refs_1_.refs_0_
  10.2 1.7 %pack_history.2 = (bf16[16,64,256]{2,1,0:T(8,128)(2,1)S(1)}, bf16[16,64,256]{2,1,0:T(8,128)(2,1)S(1)}, bf16[16,64,256]{2,1,0:T(8,128)(2,1)S(1)}) custom-call(s32[4,32]{1,0:T(4,128)S(1)} %collective-permute-done.8.refs_1_.refs_0_, s32[4,32]{1,0:T(4,128)S(1)} %collective-permute-done.9.refs_2_.refs_1_, s32[4,32]{1,0:T(4,128)S(1)} %collective-permute-done.10.refs_3_.refs_2_, ...), custom_call_target="tpu_custom_call" | custom-call | tf_op jit(solution)/shard_map/pack_history/pallas_call | solution.py:113
  12.0 2.0 %collective-permute-start.12 = (bf16[16,64,256]{2,1,0:T(8,128)(2,1)S(1)}, bf16[16,64,256]{2,1,0:T(8,128)(2,1)S(1)}, u32[]{:S(2)}, u32[]{:S(2)}) collective-permute-start(bf16[16,64,256]{2,1,0:T(8,128)(2,1)S(1)} %get-tuple-element.64), channel_id=1, source_target_pairs={{0,16},{8,24},{16,0},{24,8},{1,17},{9,25},{17,1},{25,9},{2,18},{10... | collective-permute-start | bytes 1572872 | tf_op jit(solution)/shard_map/ppermute | solution.py:420
  14.0 1.4 %collective-permute-start.13 = (bf16[16,64,256]{2,1,0:T(8,128)(2,1)S(1)}, bf16[16,64,256]{2,1,0:T(8,128)(2,1)S(1)}, u32[]{:S(2)}, u32[]{:S(2)}) collective-permute-start(bf16[16,64,256]{2,1,0:T(8,128)(2,1)S(1)} %get-tuple-element.65), channel_id=1, source_target_pairs={{0,24},{8,16},{16,8},{24,0},{1,25},{9,17},{17,9},{25,1},{2,26},{10... | collective-permute-start | bytes 1572872 | tf_op jit(solution)/shard_map/ppermute | solution.py:420
  15.5 11.4 %collective-permute-done.11.refs_0_.refs_4_ = bf16[16,64,256]{2,1,0:T(8,128)(2,1)S(1)} collective-permute-done((bf16[16,64,256]{2,1,0:T(8,128)(2,1)S(1)}, bf16[16,64,256]{2,1,0:T(8,128)(2,1)S(1)}, u32[]{:S(2)}, u32[]{:S(2)}) %collective-permute-start.11) | collective-permute-done | bytes 524320 | tf_op jit(solution)/shard_map/ppermute | solution.py:420
  26.8 1.7 %pack_history.3 = (bf16[16,64,256]{2,1,0:T(8,128)(2,1)S(1)}, bf16[16,64,256]{2,1,0:T(8,128)(2,1)S(1)}, bf16[16,64,256]{2,1,0:T(8,128)(2,1)S(1)}) custom-call(s32[4,32]{1,0:T(4,128)S(1)} %collective-permute-done.8.refs_1_.refs_0_, s32[4,32]{1,0:T(4,128)S(1)} %collective-permute-done.9.refs_2_.refs_1_, s32[4,32]{1,0:T(4,128)S(1)} %collective-permute-done.10.refs_3_.refs_2_, ...), custom_call_target="tpu_custom_call" | custom-call | tf_op jit(solution)/shard_map/pack_history/pallas_call | solution.py:113
  28.7 2.0 %collective-permute-start.20 = (bf16[16,64,256]{2,1,0:T(8,128)(2,1)S(1)}, bf16[16,64,256]{2,1,0:T(8,128)(2,1)S(1)}, u32[]{:S(2)}, u32[]{:S(2)}) collective-permute-start(bf16[16,64,256]{2,1,0:T(8,128)(2,1)S(1)} %get-tuple-element.77), channel_id=1, source_target_pairs={{0,16},{8,24},{16,0},{24,8},{1,17},{9,25},{17,1},{25,9},{2,18},{10... | collective-permute-start | bytes 1572872 | tf_op jit(solution)/shard_map/ppermute | solution.py:420
  30.7 1.4 %collective-permute-start.21 = (bf16[16,64,256]{2,1,0:T(8,128)(2,1)S(1)}, bf16[16,64,256]{2,1,0:T(8,128)(2,1)S(1)}, u32[]{:S(2)}, u32[]{:S(2)}) collective-permute-start(bf16[16,64,256]{2,1,0:T(8,128)(2,1)S(1)} %get-tuple-element.78), channel_id=1, source_target_pairs={{0,24},{8,16},{16,8},{24,0},{1,25},{9,17},{17,9},{25,1},{2,26},{10... | collective-permute-start | bytes 1572872 | tf_op jit(solution)/shard_map/ppermute | solution.py:420
  32.2 3.5 %plan_tiles.1 = (s32[5,48]{1,0:T(8,128)S(1)}, bf16[48,256,256]{2,1,0:T(8,128)(2,1)S(1)}) custom-call(s32[1,1,4,12]{3,2,1,0:T(4,128)S(1)} %copy-done.1, s32[1,1,4,12]{3,2,1,0:T(4,128)S(1)} %copy-done.3, s32[1,1,4]{2,1,0:T(1,128)S(1)} %copy-done.4, s32[4,32]{1,0:T(4,128)S(1)} %copy-done.2, s32[4,32]{1,0:T(4,128)S(1)} %collective-permute-done.8.refs_1_.refs_0_, ...), custom_call_target="tpu_custom_call" | custom-call | tf_op jit(solution)/shard_map/plan_tiles/pallas_call | solution.py:183
  35.7 3.4 %collective-permute-done.13.refs_2_ = bf16[16,64,256]{2,1,0:T(8,128)(2,1)S(1)} collective-permute-done((bf16[16,64,256]{2,1,0:T(8,128)(2,1)S(1)}, bf16[16,64,256]{2,1,0:T(8,128)(2,1)S(1)}, u32[]{:S(2)}, u32[]{:S(2)}) %collective-permute-start.13) | collective-permute-done | bytes 524320 | tf_op jit(solution)/shard_map/ppermute | solution.py:420
  39.1 3.1 %multiply_tiles.4 = (f32[32,64,256]{2,1,0:T(8,128)S(1)}, s16[528,256]{1,0:T(8,128)(2,1)S(1)}, s16[528,256]{1,0:T(8,128)(2,1)S(1)}) custom-call(s32[5,48]{1,0:T(8,128)S(1)} %get-tuple-element.61.table.refs_0_, bf16[48,256,256]{2,1,0:T(8,128)(2,1)S(1)} %get-tuple-element.62.tiles, bf16[4,128,2048]{2,1,0:T(8,128)(2,1)S(1)} %load_history.1.refs_3_.history, ...), custom_call_target="tpu_custom_call" | custom-call | tf_op jit(solution)/shard_map/multiply_tiles/pallas_call | solution.py:255
  42.2 0.5 collective-permute-start.15
  42.7 1.0 %collective-permute-done.14.refs_0_ = s16[528,256]{1,0:T(8,128)(2,1)S(1)} collective-permute-done((s16[528,256]{1,0:T(8,128)(2,1)S(1)}, s16[528,256]{1,0:T(8,128)(2,1)S(1)}, u32[]{:S(2)}, u32[]{:S(2)}) %collective-permute-start.14) | collective-permute-done | bytes 270368 | tf_op jit(solution)/shard_map/ppermute | solution.py:389
  43.8 0.4 collective-permute-done.15.refs_1_
  44.2 1.0 %add_and_code.4 = (f32[4,64,256]{2,1,0:T(8,128)S(1)}, s16[528,128]{1,0:T(8,128)(2,1)S(1)}, s16[528,128]{1,0:T(8,128)(2,1)S(1)}, s16[528,128]{1,0:T(8,128)(2,1)S(1)}) custom-call(s32[5,48]{1,0:T(8,128)S(1)} %get-tuple-element.61.table.refs_0_, f32[32,64,256]{2,1,0:T(8,128)S(1)} %get-tuple-element.66.kept, ...), custom_call_target="tpu_custom_call" | custom-call | tf_op jit(solution)/shard_map/add_and_code/pallas_call | solution.py:319
  45.2 3.1 %collective-permute-start.16 = (s16[528,128]{1,0:T(8,128)(2,1)S(1)}, s16[528,128]{1,0:T(8,128)(2,1)S(1)}, u32[]{:S(2)}, u32[]{:S(2)}) collective-permute-start(s16[528,128]{1,0:T(8,128)(2,1)S(1)} %get-tuple-element.70), channel_id=1, source_target_pairs={{0,4},{2,6},{4,0},{6,2},{1,5},{3,7},{5,1},{7,3},{8,12},{10,14},{12... | collective-permute-start | bytes 405512 | tf_op jit(solution)/shard_map/ppermute | solution.py:392
  48.3 0.9 %collective-permute-start.17 = (s16[528,128]{1,0:T(8,128)(2,1)S(1)}, s16[528,128]{1,0:T(8,128)(2,1)S(1)}, u32[]{:S(2)}, u32[]{:S(2)}) collective-permute-start(s16[528,128]{1,0:T(8,128)(2,1)S(1)} %get-tuple-element.71), channel_id=1, source_target_pairs={{0,6},{2,4},{4,2},{6,0},{1,7},{3,5},{5,3},{7,1},{8,14},{10,12},{12... | collective-permute-start | bytes 405512 | tf_op jit(solution)/shard_map/ppermute | solution.py:392
  49.1 9.3 %collective-permute-done.16.refs_6_.refs_3_ = s16[528,128]{1,0:T(8,128)(2,1)S(1)} collective-permute-done((s16[528,128]{1,0:T(8,128)(2,1)S(1)}, s16[528,128]{1,0:T(8,128)(2,1)S(1)}, u32[]{:S(2)}, u32[]{:S(2)}) %collective-permute-start.16) | collective-permute-done | bytes 135200 | tf_op jit(solution)/shard_map/ppermute | solution.py:392
  58.6 3.1 %multiply_tiles.5 = (f32[32,64,256]{2,1,0:T(8,128)S(1)}, s16[528,256]{1,0:T(8,128)(2,1)S(1)}, s16[528,256]{1,0:T(8,128)(2,1)S(1)}) custom-call(s32[5,48]{1,0:T(8,128)S(1)} %get-tuple-element.61.table.refs_0_, bf16[48,256,256]{2,1,0:T(8,128)(2,1)S(1)} %get-tuple-element.62.tiles, bf16[4,128,2048]{2,1,0:T(8,128)(2,1)S(1)} %load_history.1.refs_3_.history, ...), custom_call_target="tpu_custom_call" | custom-call | tf_op jit(solution)/shard_map/multiply_tiles/pallas_call | solution.py:255
  61.8 0.5 collective-permute-start.23
  62.3 2.8 %collective-permute-start.18 = (s16[528,128]{1,0:T(8,128)(2,1)S(1)}, s16[528,128]{1,0:T(8,128)(2,1)S(1)}, u32[]{:S(2)}, u32[]{:S(2)}) collective-permute-start(s16[528,128]{1,0:T(8,128)(2,1)S(1)} %get-tuple-element.72), channel_id=1, source_target_pairs={{0,2},{2,0},{4,6},{6,4},{1,3},{3,1},{5,7},{7,5},{8,10},{10,8},{12,... | collective-permute-start | bytes 405512 | tf_op jit(solution)/shard_map/ppermute | solution.py:392
  65.2 1.0 %add_and_code.5 = (f32[4,64,256]{2,1,0:T(8,128)S(1)}, s16[528,128]{1,0:T(8,128)(2,1)S(1)}, s16[528,128]{1,0:T(8,128)(2,1)S(1)}, s16[528,128]{1,0:T(8,128)(2,1)S(1)}) custom-call(s32[5,48]{1,0:T(8,128)S(1)} %get-tuple-element.61.table.refs_0_, f32[32,64,256]{2,1,0:T(8,128)S(1)} %get-tuple-element.79.kept, ...), custom_call_target="tpu_custom_call" | custom-call | tf_op jit(solution)/shard_map/add_and_code/pallas_call | solution.py:319
  66.1 3.7 %collective-permute-start.24 = (s16[528,128]{1,0:T(8,128)(2,1)S(1)}, s16[528,128]{1,0:T(8,128)(2,1)S(1)}, u32[]{:S(2)}, u32[]{:S(2)}) collective-permute-start(s16[528,128]{1,0:T(8,128)(2,1)S(1)} %get-tuple-element.83), channel_id=1, source_target_pairs={{0,4},{2,6},{4,0},{6,2},{1,5},{3,7},{5,1},{7,3},{8,12},{10,14},{12... | collective-permute-start | bytes 405512 | tf_op jit(solution)/shard_map/ppermute | solution.py:392
  70.0 0.5 collective-permute-start.26
  70.5 2.8 %friction_solve.4 = (s32[1]{0:T(128)}, f32[128,1024]{1,0:T(8,128)}, f32[128,1024]{1,0:T(8,128)}) custom-call(s32[5,48]{1,0:T(8,128)S(1)} %get-tuple-element.61.table.refs_0_, f32[128,1024]{1,0:T(8,128)S(1)} %copy-done.7, f32[128,1024]{1,0:T(8,128)S(1)} %copy-done.8, f32[128,1024]{1,0:T(8,128)S(1)} %copy-done.9, f32[128,1024]{1,0:T(8,128)S(1)} %copy-done.12, ...), custom_call_target="tpu_custom_call" | custom-call | tf_op jit(solution)/shard_map/friction_solve/pallas_call | solution.py:373
  74.2 5.9 %collective-permute-done.24.refs_7_ = s16[528,128]{1,0:T(8,128)(2,1)S(1)} collective-permute-done((s16[528,128]{1,0:T(8,128)(2,1)S(1)}, s16[528,128]{1,0:T(8,128)(2,1)S(1)}, u32[]{:S(2)}, u32[]{:S(2)}) %collective-permute-start.24) | collective-permute-done | bytes 135200 | tf_op jit(solution)/shard_map/ppermute | solution.py:392
  80.1 1.7 %friction_solve.5 = (f32[128,1024]{1,0:T(8,128)}, f32[128,1024]{1,0:T(8,128)}) custom-call(f32[128,1024]{1,0:T(8,128)} %get-tuple-element.74.refs_0_, f32[128,1024]{1,0:T(8,128)} %get-tuple-element.75.refs_1_, f32[128,1024]{1,0:T(8,128)S(1)} %copy-done.7, f32[128,1024]{1,0:T(8,128)S(1)} %copy-done.8, ...), custom_call_target="tpu_custom_call", output_to_operand_aliasing={{0}: (0, {}), {1}: (1, {})} | custom-call | tf_op jit(solution)/shard_map/friction_solve/pallas_call | solution.py:373
  (38 shorter events, 1.1 us)
Async XLA Ops:
  2.0 6.3 %collective-permute-start.10 = (s32[4,32]{1,0:T(4,128)}, s32[4,32]{1,0:T(4,128)S(1)}, u32[]{:S(2)}, u32[]{:S(2)}) collective-permute-start(s32[4,32]{1,0:T(4,128)} %mark_blocks.1.refs_0_), channel_id=1, source_target_pairs={{0,24},{8,16},{16,8},{24,0},{1,25},{9,17},{17,9},{25,1},{2,26},{10... | collective-permute-start | bytes 1544 | tf_op jit(solution)/shard_map/ppermute | solution.py:414
  5.9 3.8 %collective-permute-start.9 = (s32[4,32]{1,0:T(4,128)}, s32[4,32]{1,0:T(4,128)S(1)}, u32[]{:S(2)}, u32[]{:S(2)}) collective-permute-start(s32[4,32]{1,0:T(4,128)} %mark_blocks.1.refs_0_), channel_id=1, source_target_pairs={{0,16},{8,24},{16,0},{24,8},{1,17},{9,25},{17,1},{25,9},{2,18},{10... | collective-permute-start | bytes 1544 | tf_op jit(solution)/shard_map/ppermute | solution.py:414
  6.4 3.8 %collective-permute-start.8 = (s32[4,32]{1,0:T(4,128)}, s32[4,32]{1,0:T(4,128)S(1)}, u32[]{:S(2)}, u32[]{:S(2)}) collective-permute-start(s32[4,32]{1,0:T(4,128)} %mark_blocks.1.refs_0_), channel_id=1, source_target_pairs={{0,8},{8,0},{16,24},{24,16},{1,9},{9,1},{17,25},{25,17},{2,10},{10... | collective-permute-start | bytes 1544 | tf_op jit(solution)/shard_map/ppermute | solution.py:414
  6.4 25.7 %copy-start = (bf16[1,1,4,12,256,256]{5,4,3,2,1,0:T(8,128)(2,1)S(1)}, bf16[1,1,4,12,256,256]{5,4,3,2,1,0:T(8,128)(2,1)}, u32[]{:S(2)}) copy-start(bf16[1,1,4,12,256,256]{5,4,3,2,1,0:T(8,128)(2,1)} %param.12) | copy-start | bytes 18874372
  8.2 24.0 %copy-start.1 = (s32[1,1,4,12]{3,2,1,0:T(4,128)S(1)}, s32[1,1,4,12]{3,2,1,0:T(4,128)}, u32[]{:S(2)}) copy-start(s32[1,1,4,12]{3,2,1,0:T(4,128)} %cols.3) | copy-start | bytes 580
  8.2 23.9 %copy-start.2 = (s32[4,32]{1,0:T(4,128)S(1)}, s32[4,32]{1,0:T(4,128)}, u32[]{:S(2)}) copy-start(s32[4,32]{1,0:T(4,128)} %mark_blocks.1.refs_0_) | copy-start | bytes 1540
  8.2 23.9 %copy-start.3 = (s32[1,1,4,12]{3,2,1,0:T(4,128)S(1)}, s32[1,1,4,12]{3,2,1,0:T(4,128)}, u32[]{:S(2)}) copy-start(s32[1,1,4,12]{3,2,1,0:T(4,128)} %rows.1) | copy-start | bytes 580
  8.2 23.9 %copy-start.4 = (s32[1,1,4]{2,1,0:T(1,128)S(1)}, s32[1,1,4]{2,1,0:T(1,128)}, u32[]{:S(2)}) copy-start(s32[1,1,4]{2,1,0:T(1,128)} %counts.3) | copy-start | bytes 52
  11.9 14.9 %collective-permute-start.11 = (bf16[16,64,256]{2,1,0:T(8,128)(2,1)S(1)}, bf16[16,64,256]{2,1,0:T(8,128)(2,1)S(1)}, u32[]{:S(2)}, u32[]{:S(2)}) collective-permute-start(bf16[16,64,256]{2,1,0:T(8,128)(2,1)S(1)} %get-tuple-element.63), channel_id=1, source_target_pairs={{0,8},{8,0},{16,24},{24,16},{1,9},{9,1},{17,25},{25,17},{2,10},{10... | collective-permute-start | bytes 1572872 | tf_op jit(solution)/shard_map/ppermute | solution.py:420
  12.0 23.6 %collective-permute-start.12 = (bf16[16,64,256]{2,1,0:T(8,128)(2,1)S(1)}, bf16[16,64,256]{2,1,0:T(8,128)(2,1)S(1)}, u32[]{:S(2)}, u32[]{:S(2)}) collective-permute-start(bf16[16,64,256]{2,1,0:T(8,128)(2,1)S(1)} %get-tuple-element.64), channel_id=1, source_target_pairs={{0,16},{8,24},{16,0},{24,8},{1,17},{9,25},{17,1},{25,9},{2,18},{10... | collective-permute-start | bytes 1572872 | tf_op jit(solution)/shard_map/ppermute | solution.py:420
  14.0 25.0 %collective-permute-start.13 = (bf16[16,64,256]{2,1,0:T(8,128)(2,1)S(1)}, bf16[16,64,256]{2,1,0:T(8,128)(2,1)S(1)}, u32[]{:S(2)}, u32[]{:S(2)}) collective-permute-start(bf16[16,64,256]{2,1,0:T(8,128)(2,1)S(1)} %get-tuple-element.65), channel_id=1, source_target_pairs={{0,24},{8,16},{16,8},{24,0},{1,25},{9,17},{17,9},{25,1},{2,26},{10... | collective-permute-start | bytes 1572872 | tf_op jit(solution)/shard_map/ppermute | solution.py:420
  28.6 29.9 %collective-permute-start.19 = (bf16[16,64,256]{2,1,0:T(8,128)(2,1)S(1)}, bf16[16,64,256]{2,1,0:T(8,128)(2,1)S(1)}, u32[]{:S(2)}, u32[]{:S(2)}) collective-permute-start(bf16[16,64,256]{2,1,0:T(8,128)(2,1)S(1)} %get-tuple-element.76), channel_id=1, source_target_pairs={{0,8},{8,0},{16,24},{24,16},{1,9},{9,1},{17,25},{25,17},{2,10},{10... | collective-permute-start | bytes 1572872 | tf_op jit(solution)/shard_map/ppermute | solution.py:420
  28.7 29.7 %collective-permute-start.20 = (bf16[16,64,256]{2,1,0:T(8,128)(2,1)S(1)}, bf16[16,64,256]{2,1,0:T(8,128)(2,1)S(1)}, u32[]{:S(2)}, u32[]{:S(2)}) collective-permute-start(bf16[16,64,256]{2,1,0:T(8,128)(2,1)S(1)} %get-tuple-element.77), channel_id=1, source_target_pairs={{0,16},{8,24},{16,0},{24,8},{1,17},{9,25},{17,1},{25,9},{2,18},{10... | collective-permute-start | bytes 1572872 | tf_op jit(solution)/shard_map/ppermute | solution.py:420
  30.7 27.9 %collective-permute-start.21 = (bf16[16,64,256]{2,1,0:T(8,128)(2,1)S(1)}, bf16[16,64,256]{2,1,0:T(8,128)(2,1)S(1)}, u32[]{:S(2)}, u32[]{:S(2)}) collective-permute-start(bf16[16,64,256]{2,1,0:T(8,128)(2,1)S(1)} %get-tuple-element.78), channel_id=1, source_target_pairs={{0,24},{8,16},{16,8},{24,0},{1,25},{9,17},{17,9},{25,1},{2,26},{10... | collective-permute-start | bytes 1572872 | tf_op jit(solution)/shard_map/ppermute | solution.py:420
  42.2 1.6 %collective-permute-start.14 = (s16[528,256]{1,0:T(8,128)(2,1)S(1)}, s16[528,256]{1,0:T(8,128)(2,1)S(1)}, u32[]{:S(2)}, u32[]{:S(2)}) collective-permute-start(s16[528,256]{1,0:T(8,128)(2,1)S(1)} %get-tuple-element.67), channel_id=1, source_target_pairs={{0,1},{1,0},{2,3},{3,2},{4,5},{5,4},{6,7},{7,6},{8,9},{9,8},{10,11... | collective-permute-start | bytes 811016 | tf_op jit(solution)/shard_map/ppermute | solution.py:389
  42.2 1.9 %collective-permute-start.15 = (s16[528,256]{1,0:T(8,128)(2,1)S(1)}, s16[528,256]{1,0:T(8,128)(2,1)S(1)}, u32[]{:S(2)}, u32[]{:S(2)}) collective-permute-start(s16[528,256]{1,0:T(8,128)(2,1)S(1)} %get-tuple-element.68), channel_id=1, source_target_pairs={{0,1},{1,0},{2,3},{3,2},{4,5},{5,4},{6,7},{7,6},{8,9},{9,8},{10,11... | collective-permute-start | bytes 811016 | tf_op jit(solution)/shard_map/ppermute | solution.py:389
  45.2 13.3 %collective-permute-start.16 = (s16[528,128]{1,0:T(8,128)(2,1)S(1)}, s16[528,128]{1,0:T(8,128)(2,1)S(1)}, u32[]{:S(2)}, u32[]{:S(2)}) collective-permute-start(s16[528,128]{1,0:T(8,128)(2,1)S(1)} %get-tuple-element.70), channel_id=1, source_target_pairs={{0,4},{2,6},{4,0},{6,2},{1,5},{3,7},{5,1},{7,3},{8,12},{10,14},{12... | collective-permute-start | bytes 405512 | tf_op jit(solution)/shard_map/ppermute | solution.py:392
  48.3 10.2 %collective-permute-start.17 = (s16[528,128]{1,0:T(8,128)(2,1)S(1)}, s16[528,128]{1,0:T(8,128)(2,1)S(1)}, u32[]{:S(2)}, u32[]{:S(2)}) collective-permute-start(s16[528,128]{1,0:T(8,128)(2,1)S(1)} %get-tuple-element.71), channel_id=1, source_target_pairs={{0,6},{2,4},{4,2},{6,0},{1,7},{3,5},{5,3},{7,1},{8,14},{10,12},{12... | collective-permute-start | bytes 405512 | tf_op jit(solution)/shard_map/ppermute | solution.py:392
  61.7 8.8 %copy-start.7 = (f32[128,1024]{1,0:T(8,128)S(1)}, f32[128,1024]{1,0:T(8,128)}, u32[]{:S(2)}) copy-start(f32[128,1024]{1,0:T(8,128)} %refs_2_.3) | copy-start | bytes 1572868
  61.7 8.8 %copy-start.8 = (f32[128,1024]{1,0:T(8,128)S(1)}, f32[128,1024]{1,0:T(8,128)}, u32[]{:S(2)}) copy-start(f32[128,1024]{1,0:T(8,128)} %refs_3_.3) | copy-start | bytes 1572868
  61.7 8.8 %copy-start.9 = (f32[128,1024]{1,0:T(8,128)S(1)}, f32[128,1024]{1,0:T(8,128)}, u32[]{:S(2)}) copy-start(f32[128,1024]{1,0:T(8,128)} %refs_4_.3) | copy-start | bytes 1572868
  61.8 8.8 %copy-start.12 = (f32[128,1024]{1,0:T(8,128)S(1)}, f32[128,1024]{1,0:T(8,128)}, u32[]{:S(2)}) copy-start(f32[128,1024]{1,0:T(8,128)} %refs_5_.1) | copy-start | bytes 1572868
  61.8 3.4 %collective-permute-start.22 = (s16[528,256]{1,0:T(8,128)(2,1)S(1)}, s16[528,256]{1,0:T(8,128)(2,1)S(1)}, u32[]{:S(2)}, u32[]{:S(2)}) collective-permute-start(s16[528,256]{1,0:T(8,128)(2,1)S(1)} %get-tuple-element.80), channel_id=1, source_target_pairs={{0,1},{1,0},{2,3},{3,2},{4,5},{5,4},{6,7},{7,6},{8,9},{9,8},{10,11... | collective-permute-start | bytes 811016 | tf_op jit(solution)/shard_map/ppermute | solution.py:389
  61.8 3.3 %collective-permute-start.23 = (s16[528,256]{1,0:T(8,128)(2,1)S(1)}, s16[528,256]{1,0:T(8,128)(2,1)S(1)}, u32[]{:S(2)}, u32[]{:S(2)}) collective-permute-start(s16[528,256]{1,0:T(8,128)(2,1)S(1)} %get-tuple-element.81), channel_id=1, source_target_pairs={{0,1},{1,0},{2,3},{3,2},{4,5},{5,4},{6,7},{7,6},{8,9},{9,8},{10,11... | collective-permute-start | bytes 811016 | tf_op jit(solution)/shard_map/ppermute | solution.py:389
  62.3 8.1 %collective-permute-start.18 = (s16[528,128]{1,0:T(8,128)(2,1)S(1)}, s16[528,128]{1,0:T(8,128)(2,1)S(1)}, u32[]{:S(2)}, u32[]{:S(2)}) collective-permute-start(s16[528,128]{1,0:T(8,128)(2,1)S(1)} %get-tuple-element.72), channel_id=1, source_target_pairs={{0,2},{2,0},{4,6},{6,4},{1,3},{3,1},{5,7},{7,5},{8,10},{10,8},{12,... | collective-permute-start | bytes 405512 | tf_op jit(solution)/shard_map/ppermute | solution.py:392
  66.1 13.9 %collective-permute-start.24 = (s16[528,128]{1,0:T(8,128)(2,1)S(1)}, s16[528,128]{1,0:T(8,128)(2,1)S(1)}, u32[]{:S(2)}, u32[]{:S(2)}) collective-permute-start(s16[528,128]{1,0:T(8,128)(2,1)S(1)} %get-tuple-element.83), channel_id=1, source_target_pairs={{0,4},{2,6},{4,0},{6,2},{1,5},{3,7},{5,1},{7,3},{8,12},{10,14},{12... | collective-permute-start | bytes 405512 | tf_op jit(solution)/shard_map/ppermute | solution.py:392
  69.8 10.2 %collective-permute-start.25 = (s16[528,128]{1,0:T(8,128)(2,1)S(1)}, s16[528,128]{1,0:T(8,128)(2,1)S(1)}, u32[]{:S(2)}, u32[]{:S(2)}) collective-permute-start(s16[528,128]{1,0:T(8,128)(2,1)S(1)} %get-tuple-element.84), channel_id=1, source_target_pairs={{0,6},{2,4},{4,2},{6,0},{1,7},{3,5},{5,3},{7,1},{8,14},{10,12},{12... | collective-permute-start | bytes 405512 | tf_op jit(solution)/shard_map/ppermute | solution.py:392
  70.0 10.1 %collective-permute-start.26 = (s16[528,128]{1,0:T(8,128)(2,1)S(1)}, s16[528,128]{1,0:T(8,128)(2,1)S(1)}, u32[]{:S(2)}, u32[]{:S(2)}) collective-permute-start(s16[528,128]{1,0:T(8,128)(2,1)S(1)} %get-tuple-element.85), channel_id=1, source_target_pairs={{0,2},{2,0},{4,6},{6,4},{1,3},{3,1},{5,7},{7,5},{8,10},{10,8},{12,... | collective-permute-start | bytes 405512 | tf_op jit(solution)/shard_map/ppermute | solution.py:392
  73.3 8.4 %copy-start.6 = (bf16[4,1,128,2048]{3,2,1,0:T(8,128)(2,1)S(1)}, bf16[4,1,128,2048]{3,2,1,0:T(8,128)(2,1)}, u32[]{:S(2)}) copy-start(bf16[4,1,128,2048]{3,2,1,0:T(8,128)(2,1)} %param.11) | copy-start | bytes 6291460

commit v6 on v5

--- a/solution.py
+++ b/solution.py
@@ -25,6 +25,10 @@
 def params(*shapes):
     held = sum(math.prod(s.shape) * jnp.dtype(s.dtype).itemsize for s in shapes)
     return pltpu.CompilerParams(vmem_limit_bytes=held + 8 * 1024 * 1024)
+
+
+def padded(rows):
+    return (rows // PAD + 1) * PAD
 
 
 def partners(size, step):
@@ -194,8 +198,8 @@
     )(cols, rows, counts, *needs, tiles)
 
 
-def tiles_kernel(first, whole, extra, table, tiles, history, *refs):
-    received, (sums, *given), blocks = refs[: len(refs) - 2 - SPLIT - extra], refs[-2 - SPLIT : -1], refs[-1]
+def tiles_kernel(first, whole, extra, split, table, tiles, history, *refs):
+    received, (sums, *given), blocks = refs[: len(refs) - 2 - split - extra], refs[-2 - split : -1], refs[-1]
     side = tiles.shape[2]
     halves, part, _ = sums.shape
     live = table[4, len(received) + 1]
@@ -234,7 +238,7 @@
 
     lax.fori_loop(0, (live + GROUP - 1) // GROUP, multiply, 0)
     half = halves // 2
-    size = half // SPLIT
+    size = half // split
     flag = jnp.full((1, side), 1.0, jnp.float32) * table[4, OVER].astype(jnp.float32)
     for index, target in enumerate(given):
         exponents = []
@@ -242,21 +246,21 @@
             grid, exponent = to_fixed(sums[half + index * size + chunk])
             target[chunk * part : (chunk + 1) * part] = grid
             exponents.append(exponent)
-        exponents += [jnp.zeros((PAD - 1 - size, side), jnp.float32), flag]
+        exponents += [jnp.zeros((padded(size) - 1 - size, side), jnp.float32), flag]
         tail = jnp.concatenate(exponents, axis=0)
         target[size * part :] = tail.astype(jnp.int32).astype(jnp.int16)
 
 
-def multiply_tiles(first, part, whole, table, tiles, history, received, chunks, after):
+def multiply_tiles(first, part, whole, split, table, tiles, history, received, chunks, after):
     side = tiles.shape[2]
-    more = [jax.ShapeDtypeStruct((chunks // SPLIT * part + PAD, side), jnp.int16)] * SPLIT
+    more = [jax.ShapeDtypeStruct((chunks // split * part + padded(chunks // split), side), jnp.int16)] * split
     blocks = pltpu.VMEM((table.shape[1], part, side), history.dtype)
     sums = jax.ShapeDtypeStruct((2 * chunks, part, side), jnp.float32)
     return pl.pallas_call(
-        functools.partial(tiles_kernel, first, whole, len(after)),
+        functools.partial(tiles_kernel, first, whole, len(after), split),
         out_shape=[sums, *more],
         in_specs=[SMEM] + [VMEM] * (2 + len(received)) + [ANY] * len(after),
-        out_specs=[VMEM] * (1 + SPLIT),
+        out_specs=[VMEM] * (1 + split),
         scratch_shapes=[blocks],
         compiler_params=params(tiles, history, *received, *more, blocks, sums),
         name="multiply_tiles",
@@ -274,15 +278,14 @@
     return grid.astype(jnp.int32).astype(jnp.float32) * jnp.exp2(exponent - 15.0)
 
 
-def code_kernel(per_owner, extra, table, kept, *refs):
-    got, own, coded = refs[:SPLIT], refs[SPLIT + extra], refs[SPLIT + extra + 1 : -1]
-    theirs = refs[-1]
+def code_kernel(per_owner, split, given, kept, *refs):
+    got, own, coded, theirs = refs[:split], refs[split], refs[split + 1 : -1], refs[-1]
     chunks, part, side = theirs.shape
-    size = chunks // SPLIT
-    flag = table[4, OVER].astype(jnp.float32)
+    size = chunks // split
+    flag = given[given.shape[0] - PAD :, :].astype(jnp.int32).astype(jnp.float32)[PAD - 1 :, :LANES]
     for index, source in enumerate(got):
         tail = source[size * part :, :].astype(jnp.int32).astype(jnp.float32)
-        flag = jnp.maximum(flag, tail[PAD - 1 :, :LANES])
+        flag = jnp.maximum(flag, tail[padded(size) - 1 :, :LANES])
         for chunk in range(size):
             theirs[index * size + chunk] = from_fixed(
                 source[chunk * part : (chunk + 1) * part, :], tail[chunk : chunk + 1, :]
@@ -310,21 +313,21 @@
             out[pl.ds(at * part, PAD), :] = tail.astype(jnp.int32).astype(jnp.int16)
 
 
-def code(table, kept, got, per_owner, after):
+def code(given, kept, got, per_owner):
     chunks, part, side = kept.shape
     chunks = chunks // 2
     chunk = jax.ShapeDtypeStruct((per_owner * part * (side // LANES) + PAD, LANES), jnp.int16)
     own = jax.ShapeDtypeStruct((per_owner, part, side), jnp.float32)
     outs = [own] + [chunk] * (chunks // per_owner - 1)
     return pl.pallas_call(
-        functools.partial(code_kernel, per_owner, len(after)),
+        functools.partial(code_kernel, per_owner, len(got)),
         out_shape=outs,
-        in_specs=[SMEM] + [VMEM] * (1 + len(got)) + [ANY] * len(after),
+        in_specs=[VMEM] * (2 + len(got)),
         out_specs=[VMEM] * len(outs),
         scratch_shapes=[pltpu.VMEM((chunks, part, side), jnp.float32)],
-        compiler_params=params(kept, kept, *got, *outs),
+        compiler_params=params(given, kept, kept, *got, *outs),
         name="add_and_code",
-    )(table, kept, *got, *after)
+    )(given, kept, *got)
 
 
 def solve_kernel(first, fresh, *refs):
@@ -383,11 +386,11 @@
     return results[:-2], results[-2:]
 
 
-def reduce(first, table, fields, kept, given, before, after):
+def reduce(first, table, fields, kept, given, before):
     per_owner = fields[0].shape[1] // kept.shape[2]
     col_size = lax.axis_size("col")
     got = [lax.ppermute(array, "lag", partners(lax.axis_size("lag"), 1)) for array in given]
-    own, *coded = code(table, kept, got, per_owner, after)
+    own, *coded = code(given[0], kept, got, per_owner)
     arrived = [
         lax.ppermute(coded[step - 1], "col", partners(col_size, step)) for step in [*range(2, col_size), 1]
     ]
@@ -427,17 +430,17 @@
     flags = result = None
     for (first, part), blocks in zip(pieces, received):
         kept, *given = multiply_tiles(
-            first, part, False, table, live_tiles, held, blocks, chunks, after
+            first, part, False, 1 if first + part == sims else SPLIT, table, live_tiles, held, blocks, chunks, after
         )
-        (flag, result), after, _ = reduce(first, table, fields, kept, given, result, ())
+        (flag, result), after, _ = reduce(first, table, fields, kept, given, result)
         flags = flags or flag
 
     def general():
         everything = [lax.ppermute(history, "row", partners(row_size, step)) for step in range(1, row_size)]
         kept, *given = multiply_tiles(
-            0, sims, True, table, live_tiles, history, everything, chunks, ()
+            0, sims, True, 1, table, live_tiles, history, everything, chunks, ()
         )
-        return tuple(reduce(0, table, fields, kept, given, None, ())[0][1])
+        return tuple(reduce(0, table, fields, kept, given, None)[0][1])
 
     return lax.cond(flags[0][0] > 0, general, lambda: tuple(result))
 

time: 82.3 us -> 81.4 us (0.989)
  starting transfers between devices: 23.8 us -> 21.5 us
  Pallas kernels: 22.7 us -> 24.1 us
    ppermute x6, starting transfers between devices: 11.1 us -> 9.26 us  [reduce(): lax.ppermute(coded[step - 1], 'col', partners(col_size, step))]
  transfers between devices with their start and end apart: 19 -> 18, of which waited for: 9 -> 10; matrix products, arithmetic and copies ran while one was open for 0% -> 0% of each run, Pallas kernels for 18% -> 19%
where the time goes in v6:
time: 81.4 us; the launch traced here: 81.1 us
  waiting for transfers between devices  33.4 us (41%)
  Pallas kernels  24.1 us (30%)
  starting transfers between devices  21.5 us (26%)
  between operations  1.83 us (2%)
    ppermute x6, waiting for transfers between devices, reduce(): lax.ppermute(coded[step - 1], 'col', partners(col_size, step))  15.3 us
    ppermute x6, waiting for transfers between devices, local(): lax.ppermute(packed[step - 1], 'row', partners(row_size, step))  14.8 us
    ppermute x6, starting transfers between devices, reduce(): lax.ppermute(coded[step - 1], 'col', partners(col_size, step))  9.26 us
    pallas_call x2, Pallas kernels, multiply_tiles(): pl.pallas_call(functools.partial(tiles_kernel, first, whole, len(after),...  8.17 us
    ppermute x6, starting transfers between devices, local(): lax.ppermute(packed[step - 1], 'row', partners(row_size, step))  7.11 us
    pallas_call x2, Pallas kernels, solve(): pl.pallas_call(functools.partial(solve_kernel, first, fresh), out_shape=f...  4.48 us
    ppermute x3, starting transfers between devices, local(): lax.ppermute(need, 'row', partners(row_size, step))  4.46 us
    pallas_call x1, Pallas kernels, make_plan(): pl.pallas_call(functools.partial(plan_kernel, cap, col_size, per_owner),...  4.12 us
  transfers between devices with their start and end apart: 18, of which 10 were waited for; matrix products, arithmetic and copies ran while one was open for 0% of the time, Pallas kernels for 19%

profile of v6, /device:TPU:0, one launch (start us, length us, event | category | flops | bytes accessed | tf_op | source)
XLA Modules:
  0.0 81.1 jit_solution(2115113114123973936)
XLA Ops:
  0.6 1.3 %mark_blocks.1.refs_0_ = s32[4,32]{1,0:T(4,128)} custom-call(s32[1,1,4,12]{3,2,1,0:T(4,128)} %cols.3, s32[1,1,4]{2,1,0:T(1,128)} %counts.3), custom_call_target="tpu_custom_call" | custom-call | tf_op jit(solution)/shard_map/mark_blocks/pallas_call | solution.py:66
  2.0 3.9 %collective-permute-start.9 = (s32[4,32]{1,0:T(4,128)}, s32[4,32]{1,0:T(4,128)S(1)}, u32[]{:S(2)}, u32[]{:S(2)}) collective-permute-start(s32[4,32]{1,0:T(4,128)} %mark_blocks.1.refs_0_), channel_id=1, source_target_pairs={{0,24},{8,16},{16,8},{24,0},{1,25},{9,17},{17,9},{25,1},{2,26},{10... | collective-permute-start | bytes 1544 | tf_op jit(solution)/shard_map/ppermute | solution.py:417
  5.9 0.5 collective-permute-start.8
  6.4 1.7 %load_history.1.refs_3_.history = bf16[4,128,2048]{2,1,0:T(8,128)(2,1)S(1)} custom-call(bf16[4,128,2048]{2,1,0:T(8,128)(2,1)} %bitcast.4), custom_call_target="tpu_custom_call" | custom-call | tf_op jit(solution)/shard_map/load_history/pallas_call | solution.py:82
  8.2 1.4 %collective-permute-done.8.refs_2_.refs_1_ = s32[4,32]{1,0:T(4,128)S(1)} collective-permute-done((s32[4,32]{1,0:T(4,128)}, s32[4,32]{1,0:T(4,128)S(1)}, u32[]{:S(2)}, u32[]{:S(2)}) %collective-permute-start.8) | collective-permute-done | bytes 544 | tf_op jit(solution)/shard_map/ppermute | solution.py:417
  9.7 0.5 collective-permute-done.7.refs_1_.refs_0_
  10.2 1.7 %pack_history.2 = (bf16[16,64,256]{2,1,0:T(8,128)(2,1)S(1)}, bf16[16,64,256]{2,1,0:T(8,128)(2,1)S(1)}, bf16[16,64,256]{2,1,0:T(8,128)(2,1)S(1)}) custom-call(s32[4,32]{1,0:T(4,128)S(1)} %collective-permute-done.7.refs_1_.refs_0_, s32[4,32]{1,0:T(4,128)S(1)} %collective-permute-done.8.refs_2_.refs_1_, s32[4,32]{1,0:T(4,128)S(1)} %collective-permute-done.9.refs_3_.refs_2_, ...), custom_call_target="tpu_custom_call" | custom-call | tf_op jit(solution)/shard_map/pack_history/pallas_call | solution.py:117
  12.0 2.0 %collective-permute-start.11 = (bf16[16,64,256]{2,1,0:T(8,128)(2,1)S(1)}, bf16[16,64,256]{2,1,0:T(8,128)(2,1)S(1)}, u32[]{:S(2)}, u32[]{:S(2)}) collective-permute-start(bf16[16,64,256]{2,1,0:T(8,128)(2,1)S(1)} %get-tuple-element.62), channel_id=1, source_target_pairs={{0,16},{8,24},{16,0},{24,8},{1,17},{9,25},{17,1},{25,9},{2,18},{10... | collective-permute-start | bytes 1572872 | tf_op jit(solution)/shard_map/ppermute | solution.py:423
  14.0 1.4 %collective-permute-start.12 = (bf16[16,64,256]{2,1,0:T(8,128)(2,1)S(1)}, bf16[16,64,256]{2,1,0:T(8,128)(2,1)S(1)}, u32[]{:S(2)}, u32[]{:S(2)}) collective-permute-start(bf16[16,64,256]{2,1,0:T(8,128)(2,1)S(1)} %get-tuple-element.63), channel_id=1, source_target_pairs={{0,24},{8,16},{16,8},{24,0},{1,25},{9,17},{17,9},{25,1},{2,26},{10... | collective-permute-start | bytes 1572872 | tf_op jit(solution)/shard_map/ppermute | solution.py:423
  15.5 11.4 %collective-permute-done.10.refs_0_.refs_4_ = bf16[16,64,256]{2,1,0:T(8,128)(2,1)S(1)} collective-permute-done((bf16[16,64,256]{2,1,0:T(8,128)(2,1)S(1)}, bf16[16,64,256]{2,1,0:T(8,128)(2,1)S(1)}, u32[]{:S(2)}, u32[]{:S(2)}) %collective-permute-start.10) | collective-permute-done | bytes 524320 | tf_op jit(solution)/shard_map/ppermute | solution.py:423
  26.8 1.7 %pack_history.3 = (bf16[16,64,256]{2,1,0:T(8,128)(2,1)S(1)}, bf16[16,64,256]{2,1,0:T(8,128)(2,1)S(1)}, bf16[16,64,256]{2,1,0:T(8,128)(2,1)S(1)}) custom-call(s32[4,32]{1,0:T(4,128)S(1)} %collective-permute-done.7.refs_1_.refs_0_, s32[4,32]{1,0:T(4,128)S(1)} %collective-permute-done.8.refs_2_.refs_1_, s32[4,32]{1,0:T(4,128)S(1)} %collective-permute-done.9.refs_3_.refs_2_, ...), custom_call_target="tpu_custom_call" | custom-call | tf_op jit(solution)/shard_map/pack_history/pallas_call | solution.py:117
  28.7 2.0 %collective-permute-start.19 = (bf16[16,64,256]{2,1,0:T(8,128)(2,1)S(1)}, bf16[16,64,256]{2,1,0:T(8,128)(2,1)S(1)}, u32[]{:S(2)}, u32[]{:S(2)}) collective-permute-start(bf16[16,64,256]{2,1,0:T(8,128)(2,1)S(1)} %get-tuple-element.75), channel_id=1, source_target_pairs={{0,16},{8,24},{16,0},{24,8},{1,17},{9,25},{17,1},{25,9},{2,18},{10... | collective-permute-start | bytes 1572872 | tf_op jit(solution)/shard_map/ppermute | solution.py:423
  30.7 1.4 %collective-permute-start.20 = (bf16[16,64,256]{2,1,0:T(8,128)(2,1)S(1)}, bf16[16,64,256]{2,1,0:T(8,128)(2,1)S(1)}, u32[]{:S(2)}, u32[]{:S(2)}) collective-permute-start(bf16[16,64,256]{2,1,0:T(8,128)(2,1)S(1)} %get-tuple-element.76), channel_id=1, source_target_pairs={{0,24},{8,16},{16,8},{24,0},{1,25},{9,17},{17,9},{25,1},{2,26},{10... | collective-permute-start | bytes 1572872 | tf_op jit(solution)/shard_map/ppermute | solution.py:423
  32.1 4.1 %plan_tiles.1 = (s32[5,48]{1,0:T(8,128)S(1)}, bf16[48,256,256]{2,1,0:T(8,128)(2,1)S(1)}) custom-call(s32[1,1,4,12]{3,2,1,0:T(4,128)S(1)} %copy-done.1, s32[1,1,4,12]{3,2,1,0:T(4,128)S(1)} %copy-done.3, s32[1,1,4]{2,1,0:T(1,128)S(1)} %copy-done.4, s32[4,32]{1,0:T(4,128)S(1)} %copy-done.2, s32[4,32]{1,0:T(4,128)S(1)} %collective-permute-done.7.refs_1_.refs_0_, ...), custom_call_target="tpu_custom_call" | custom-call | tf_op jit(solution)/shard_map/plan_tiles/pallas_call | solution.py:187
  36.3 2.8 %collective-permute-done.12.refs_2_ = bf16[16,64,256]{2,1,0:T(8,128)(2,1)S(1)} collective-permute-done((bf16[16,64,256]{2,1,0:T(8,128)(2,1)S(1)}, bf16[16,64,256]{2,1,0:T(8,128)(2,1)S(1)}, u32[]{:S(2)}, u32[]{:S(2)}) %collective-permute-start.12) | collective-permute-done | bytes 524320 | tf_op jit(solution)/shard_map/ppermute | solution.py:423
  39.1 4.1 %multiply_tiles.4 = (f32[32,64,256]{2,1,0:T(8,128)S(1)}, s16[528,256]{1,0:T(8,128)(2,1)S(1)}, s16[528,256]{1,0:T(8,128)(2,1)S(1)}) custom-call(s32[5,48]{1,0:T(8,128)S(1)} %get-tuple-element.59.table.refs_0_, bf16[48,256,256]{2,1,0:T(8,128)(2,1)S(1)} %get-tuple-element.60.tiles, bf16[4,128,2048]{2,1,0:T(8,128)(2,1)S(1)} %load_history.1.refs_3_.history, ...), custom_call_target="tpu_custom_call" | custom-call | tf_op jit(solution)/shard_map/multiply_tiles/pallas_call | solution.py:259
  43.2 0.5 collective-permute-start.13
  43.7 1.0 %collective-permute-done.14.refs_1_ = s16[528,256]{1,0:T(8,128)(2,1)S(1)} collective-permute-done((s16[528,256]{1,0:T(8,128)(2,1)S(1)}, s16[528,256]{1,0:T(8,128)(2,1)S(1)}, u32[]{:S(2)}, u32[]{:S(2)}) %collective-permute-start.14) | collective-permute-done | bytes 270368 | tf_op jit(solution)/shard_map/ppermute | solution.py:392
  44.8 0.4 collective-permute-done.13.refs_0_
  45.2 0.4 add_and_code.4
  45.5 1.1 %collective-permute-start.15 = (s16[528,128]{1,0:T(8,128)(2,1)S(1)}, s16[528,128]{1,0:T(8,128)(2,1)S(1)}, u32[]{:S(2)}, u32[]{:S(2)}) collective-permute-start(s16[528,128]{1,0:T(8,128)(2,1)S(1)} %get-tuple-element.68), channel_id=1, source_target_pairs={{0,4},{2,6},{4,0},{6,2},{1,5},{3,7},{5,1},{7,3},{8,12},{10,14},{12... | collective-permute-start | bytes 405512 | tf_op jit(solution)/shard_map/ppermute | solution.py:395
  46.7 1.8 %collective-permute-start.16 = (s16[528,128]{1,0:T(8,128)(2,1)S(1)}, s16[528,128]{1,0:T(8,128)(2,1)S(1)}, u32[]{:S(2)}, u32[]{:S(2)}) collective-permute-start(s16[528,128]{1,0:T(8,128)(2,1)S(1)} %get-tuple-element.69), channel_id=1, source_target_pairs={{0,6},{2,4},{4,2},{6,0},{1,7},{3,5},{5,3},{7,1},{8,14},{10,12},{12... | collective-permute-start | bytes 405512 | tf_op jit(solution)/shard_map/ppermute | solution.py:395
  48.5 9.5 %collective-permute-done.15.refs_6_.refs_3_ = s16[528,128]{1,0:T(8,128)(2,1)S(1)} collective-permute-done((s16[528,128]{1,0:T(8,128)(2,1)S(1)}, s16[528,128]{1,0:T(8,128)(2,1)S(1)}, u32[]{:S(2)}, u32[]{:S(2)}) %collective-permute-start.15) | collective-permute-done | bytes 135200 | tf_op jit(solution)/shard_map/ppermute | solution.py:395
  58.0 0.6 collective-permute-done.20.refs_2_
  58.6 4.1 %multiply_tiles.5 = (f32[32,64,256]{2,1,0:T(8,128)S(1)}, s16[1056,256]{1,0:T(8,128)(2,1)S(1)}) custom-call(s32[5,48]{1,0:T(8,128)S(1)} %get-tuple-element.59.table.refs_0_, bf16[48,256,256]{2,1,0:T(8,128)(2,1)S(1)} %get-tuple-element.60.tiles, bf16[4,128,2048]{2,1,0:T(8,128)(2,1)S(1)} %load_history.1.refs_3_.history, ...), custom_call_target="tpu_custom_call" | custom-call | tf_op jit(solution)/shard_map/multiply_tiles/pallas_call | solution.py:259
  62.9 2.3 %collective-permute-start.17 = (s16[528,128]{1,0:T(8,128)(2,1)S(1)}, s16[528,128]{1,0:T(8,128)(2,1)S(1)}, u32[]{:S(2)}, u32[]{:S(2)}) collective-permute-start(s16[528,128]{1,0:T(8,128)(2,1)S(1)} %get-tuple-element.70), channel_id=1, source_target_pairs={{0,2},{2,0},{4,6},{6,4},{1,3},{3,1},{5,7},{7,5},{8,10},{10,8},{12,... | collective-permute-start | bytes 405512 | tf_op jit(solution)/shard_map/ppermute | solution.py:395
  65.1 0.4 add_and_code.5
  65.5 1.6 %collective-permute-start.22 = (s16[528,128]{1,0:T(8,128)(2,1)S(1)}, s16[528,128]{1,0:T(8,128)(2,1)S(1)}, u32[]{:S(2)}, u32[]{:S(2)}) collective-permute-start(s16[528,128]{1,0:T(8,128)(2,1)S(1)} %get-tuple-element.80), channel_id=1, source_target_pairs={{0,4},{2,6},{4,0},{6,2},{1,5},{3,7},{5,1},{7,3},{8,12},{10,14},{12... | collective-permute-start | bytes 405512 | tf_op jit(solution)/shard_map/ppermute | solution.py:395
  67.2 2.4 %collective-permute-start.23 = (s16[528,128]{1,0:T(8,128)(2,1)S(1)}, s16[528,128]{1,0:T(8,128)(2,1)S(1)}, u32[]{:S(2)}, u32[]{:S(2)}) collective-permute-start(s16[528,128]{1,0:T(8,128)(2,1)S(1)} %get-tuple-element.81), channel_id=1, source_target_pairs={{0,6},{2,4},{4,2},{6,0},{1,7},{3,5},{5,3},{7,1},{8,14},{10,12},{12... | collective-permute-start | bytes 405512 | tf_op jit(solution)/shard_map/ppermute | solution.py:395
  69.6 2.8 %friction_solve.4 = (s32[1]{0:T(128)}, f32[128,1024]{1,0:T(8,128)}, f32[128,1024]{1,0:T(8,128)}) custom-call(s32[5,48]{1,0:T(8,128)S(1)} %get-tuple-element.59.table.refs_0_, f32[128,1024]{1,0:T(8,128)S(1)} %copy-done.7, f32[128,1024]{1,0:T(8,128)S(1)} %copy-done.8, f32[128,1024]{1,0:T(8,128)S(1)} %copy-done.9, f32[128,1024]{1,0:T(8,128)S(1)} %copy-done.12, ...), custom_call_target="tpu_custom_call" | custom-call | tf_op jit(solution)/shard_map/friction_solve/pallas_call | solution.py:376
  73.2 5.6 %collective-permute-done.22.refs_7_ = s16[528,128]{1,0:T(8,128)(2,1)S(1)} collective-permute-done((s16[528,128]{1,0:T(8,128)(2,1)S(1)}, s16[528,128]{1,0:T(8,128)(2,1)S(1)}, u32[]{:S(2)}, u32[]{:S(2)}) %collective-permute-start.22) | collective-permute-done | bytes 135200 | tf_op jit(solution)/shard_map/ppermute | solution.py:395
  79.0 1.7 %friction_solve.5 = (f32[128,1024]{1,0:T(8,128)}, f32[128,1024]{1,0:T(8,128)}) custom-call(f32[128,1024]{1,0:T(8,128)} %get-tuple-element.72.refs_0_, f32[128,1024]{1,0:T(8,128)} %get-tuple-element.73.refs_1_, f32[128,1024]{1,0:T(8,128)S(1)} %copy-done.7, f32[128,1024]{1,0:T(8,128)S(1)} %copy-done.8, ...), custom_call_target="tpu_custom_call", output_to_operand_aliasing={{0}: (0, {}), {1}: (1, {})} | custom-call | tf_op jit(solution)/shard_map/friction_solve/pallas_call | solution.py:376
  (36 shorter events, 1.0 us)
Async XLA Ops:
  2.0 6.3 %collective-permute-start.9 = (s32[4,32]{1,0:T(4,128)}, s32[4,32]{1,0:T(4,128)S(1)}, u32[]{:S(2)}, u32[]{:S(2)}) collective-permute-start(s32[4,32]{1,0:T(4,128)} %mark_blocks.1.refs_0_), channel_id=1, source_target_pairs={{0,24},{8,16},{16,8},{24,0},{1,25},{9,17},{17,9},{25,1},{2,26},{10... | collective-permute-start | bytes 1544 | tf_op jit(solution)/shard_map/ppermute | solution.py:417
  5.9 3.8 %collective-permute-start.8 = (s32[4,32]{1,0:T(4,128)}, s32[4,32]{1,0:T(4,128)S(1)}, u32[]{:S(2)}, u32[]{:S(2)}) collective-permute-start(s32[4,32]{1,0:T(4,128)} %mark_blocks.1.refs_0_), channel_id=1, source_target_pairs={{0,16},{8,24},{16,0},{24,8},{1,17},{9,25},{17,1},{25,9},{2,18},{10... | collective-permute-start | bytes 1544 | tf_op jit(solution)/shard_map/ppermute | solution.py:417
  6.4 3.8 %collective-permute-start.7 = (s32[4,32]{1,0:T(4,128)}, s32[4,32]{1,0:T(4,128)S(1)}, u32[]{:S(2)}, u32[]{:S(2)}) collective-permute-start(s32[4,32]{1,0:T(4,128)} %mark_blocks.1.refs_0_), channel_id=1, source_target_pairs={{0,8},{8,0},{16,24},{24,16},{1,9},{9,1},{17,25},{25,17},{2,10},{10... | collective-permute-start | bytes 1544 | tf_op jit(solution)/shard_map/ppermute | solution.py:417
  6.4 25.7 %copy-start = (bf16[1,1,4,12,256,256]{5,4,3,2,1,0:T(8,128)(2,1)S(1)}, bf16[1,1,4,12,256,256]{5,4,3,2,1,0:T(8,128)(2,1)}, u32[]{:S(2)}) copy-start(bf16[1,1,4,12,256,256]{5,4,3,2,1,0:T(8,128)(2,1)} %param.12) | copy-start | bytes 18874372
  8.2 23.9 %copy-start.1 = (s32[1,1,4,12]{3,2,1,0:T(4,128)S(1)}, s32[1,1,4,12]{3,2,1,0:T(4,128)}, u32[]{:S(2)}) copy-start(s32[1,1,4,12]{3,2,1,0:T(4,128)} %cols.3) | copy-start | bytes 580
  8.2 23.9 %copy-start.2 = (s32[4,32]{1,0:T(4,128)S(1)}, s32[4,32]{1,0:T(4,128)}, u32[]{:S(2)}) copy-start(s32[4,32]{1,0:T(4,128)} %mark_blocks.1.refs_0_) | copy-start | bytes 1540
  8.2 23.9 %copy-start.3 = (s32[1,1,4,12]{3,2,1,0:T(4,128)S(1)}, s32[1,1,4,12]{3,2,1,0:T(4,128)}, u32[]{:S(2)}) copy-start(s32[1,1,4,12]{3,2,1,0:T(4,128)} %rows.1) | copy-start | bytes 580
  8.2 23.9 %copy-start.4 = (s32[1,1,4]{2,1,0:T(1,128)S(1)}, s32[1,1,4]{2,1,0:T(1,128)}, u32[]{:S(2)}) copy-start(s32[1,1,4]{2,1,0:T(1,128)} %counts.3) | copy-start | bytes 52
  11.9 14.9 %collective-permute-start.10 = (bf16[16,64,256]{2,1,0:T(8,128)(2,1)S(1)}, bf16[16,64,256]{2,1,0:T(8,128)(2,1)S(1)}, u32[]{:S(2)}, u32[]{:S(2)}) collective-permute-start(bf16[16,64,256]{2,1,0:T(8,128)(2,1)S(1)} %get-tuple-element.61), channel_id=1, source_target_pairs={{0,8},{8,0},{16,24},{24,16},{1,9},{9,1},{17,25},{25,17},{2,10},{10... | collective-permute-start | bytes 1572872 | tf_op jit(solution)/shard_map/ppermute | solution.py:423
  12.0 24.2 %collective-permute-start.11 = (bf16[16,64,256]{2,1,0:T(8,128)(2,1)S(1)}, bf16[16,64,256]{2,1,0:T(8,128)(2,1)S(1)}, u32[]{:S(2)}, u32[]{:S(2)}) collective-permute-start(bf16[16,64,256]{2,1,0:T(8,128)(2,1)S(1)} %get-tuple-element.62), channel_id=1, source_target_pairs={{0,16},{8,24},{16,0},{24,8},{1,17},{9,25},{17,1},{25,9},{2,18},{10... | collective-permute-start | bytes 1572872 | tf_op jit(solution)/shard_map/ppermute | solution.py:423
  14.0 25.0 %collective-permute-start.12 = (bf16[16,64,256]{2,1,0:T(8,128)(2,1)S(1)}, bf16[16,64,256]{2,1,0:T(8,128)(2,1)S(1)}, u32[]{:S(2)}, u32[]{:S(2)}) collective-permute-start(bf16[16,64,256]{2,1,0:T(8,128)(2,1)S(1)} %get-tuple-element.63), channel_id=1, source_target_pairs={{0,24},{8,16},{16,8},{24,0},{1,25},{9,17},{17,9},{25,1},{2,26},{10... | collective-permute-start | bytes 1572872 | tf_op jit(solution)/shard_map/ppermute | solution.py:423
  28.6 29.4 %collective-permute-start.18 = (bf16[16,64,256]{2,1,0:T(8,128)(2,1)S(1)}, bf16[16,64,256]{2,1,0:T(8,128)(2,1)S(1)}, u32[]{:S(2)}, u32[]{:S(2)}) collective-permute-start(bf16[16,64,256]{2,1,0:T(8,128)(2,1)S(1)} %get-tuple-element.74), channel_id=1, source_target_pairs={{0,8},{8,0},{16,24},{24,16},{1,9},{9,1},{17,25},{25,17},{2,10},{10... | collective-permute-start | bytes 1572872 | tf_op jit(solution)/shard_map/ppermute | solution.py:423
  28.7 29.3 %collective-permute-start.19 = (bf16[16,64,256]{2,1,0:T(8,128)(2,1)S(1)}, bf16[16,64,256]{2,1,0:T(8,128)(2,1)S(1)}, u32[]{:S(2)}, u32[]{:S(2)}) collective-permute-start(bf16[16,64,256]{2,1,0:T(8,128)(2,1)S(1)} %get-tuple-element.75), channel_id=1, source_target_pairs={{0,16},{8,24},{16,0},{24,8},{1,17},{9,25},{17,1},{25,9},{2,18},{10... | collective-permute-start | bytes 1572872 | tf_op jit(solution)/shard_map/ppermute | solution.py:423
  30.7 27.9 %collective-permute-start.20 = (bf16[16,64,256]{2,1,0:T(8,128)(2,1)S(1)}, bf16[16,64,256]{2,1,0:T(8,128)(2,1)S(1)}, u32[]{:S(2)}, u32[]{:S(2)}) collective-permute-start(bf16[16,64,256]{2,1,0:T(8,128)(2,1)S(1)} %get-tuple-element.76), channel_id=1, source_target_pairs={{0,24},{8,16},{16,8},{24,0},{1,25},{9,17},{17,9},{25,1},{2,26},{10... | collective-permute-start | bytes 1572872 | tf_op jit(solution)/shard_map/ppermute | solution.py:423
  43.2 1.6 %collective-permute-start.14 = (s16[528,256]{1,0:T(8,128)(2,1)S(1)}, s16[528,256]{1,0:T(8,128)(2,1)S(1)}, u32[]{:S(2)}, u32[]{:S(2)}) collective-permute-start(s16[528,256]{1,0:T(8,128)(2,1)S(1)} %get-tuple-element.66), channel_id=1, source_target_pairs={{0,1},{1,0},{2,3},{3,2},{4,5},{5,4},{6,7},{7,6},{8,9},{9,8},{10,11... | collective-permute-start | bytes 811016 | tf_op jit(solution)/shard_map/ppermute | solution.py:392
  43.2 1.9 %collective-permute-start.13 = (s16[528,256]{1,0:T(8,128)(2,1)S(1)}, s16[528,256]{1,0:T(8,128)(2,1)S(1)}, u32[]{:S(2)}, u32[]{:S(2)}) collective-permute-start(s16[528,256]{1,0:T(8,128)(2,1)S(1)} %get-tuple-element.64.given), channel_id=1, source_target_pairs={{0,1},{1,0},{2,3},{3,2},{4,5},{5,4},{6,7},{7,6},{8,9},{9,8},{10,11... | collective-permute-start | bytes 811016 | tf_op jit(solution)/shard_map/ppermute | solution.py:392
  45.5 12.4 %collective-permute-start.15 = (s16[528,128]{1,0:T(8,128)(2,1)S(1)}, s16[528,128]{1,0:T(8,128)(2,1)S(1)}, u32[]{:S(2)}, u32[]{:S(2)}) collective-permute-start(s16[528,128]{1,0:T(8,128)(2,1)S(1)} %get-tuple-element.68), channel_id=1, source_target_pairs={{0,4},{2,6},{4,0},{6,2},{1,5},{3,7},{5,1},{7,3},{8,12},{10,14},{12... | collective-permute-start | bytes 405512 | tf_op jit(solution)/shard_map/ppermute | solution.py:395
  46.7 11.3 %collective-permute-start.16 = (s16[528,128]{1,0:T(8,128)(2,1)S(1)}, s16[528,128]{1,0:T(8,128)(2,1)S(1)}, u32[]{:S(2)}, u32[]{:S(2)}) collective-permute-start(s16[528,128]{1,0:T(8,128)(2,1)S(1)} %get-tuple-element.69), channel_id=1, source_target_pairs={{0,6},{2,4},{4,2},{6,0},{1,7},{3,5},{5,3},{7,1},{8,14},{10,12},{12... | collective-permute-start | bytes 405512 | tf_op jit(solution)/shard_map/ppermute | solution.py:395
  62.7 6.8 %copy-start.7 = (f32[128,1024]{1,0:T(8,128)S(1)}, f32[128,1024]{1,0:T(8,128)}, u32[]{:S(2)}) copy-start(f32[128,1024]{1,0:T(8,128)} %refs_2_.3) | copy-start | bytes 1572868
  62.7 6.8 %copy-start.8 = (f32[128,1024]{1,0:T(8,128)S(1)}, f32[128,1024]{1,0:T(8,128)}, u32[]{:S(2)}) copy-start(f32[128,1024]{1,0:T(8,128)} %refs_3_.3) | copy-start | bytes 1572868
  62.7 6.8 %copy-start.9 = (f32[128,1024]{1,0:T(8,128)S(1)}, f32[128,1024]{1,0:T(8,128)}, u32[]{:S(2)}) copy-start(f32[128,1024]{1,0:T(8,128)} %refs_4_.3) | copy-start | bytes 1572868
  62.8 6.8 %copy-start.12 = (f32[128,1024]{1,0:T(8,128)S(1)}, f32[128,1024]{1,0:T(8,128)}, u32[]{:S(2)}) copy-start(f32[128,1024]{1,0:T(8,128)} %refs_5_.1) | copy-start | bytes 1572868
  62.8 2.4 %collective-permute-start.21 = (s16[1056,256]{1,0:T(8,128)(2,1)S(1)}, s16[1056,256]{1,0:T(8,128)(2,1)S(1)}, u32[]{:S(2)}, u32[]{:S(2)}) collective-permute-start(s16[1056,256]{1,0:T(8,128)(2,1)S(1)} %get-tuple-element.77.given), channel_id=1, source_target_pairs={{0,1},{1,0},{2,3},{3,2},{4,5},{5,4},{6,7},{7,6},{8,9},{9,8},{10,11... | collective-permute-start | bytes 1622024 | tf_op jit(solution)/shard_map/ppermute | solution.py:392
  62.9 6.7 %collective-permute-start.17 = (s16[528,128]{1,0:T(8,128)(2,1)S(1)}, s16[528,128]{1,0:T(8,128)(2,1)S(1)}, u32[]{:S(2)}, u32[]{:S(2)}) collective-permute-start(s16[528,128]{1,0:T(8,128)(2,1)S(1)} %get-tuple-element.70), channel_id=1, source_target_pairs={{0,2},{2,0},{4,6},{6,4},{1,3},{3,1},{5,7},{7,5},{8,10},{10,8},{12,... | collective-permute-start | bytes 405512 | tf_op jit(solution)/shard_map/ppermute | solution.py:395
  65.5 13.3 %collective-permute-start.22 = (s16[528,128]{1,0:T(8,128)(2,1)S(1)}, s16[528,128]{1,0:T(8,128)(2,1)S(1)}, u32[]{:S(2)}, u32[]{:S(2)}) collective-permute-start(s16[528,128]{1,0:T(8,128)(2,1)S(1)} %get-tuple-element.80), channel_id=1, source_target_pairs={{0,4},{2,6},{4,0},{6,2},{1,5},{3,7},{5,1},{7,3},{8,12},{10,14},{12... | collective-permute-start | bytes 405512 | tf_op jit(solution)/shard_map/ppermute | solution.py:395
  67.2 11.7 %collective-permute-start.23 = (s16[528,128]{1,0:T(8,128)(2,1)S(1)}, s16[528,128]{1,0:T(8,128)(2,1)S(1)}, u32[]{:S(2)}, u32[]{:S(2)}) collective-permute-start(s16[528,128]{1,0:T(8,128)(2,1)S(1)} %get-tuple-element.81), channel_id=1, source_target_pairs={{0,6},{2,4},{4,2},{6,0},{1,7},{3,5},{5,3},{7,1},{8,14},{10,12},{12... | collective-permute-start | bytes 405512 | tf_op jit(solution)/shard_map/ppermute | solution.py:395
  69.5 9.4 %collective-permute-start.24 = (s16[528,128]{1,0:T(8,128)(2,1)S(1)}, s16[528,128]{1,0:T(8,128)(2,1)S(1)}, u32[]{:S(2)}, u32[]{:S(2)}) collective-permute-start(s16[528,128]{1,0:T(8,128)(2,1)S(1)} %get-tuple-element.82), channel_id=1, source_target_pairs={{0,2},{2,0},{4,6},{6,4},{1,3},{3,1},{5,7},{7,5},{8,10},{10,8},{12,... | collective-permute-start | bytes 405512 | tf_op jit(solution)/shard_map/ppermute | solution.py:395
  72.4 8.3 %copy-start.6 = (bf16[4,1,128,2048]{3,2,1,0:T(8,128)(2,1)S(1)}, bf16[4,1,128,2048]{3,2,1,0:T(8,128)(2,1)}, u32[]{:S(2)}) copy-start(bf16[4,1,128,2048]{3,2,1,0:T(8,128)(2,1)} %param.11) | copy-start | bytes 6291460

commit v7 on v6

--- a/solution.py
+++ b/solution.py
@@ -15,7 +15,6 @@
 LANES = 128
 OVER = 16
 SPLIT = 2
-WAIT = 1
 GROUP = 8
 ANY = pl.BlockSpec(memory_space=pl.ANY)
 SMEM = pl.BlockSpec(memory_space=pltpu.SMEM)
@@ -198,45 +197,59 @@
     )(cols, rows, counts, *needs, tiles)
 
 
-def tiles_kernel(first, whole, extra, split, table, tiles, history, *refs):
-    received, (sums, *given), blocks = refs[: len(refs) - 2 - split - extra], refs[-2 - split : -1], refs[-1]
-    side = tiles.shape[2]
-    halves, part, _ = sums.shape
-    live = table[4, len(received) + 1]
-    sums[...] = jnp.zeros_like(sums)
-
-    def fetch(source):
-        def one(index, carry):
-            lanes = pl.ds(pl.multiple_of(table[2, index] * side, side), side)
-            if source == 0:
-                blocks[index] = history[table[0, index], pl.ds(first, part), lanes]
-            elif whole:
-                blocks[index] = received[source - 1][table[0, index], pl.ds(first, part), lanes]
-            else:
-                blocks[index] = received[source - 1][table[3, index]]
-            return carry
-
-        return one
-
-    for source in range(len(received) + 1):
-        lax.fori_loop(table[4, source], table[4, source + 1], fetch(source), 0)
-
+def add_products(begin, end, table, tiles, blocks, sums):
     def multiply(group, carry):
         products = []
         for offset in range(GROUP):
-            index = jnp.minimum(group * GROUP + offset, live - 1)
+            index = jnp.minimum(begin + group * GROUP + offset, end - 1)
             products.append(
                 lax.dot_general(
                     blocks[index], tiles[index], (((1,), (1,)), ((), ())), preferred_element_type=jnp.float32
                 )
             )
         for offset, product in enumerate(products):
-            index = group * GROUP + offset
-            spot = table[1, jnp.minimum(index, live - 1)]
-            sums[spot] += product if offset == 0 else jnp.where(index < live, product, 0.0)
+            index = begin + group * GROUP + offset
+            spot = table[1, jnp.minimum(index, end - 1)]
+            sums[spot] += product if offset == 0 else jnp.where(index < end, product, 0.0)
         return carry
 
-    lax.fori_loop(0, (live + GROUP - 1) // GROUP, multiply, 0)
+    lax.fori_loop(0, (end - begin + GROUP - 1) // GROUP, multiply, 0)
+
+
+def own_kernel(first, table, tiles, history, sums, blocks):
+    side = tiles.shape[2]
+    part = sums.shape[1]
+    sums[...] = jnp.zeros_like(sums)
+
+    def fetch(index, carry):
+        lanes = pl.ds(pl.multiple_of(table[2, index] * side, side), side)
+        blocks[index] = history[table[0, index], pl.ds(first, part), lanes]
+        return carry
+
+    lax.fori_loop(0, table[4, 1], fetch, 0)
+    add_products(0, table[4, 1], table, tiles, blocks, sums)
+
+
+def tiles_kernel(first, whole, extra, split, table, tiles, begun, *refs):
+    received, (sums, *given), blocks = refs[: len(refs) - 2 - split - extra], refs[-2 - split : -1], refs[-1]
+    side = tiles.shape[2]
+    halves, part, _ = sums.shape
+    sums[...] = begun[...]
+
+    def fetch(source):
+        def one(index, carry):
+            if whole:
+                lanes = pl.ds(pl.multiple_of(table[2, index] * side, side), side)
+                blocks[index] = received[source - 1][table[0, index], pl.ds(first, part), lanes]
+            else:
+                blocks[index] = received[source - 1][table[3, index]]
+            return carry
+
+        return one
+
+    for source in range(1, len(received) + 1):
+        lax.fori_loop(table[4, source], table[4, source + 1], fetch(source), 0)
+    add_products(table[4, 1], table[4, len(received) + 1], table, tiles, blocks, sums)
     half = halves // 2
     size = half // split
     flag = jnp.full((1, side), 1.0, jnp.float32) * table[4, OVER].astype(jnp.float32)
@@ -251,20 +264,36 @@
         target[size * part :] = tail.astype(jnp.int32).astype(jnp.int16)
 
 
-def multiply_tiles(first, part, whole, split, table, tiles, history, received, chunks, after):
+def multiply_own(first, part, table, tiles, history, chunks):
     side = tiles.shape[2]
-    more = [jax.ShapeDtypeStruct((chunks // split * part + padded(chunks // split), side), jnp.int16)] * split
     blocks = pltpu.VMEM((table.shape[1], part, side), history.dtype)
     sums = jax.ShapeDtypeStruct((2 * chunks, part, side), jnp.float32)
+    return pl.pallas_call(
+        functools.partial(own_kernel, first),
+        out_shape=sums,
+        in_specs=[SMEM, VMEM, VMEM],
+        out_specs=VMEM,
+        scratch_shapes=[blocks],
+        compiler_params=params(tiles, history, blocks, sums),
+        name="multiply_own",
+    )(table, tiles, history)
+
+
+def multiply_tiles(first, whole, split, table, tiles, begun, received, after):
+    halves, part, side = begun.shape
+    chunks = halves // 2
+    more = [jax.ShapeDtypeStruct((chunks // split * part + padded(chunks // split), side), jnp.int16)] * split
+    blocks = pltpu.VMEM((table.shape[1], part, side), tiles.dtype)
+    sums = jax.ShapeDtypeStruct(begun.shape, jnp.float32)
     return pl.pallas_call(
         functools.partial(tiles_kernel, first, whole, len(after), split),
         out_shape=[sums, *more],
         in_specs=[SMEM] + [VMEM] * (2 + len(received)) + [ANY] * len(after),
         out_specs=[VMEM] * (1 + split),
         scratch_shapes=[blocks],
-        compiler_params=params(tiles, history, *received, *more, blocks, sums),
+        compiler_params=params(tiles, begun, *received, *more, blocks, sums),
         name="multiply_tiles",
-    )(table, tiles, history, *received, *after)
+    )(table, tiles, begun, *received, *after)
 
 
 def to_fixed(value):
@@ -416,29 +445,33 @@
     need = make_request(tile_cols, tile_count, total)
     requests = [lax.ppermute(need, "row", partners(row_size, step)) for step in range(1, row_size)]
     held = load(history)
+    table, live_tiles = make_plan(
+        tile_cols, tile_rows, tile_count, [need, *requests], tiles, cap, col_size, per_owner
+    )
+
+    begun = [multiply_own(first, part, table, live_tiles, held, chunks) for first, part in pieces]
     received = []
     for piece in pieces:
-        packed = pack(requests, held, side, cap, piece, received[-1][:WAIT] if received else ())
+        after = (received[-1][0], *begun) if received else ()
+        packed = pack(requests, held, side, cap, piece, after)
         received.append(
             [lax.ppermute(packed[step - 1], "row", partners(row_size, step)) for step in range(1, row_size)]
         )
-    table, live_tiles = make_plan(
-        tile_cols, tile_rows, tile_count, [need, *requests], tiles, cap, col_size, per_owner
-    )
 
     after = ()
     flags = result = None
-    for (first, part), blocks in zip(pieces, received):
+    for (first, part), blocks, own in zip(pieces, received, begun):
         kept, *given = multiply_tiles(
-            first, part, False, 1 if first + part == sims else SPLIT, table, live_tiles, held, blocks, chunks, after
+            first, False, 1 if first + part == sims else SPLIT, table, live_tiles, own, blocks, after
         )
         (flag, result), after, _ = reduce(first, table, fields, kept, given, result)
         flags = flags or flag
 
     def general():
         everything = [lax.ppermute(history, "row", partners(row_size, step)) for step in range(1, row_size)]
+        own = multiply_own(0, sims, table, live_tiles, history, chunks)
         kept, *given = multiply_tiles(
-            0, sims, True, 1, table, live_tiles, history, everything, chunks, ()
+            0, True, 1, table, live_tiles, own, everything, ()
         )
         return tuple(reduce(0, table, fields, kept, given, None)[0][1])
 

time: 81.4 us -> 80.3 us (0.986)
  Pallas kernels: 24.1 us -> 22.3 us
  starting transfers between devices: 21.5 us -> 22.9 us
  waiting for transfers between devices: 33.4 us -> 32.2 us
    pallas_call x2, Pallas kernels: 8.17 us -> 4.97 us  [multiply_tiles(): pl.pallas_call(functools.partial(tiles_kernel, first, whole, len(after),...]
    pallas_call x0 -> x2, Pallas kernels: none -> 2.53 us  [multiply_own(): pl.pallas_call(functools.partial(own_kernel, first), out_shape=sums, in_s...]
    ppermute x6, starting transfers between devices: 9.26 us -> 10.7 us  [reduce(): lax.ppermute(coded[step - 1], 'col', partners(col_size, step))]
    pallas_call x1, Pallas kernels: 4.12 us -> 3.04 us  [make_plan(): pl.pallas_call(functools.partial(plan_kernel, cap, col_size, per_owner),...]
    ppermute x6, waiting for transfers between devices: 15.3 us -> 14.4 us  [reduce(): lax.ppermute(coded[step - 1], 'col', partners(col_size, step))]
  transfers between devices with their start and end apart: 18 -> 18, of which waited for: 10 -> 13; matrix products, arithmetic and copies ran while one was open for 0% -> 0% of each run, Pallas kernels for 19% -> 19%
where the time goes in v7:
time: 80.3 us; the launch traced here: 79.6 us
  waiting for transfers between devices  32.2 us (40%)
  starting transfers between devices  22.9 us (29%)
  Pallas kernels  22.3 us (28%)
  between operations  1.87 us (2%)
    ppermute x6, waiting for transfers between devices, reduce(): lax.ppermute(coded[step - 1], 'col', partners(col_size, step))  14.4 us
    ppermute x6, waiting for transfers between devices, local(): lax.ppermute(packed[step - 1], 'row', partners(row_size, step))  14.2 us
    ppermute x6, starting transfers between devices, reduce(): lax.ppermute(coded[step - 1], 'col', partners(col_size, step))  10.7 us
    ppermute x6, starting transfers between devices, local(): lax.ppermute(packed[step - 1], 'row', partners(row_size, step))  7.11 us
    pallas_call x2, Pallas kernels, multiply_tiles(): pl.pallas_call(functools.partial(tiles_kernel, first, whole, len(after),...  4.97 us
    pallas_call x2, Pallas kernels, solve(): pl.pallas_call(functools.partial(solve_kernel, first, fresh), out_shape=f...  4.48 us
    ppermute x3, starting transfers between devices, local(): lax.ppermute(need, 'row', partners(row_size, step))  4.46 us
    pallas_call x2, Pallas kernels, pack(): pl.pallas_call(functools.partial(pack_kernel, cap, piece, side, len(after...  3.49 us
  transfers between devices with their start and end apart: 18, of which 13 were waited for; matrix products, arithmetic and copies ran while one was open for 0% of the time, Pallas kernels for 19%

profile of v7, /device:TPU:0, one launch (start us, length us, event | category | flops | bytes accessed | tf_op | source)
XLA Modules:
  0.0 79.6 jit_solution(5603126215330846724)
XLA Ops:
  0.6 1.3 %mark_blocks.1.refs_0_ = s32[4,32]{1,0:T(4,128)} custom-call(s32[1,1,4,12]{3,2,1,0:T(4,128)} %cols.3, s32[1,1,4]{2,1,0:T(1,128)} %counts.3), custom_call_target="tpu_custom_call" | custom-call | tf_op jit(solution)/shard_map/mark_blocks/pallas_call | solution.py:65
  2.0 3.9 %collective-permute-start.9 = (s32[4,32]{1,0:T(4,128)}, s32[4,32]{1,0:T(4,128)S(1)}, u32[]{:S(2)}, u32[]{:S(2)}) collective-permute-start(s32[4,32]{1,0:T(4,128)} %mark_blocks.1.refs_0_), channel_id=1, source_target_pairs={{0,24},{8,16},{16,8},{24,0},{1,25},{9,17},{17,9},{25,1},{2,26},{10... | collective-permute-start | bytes 1544 | tf_op jit(solution)/shard_map/ppermute | solution.py:446
  5.9 0.5 collective-permute-start.8
  6.4 1.7 %load_history.1.history.refs_3_ = bf16[4,128,2048]{2,1,0:T(8,128)(2,1)S(1)} custom-call(bf16[4,128,2048]{2,1,0:T(8,128)(2,1)} %bitcast.6), custom_call_target="tpu_custom_call" | custom-call | tf_op jit(solution)/shard_map/load_history/pallas_call | solution.py:81
  8.2 1.4 %collective-permute-done.8.refs_2_.refs_1_ = s32[4,32]{1,0:T(4,128)S(1)} collective-permute-done((s32[4,32]{1,0:T(4,128)}, s32[4,32]{1,0:T(4,128)S(1)}, u32[]{:S(2)}, u32[]{:S(2)}) %collective-permute-start.8) | collective-permute-done | bytes 544 | tf_op jit(solution)/shard_map/ppermute | solution.py:446
  9.7 0.5 collective-permute-done.7.refs_1_.refs_0_
  10.2 1.7 %pack_history.2 = (bf16[16,64,256]{2,1,0:T(8,128)(2,1)S(1)}, bf16[16,64,256]{2,1,0:T(8,128)(2,1)S(1)}, bf16[16,64,256]{2,1,0:T(8,128)(2,1)S(1)}) custom-call(s32[4,32]{1,0:T(4,128)S(1)} %collective-permute-done.7.refs_1_.refs_0_, s32[4,32]{1,0:T(4,128)S(1)} %collective-permute-done.8.refs_2_.refs_1_, s32[4,32]{1,0:T(4,128)S(1)} %collective-permute-done.9.refs_3_.refs_2_, ...), custom_call_target="tpu_custom_call" | custom-call | tf_op jit(solution)/shard_map/pack_history/pallas_call | solution.py:116
  12.0 2.0 %collective-permute-start.11 = (bf16[16,64,256]{2,1,0:T(8,128)(2,1)S(1)}, bf16[16,64,256]{2,1,0:T(8,128)(2,1)S(1)}, u32[]{:S(2)}, u32[]{:S(2)}) collective-permute-start(bf16[16,64,256]{2,1,0:T(8,128)(2,1)S(1)} %get-tuple-element.62), channel_id=1, source_target_pairs={{0,16},{8,24},{16,0},{24,8},{1,17},{9,25},{17,1},{25,9},{2,18},{10... | collective-permute-start | bytes 1572872 | tf_op jit(solution)/shard_map/ppermute | solution.py:458
  14.0 1.4 %collective-permute-start.12 = (bf16[16,64,256]{2,1,0:T(8,128)(2,1)S(1)}, bf16[16,64,256]{2,1,0:T(8,128)(2,1)S(1)}, u32[]{:S(2)}, u32[]{:S(2)}) collective-permute-start(bf16[16,64,256]{2,1,0:T(8,128)(2,1)S(1)} %get-tuple-element.63), channel_id=1, source_target_pairs={{0,24},{8,16},{16,8},{24,0},{1,25},{9,17},{17,9},{25,1},{2,26},{10... | collective-permute-start | bytes 1572872 | tf_op jit(solution)/shard_map/ppermute | solution.py:458
  15.5 3.0 %plan_tiles.1 = (s32[5,48]{1,0:T(8,128)S(1)}, bf16[48,256,256]{2,1,0:T(8,128)(2,1)S(1)}) custom-call(s32[1,1,4,12]{3,2,1,0:T(4,128)S(1)} %copy-done.1, s32[1,1,4,12]{3,2,1,0:T(4,128)S(1)} %copy-done.3, s32[1,1,4]{2,1,0:T(1,128)S(1)} %copy-done.4, s32[4,32]{1,0:T(4,128)S(1)} %copy-done.2, s32[4,32]{1,0:T(4,128)S(1)} %collective-permute-done.7.refs_1_.refs_0_, ...), custom_call_target="tpu_custom_call" | custom-call | tf_op jit(solution)/shard_map/plan_tiles/pallas_call | solution.py:186
  18.5 1.3 %multiply_own.5.refs_6_.begun = f32[32,64,256]{2,1,0:T(8,128)S(1)} custom-call(s32[5,48]{1,0:T(8,128)S(1)} %get-tuple-element.59.table.refs_0_, bf16[48,256,256]{2,1,0:T(8,128)(2,1)S(1)} %get-tuple-element.60.tiles, bf16[4,128,2048]{2,1,0:T(8,128)(2,1)S(1)} %load_history.1.history.refs_3_), custom_call_target="tpu_custom_call" | custom-call | tf_op jit(solution)/shard_map/multiply_own/pallas_call | solution.py:271
  19.8 1.3 %multiply_own.4.begun.refs_5_ = f32[32,64,256]{2,1,0:T(8,128)S(1)} custom-call(s32[5,48]{1,0:T(8,128)S(1)} %get-tuple-element.59.table.refs_0_, bf16[48,256,256]{2,1,0:T(8,128)(2,1)S(1)} %get-tuple-element.60.tiles, bf16[4,128,2048]{2,1,0:T(8,128)(2,1)S(1)} %load_history.1.history.refs_3_), custom_call_target="tpu_custom_call" | custom-call | tf_op jit(solution)/shard_map/multiply_own/pallas_call | solution.py:271
  21.1 5.8 %collective-permute-done.10.refs_0_.refs_4_ = bf16[16,64,256]{2,1,0:T(8,128)(2,1)S(1)} collective-permute-done((bf16[16,64,256]{2,1,0:T(8,128)(2,1)S(1)}, bf16[16,64,256]{2,1,0:T(8,128)(2,1)S(1)}, u32[]{:S(2)}, u32[]{:S(2)}) %collective-permute-start.10) | collective-permute-done | bytes 524320 | tf_op jit(solution)/shard_map/ppermute | solution.py:458
  26.8 1.7 %pack_history.3 = (bf16[16,64,256]{2,1,0:T(8,128)(2,1)S(1)}, bf16[16,64,256]{2,1,0:T(8,128)(2,1)S(1)}, bf16[16,64,256]{2,1,0:T(8,128)(2,1)S(1)}) custom-call(s32[4,32]{1,0:T(4,128)S(1)} %collective-permute-done.7.refs_1_.refs_0_, s32[4,32]{1,0:T(4,128)S(1)} %collective-permute-done.8.refs_2_.refs_1_, s32[4,32]{1,0:T(4,128)S(1)} %collective-permute-done.9.refs_3_.refs_2_, ...), custom_call_target="tpu_custom_call" | custom-call | tf_op jit(solution)/shard_map/pack_history/pallas_call | solution.py:116
  28.7 2.0 %collective-permute-start.19 = (bf16[16,64,256]{2,1,0:T(8,128)(2,1)S(1)}, bf16[16,64,256]{2,1,0:T(8,128)(2,1)S(1)}, u32[]{:S(2)}, u32[]{:S(2)}) collective-permute-start(bf16[16,64,256]{2,1,0:T(8,128)(2,1)S(1)} %get-tuple-element.75), channel_id=1, source_target_pairs={{0,16},{8,24},{16,0},{24,8},{1,17},{9,25},{17,1},{25,9},{2,18},{10... | collective-permute-start | bytes 1572872 | tf_op jit(solution)/shard_map/ppermute | solution.py:458
  30.7 1.5 %collective-permute-start.20 = (bf16[16,64,256]{2,1,0:T(8,128)(2,1)S(1)}, bf16[16,64,256]{2,1,0:T(8,128)(2,1)S(1)}, u32[]{:S(2)}, u32[]{:S(2)}) collective-permute-start(bf16[16,64,256]{2,1,0:T(8,128)(2,1)S(1)} %get-tuple-element.76), channel_id=1, source_target_pairs={{0,24},{8,16},{16,8},{24,0},{1,25},{9,17},{17,9},{25,1},{2,26},{10... | collective-permute-start | bytes 1572872 | tf_op jit(solution)/shard_map/ppermute | solution.py:458
  32.2 1.5 %collective-permute-done.11.refs_1_ = bf16[16,64,256]{2,1,0:T(8,128)(2,1)S(1)} collective-permute-done((bf16[16,64,256]{2,1,0:T(8,128)(2,1)S(1)}, bf16[16,64,256]{2,1,0:T(8,128)(2,1)S(1)}, u32[]{:S(2)}, u32[]{:S(2)}) %collective-permute-start.11) | collective-permute-done | bytes 524320 | tf_op jit(solution)/shard_map/ppermute | solution.py:458
  33.6 5.4 %collective-permute-done.12.refs_2_ = bf16[16,64,256]{2,1,0:T(8,128)(2,1)S(1)} collective-permute-done((bf16[16,64,256]{2,1,0:T(8,128)(2,1)S(1)}, bf16[16,64,256]{2,1,0:T(8,128)(2,1)S(1)}, u32[]{:S(2)}, u32[]{:S(2)}) %collective-permute-start.12) | collective-permute-done | bytes 524320 | tf_op jit(solution)/shard_map/ppermute | solution.py:458
  39.1 2.5 %multiply_tiles.4 = (f32[32,64,256]{2,1,0:T(8,128)S(1)}, s16[528,256]{1,0:T(8,128)(2,1)S(1)}, s16[528,256]{1,0:T(8,128)(2,1)S(1)}) custom-call(s32[5,48]{1,0:T(8,128)S(1)} %get-tuple-element.59.table.refs_0_, bf16[48,256,256]{2,1,0:T(8,128)(2,1)S(1)} %get-tuple-element.60.tiles, f32[32,64,256]{2,1,0:T(8,128)S(1)} %multiply_own.4.begun.refs_5_, ...), custom_call_target="tpu_custom_call" | custom-call | tf_op jit(solution)/shard_map/multiply_tiles/pallas_call | solution.py:288
  41.6 0.5 collective-permute-start.13
  42.1 1.0 %collective-permute-done.14.refs_1_ = s16[528,256]{1,0:T(8,128)(2,1)S(1)} collective-permute-done((s16[528,256]{1,0:T(8,128)(2,1)S(1)}, s16[528,256]{1,0:T(8,128)(2,1)S(1)}, u32[]{:S(2)}, u32[]{:S(2)}) %collective-permute-start.14) | collective-permute-done | bytes 270368 | tf_op jit(solution)/shard_map/ppermute | solution.py:421
  43.9 2.7 %collective-permute-start.15 = (s16[528,128]{1,0:T(8,128)(2,1)S(1)}, s16[528,128]{1,0:T(8,128)(2,1)S(1)}, u32[]{:S(2)}, u32[]{:S(2)}) collective-permute-start(s16[528,128]{1,0:T(8,128)(2,1)S(1)} %get-tuple-element.68), channel_id=1, source_target_pairs={{0,4},{2,6},{4,0},{6,2},{1,5},{3,7},{5,1},{7,3},{8,12},{10,14},{12... | collective-permute-start | bytes 405512 | tf_op jit(solution)/shard_map/ppermute | solution.py:424
  46.6 1.6 %collective-permute-start.16 = (s16[528,128]{1,0:T(8,128)(2,1)S(1)}, s16[528,128]{1,0:T(8,128)(2,1)S(1)}, u32[]{:S(2)}, u32[]{:S(2)}) collective-permute-start(s16[528,128]{1,0:T(8,128)(2,1)S(1)} %get-tuple-element.69), channel_id=1, source_target_pairs={{0,6},{2,4},{4,2},{6,0},{1,7},{3,5},{5,3},{7,1},{8,14},{10,12},{12... | collective-permute-start | bytes 405512 | tf_op jit(solution)/shard_map/ppermute | solution.py:424
  48.2 8.9 %collective-permute-done.15.refs_6_.refs_3_ = s16[528,128]{1,0:T(8,128)(2,1)S(1)} collective-permute-done((s16[528,128]{1,0:T(8,128)(2,1)S(1)}, s16[528,128]{1,0:T(8,128)(2,1)S(1)}, u32[]{:S(2)}, u32[]{:S(2)}) %collective-permute-start.15) | collective-permute-done | bytes 135200 | tf_op jit(solution)/shard_map/ppermute | solution.py:424
  57.4 1.3 %collective-permute-done.20.refs_2_ = bf16[16,64,256]{2,1,0:T(8,128)(2,1)S(1)} collective-permute-done((bf16[16,64,256]{2,1,0:T(8,128)(2,1)S(1)}, bf16[16,64,256]{2,1,0:T(8,128)(2,1)S(1)}, u32[]{:S(2)}, u32[]{:S(2)}) %collective-permute-start.20) | collective-permute-done | bytes 524320 | tf_op jit(solution)/shard_map/ppermute | solution.py:458
  58.6 2.5 %multiply_tiles.5 = (f32[32,64,256]{2,1,0:T(8,128)S(1)}, s16[1056,256]{1,0:T(8,128)(2,1)S(1)}) custom-call(s32[5,48]{1,0:T(8,128)S(1)} %get-tuple-element.59.table.refs_0_, bf16[48,256,256]{2,1,0:T(8,128)(2,1)S(1)} %get-tuple-element.60.tiles, f32[32,64,256]{2,1,0:T(8,128)S(1)} %multiply_own.5.refs_6_.begun, ...), custom_call_target="tpu_custom_call" | custom-call | tf_op jit(solution)/shard_map/multiply_tiles/pallas_call | solution.py:288
  61.3 1.6 %collective-permute-start.17 = (s16[528,128]{1,0:T(8,128)(2,1)S(1)}, s16[528,128]{1,0:T(8,128)(2,1)S(1)}, u32[]{:S(2)}, u32[]{:S(2)}) collective-permute-start(s16[528,128]{1,0:T(8,128)(2,1)S(1)} %get-tuple-element.70), channel_id=1, source_target_pairs={{0,2},{2,0},{4,6},{6,4},{1,3},{3,1},{5,7},{7,5},{8,10},{10,8},{12,... | collective-permute-start | bytes 405512 | tf_op jit(solution)/shard_map/ppermute | solution.py:424
  63.6 3.5 %collective-permute-start.22 = (s16[528,128]{1,0:T(8,128)(2,1)S(1)}, s16[528,128]{1,0:T(8,128)(2,1)S(1)}, u32[]{:S(2)}, u32[]{:S(2)}) collective-permute-start(s16[528,128]{1,0:T(8,128)(2,1)S(1)} %get-tuple-element.80), channel_id=1, source_target_pairs={{0,4},{2,6},{4,0},{6,2},{1,5},{3,7},{5,1},{7,3},{8,12},{10,14},{12... | collective-permute-start | bytes 405512 | tf_op jit(solution)/shard_map/ppermute | solution.py:424
  67.0 0.8 %collective-permute-start.23 = (s16[528,128]{1,0:T(8,128)(2,1)S(1)}, s16[528,128]{1,0:T(8,128)(2,1)S(1)}, u32[]{:S(2)}, u32[]{:S(2)}) collective-permute-start(s16[528,128]{1,0:T(8,128)(2,1)S(1)} %get-tuple-element.81), channel_id=1, source_target_pairs={{0,6},{2,4},{4,2},{6,0},{1,7},{3,5},{5,3},{7,1},{8,14},{10,12},{12... | collective-permute-start | bytes 405512 | tf_op jit(solution)/shard_map/ppermute | solution.py:424
  68.4 2.8 %friction_solve.4 = (s32[1]{0:T(128)}, f32[128,1024]{1,0:T(8,128)}, f32[128,1024]{1,0:T(8,128)}) custom-call(s32[5,48]{1,0:T(8,128)S(1)} %get-tuple-element.59.table.refs_0_, f32[128,1024]{1,0:T(8,128)S(1)} %copy-done.7, f32[128,1024]{1,0:T(8,128)S(1)} %copy-done.8, f32[128,1024]{1,0:T(8,128)S(1)} %copy-done.9, f32[128,1024]{1,0:T(8,128)S(1)} %copy-done.12, ...), custom_call_target="tpu_custom_call" | custom-call | tf_op jit(solution)/shard_map/friction_solve/pallas_call | solution.py:405
  72.0 5.3 %collective-permute-done.22.refs_7_ = s16[528,128]{1,0:T(8,128)(2,1)S(1)} collective-permute-done((s16[528,128]{1,0:T(8,128)(2,1)S(1)}, s16[528,128]{1,0:T(8,128)(2,1)S(1)}, u32[]{:S(2)}, u32[]{:S(2)}) %collective-permute-start.22) | collective-permute-done | bytes 135200 | tf_op jit(solution)/shard_map/ppermute | solution.py:424
  77.5 1.7 %friction_solve.5 = (f32[128,1024]{1,0:T(8,128)}, f32[128,1024]{1,0:T(8,128)}) custom-call(f32[128,1024]{1,0:T(8,128)} %get-tuple-element.72.refs_0_, f32[128,1024]{1,0:T(8,128)} %get-tuple-element.73.refs_1_, f32[128,1024]{1,0:T(8,128)S(1)} %copy-done.7, f32[128,1024]{1,0:T(8,128)S(1)} %copy-done.8, ...), custom_call_target="tpu_custom_call", output_to_operand_aliasing={{0}: (0, {}), {1}: (1, {})} | custom-call | tf_op jit(solution)/shard_map/friction_solve/pallas_call | solution.py:405
  (38 shorter events, 3.1 us)
Async XLA Ops:
  2.0 6.3 %collective-permute-start.9 = (s32[4,32]{1,0:T(4,128)}, s32[4,32]{1,0:T(4,128)S(1)}, u32[]{:S(2)}, u32[]{:S(2)}) collective-permute-start(s32[4,32]{1,0:T(4,128)} %mark_blocks.1.refs_0_), channel_id=1, source_target_pairs={{0,24},{8,16},{16,8},{24,0},{1,25},{9,17},{17,9},{25,1},{2,26},{10... | collective-permute-start | bytes 1544 | tf_op jit(solution)/shard_map/ppermute | solution.py:446
  5.9 3.8 %collective-permute-start.8 = (s32[4,32]{1,0:T(4,128)}, s32[4,32]{1,0:T(4,128)S(1)}, u32[]{:S(2)}, u32[]{:S(2)}) collective-permute-start(s32[4,32]{1,0:T(4,128)} %mark_blocks.1.refs_0_), channel_id=1, source_target_pairs={{0,16},{8,24},{16,0},{24,8},{1,17},{9,25},{17,1},{25,9},{2,18},{10... | collective-permute-start | bytes 1544 | tf_op jit(solution)/shard_map/ppermute | solution.py:446
  6.4 3.8 %collective-permute-start.7 = (s32[4,32]{1,0:T(4,128)}, s32[4,32]{1,0:T(4,128)S(1)}, u32[]{:S(2)}, u32[]{:S(2)}) collective-permute-start(s32[4,32]{1,0:T(4,128)} %mark_blocks.1.refs_0_), channel_id=1, source_target_pairs={{0,8},{8,0},{16,24},{24,16},{1,9},{9,1},{17,25},{25,17},{2,10},{10... | collective-permute-start | bytes 1544 | tf_op jit(solution)/shard_map/ppermute | solution.py:446
  6.4 9.0 %copy-start = (bf16[1,1,4,12,256,256]{5,4,3,2,1,0:T(8,128)(2,1)S(1)}, bf16[1,1,4,12,256,256]{5,4,3,2,1,0:T(8,128)(2,1)}, u32[]{:S(2)}) copy-start(bf16[1,1,4,12,256,256]{5,4,3,2,1,0:T(8,128)(2,1)} %param.12) | copy-start | bytes 18874372
  8.2 7.3 %copy-start.1 = (s32[1,1,4,12]{3,2,1,0:T(4,128)S(1)}, s32[1,1,4,12]{3,2,1,0:T(4,128)}, u32[]{:S(2)}) copy-start(s32[1,1,4,12]{3,2,1,0:T(4,128)} %cols.3) | copy-start | bytes 580
  8.2 7.3 %copy-start.2 = (s32[4,32]{1,0:T(4,128)S(1)}, s32[4,32]{1,0:T(4,128)}, u32[]{:S(2)}) copy-start(s32[4,32]{1,0:T(4,128)} %mark_blocks.1.refs_0_) | copy-start | bytes 1540
  8.2 7.3 %copy-start.3 = (s32[1,1,4,12]{3,2,1,0:T(4,128)S(1)}, s32[1,1,4,12]{3,2,1,0:T(4,128)}, u32[]{:S(2)}) copy-start(s32[1,1,4,12]{3,2,1,0:T(4,128)} %rows.1) | copy-start | bytes 580
  8.2 7.3 %copy-start.4 = (s32[1,1,4]{2,1,0:T(1,128)S(1)}, s32[1,1,4]{2,1,0:T(1,128)}, u32[]{:S(2)}) copy-start(s32[1,1,4]{2,1,0:T(1,128)} %counts.3) | copy-start | bytes 52
  11.9 14.9 %collective-permute-start.10 = (bf16[16,64,256]{2,1,0:T(8,128)(2,1)S(1)}, bf16[16,64,256]{2,1,0:T(8,128)(2,1)S(1)}, u32[]{:S(2)}, u32[]{:S(2)}) collective-permute-start(bf16[16,64,256]{2,1,0:T(8,128)(2,1)S(1)} %get-tuple-element.61), channel_id=1, source_target_pairs={{0,8},{8,0},{16,24},{24,16},{1,9},{9,1},{17,25},{25,17},{2,10},{10... | collective-permute-start | bytes 1572872 | tf_op jit(solution)/shard_map/ppermute | solution.py:458
  12.0 21.6 %collective-permute-start.11 = (bf16[16,64,256]{2,1,0:T(8,128)(2,1)S(1)}, bf16[16,64,256]{2,1,0:T(8,128)(2,1)S(1)}, u32[]{:S(2)}, u32[]{:S(2)}) collective-permute-start(bf16[16,64,256]{2,1,0:T(8,128)(2,1)S(1)} %get-tuple-element.62), channel_id=1, source_target_pairs={{0,16},{8,24},{16,0},{24,8},{1,17},{9,25},{17,1},{25,9},{2,18},{10... | collective-permute-start | bytes 1572872 | tf_op jit(solution)/shard_map/ppermute | solution.py:458
  14.0 25.0 %collective-permute-start.12 = (bf16[16,64,256]{2,1,0:T(8,128)(2,1)S(1)}, bf16[16,64,256]{2,1,0:T(8,128)(2,1)S(1)}, u32[]{:S(2)}, u32[]{:S(2)}) collective-permute-start(bf16[16,64,256]{2,1,0:T(8,128)(2,1)S(1)} %get-tuple-element.63), channel_id=1, source_target_pairs={{0,24},{8,16},{16,8},{24,0},{1,25},{9,17},{17,9},{25,1},{2,26},{10... | collective-permute-start | bytes 1572872 | tf_op jit(solution)/shard_map/ppermute | solution.py:458
  28.6 28.5 %collective-permute-start.18 = (bf16[16,64,256]{2,1,0:T(8,128)(2,1)S(1)}, bf16[16,64,256]{2,1,0:T(8,128)(2,1)S(1)}, u32[]{:S(2)}, u32[]{:S(2)}) collective-permute-start(bf16[16,64,256]{2,1,0:T(8,128)(2,1)S(1)} %get-tuple-element.74), channel_id=1, source_target_pairs={{0,8},{8,0},{16,24},{24,16},{1,9},{9,1},{17,25},{25,17},{2,10},{10... | collective-permute-start | bytes 1572872 | tf_op jit(solution)/shard_map/ppermute | solution.py:458
  28.7 28.7 %collective-permute-start.19 = (bf16[16,64,256]{2,1,0:T(8,128)(2,1)S(1)}, bf16[16,64,256]{2,1,0:T(8,128)(2,1)S(1)}, u32[]{:S(2)}, u32[]{:S(2)}) collective-permute-start(bf16[16,64,256]{2,1,0:T(8,128)(2,1)S(1)} %get-tuple-element.75), channel_id=1, source_target_pairs={{0,16},{8,24},{16,0},{24,8},{1,17},{9,25},{17,1},{25,9},{2,18},{10... | collective-permute-start | bytes 1572872 | tf_op jit(solution)/shard_map/ppermute | solution.py:458
  30.7 27.9 %collective-permute-start.20 = (bf16[16,64,256]{2,1,0:T(8,128)(2,1)S(1)}, bf16[16,64,256]{2,1,0:T(8,128)(2,1)S(1)}, u32[]{:S(2)}, u32[]{:S(2)}) collective-permute-start(bf16[16,64,256]{2,1,0:T(8,128)(2,1)S(1)} %get-tuple-element.76), channel_id=1, source_target_pairs={{0,24},{8,16},{16,8},{24,0},{1,25},{9,17},{17,9},{25,1},{2,26},{10... | collective-permute-start | bytes 1572872 | tf_op jit(solution)/shard_map/ppermute | solution.py:458
  41.6 1.6 %collective-permute-start.14 = (s16[528,256]{1,0:T(8,128)(2,1)S(1)}, s16[528,256]{1,0:T(8,128)(2,1)S(1)}, u32[]{:S(2)}, u32[]{:S(2)}) collective-permute-start(s16[528,256]{1,0:T(8,128)(2,1)S(1)} %get-tuple-element.66), channel_id=1, source_target_pairs={{0,1},{1,0},{2,3},{3,2},{4,5},{5,4},{6,7},{7,6},{8,9},{9,8},{10,11... | collective-permute-start | bytes 811016 | tf_op jit(solution)/shard_map/ppermute | solution.py:421
  41.6 1.9 %collective-permute-start.13 = (s16[528,256]{1,0:T(8,128)(2,1)S(1)}, s16[528,256]{1,0:T(8,128)(2,1)S(1)}, u32[]{:S(2)}, u32[]{:S(2)}) collective-permute-start(s16[528,256]{1,0:T(8,128)(2,1)S(1)} %get-tuple-element.64.given), channel_id=1, source_target_pairs={{0,1},{1,0},{2,3},{3,2},{4,5},{5,4},{6,7},{7,6},{8,9},{9,8},{10,11... | collective-permute-start | bytes 811016 | tf_op jit(solution)/shard_map/ppermute | solution.py:421
  43.9 13.2 %collective-permute-start.15 = (s16[528,128]{1,0:T(8,128)(2,1)S(1)}, s16[528,128]{1,0:T(8,128)(2,1)S(1)}, u32[]{:S(2)}, u32[]{:S(2)}) collective-permute-start(s16[528,128]{1,0:T(8,128)(2,1)S(1)} %get-tuple-element.68), channel_id=1, source_target_pairs={{0,4},{2,6},{4,0},{6,2},{1,5},{3,7},{5,1},{7,3},{8,12},{10,14},{12... | collective-permute-start | bytes 405512 | tf_op jit(solution)/shard_map/ppermute | solution.py:424
  46.6 10.5 %collective-permute-start.16 = (s16[528,128]{1,0:T(8,128)(2,1)S(1)}, s16[528,128]{1,0:T(8,128)(2,1)S(1)}, u32[]{:S(2)}, u32[]{:S(2)}) collective-permute-start(s16[528,128]{1,0:T(8,128)(2,1)S(1)} %get-tuple-element.69), channel_id=1, source_target_pairs={{0,6},{2,4},{4,2},{6,0},{1,7},{3,5},{5,3},{7,1},{8,14},{10,12},{12... | collective-permute-start | bytes 405512 | tf_op jit(solution)/shard_map/ppermute | solution.py:424
  61.1 7.2 %copy-start.7 = (f32[128,1024]{1,0:T(8,128)S(1)}, f32[128,1024]{1,0:T(8,128)}, u32[]{:S(2)}) copy-start(f32[128,1024]{1,0:T(8,128)} %refs_2_.3) | copy-start | bytes 1572868
  61.1 7.2 %copy-start.8 = (f32[128,1024]{1,0:T(8,128)S(1)}, f32[128,1024]{1,0:T(8,128)}, u32[]{:S(2)}) copy-start(f32[128,1024]{1,0:T(8,128)} %refs_3_.3) | copy-start | bytes 1572868
  61.2 7.2 %copy-start.9 = (f32[128,1024]{1,0:T(8,128)S(1)}, f32[128,1024]{1,0:T(8,128)}, u32[]{:S(2)}) copy-start(f32[128,1024]{1,0:T(8,128)} %refs_4_.3) | copy-start | bytes 1572868
  61.2 7.2 %copy-start.12 = (f32[128,1024]{1,0:T(8,128)S(1)}, f32[128,1024]{1,0:T(8,128)}, u32[]{:S(2)}) copy-start(f32[128,1024]{1,0:T(8,128)} %refs_5_.1) | copy-start | bytes 1572868
  61.2 2.0 %collective-permute-start.21 = (s16[1056,256]{1,0:T(8,128)(2,1)S(1)}, s16[1056,256]{1,0:T(8,128)(2,1)S(1)}, u32[]{:S(2)}, u32[]{:S(2)}) collective-permute-start(s16[1056,256]{1,0:T(8,128)(2,1)S(1)} %get-tuple-element.77.given), channel_id=1, source_target_pairs={{0,1},{1,0},{2,3},{3,2},{4,5},{5,4},{6,7},{7,6},{8,9},{9,8},{10,11... | collective-permute-start | bytes 1622024 | tf_op jit(solution)/shard_map/ppermute | solution.py:421
  61.3 7.1 %collective-permute-start.17 = (s16[528,128]{1,0:T(8,128)(2,1)S(1)}, s16[528,128]{1,0:T(8,128)(2,1)S(1)}, u32[]{:S(2)}, u32[]{:S(2)}) collective-permute-start(s16[528,128]{1,0:T(8,128)(2,1)S(1)} %get-tuple-element.70), channel_id=1, source_target_pairs={{0,2},{2,0},{4,6},{6,4},{1,3},{3,1},{5,7},{7,5},{8,10},{10,8},{12,... | collective-permute-start | bytes 405512 | tf_op jit(solution)/shard_map/ppermute | solution.py:424
  63.6 13.7 %collective-permute-start.22 = (s16[528,128]{1,0:T(8,128)(2,1)S(1)}, s16[528,128]{1,0:T(8,128)(2,1)S(1)}, u32[]{:S(2)}, u32[]{:S(2)}) collective-permute-start(s16[528,128]{1,0:T(8,128)(2,1)S(1)} %get-tuple-element.80), channel_id=1, source_target_pairs={{0,4},{2,6},{4,0},{6,2},{1,5},{3,7},{5,1},{7,3},{8,12},{10,14},{12... | collective-permute-start | bytes 405512 | tf_op jit(solution)/shard_map/ppermute | solution.py:424
  67.0 10.3 %collective-permute-start.23 = (s16[528,128]{1,0:T(8,128)(2,1)S(1)}, s16[528,128]{1,0:T(8,128)(2,1)S(1)}, u32[]{:S(2)}, u32[]{:S(2)}) collective-permute-start(s16[528,128]{1,0:T(8,128)(2,1)S(1)} %get-tuple-element.81), channel_id=1, source_target_pairs={{0,6},{2,4},{4,2},{6,0},{1,7},{3,5},{5,3},{7,1},{8,14},{10,12},{12... | collective-permute-start | bytes 405512 | tf_op jit(solution)/shard_map/ppermute | solution.py:424
  67.8 9.7 %collective-permute-start.24 = (s16[528,128]{1,0:T(8,128)(2,1)S(1)}, s16[528,128]{1,0:T(8,128)(2,1)S(1)}, u32[]{:S(2)}, u32[]{:S(2)}) collective-permute-start(s16[528,128]{1,0:T(8,128)(2,1)S(1)} %get-tuple-element.82), channel_id=1, source_target_pairs={{0,2},{2,0},{4,6},{6,4},{1,3},{3,1},{5,7},{7,5},{8,10},{10,8},{12,... | collective-permute-start | bytes 405512 | tf_op jit(solution)/shard_map/ppermute | solution.py:424
  71.2 8.0 %copy-start.6 = (bf16[4,1,128,2048]{3,2,1,0:T(8,128)(2,1)S(1)}, bf16[4,1,128,2048]{3,2,1,0:T(8,128)(2,1)}, u32[]{:S(2)}) copy-start(bf16[4,1,128,2048]{3,2,1,0:T(8,128)(2,1)} %param.11) | copy-start | bytes 6291460

commit v8 on v7

--- a/solution.py
+++ b/solution.py
@@ -230,6 +230,32 @@
     add_products(0, table[4, 1], table, tiles, blocks, sums)
 
 
+def early_kernel(table, tiles, begun, received, sums, blocks):
+    sums[...] = begun[...]
+
+    def fetch(index, carry):
+        blocks[index] = received[table[3, index]]
+        return carry
+
+    lax.fori_loop(table[4, 1], table[4, 2], fetch, 0)
+    add_products(table[4, 1], table[4, 2], table, tiles, blocks, sums)
+
+
+def multiply_early(table, tiles, begun, received):
+    _, part, side = begun.shape
+    blocks = pltpu.VMEM((table.shape[1], part, side), tiles.dtype)
+    sums = jax.ShapeDtypeStruct(begun.shape, jnp.float32)
+    return pl.pallas_call(
+        early_kernel,
+        out_shape=sums,
+        in_specs=[SMEM, VMEM, VMEM, VMEM],
+        out_specs=VMEM,
+        scratch_shapes=[blocks],
+        compiler_params=params(tiles, begun, received, blocks, sums),
+        name="multiply_early",
+    )(table, tiles, begun, received)
+
+
 def tiles_kernel(first, whole, extra, split, table, tiles, begun, *refs):
     received, (sums, *given), blocks = refs[: len(refs) - 2 - split - extra], refs[-2 - split : -1], refs[-1]
     side = tiles.shape[2]
@@ -247,9 +273,11 @@
 
         return one
 
-    for source in range(1, len(received) + 1):
-        lax.fori_loop(table[4, source], table[4, source + 1], fetch(source), 0)
-    add_products(table[4, 1], table[4, len(received) + 1], table, tiles, blocks, sums)
+    done = 1 if whole else 2
+    last = done + len(received)
+    for source in range(done, last):
+        lax.fori_loop(table[4, source], table[4, source + 1], fetch(source - done + 1), 0)
+    add_products(table[4, done], table[4, last], table, tiles, blocks, sums)
     half = halves // 2
     size = half // split
     flag = jnp.full((1, side), 1.0, jnp.float32) * table[4, OVER].astype(jnp.float32)
@@ -462,7 +490,7 @@
     flags = result = None
     for (first, part), blocks, own in zip(pieces, received, begun):
         kept, *given = multiply_tiles(
-            first, False, 1 if first + part == sims else SPLIT, table, live_tiles, own, blocks, after
+            first, False, 1 if first + part == sims else SPLIT, table, live_tiles, multiply_early(table, live_tiles, own, blocks[0]), blocks[1:], after
         )
         (flag, result), after, _ = reduce(first, table, fields, kept, given, result)
         flags = flags or flag

time: 80.3 us -> 79.5 us (0.990)
  waiting for transfers between devices: 32.2 us -> 28.2 us
  Pallas kernels: 22.3 us -> 25.4 us
    pallas_call x0 -> x2, Pallas kernels: none -> 3.48 us  [multiply_early(): pl.pallas_call(early_kernel, out_shape=sums, in_specs=[SMEM, VMEM, VMEM,...]
    ppermute x6, waiting for transfers between devices: 14.4 us -> 11 us  [reduce(): lax.ppermute(coded[step - 1], 'col', partners(col_size, step))]
    pallas_call x2, Pallas kernels: 4.97 us -> 3.99 us  [multiply_tiles(): pl.pallas_call(functools.partial(tiles_kernel, first, whole, len(after),...]
  transfers between devices with their start and end apart: 18 -> 18, of which waited for: 13 -> 12; matrix products, arithmetic and copies ran while one was open for 0% -> 0% of each run, Pallas kernels for 19% -> 24%
where the time goes in v8:
time: 79.5 us; the launch traced here: 78.8 us
  waiting for transfers between devices  28.2 us (35%)
  Pallas kernels  25.4 us (32%)
  starting transfers between devices  23.1 us (29%)
  between operations  1.89 us (2%)
    ppermute x6, waiting for transfers between devices, local(): lax.ppermute(packed[step - 1], 'row', partners(row_size, step))  13.8 us
    ppermute x6, waiting for transfers between devices, reduce(): lax.ppermute(coded[step - 1], 'col', partners(col_size, step))  11 us
    ppermute x6, starting transfers between devices, reduce(): lax.ppermute(coded[step - 1], 'col', partners(col_size, step))  10.9 us
    ppermute x6, starting transfers between devices, local(): lax.ppermute(packed[step - 1], 'row', partners(row_size, step))  7.11 us
    pallas_call x2, Pallas kernels, solve(): pl.pallas_call(functools.partial(solve_kernel, first, fresh), out_shape=f...  4.48 us
    ppermute x3, starting transfers between devices, local(): lax.ppermute(need, 'row', partners(row_size, step))  4.46 us
    pallas_call x2, Pallas kernels, multiply_tiles(): pl.pallas_call(functools.partial(tiles_kernel, first, whole, len(after),...  3.99 us
    pallas_call x1, Pallas kernels, make_plan(): pl.pallas_call(functools.partial(plan_kernel, cap, col_size, per_owner),...  3.52 us
  transfers between devices with their start and end apart: 18, of which 12 were waited for; matrix products, arithmetic and copies ran while one was open for 0% of the time, Pallas kernels for 24%

profile of v8, /device:TPU:0, one launch (start us, length us, event | category | flops | bytes accessed | tf_op | source)
XLA Modules:
  0.0 78.8 jit_solution(788798241206746107)
XLA Ops:
  0.6 1.3 %mark_blocks.1.refs_0_ = s32[4,32]{1,0:T(4,128)} custom-call(s32[1,1,4,12]{3,2,1,0:T(4,128)} %cols.3, s32[1,1,4]{2,1,0:T(1,128)} %counts.3), custom_call_target="tpu_custom_call" | custom-call | tf_op jit(solution)/shard_map/mark_blocks/pallas_call | solution.py:65
  2.0 3.9 %collective-permute-start.9 = (s32[4,32]{1,0:T(4,128)}, s32[4,32]{1,0:T(4,128)S(1)}, u32[]{:S(2)}, u32[]{:S(2)}) collective-permute-start(s32[4,32]{1,0:T(4,128)} %mark_blocks.1.refs_0_), channel_id=1, source_target_pairs={{0,24},{8,16},{16,8},{24,0},{1,25},{9,17},{17,9},{25,1},{2,26},{10... | collective-permute-start | bytes 1544 | tf_op jit(solution)/shard_map/ppermute | solution.py:474
  6.4 1.7 %load_history.1.history.refs_3_ = bf16[4,128,2048]{2,1,0:T(8,128)(2,1)S(1)} custom-call(bf16[4,128,2048]{2,1,0:T(8,128)(2,1)} %bitcast.6), custom_call_target="tpu_custom_call" | custom-call | tf_op jit(solution)/shard_map/load_history/pallas_call | solution.py:81
  8.2 1.4 %collective-permute-done.8.refs_2_.refs_1_ = s32[4,32]{1,0:T(4,128)S(1)} collective-permute-done((s32[4,32]{1,0:T(4,128)}, s32[4,32]{1,0:T(4,128)S(1)}, u32[]{:S(2)}, u32[]{:S(2)}) %collective-permute-start.8) | collective-permute-done | bytes 544 | tf_op jit(solution)/shard_map/ppermute | solution.py:474
  10.2 1.7 %pack_history.2 = (bf16[16,64,256]{2,1,0:T(8,128)(2,1)S(1)}, bf16[16,64,256]{2,1,0:T(8,128)(2,1)S(1)}, bf16[16,64,256]{2,1,0:T(8,128)(2,1)S(1)}) custom-call(s32[4,32]{1,0:T(4,128)S(1)} %collective-permute-done.7.refs_1_.refs_0_, s32[4,32]{1,0:T(4,128)S(1)} %collective-permute-done.8.refs_2_.refs_1_, s32[4,32]{1,0:T(4,128)S(1)} %collective-permute-done.9.refs_3_.refs_2_, ...), custom_call_target="tpu_custom_call" | custom-call | tf_op jit(solution)/shard_map/pack_history/pallas_call | solution.py:116
  12.0 2.0 %collective-permute-start.11 = (bf16[16,64,256]{2,1,0:T(8,128)(2,1)S(1)}, bf16[16,64,256]{2,1,0:T(8,128)(2,1)S(1)}, u32[]{:S(2)}, u32[]{:S(2)}) collective-permute-start(bf16[16,64,256]{2,1,0:T(8,128)(2,1)S(1)} %get-tuple-element.62), channel_id=1, source_target_pairs={{0,16},{8,24},{16,0},{24,8},{1,17},{9,25},{17,1},{25,9},{2,18},{10... | collective-permute-start | bytes 1572872 | tf_op jit(solution)/shard_map/ppermute | solution.py:486
  14.0 1.4 %collective-permute-start.12 = (bf16[16,64,256]{2,1,0:T(8,128)(2,1)S(1)}, bf16[16,64,256]{2,1,0:T(8,128)(2,1)S(1)}, u32[]{:S(2)}, u32[]{:S(2)}) collective-permute-start(bf16[16,64,256]{2,1,0:T(8,128)(2,1)S(1)} %get-tuple-element.63), channel_id=1, source_target_pairs={{0,24},{8,16},{16,8},{24,0},{1,25},{9,17},{17,9},{25,1},{2,26},{10... | collective-permute-start | bytes 1572872 | tf_op jit(solution)/shard_map/ppermute | solution.py:486
  15.5 3.5 %plan_tiles.1 = (s32[5,48]{1,0:T(8,128)S(1)}, bf16[48,256,256]{2,1,0:T(8,128)(2,1)S(1)}) custom-call(s32[1,1,4,12]{3,2,1,0:T(4,128)S(1)} %copy-done.1, s32[1,1,4,12]{3,2,1,0:T(4,128)S(1)} %copy-done.3, s32[1,1,4]{2,1,0:T(1,128)S(1)} %copy-done.4, s32[4,32]{1,0:T(4,128)S(1)} %copy-done.2, s32[4,32]{1,0:T(4,128)S(1)} %collective-permute-done.7.refs_1_.refs_0_, ...), custom_call_target="tpu_custom_call" | custom-call | tf_op jit(solution)/shard_map/plan_tiles/pallas_call | solution.py:186
  19.0 1.3 %multiply_own.5.refs_6_.begun = f32[32,64,256]{2,1,0:T(8,128)S(1)} custom-call(s32[5,48]{1,0:T(8,128)S(1)} %get-tuple-element.59.table.refs_0_, bf16[48,256,256]{2,1,0:T(8,128)(2,1)S(1)} %get-tuple-element.60.tiles, bf16[4,128,2048]{2,1,0:T(8,128)(2,1)S(1)} %load_history.1.history.refs_3_), custom_call_target="tpu_custom_call" | custom-call | tf_op jit(solution)/shard_map/multiply_own/pallas_call | solution.py:299
  20.3 1.3 %multiply_own.4.begun.refs_5_ = f32[32,64,256]{2,1,0:T(8,128)S(1)} custom-call(s32[5,48]{1,0:T(8,128)S(1)} %get-tuple-element.59.table.refs_0_, bf16[48,256,256]{2,1,0:T(8,128)(2,1)S(1)} %get-tuple-element.60.tiles, bf16[4,128,2048]{2,1,0:T(8,128)(2,1)S(1)} %load_history.1.history.refs_3_), custom_call_target="tpu_custom_call" | custom-call | tf_op jit(solution)/shard_map/multiply_own/pallas_call | solution.py:299
  21.6 5.2 %collective-permute-done.10.received.refs_4_ = bf16[16,64,256]{2,1,0:T(8,128)(2,1)S(1)} collective-permute-done((bf16[16,64,256]{2,1,0:T(8,128)(2,1)S(1)}, bf16[16,64,256]{2,1,0:T(8,128)(2,1)S(1)}, u32[]{:S(2)}, u32[]{:S(2)}) %collective-permute-start.10) | collective-permute-done | bytes 524320 | tf_op jit(solution)/shard_map/ppermute | solution.py:486
  26.8 1.7 %pack_history.3 = (bf16[16,64,256]{2,1,0:T(8,128)(2,1)S(1)}, bf16[16,64,256]{2,1,0:T(8,128)(2,1)S(1)}, bf16[16,64,256]{2,1,0:T(8,128)(2,1)S(1)}) custom-call(s32[4,32]{1,0:T(4,128)S(1)} %collective-permute-done.7.refs_1_.refs_0_, s32[4,32]{1,0:T(4,128)S(1)} %collective-permute-done.8.refs_2_.refs_1_, s32[4,32]{1,0:T(4,128)S(1)} %collective-permute-done.9.refs_3_.refs_2_, ...), custom_call_target="tpu_custom_call" | custom-call | tf_op jit(solution)/shard_map/pack_history/pallas_call | solution.py:116
  28.7 2.0 %collective-permute-start.19 = (bf16[16,64,256]{2,1,0:T(8,128)(2,1)S(1)}, bf16[16,64,256]{2,1,0:T(8,128)(2,1)S(1)}, u32[]{:S(2)}, u32[]{:S(2)}) collective-permute-start(bf16[16,64,256]{2,1,0:T(8,128)(2,1)S(1)} %get-tuple-element.75), channel_id=1, source_target_pairs={{0,16},{8,24},{16,0},{24,8},{1,17},{9,25},{17,1},{25,9},{2,18},{10... | collective-permute-start | bytes 1572872 | tf_op jit(solution)/shard_map/ppermute | solution.py:486
  30.7 1.4 %collective-permute-start.20 = (bf16[16,64,256]{2,1,0:T(8,128)(2,1)S(1)}, bf16[16,64,256]{2,1,0:T(8,128)(2,1)S(1)}, u32[]{:S(2)}, u32[]{:S(2)}) collective-permute-start(bf16[16,64,256]{2,1,0:T(8,128)(2,1)S(1)} %get-tuple-element.76), channel_id=1, source_target_pairs={{0,24},{8,16},{16,8},{24,0},{1,25},{9,17},{17,9},{25,1},{2,26},{10... | collective-permute-start | bytes 1572872 | tf_op jit(solution)/shard_map/ppermute | solution.py:486
  32.1 1.7 %multiply_early.2.begun = f32[32,64,256]{2,1,0:T(8,128)S(1)} custom-call(s32[5,48]{1,0:T(8,128)S(1)} %get-tuple-element.59.table.refs_0_, bf16[48,256,256]{2,1,0:T(8,128)(2,1)S(1)} %get-tuple-element.60.tiles, f32[32,64,256]{2,1,0:T(8,128)S(1)} %multiply_own.4.begun.refs_5_, bf16[16,64,256]{2,1,0:T(8,128)(2,1)S(1)} %collective-permute-done.10.received.refs_4_), custom_call_target="tpu_custom_call" | custom-call | tf_op jit(solution)/shard_map/multiply_early/pallas_call | solution.py:248
  33.9 5.2 %collective-permute-done.12.refs_1_ = bf16[16,64,256]{2,1,0:T(8,128)(2,1)S(1)} collective-permute-done((bf16[16,64,256]{2,1,0:T(8,128)(2,1)S(1)}, bf16[16,64,256]{2,1,0:T(8,128)(2,1)S(1)}, u32[]{:S(2)}, u32[]{:S(2)}) %collective-permute-start.12) | collective-permute-done | bytes 524320 | tf_op jit(solution)/shard_map/ppermute | solution.py:486
  39.1 2.0 %multiply_tiles.4 = (f32[32,64,256]{2,1,0:T(8,128)S(1)}, s16[528,256]{1,0:T(8,128)(2,1)S(1)}, s16[528,256]{1,0:T(8,128)(2,1)S(1)}) custom-call(s32[5,48]{1,0:T(8,128)S(1)} %get-tuple-element.59.table.refs_0_, bf16[48,256,256]{2,1,0:T(8,128)(2,1)S(1)} %get-tuple-element.60.tiles, f32[32,64,256]{2,1,0:T(8,128)S(1)} %multiply_early.2.begun, ...), custom_call_target="tpu_custom_call" | custom-call | tf_op jit(solution)/shard_map/multiply_tiles/pallas_call | solution.py:316
  41.6 1.0 %collective-permute-done.14.refs_1_ = s16[528,256]{1,0:T(8,128)(2,1)S(1)} collective-permute-done((s16[528,256]{1,0:T(8,128)(2,1)S(1)}, s16[528,256]{1,0:T(8,128)(2,1)S(1)}, u32[]{:S(2)}, u32[]{:S(2)}) %collective-permute-start.14) | collective-permute-done | bytes 270368 | tf_op jit(solution)/shard_map/ppermute | solution.py:449
  43.5 2.1 %collective-permute-start.15 = (s16[528,128]{1,0:T(8,128)(2,1)S(1)}, s16[528,128]{1,0:T(8,128)(2,1)S(1)}, u32[]{:S(2)}, u32[]{:S(2)}) collective-permute-start(s16[528,128]{1,0:T(8,128)(2,1)S(1)} %get-tuple-element.68), channel_id=1, source_target_pairs={{0,4},{2,6},{4,0},{6,2},{1,5},{3,7},{5,1},{7,3},{8,12},{10,14},{12... | collective-permute-start | bytes 405512 | tf_op jit(solution)/shard_map/ppermute | solution.py:452
  45.6 2.4 %collective-permute-start.16 = (s16[528,128]{1,0:T(8,128)(2,1)S(1)}, s16[528,128]{1,0:T(8,128)(2,1)S(1)}, u32[]{:S(2)}, u32[]{:S(2)}) collective-permute-start(s16[528,128]{1,0:T(8,128)(2,1)S(1)} %get-tuple-element.69), channel_id=1, source_target_pairs={{0,6},{2,4},{4,2},{6,0},{1,7},{3,5},{5,3},{7,1},{8,14},{10,12},{12... | collective-permute-start | bytes 405512 | tf_op jit(solution)/shard_map/ppermute | solution.py:452
  48.0 1.4 %collective-permute-done.18.received = bf16[16,64,256]{2,1,0:T(8,128)(2,1)S(1)} collective-permute-done((bf16[16,64,256]{2,1,0:T(8,128)(2,1)S(1)}, bf16[16,64,256]{2,1,0:T(8,128)(2,1)S(1)}, u32[]{:S(2)}, u32[]{:S(2)}) %collective-permute-start.18) | collective-permute-done | bytes 524320 | tf_op jit(solution)/shard_map/ppermute | solution.py:486
  49.3 1.7 %multiply_early.3.begun = f32[32,64,256]{2,1,0:T(8,128)S(1)} custom-call(s32[5,48]{1,0:T(8,128)S(1)} %get-tuple-element.59.table.refs_0_, bf16[48,256,256]{2,1,0:T(8,128)(2,1)S(1)} %get-tuple-element.60.tiles, f32[32,64,256]{2,1,0:T(8,128)S(1)} %multiply_own.5.refs_6_.begun, bf16[16,64,256]{2,1,0:T(8,128)(2,1)S(1)} %collective-permute-done.18.received), custom_call_target="tpu_custom_call" | custom-call | tf_op jit(solution)/shard_map/multiply_early/pallas_call | solution.py:248
  51.1 5.6 %collective-permute-done.15.refs_6_.refs_2_ = s16[528,128]{1,0:T(8,128)(2,1)S(1)} collective-permute-done((s16[528,128]{1,0:T(8,128)(2,1)S(1)}, s16[528,128]{1,0:T(8,128)(2,1)S(1)}, u32[]{:S(2)}, u32[]{:S(2)}) %collective-permute-start.15) | collective-permute-done | bytes 135200 | tf_op jit(solution)/shard_map/ppermute | solution.py:452
  56.7 0.7 collective-permute-done.19.refs_0_
  57.4 1.3 %collective-permute-done.20.refs_1_ = bf16[16,64,256]{2,1,0:T(8,128)(2,1)S(1)} collective-permute-done((bf16[16,64,256]{2,1,0:T(8,128)(2,1)S(1)}, bf16[16,64,256]{2,1,0:T(8,128)(2,1)S(1)}, u32[]{:S(2)}, u32[]{:S(2)}) %collective-permute-start.20) | collective-permute-done | bytes 524320 | tf_op jit(solution)/shard_map/ppermute | solution.py:486
  58.6 2.0 %multiply_tiles.5 = (f32[32,64,256]{2,1,0:T(8,128)S(1)}, s16[1056,256]{1,0:T(8,128)(2,1)S(1)}) custom-call(s32[5,48]{1,0:T(8,128)S(1)} %get-tuple-element.59.table.refs_0_, bf16[48,256,256]{2,1,0:T(8,128)(2,1)S(1)} %get-tuple-element.60.tiles, f32[32,64,256]{2,1,0:T(8,128)S(1)} %multiply_early.3.begun, ...), custom_call_target="tpu_custom_call" | custom-call | tf_op jit(solution)/shard_map/multiply_tiles/pallas_call | solution.py:316
  60.8 2.1 %collective-permute-start.17 = (s16[528,128]{1,0:T(8,128)(2,1)S(1)}, s16[528,128]{1,0:T(8,128)(2,1)S(1)}, u32[]{:S(2)}, u32[]{:S(2)}) collective-permute-start(s16[528,128]{1,0:T(8,128)(2,1)S(1)} %get-tuple-element.70), channel_id=1, source_target_pairs={{0,2},{2,0},{4,6},{6,4},{1,3},{3,1},{5,7},{7,5},{8,10},{10,8},{12,... | collective-permute-start | bytes 405512 | tf_op jit(solution)/shard_map/ppermute | solution.py:452
  63.3 2.2 %collective-permute-start.22 = (s16[528,128]{1,0:T(8,128)(2,1)S(1)}, s16[528,128]{1,0:T(8,128)(2,1)S(1)}, u32[]{:S(2)}, u32[]{:S(2)}) collective-permute-start(s16[528,128]{1,0:T(8,128)(2,1)S(1)} %get-tuple-element.80), channel_id=1, source_target_pairs={{0,4},{2,6},{4,0},{6,2},{1,5},{3,7},{5,1},{7,3},{8,12},{10,14},{12... | collective-permute-start | bytes 405512 | tf_op jit(solution)/shard_map/ppermute | solution.py:452
  65.5 2.1 %collective-permute-start.23 = (s16[528,128]{1,0:T(8,128)(2,1)S(1)}, s16[528,128]{1,0:T(8,128)(2,1)S(1)}, u32[]{:S(2)}, u32[]{:S(2)}) collective-permute-start(s16[528,128]{1,0:T(8,128)(2,1)S(1)} %get-tuple-element.81), channel_id=1, source_target_pairs={{0,6},{2,4},{4,2},{6,0},{1,7},{3,5},{5,3},{7,1},{8,14},{10,12},{12... | collective-permute-start | bytes 405512 | tf_op jit(solution)/shard_map/ppermute | solution.py:452
  67.6 2.8 %friction_solve.4 = (s32[1]{0:T(128)}, f32[128,1024]{1,0:T(8,128)}, f32[128,1024]{1,0:T(8,128)}) custom-call(s32[5,48]{1,0:T(8,128)S(1)} %get-tuple-element.59.table.refs_0_, f32[128,1024]{1,0:T(8,128)S(1)} %copy-done.7, f32[128,1024]{1,0:T(8,128)S(1)} %copy-done.8, f32[128,1024]{1,0:T(8,128)S(1)} %copy-done.9, f32[128,1024]{1,0:T(8,128)S(1)} %copy-done.12, ...), custom_call_target="tpu_custom_call" | custom-call | tf_op jit(solution)/shard_map/friction_solve/pallas_call | solution.py:433
  71.2 5.3 %collective-permute-done.22.refs_7_ = s16[528,128]{1,0:T(8,128)(2,1)S(1)} collective-permute-done((s16[528,128]{1,0:T(8,128)(2,1)S(1)}, s16[528,128]{1,0:T(8,128)(2,1)S(1)}, u32[]{:S(2)}, u32[]{:S(2)}) %collective-permute-start.22) | collective-permute-done | bytes 135200 | tf_op jit(solution)/shard_map/ppermute | solution.py:452
  76.7 1.7 %friction_solve.5 = (f32[128,1024]{1,0:T(8,128)}, f32[128,1024]{1,0:T(8,128)}) custom-call(f32[128,1024]{1,0:T(8,128)} %get-tuple-element.72.refs_0_, f32[128,1024]{1,0:T(8,128)} %get-tuple-element.73.refs_1_, f32[128,1024]{1,0:T(8,128)S(1)} %copy-done.7, f32[128,1024]{1,0:T(8,128)S(1)} %copy-done.8, ...), custom_call_target="tpu_custom_call", output_to_operand_aliasing={{0}: (0, {}), {1}: (1, {})} | custom-call | tf_op jit(solution)/shard_map/friction_solve/pallas_call | solution.py:433
  (40 shorter events, 3.7 us)
Async XLA Ops:
  2.0 6.3 %collective-permute-start.9 = (s32[4,32]{1,0:T(4,128)}, s32[4,32]{1,0:T(4,128)S(1)}, u32[]{:S(2)}, u32[]{:S(2)}) collective-permute-start(s32[4,32]{1,0:T(4,128)} %mark_blocks.1.refs_0_), channel_id=1, source_target_pairs={{0,24},{8,16},{16,8},{24,0},{1,25},{9,17},{17,9},{25,1},{2,26},{10... | collective-permute-start | bytes 1544 | tf_op jit(solution)/shard_map/ppermute | solution.py:474
  5.9 3.8 %collective-permute-start.8 = (s32[4,32]{1,0:T(4,128)}, s32[4,32]{1,0:T(4,128)S(1)}, u32[]{:S(2)}, u32[]{:S(2)}) collective-permute-start(s32[4,32]{1,0:T(4,128)} %mark_blocks.1.refs_0_), channel_id=1, source_target_pairs={{0,16},{8,24},{16,0},{24,8},{1,17},{9,25},{17,1},{25,9},{2,18},{10... | collective-permute-start | bytes 1544 | tf_op jit(solution)/shard_map/ppermute | solution.py:474
  6.4 3.8 %collective-permute-start.7 = (s32[4,32]{1,0:T(4,128)}, s32[4,32]{1,0:T(4,128)S(1)}, u32[]{:S(2)}, u32[]{:S(2)}) collective-permute-start(s32[4,32]{1,0:T(4,128)} %mark_blocks.1.refs_0_), channel_id=1, source_target_pairs={{0,8},{8,0},{16,24},{24,16},{1,9},{9,1},{17,25},{25,17},{2,10},{10... | collective-permute-start | bytes 1544 | tf_op jit(solution)/shard_map/ppermute | solution.py:474
  6.4 9.0 %copy-start = (bf16[1,1,4,12,256,256]{5,4,3,2,1,0:T(8,128)(2,1)S(1)}, bf16[1,1,4,12,256,256]{5,4,3,2,1,0:T(8,128)(2,1)}, u32[]{:S(2)}) copy-start(bf16[1,1,4,12,256,256]{5,4,3,2,1,0:T(8,128)(2,1)} %param.12) | copy-start | bytes 18874372
  8.2 7.3 %copy-start.1 = (s32[1,1,4,12]{3,2,1,0:T(4,128)S(1)}, s32[1,1,4,12]{3,2,1,0:T(4,128)}, u32[]{:S(2)}) copy-start(s32[1,1,4,12]{3,2,1,0:T(4,128)} %cols.3) | copy-start | bytes 580
  8.2 7.3 %copy-start.2 = (s32[4,32]{1,0:T(4,128)S(1)}, s32[4,32]{1,0:T(4,128)}, u32[]{:S(2)}) copy-start(s32[4,32]{1,0:T(4,128)} %mark_blocks.1.refs_0_) | copy-start | bytes 1540
  8.2 7.3 %copy-start.3 = (s32[1,1,4,12]{3,2,1,0:T(4,128)S(1)}, s32[1,1,4,12]{3,2,1,0:T(4,128)}, u32[]{:S(2)}) copy-start(s32[1,1,4,12]{3,2,1,0:T(4,128)} %rows.1) | copy-start | bytes 580
  8.2 7.2 %copy-start.4 = (s32[1,1,4]{2,1,0:T(1,128)S(1)}, s32[1,1,4]{2,1,0:T(1,128)}, u32[]{:S(2)}) copy-start(s32[1,1,4]{2,1,0:T(1,128)} %counts.3) | copy-start | bytes 52
  11.9 14.9 %collective-permute-start.10 = (bf16[16,64,256]{2,1,0:T(8,128)(2,1)S(1)}, bf16[16,64,256]{2,1,0:T(8,128)(2,1)S(1)}, u32[]{:S(2)}, u32[]{:S(2)}) collective-permute-start(bf16[16,64,256]{2,1,0:T(8,128)(2,1)S(1)} %get-tuple-element.61), channel_id=1, source_target_pairs={{0,8},{8,0},{16,24},{24,16},{1,9},{9,1},{17,25},{25,17},{2,10},{10... | collective-permute-start | bytes 1572872 | tf_op jit(solution)/shard_map/ppermute | solution.py:486
  12.0 21.8 %collective-permute-start.11 = (bf16[16,64,256]{2,1,0:T(8,128)(2,1)S(1)}, bf16[16,64,256]{2,1,0:T(8,128)(2,1)S(1)}, u32[]{:S(2)}, u32[]{:S(2)}) collective-permute-start(bf16[16,64,256]{2,1,0:T(8,128)(2,1)S(1)} %get-tuple-element.62), channel_id=1, source_target_pairs={{0,16},{8,24},{16,0},{24,8},{1,17},{9,25},{17,1},{25,9},{2,18},{10... | collective-permute-start | bytes 1572872 | tf_op jit(solution)/shard_map/ppermute | solution.py:486
  14.0 25.0 %collective-permute-start.12 = (bf16[16,64,256]{2,1,0:T(8,128)(2,1)S(1)}, bf16[16,64,256]{2,1,0:T(8,128)(2,1)S(1)}, u32[]{:S(2)}, u32[]{:S(2)}) collective-permute-start(bf16[16,64,256]{2,1,0:T(8,128)(2,1)S(1)} %get-tuple-element.63), channel_id=1, source_target_pairs={{0,24},{8,16},{16,8},{24,0},{1,25},{9,17},{17,9},{25,1},{2,26},{10... | collective-permute-start | bytes 1572872 | tf_op jit(solution)/shard_map/ppermute | solution.py:486
  28.6 20.8 %collective-permute-start.18 = (bf16[16,64,256]{2,1,0:T(8,128)(2,1)S(1)}, bf16[16,64,256]{2,1,0:T(8,128)(2,1)S(1)}, u32[]{:S(2)}, u32[]{:S(2)}) collective-permute-start(bf16[16,64,256]{2,1,0:T(8,128)(2,1)S(1)} %get-tuple-element.74), channel_id=1, source_target_pairs={{0,8},{8,0},{16,24},{24,16},{1,9},{9,1},{17,25},{25,17},{2,10},{10... | collective-permute-start | bytes 1572872 | tf_op jit(solution)/shard_map/ppermute | solution.py:486
  28.7 28.7 %collective-permute-start.19 = (bf16[16,64,256]{2,1,0:T(8,128)(2,1)S(1)}, bf16[16,64,256]{2,1,0:T(8,128)(2,1)S(1)}, u32[]{:S(2)}, u32[]{:S(2)}) collective-permute-start(bf16[16,64,256]{2,1,0:T(8,128)(2,1)S(1)} %get-tuple-element.75), channel_id=1, source_target_pairs={{0,16},{8,24},{16,0},{24,8},{1,17},{9,25},{17,1},{25,9},{2,18},{10... | collective-permute-start | bytes 1572872 | tf_op jit(solution)/shard_map/ppermute | solution.py:486
  30.7 27.9 %collective-permute-start.20 = (bf16[16,64,256]{2,1,0:T(8,128)(2,1)S(1)}, bf16[16,64,256]{2,1,0:T(8,128)(2,1)S(1)}, u32[]{:S(2)}, u32[]{:S(2)}) collective-permute-start(bf16[16,64,256]{2,1,0:T(8,128)(2,1)S(1)} %get-tuple-element.76), channel_id=1, source_target_pairs={{0,24},{8,16},{16,8},{24,0},{1,25},{9,17},{17,9},{25,1},{2,26},{10... | collective-permute-start | bytes 1572872 | tf_op jit(solution)/shard_map/ppermute | solution.py:486
  41.1 1.6 %collective-permute-start.14 = (s16[528,256]{1,0:T(8,128)(2,1)S(1)}, s16[528,256]{1,0:T(8,128)(2,1)S(1)}, u32[]{:S(2)}, u32[]{:S(2)}) collective-permute-start(s16[528,256]{1,0:T(8,128)(2,1)S(1)} %get-tuple-element.66), channel_id=1, source_target_pairs={{0,1},{1,0},{2,3},{3,2},{4,5},{5,4},{6,7},{7,6},{8,9},{9,8},{10,11... | collective-permute-start | bytes 811016 | tf_op jit(solution)/shard_map/ppermute | solution.py:449
  41.1 1.9 %collective-permute-start.13 = (s16[528,256]{1,0:T(8,128)(2,1)S(1)}, s16[528,256]{1,0:T(8,128)(2,1)S(1)}, u32[]{:S(2)}, u32[]{:S(2)}) collective-permute-start(s16[528,256]{1,0:T(8,128)(2,1)S(1)} %get-tuple-element.64.given), channel_id=1, source_target_pairs={{0,1},{1,0},{2,3},{3,2},{4,5},{5,4},{6,7},{7,6},{8,9},{9,8},{10,11... | collective-permute-start | bytes 811016 | tf_op jit(solution)/shard_map/ppermute | solution.py:449
  43.5 13.2 %collective-permute-start.15 = (s16[528,128]{1,0:T(8,128)(2,1)S(1)}, s16[528,128]{1,0:T(8,128)(2,1)S(1)}, u32[]{:S(2)}, u32[]{:S(2)}) collective-permute-start(s16[528,128]{1,0:T(8,128)(2,1)S(1)} %get-tuple-element.68), channel_id=1, source_target_pairs={{0,4},{2,6},{4,0},{6,2},{1,5},{3,7},{5,1},{7,3},{8,12},{10,14},{12... | collective-permute-start | bytes 405512 | tf_op jit(solution)/shard_map/ppermute | solution.py:452
  45.6 11.1 %collective-permute-start.16 = (s16[528,128]{1,0:T(8,128)(2,1)S(1)}, s16[528,128]{1,0:T(8,128)(2,1)S(1)}, u32[]{:S(2)}, u32[]{:S(2)}) collective-permute-start(s16[528,128]{1,0:T(8,128)(2,1)S(1)} %get-tuple-element.69), channel_id=1, source_target_pairs={{0,6},{2,4},{4,2},{6,0},{1,7},{3,5},{5,3},{7,1},{8,14},{10,12},{12... | collective-permute-start | bytes 405512 | tf_op jit(solution)/shard_map/ppermute | solution.py:452
  60.6 6.9 %copy-start.7 = (f32[128,1024]{1,0:T(8,128)S(1)}, f32[128,1024]{1,0:T(8,128)}, u32[]{:S(2)}) copy-start(f32[128,1024]{1,0:T(8,128)} %refs_2_.3) | copy-start | bytes 1572868
  60.6 6.9 %copy-start.8 = (f32[128,1024]{1,0:T(8,128)S(1)}, f32[128,1024]{1,0:T(8,128)}, u32[]{:S(2)}) copy-start(f32[128,1024]{1,0:T(8,128)} %refs_3_.3) | copy-start | bytes 1572868
  60.7 6.9 %copy-start.9 = (f32[128,1024]{1,0:T(8,128)S(1)}, f32[128,1024]{1,0:T(8,128)}, u32[]{:S(2)}) copy-start(f32[128,1024]{1,0:T(8,128)} %refs_4_.3) | copy-start | bytes 1572868
  60.7 6.9 %copy-start.12 = (f32[128,1024]{1,0:T(8,128)S(1)}, f32[128,1024]{1,0:T(8,128)}, u32[]{:S(2)}) copy-start(f32[128,1024]{1,0:T(8,128)} %refs_5_.1) | copy-start | bytes 1572868
  60.7 2.2 %collective-permute-start.21 = (s16[1056,256]{1,0:T(8,128)(2,1)S(1)}, s16[1056,256]{1,0:T(8,128)(2,1)S(1)}, u32[]{:S(2)}, u32[]{:S(2)}) collective-permute-start(s16[1056,256]{1,0:T(8,128)(2,1)S(1)} %get-tuple-element.77.given), channel_id=1, source_target_pairs={{0,1},{1,0},{2,3},{3,2},{4,5},{5,4},{6,7},{7,6},{8,9},{9,8},{10,11... | collective-permute-start | bytes 1622024 | tf_op jit(solution)/shard_map/ppermute | solution.py:449
  60.8 6.8 %collective-permute-start.17 = (s16[528,128]{1,0:T(8,128)(2,1)S(1)}, s16[528,128]{1,0:T(8,128)(2,1)S(1)}, u32[]{:S(2)}, u32[]{:S(2)}) collective-permute-start(s16[528,128]{1,0:T(8,128)(2,1)S(1)} %get-tuple-element.70), channel_id=1, source_target_pairs={{0,2},{2,0},{4,6},{6,4},{1,3},{3,1},{5,7},{7,5},{8,10},{10,8},{12,... | collective-permute-start | bytes 405512 | tf_op jit(solution)/shard_map/ppermute | solution.py:452
  63.3 13.2 %collective-permute-start.22 = (s16[528,128]{1,0:T(8,128)(2,1)S(1)}, s16[528,128]{1,0:T(8,128)(2,1)S(1)}, u32[]{:S(2)}, u32[]{:S(2)}) collective-permute-start(s16[528,128]{1,0:T(8,128)(2,1)S(1)} %get-tuple-element.80), channel_id=1, source_target_pairs={{0,4},{2,6},{4,0},{6,2},{1,5},{3,7},{5,1},{7,3},{8,12},{10,14},{12... | collective-permute-start | bytes 405512 | tf_op jit(solution)/shard_map/ppermute | solution.py:452
  65.5 11.1 %collective-permute-start.23 = (s16[528,128]{1,0:T(8,128)(2,1)S(1)}, s16[528,128]{1,0:T(8,128)(2,1)S(1)}, u32[]{:S(2)}, u32[]{:S(2)}) collective-permute-start(s16[528,128]{1,0:T(8,128)(2,1)S(1)} %get-tuple-element.81), channel_id=1, source_target_pairs={{0,6},{2,4},{4,2},{6,0},{1,7},{3,5},{5,3},{7,1},{8,14},{10,12},{12... | collective-permute-start | bytes 405512 | tf_op jit(solution)/shard_map/ppermute | solution.py:452
  67.6 9.2 %collective-permute-start.24 = (s16[528,128]{1,0:T(8,128)(2,1)S(1)}, s16[528,128]{1,0:T(8,128)(2,1)S(1)}, u32[]{:S(2)}, u32[]{:S(2)}) collective-permute-start(s16[528,128]{1,0:T(8,128)(2,1)S(1)} %get-tuple-element.82), channel_id=1, source_target_pairs={{0,2},{2,0},{4,6},{6,4},{1,3},{3,1},{5,7},{7,5},{8,10},{10,8},{12,... | collective-permute-start | bytes 405512 | tf_op jit(solution)/shard_map/ppermute | solution.py:452
  70.4 8.0 %copy-start.6 = (bf16[4,1,128,2048]{3,2,1,0:T(8,128)(2,1)S(1)}, bf16[4,1,128,2048]{3,2,1,0:T(8,128)(2,1)}, u32[]{:S(2)}) copy-start(bf16[4,1,128,2048]{3,2,1,0:T(8,128)(2,1)} %param.11) | copy-start | bytes 6291460

commit v9 on v8

--- a/solution.py
+++ b/solution.py
@@ -15,7 +15,7 @@
 LANES = 128
 OVER = 16
 SPLIT = 2
-GROUP = 8
+GROUP = 6
 ANY = pl.BlockSpec(memory_space=pl.ANY)
 SMEM = pl.BlockSpec(memory_space=pltpu.SMEM)
 VMEM = pl.BlockSpec(memory_space=pltpu.VMEM)

time: 79.5 us -> 79.8 us (level)
  starting transfers between devices: 23.1 us -> 22 us
  waiting for transfers between devices: 28.2 us -> 29.3 us
    pallas_call x2, Pallas kernels: 3.48 us -> 2.35 us  [multiply_early(): pl.pallas_call(early_kernel, out_shape=sums, in_specs=[SMEM, VMEM, VMEM,...]
    ppermute x6, starting transfers between devices: 10.9 us -> 9.83 us  [reduce(): lax.ppermute(coded[step - 1], 'col', partners(col_size, step))]
  transfers between devices with their start and end apart: 18 -> 18, of which waited for: 12 -> 13; matrix products, arithmetic and copies ran while one was open for 0% -> 0% of each run, Pallas kernels for 24% -> 23%
where the time goes in v9:
time: 79.8 us; the launch traced here: 78.6 us
  waiting for transfers between devices  29.3 us (37%)
  Pallas kernels  25.2 us (32%)
  starting transfers between devices  22 us (28%)
  between operations  1.88 us (2%)
    ppermute x6, waiting for transfers between devices, local(): lax.ppermute(packed[step - 1], 'row', partners(row_size, step))  14 us
    ppermute x6, waiting for transfers between devices, reduce(): lax.ppermute(coded[step - 1], 'col', partners(col_size, step))  11.7 us
    ppermute x6, starting transfers between devices, reduce(): lax.ppermute(coded[step - 1], 'col', partners(col_size, step))  9.83 us
    ppermute x6, starting transfers between devices, local(): lax.ppermute(packed[step - 1], 'row', partners(row_size, step))  7.11 us
    pallas_call x2, Pallas kernels, solve(): pl.pallas_call(functools.partial(solve_kernel, first, fresh), out_shape=f...  4.48 us
    ppermute x3, starting transfers between devices, local(): lax.ppermute(need, 'row', partners(row_size, step))  4.46 us
    pallas_call x2, Pallas kernels, multiply_tiles(): pl.pallas_call(functools.partial(tiles_kernel, first, whole, len(after),...  4.45 us
    pallas_call x2, Pallas kernels, pack(): pl.pallas_call(functools.partial(pack_kernel, cap, piece, side, len(after...  3.46 us
  transfers between devices with their start and end apart: 18, of which 13 were waited for; matrix products, arithmetic and copies ran while one was open for 0% of the time, Pallas kernels for 23%

profile of v9, /device:TPU:0, one launch (start us, length us, event | category | flops | bytes accessed | tf_op | source)
XLA Modules:
  0.0 78.6 jit_solution(2317312311828334578)
XLA Ops:
  0.6 1.3 %mark_blocks.1.refs_0_ = s32[4,32]{1,0:T(4,128)} custom-call(s32[1,1,4,12]{3,2,1,0:T(4,128)} %cols.3, s32[1,1,4]{2,1,0:T(1,128)} %counts.3), custom_call_target="tpu_custom_call" | custom-call | tf_op jit(solution)/shard_map/mark_blocks/pallas_call | solution.py:65
  2.0 3.9 %collective-permute-start.9 = (s32[4,32]{1,0:T(4,128)}, s32[4,32]{1,0:T(4,128)S(1)}, u32[]{:S(2)}, u32[]{:S(2)}) collective-permute-start(s32[4,32]{1,0:T(4,128)} %mark_blocks.1.refs_0_), channel_id=1, source_target_pairs={{0,24},{8,16},{16,8},{24,0},{1,25},{9,17},{17,9},{25,1},{2,26},{10... | collective-permute-start | bytes 1544 | tf_op jit(solution)/shard_map/ppermute | solution.py:474
  5.9 0.5 collective-permute-start.8
  6.4 1.7 %load_history.1.history.refs_3_ = bf16[4,128,2048]{2,1,0:T(8,128)(2,1)S(1)} custom-call(bf16[4,128,2048]{2,1,0:T(8,128)(2,1)} %bitcast.6), custom_call_target="tpu_custom_call" | custom-call | tf_op jit(solution)/shard_map/load_history/pallas_call | solution.py:81
  8.2 1.4 %collective-permute-done.8.refs_2_.refs_1_ = s32[4,32]{1,0:T(4,128)S(1)} collective-permute-done((s32[4,32]{1,0:T(4,128)}, s32[4,32]{1,0:T(4,128)S(1)}, u32[]{:S(2)}, u32[]{:S(2)}) %collective-permute-start.8) | collective-permute-done | bytes 544 | tf_op jit(solution)/shard_map/ppermute | solution.py:474
  10.2 1.7 %pack_history.2 = (bf16[16,64,256]{2,1,0:T(8,128)(2,1)S(1)}, bf16[16,64,256]{2,1,0:T(8,128)(2,1)S(1)}, bf16[16,64,256]{2,1,0:T(8,128)(2,1)S(1)}) custom-call(s32[4,32]{1,0:T(4,128)S(1)} %collective-permute-done.7.refs_1_.refs_0_, s32[4,32]{1,0:T(4,128)S(1)} %collective-permute-done.8.refs_2_.refs_1_, s32[4,32]{1,0:T(4,128)S(1)} %collective-permute-done.9.refs_3_.refs_2_, ...), custom_call_target="tpu_custom_call" | custom-call | tf_op jit(solution)/shard_map/pack_history/pallas_call | solution.py:116
  12.0 2.0 %collective-permute-start.11 = (bf16[16,64,256]{2,1,0:T(8,128)(2,1)S(1)}, bf16[16,64,256]{2,1,0:T(8,128)(2,1)S(1)}, u32[]{:S(2)}, u32[]{:S(2)}) collective-permute-start(bf16[16,64,256]{2,1,0:T(8,128)(2,1)S(1)} %get-tuple-element.62), channel_id=1, source_target_pairs={{0,16},{8,24},{16,0},{24,8},{1,17},{9,25},{17,1},{25,9},{2,18},{10... | collective-permute-start | bytes 1572872 | tf_op jit(solution)/shard_map/ppermute | solution.py:486
  14.0 1.4 %collective-permute-start.12 = (bf16[16,64,256]{2,1,0:T(8,128)(2,1)S(1)}, bf16[16,64,256]{2,1,0:T(8,128)(2,1)S(1)}, u32[]{:S(2)}, u32[]{:S(2)}) collective-permute-start(bf16[16,64,256]{2,1,0:T(8,128)(2,1)S(1)} %get-tuple-element.63), channel_id=1, source_target_pairs={{0,24},{8,16},{16,8},{24,0},{1,25},{9,17},{17,9},{25,1},{2,26},{10... | collective-permute-start | bytes 1572872 | tf_op jit(solution)/shard_map/ppermute | solution.py:486
  15.5 3.4 %plan_tiles.1 = (s32[5,48]{1,0:T(8,128)S(1)}, bf16[48,256,256]{2,1,0:T(8,128)(2,1)S(1)}) custom-call(s32[1,1,4,12]{3,2,1,0:T(4,128)S(1)} %copy-done.1, s32[1,1,4,12]{3,2,1,0:T(4,128)S(1)} %copy-done.3, s32[1,1,4]{2,1,0:T(1,128)S(1)} %copy-done.4, s32[4,32]{1,0:T(4,128)S(1)} %copy-done.2, s32[4,32]{1,0:T(4,128)S(1)} %collective-permute-done.7.refs_1_.refs_0_, ...), custom_call_target="tpu_custom_call" | custom-call | tf_op jit(solution)/shard_map/plan_tiles/pallas_call | solution.py:186
  18.9 1.6 %multiply_own.5.refs_6_.begun = f32[32,64,256]{2,1,0:T(8,128)S(1)} custom-call(s32[5,48]{1,0:T(8,128)S(1)} %get-tuple-element.59.table.refs_0_, bf16[48,256,256]{2,1,0:T(8,128)(2,1)S(1)} %get-tuple-element.60.tiles, bf16[4,128,2048]{2,1,0:T(8,128)(2,1)S(1)} %load_history.1.history.refs_3_), custom_call_target="tpu_custom_call" | custom-call | tf_op jit(solution)/shard_map/multiply_own/pallas_call | solution.py:299
  20.5 1.6 %multiply_own.4.begun.refs_5_ = f32[32,64,256]{2,1,0:T(8,128)S(1)} custom-call(s32[5,48]{1,0:T(8,128)S(1)} %get-tuple-element.59.table.refs_0_, bf16[48,256,256]{2,1,0:T(8,128)(2,1)S(1)} %get-tuple-element.60.tiles, bf16[4,128,2048]{2,1,0:T(8,128)(2,1)S(1)} %load_history.1.history.refs_3_), custom_call_target="tpu_custom_call" | custom-call | tf_op jit(solution)/shard_map/multiply_own/pallas_call | solution.py:299
  22.0 4.8 %collective-permute-done.10.received.refs_4_ = bf16[16,64,256]{2,1,0:T(8,128)(2,1)S(1)} collective-permute-done((bf16[16,64,256]{2,1,0:T(8,128)(2,1)S(1)}, bf16[16,64,256]{2,1,0:T(8,128)(2,1)S(1)}, u32[]{:S(2)}, u32[]{:S(2)}) %collective-permute-start.10) | collective-permute-done | bytes 524320 | tf_op jit(solution)/shard_map/ppermute | solution.py:486
  26.8 1.7 %pack_history.3 = (bf16[16,64,256]{2,1,0:T(8,128)(2,1)S(1)}, bf16[16,64,256]{2,1,0:T(8,128)(2,1)S(1)}, bf16[16,64,256]{2,1,0:T(8,128)(2,1)S(1)}) custom-call(s32[4,32]{1,0:T(4,128)S(1)} %collective-permute-done.7.refs_1_.refs_0_, s32[4,32]{1,0:T(4,128)S(1)} %collective-permute-done.8.refs_2_.refs_1_, s32[4,32]{1,0:T(4,128)S(1)} %collective-permute-done.9.refs_3_.refs_2_, ...), custom_call_target="tpu_custom_call" | custom-call | tf_op jit(solution)/shard_map/pack_history/pallas_call | solution.py:116
  28.7 2.0 %collective-permute-start.19 = (bf16[16,64,256]{2,1,0:T(8,128)(2,1)S(1)}, bf16[16,64,256]{2,1,0:T(8,128)(2,1)S(1)}, u32[]{:S(2)}, u32[]{:S(2)}) collective-permute-start(bf16[16,64,256]{2,1,0:T(8,128)(2,1)S(1)} %get-tuple-element.75), channel_id=1, source_target_pairs={{0,16},{8,24},{16,0},{24,8},{1,17},{9,25},{17,1},{25,9},{2,18},{10... | collective-permute-start | bytes 1572872 | tf_op jit(solution)/shard_map/ppermute | solution.py:486
  30.7 1.4 %collective-permute-start.20 = (bf16[16,64,256]{2,1,0:T(8,128)(2,1)S(1)}, bf16[16,64,256]{2,1,0:T(8,128)(2,1)S(1)}, u32[]{:S(2)}, u32[]{:S(2)}) collective-permute-start(bf16[16,64,256]{2,1,0:T(8,128)(2,1)S(1)} %get-tuple-element.76), channel_id=1, source_target_pairs={{0,24},{8,16},{16,8},{24,0},{1,25},{9,17},{17,9},{25,1},{2,26},{10... | collective-permute-start | bytes 1572872 | tf_op jit(solution)/shard_map/ppermute | solution.py:486
  32.1 1.2 %multiply_early.2.begun = f32[32,64,256]{2,1,0:T(8,128)S(1)} custom-call(s32[5,48]{1,0:T(8,128)S(1)} %get-tuple-element.59.table.refs_0_, bf16[48,256,256]{2,1,0:T(8,128)(2,1)S(1)} %get-tuple-element.60.tiles, f32[32,64,256]{2,1,0:T(8,128)S(1)} %multiply_own.4.begun.refs_5_, bf16[16,64,256]{2,1,0:T(8,128)(2,1)S(1)} %collective-permute-done.10.received.refs_4_), custom_call_target="tpu_custom_call" | custom-call | tf_op jit(solution)/shard_map/multiply_early/pallas_call | solution.py:248
  33.6 5.5 %collective-permute-done.12.refs_1_ = bf16[16,64,256]{2,1,0:T(8,128)(2,1)S(1)} collective-permute-done((bf16[16,64,256]{2,1,0:T(8,128)(2,1)S(1)}, bf16[16,64,256]{2,1,0:T(8,128)(2,1)S(1)}, u32[]{:S(2)}, u32[]{:S(2)}) %collective-permute-start.12) | collective-permute-done | bytes 524320 | tf_op jit(solution)/shard_map/ppermute | solution.py:486
  39.1 2.2 %multiply_tiles.4 = (f32[32,64,256]{2,1,0:T(8,128)S(1)}, s16[528,256]{1,0:T(8,128)(2,1)S(1)}, s16[528,256]{1,0:T(8,128)(2,1)S(1)}) custom-call(s32[5,48]{1,0:T(8,128)S(1)} %get-tuple-element.59.table.refs_0_, bf16[48,256,256]{2,1,0:T(8,128)(2,1)S(1)} %get-tuple-element.60.tiles, f32[32,64,256]{2,1,0:T(8,128)S(1)} %multiply_early.2.begun, ...), custom_call_target="tpu_custom_call" | custom-call | tf_op jit(solution)/shard_map/multiply_tiles/pallas_call | solution.py:316
  41.9 1.0 %collective-permute-done.14.refs_1_ = s16[528,256]{1,0:T(8,128)(2,1)S(1)} collective-permute-done((s16[528,256]{1,0:T(8,128)(2,1)S(1)}, s16[528,256]{1,0:T(8,128)(2,1)S(1)}, u32[]{:S(2)}, u32[]{:S(2)}) %collective-permute-start.14) | collective-permute-done | bytes 270368 | tf_op jit(solution)/shard_map/ppermute | solution.py:449
  43.7 2.2 %collective-permute-start.15 = (s16[528,128]{1,0:T(8,128)(2,1)S(1)}, s16[528,128]{1,0:T(8,128)(2,1)S(1)}, u32[]{:S(2)}, u32[]{:S(2)}) collective-permute-start(s16[528,128]{1,0:T(8,128)(2,1)S(1)} %get-tuple-element.68), channel_id=1, source_target_pairs={{0,4},{2,6},{4,0},{6,2},{1,5},{3,7},{5,1},{7,3},{8,12},{10,14},{12... | collective-permute-start | bytes 405512 | tf_op jit(solution)/shard_map/ppermute | solution.py:452
  45.9 1.7 %collective-permute-start.16 = (s16[528,128]{1,0:T(8,128)(2,1)S(1)}, s16[528,128]{1,0:T(8,128)(2,1)S(1)}, u32[]{:S(2)}, u32[]{:S(2)}) collective-permute-start(s16[528,128]{1,0:T(8,128)(2,1)S(1)} %get-tuple-element.69), channel_id=1, source_target_pairs={{0,6},{2,4},{4,2},{6,0},{1,7},{3,5},{5,3},{7,1},{8,14},{10,12},{12... | collective-permute-start | bytes 405512 | tf_op jit(solution)/shard_map/ppermute | solution.py:452
  47.7 1.7 %collective-permute-done.18.received = bf16[16,64,256]{2,1,0:T(8,128)(2,1)S(1)} collective-permute-done((bf16[16,64,256]{2,1,0:T(8,128)(2,1)S(1)}, bf16[16,64,256]{2,1,0:T(8,128)(2,1)S(1)}, u32[]{:S(2)}, u32[]{:S(2)}) %collective-permute-start.18) | collective-permute-done | bytes 524320 | tf_op jit(solution)/shard_map/ppermute | solution.py:486
  49.3 1.2 %multiply_early.3.begun = f32[32,64,256]{2,1,0:T(8,128)S(1)} custom-call(s32[5,48]{1,0:T(8,128)S(1)} %get-tuple-element.59.table.refs_0_, bf16[48,256,256]{2,1,0:T(8,128)(2,1)S(1)} %get-tuple-element.60.tiles, f32[32,64,256]{2,1,0:T(8,128)S(1)} %multiply_own.5.refs_6_.begun, bf16[16,64,256]{2,1,0:T(8,128)(2,1)S(1)} %collective-permute-done.18.received), custom_call_target="tpu_custom_call" | custom-call | tf_op jit(solution)/shard_map/multiply_early/pallas_call | solution.py:248
  50.5 6.3 %collective-permute-done.15.refs_6_.refs_2_ = s16[528,128]{1,0:T(8,128)(2,1)S(1)} collective-permute-done((s16[528,128]{1,0:T(8,128)(2,1)S(1)}, s16[528,128]{1,0:T(8,128)(2,1)S(1)}, u32[]{:S(2)}, u32[]{:S(2)}) %collective-permute-start.15) | collective-permute-done | bytes 135200 | tf_op jit(solution)/shard_map/ppermute | solution.py:452
  57.4 1.3 %collective-permute-done.20.refs_1_ = bf16[16,64,256]{2,1,0:T(8,128)(2,1)S(1)} collective-permute-done((bf16[16,64,256]{2,1,0:T(8,128)(2,1)S(1)}, bf16[16,64,256]{2,1,0:T(8,128)(2,1)S(1)}, u32[]{:S(2)}, u32[]{:S(2)}) %collective-permute-start.20) | collective-permute-done | bytes 524320 | tf_op jit(solution)/shard_map/ppermute | solution.py:486
  58.6 2.2 %multiply_tiles.5 = (f32[32,64,256]{2,1,0:T(8,128)S(1)}, s16[1056,256]{1,0:T(8,128)(2,1)S(1)}) custom-call(s32[5,48]{1,0:T(8,128)S(1)} %get-tuple-element.59.table.refs_0_, bf16[48,256,256]{2,1,0:T(8,128)(2,1)S(1)} %get-tuple-element.60.tiles, f32[32,64,256]{2,1,0:T(8,128)S(1)} %multiply_early.3.begun, ...), custom_call_target="tpu_custom_call" | custom-call | tf_op jit(solution)/shard_map/multiply_tiles/pallas_call | solution.py:316
  61.0 1.6 %collective-permute-start.17 = (s16[528,128]{1,0:T(8,128)(2,1)S(1)}, s16[528,128]{1,0:T(8,128)(2,1)S(1)}, u32[]{:S(2)}, u32[]{:S(2)}) collective-permute-start(s16[528,128]{1,0:T(8,128)(2,1)S(1)} %get-tuple-element.70), channel_id=1, source_target_pairs={{0,2},{2,0},{4,6},{6,4},{1,3},{3,1},{5,7},{7,5},{8,10},{10,8},{12,... | collective-permute-start | bytes 405512 | tf_op jit(solution)/shard_map/ppermute | solution.py:452
  63.3 2.4 %collective-permute-start.22 = (s16[528,128]{1,0:T(8,128)(2,1)S(1)}, s16[528,128]{1,0:T(8,128)(2,1)S(1)}, u32[]{:S(2)}, u32[]{:S(2)}) collective-permute-start(s16[528,128]{1,0:T(8,128)(2,1)S(1)} %get-tuple-element.80), channel_id=1, source_target_pairs={{0,4},{2,6},{4,0},{6,2},{1,5},{3,7},{5,1},{7,3},{8,12},{10,14},{12... | collective-permute-start | bytes 405512 | tf_op jit(solution)/shard_map/ppermute | solution.py:452
  65.7 1.6 %collective-permute-start.23 = (s16[528,128]{1,0:T(8,128)(2,1)S(1)}, s16[528,128]{1,0:T(8,128)(2,1)S(1)}, u32[]{:S(2)}, u32[]{:S(2)}) collective-permute-start(s16[528,128]{1,0:T(8,128)(2,1)S(1)} %get-tuple-element.81), channel_id=1, source_target_pairs={{0,6},{2,4},{4,2},{6,0},{1,7},{3,5},{5,3},{7,1},{8,14},{10,12},{12... | collective-permute-start | bytes 405512 | tf_op jit(solution)/shard_map/ppermute | solution.py:452
  67.5 2.8 %friction_solve.4 = (s32[1]{0:T(128)}, f32[128,1024]{1,0:T(8,128)}, f32[128,1024]{1,0:T(8,128)}) custom-call(s32[5,48]{1,0:T(8,128)S(1)} %get-tuple-element.59.table.refs_0_, f32[128,1024]{1,0:T(8,128)S(1)} %copy-done.7, f32[128,1024]{1,0:T(8,128)S(1)} %copy-done.8, f32[128,1024]{1,0:T(8,128)S(1)} %copy-done.9, f32[128,1024]{1,0:T(8,128)S(1)} %copy-done.12, ...), custom_call_target="tpu_custom_call" | custom-call | tf_op jit(solution)/shard_map/friction_solve/pallas_call | solution.py:433
  71.2 5.3 %collective-permute-done.22.refs_7_ = s16[528,128]{1,0:T(8,128)(2,1)S(1)} collective-permute-done((s16[528,128]{1,0:T(8,128)(2,1)S(1)}, s16[528,128]{1,0:T(8,128)(2,1)S(1)}, u32[]{:S(2)}, u32[]{:S(2)}) %collective-permute-start.22) | collective-permute-done | bytes 135200 | tf_op jit(solution)/shard_map/ppermute | solution.py:452
  76.5 1.7 %friction_solve.5 = (f32[128,1024]{1,0:T(8,128)}, f32[128,1024]{1,0:T(8,128)}) custom-call(f32[128,1024]{1,0:T(8,128)} %get-tuple-element.72.refs_0_, f32[128,1024]{1,0:T(8,128)} %get-tuple-element.73.refs_1_, f32[128,1024]{1,0:T(8,128)S(1)} %copy-done.7, f32[128,1024]{1,0:T(8,128)S(1)} %copy-done.8, ...), custom_call_target="tpu_custom_call", output_to_operand_aliasing={{0}: (0, {}), {1}: (1, {})} | custom-call | tf_op jit(solution)/shard_map/friction_solve/pallas_call | solution.py:433
  (40 shorter events, 4.2 us)
Async XLA Ops:
  2.0 6.3 %collective-permute-start.9 = (s32[4,32]{1,0:T(4,128)}, s32[4,32]{1,0:T(4,128)S(1)}, u32[]{:S(2)}, u32[]{:S(2)}) collective-permute-start(s32[4,32]{1,0:T(4,128)} %mark_blocks.1.refs_0_), channel_id=1, source_target_pairs={{0,24},{8,16},{16,8},{24,0},{1,25},{9,17},{17,9},{25,1},{2,26},{10... | collective-permute-start | bytes 1544 | tf_op jit(solution)/shard_map/ppermute | solution.py:474
  5.9 3.8 %collective-permute-start.8 = (s32[4,32]{1,0:T(4,128)}, s32[4,32]{1,0:T(4,128)S(1)}, u32[]{:S(2)}, u32[]{:S(2)}) collective-permute-start(s32[4,32]{1,0:T(4,128)} %mark_blocks.1.refs_0_), channel_id=1, source_target_pairs={{0,16},{8,24},{16,0},{24,8},{1,17},{9,25},{17,1},{25,9},{2,18},{10... | collective-permute-start | bytes 1544 | tf_op jit(solution)/shard_map/ppermute | solution.py:474
  6.4 3.8 %collective-permute-start.7 = (s32[4,32]{1,0:T(4,128)}, s32[4,32]{1,0:T(4,128)S(1)}, u32[]{:S(2)}, u32[]{:S(2)}) collective-permute-start(s32[4,32]{1,0:T(4,128)} %mark_blocks.1.refs_0_), channel_id=1, source_target_pairs={{0,8},{8,0},{16,24},{24,16},{1,9},{9,1},{17,25},{25,17},{2,10},{10... | collective-permute-start | bytes 1544 | tf_op jit(solution)/shard_map/ppermute | solution.py:474
  6.4 9.0 %copy-start = (bf16[1,1,4,12,256,256]{5,4,3,2,1,0:T(8,128)(2,1)S(1)}, bf16[1,1,4,12,256,256]{5,4,3,2,1,0:T(8,128)(2,1)}, u32[]{:S(2)}) copy-start(bf16[1,1,4,12,256,256]{5,4,3,2,1,0:T(8,128)(2,1)} %param.12) | copy-start | bytes 18874372
  8.2 7.3 %copy-start.1 = (s32[1,1,4,12]{3,2,1,0:T(4,128)S(1)}, s32[1,1,4,12]{3,2,1,0:T(4,128)}, u32[]{:S(2)}) copy-start(s32[1,1,4,12]{3,2,1,0:T(4,128)} %cols.3) | copy-start | bytes 580
  8.2 7.3 %copy-start.2 = (s32[4,32]{1,0:T(4,128)S(1)}, s32[4,32]{1,0:T(4,128)}, u32[]{:S(2)}) copy-start(s32[4,32]{1,0:T(4,128)} %mark_blocks.1.refs_0_) | copy-start | bytes 1540
  8.2 7.3 %copy-start.3 = (s32[1,1,4,12]{3,2,1,0:T(4,128)S(1)}, s32[1,1,4,12]{3,2,1,0:T(4,128)}, u32[]{:S(2)}) copy-start(s32[1,1,4,12]{3,2,1,0:T(4,128)} %rows.1) | copy-start | bytes 580
  8.2 7.3 %copy-start.4 = (s32[1,1,4]{2,1,0:T(1,128)S(1)}, s32[1,1,4]{2,1,0:T(1,128)}, u32[]{:S(2)}) copy-start(s32[1,1,4]{2,1,0:T(1,128)} %counts.3) | copy-start | bytes 52
  11.9 14.9 %collective-permute-start.10 = (bf16[16,64,256]{2,1,0:T(8,128)(2,1)S(1)}, bf16[16,64,256]{2,1,0:T(8,128)(2,1)S(1)}, u32[]{:S(2)}, u32[]{:S(2)}) collective-permute-start(bf16[16,64,256]{2,1,0:T(8,128)(2,1)S(1)} %get-tuple-element.61), channel_id=1, source_target_pairs={{0,8},{8,0},{16,24},{24,16},{1,9},{9,1},{17,25},{25,17},{2,10},{10... | collective-permute-start | bytes 1572872 | tf_op jit(solution)/shard_map/ppermute | solution.py:486
  12.0 21.6 %collective-permute-start.11 = (bf16[16,64,256]{2,1,0:T(8,128)(2,1)S(1)}, bf16[16,64,256]{2,1,0:T(8,128)(2,1)S(1)}, u32[]{:S(2)}, u32[]{:S(2)}) collective-permute-start(bf16[16,64,256]{2,1,0:T(8,128)(2,1)S(1)} %get-tuple-element.62), channel_id=1, source_target_pairs={{0,16},{8,24},{16,0},{24,8},{1,17},{9,25},{17,1},{25,9},{2,18},{10... | collective-permute-start | bytes 1572872 | tf_op jit(solution)/shard_map/ppermute | solution.py:486
  14.0 25.0 %collective-permute-start.12 = (bf16[16,64,256]{2,1,0:T(8,128)(2,1)S(1)}, bf16[16,64,256]{2,1,0:T(8,128)(2,1)S(1)}, u32[]{:S(2)}, u32[]{:S(2)}) collective-permute-start(bf16[16,64,256]{2,1,0:T(8,128)(2,1)S(1)} %get-tuple-element.63), channel_id=1, source_target_pairs={{0,24},{8,16},{16,8},{24,0},{1,25},{9,17},{17,9},{25,1},{2,26},{10... | collective-permute-start | bytes 1572872 | tf_op jit(solution)/shard_map/ppermute | solution.py:486
  28.6 20.8 %collective-permute-start.18 = (bf16[16,64,256]{2,1,0:T(8,128)(2,1)S(1)}, bf16[16,64,256]{2,1,0:T(8,128)(2,1)S(1)}, u32[]{:S(2)}, u32[]{:S(2)}) collective-permute-start(bf16[16,64,256]{2,1,0:T(8,128)(2,1)S(1)} %get-tuple-element.74), channel_id=1, source_target_pairs={{0,8},{8,0},{16,24},{24,16},{1,9},{9,1},{17,25},{25,17},{2,10},{10... | collective-permute-start | bytes 1572872 | tf_op jit(solution)/shard_map/ppermute | solution.py:486
  28.7 28.6 %collective-permute-start.19 = (bf16[16,64,256]{2,1,0:T(8,128)(2,1)S(1)}, bf16[16,64,256]{2,1,0:T(8,128)(2,1)S(1)}, u32[]{:S(2)}, u32[]{:S(2)}) collective-permute-start(bf16[16,64,256]{2,1,0:T(8,128)(2,1)S(1)} %get-tuple-element.75), channel_id=1, source_target_pairs={{0,16},{8,24},{16,0},{24,8},{1,17},{9,25},{17,1},{25,9},{2,18},{10... | collective-permute-start | bytes 1572872 | tf_op jit(solution)/shard_map/ppermute | solution.py:486
  30.7 27.9 %collective-permute-start.20 = (bf16[16,64,256]{2,1,0:T(8,128)(2,1)S(1)}, bf16[16,64,256]{2,1,0:T(8,128)(2,1)S(1)}, u32[]{:S(2)}, u32[]{:S(2)}) collective-permute-start(bf16[16,64,256]{2,1,0:T(8,128)(2,1)S(1)} %get-tuple-element.76), channel_id=1, source_target_pairs={{0,24},{8,16},{16,8},{24,0},{1,25},{9,17},{17,9},{25,1},{2,26},{10... | collective-permute-start | bytes 1572872 | tf_op jit(solution)/shard_map/ppermute | solution.py:486
  41.3 1.6 %collective-permute-start.14 = (s16[528,256]{1,0:T(8,128)(2,1)S(1)}, s16[528,256]{1,0:T(8,128)(2,1)S(1)}, u32[]{:S(2)}, u32[]{:S(2)}) collective-permute-start(s16[528,256]{1,0:T(8,128)(2,1)S(1)} %get-tuple-element.66), channel_id=1, source_target_pairs={{0,1},{1,0},{2,3},{3,2},{4,5},{5,4},{6,7},{7,6},{8,9},{9,8},{10,11... | collective-permute-start | bytes 811016 | tf_op jit(solution)/shard_map/ppermute | solution.py:449
  41.4 1.9 %collective-permute-start.13 = (s16[528,256]{1,0:T(8,128)(2,1)S(1)}, s16[528,256]{1,0:T(8,128)(2,1)S(1)}, u32[]{:S(2)}, u32[]{:S(2)}) collective-permute-start(s16[528,256]{1,0:T(8,128)(2,1)S(1)} %get-tuple-element.64.given), channel_id=1, source_target_pairs={{0,1},{1,0},{2,3},{3,2},{4,5},{5,4},{6,7},{7,6},{8,9},{9,8},{10,11... | collective-permute-start | bytes 811016 | tf_op jit(solution)/shard_map/ppermute | solution.py:449
  43.7 13.2 %collective-permute-start.15 = (s16[528,128]{1,0:T(8,128)(2,1)S(1)}, s16[528,128]{1,0:T(8,128)(2,1)S(1)}, u32[]{:S(2)}, u32[]{:S(2)}) collective-permute-start(s16[528,128]{1,0:T(8,128)(2,1)S(1)} %get-tuple-element.68), channel_id=1, source_target_pairs={{0,4},{2,6},{4,0},{6,2},{1,5},{3,7},{5,1},{7,3},{8,12},{10,14},{12... | collective-permute-start | bytes 405512 | tf_op jit(solution)/shard_map/ppermute | solution.py:452
  45.9 11.0 %collective-permute-start.16 = (s16[528,128]{1,0:T(8,128)(2,1)S(1)}, s16[528,128]{1,0:T(8,128)(2,1)S(1)}, u32[]{:S(2)}, u32[]{:S(2)}) collective-permute-start(s16[528,128]{1,0:T(8,128)(2,1)S(1)} %get-tuple-element.69), channel_id=1, source_target_pairs={{0,6},{2,4},{4,2},{6,0},{1,7},{3,5},{5,3},{7,1},{8,14},{10,12},{12... | collective-permute-start | bytes 405512 | tf_op jit(solution)/shard_map/ppermute | solution.py:452
  60.9 6.7 %copy-start.7 = (f32[128,1024]{1,0:T(8,128)S(1)}, f32[128,1024]{1,0:T(8,128)}, u32[]{:S(2)}) copy-start(f32[128,1024]{1,0:T(8,128)} %refs_2_.3) | copy-start | bytes 1572868
  60.9 6.7 %copy-start.8 = (f32[128,1024]{1,0:T(8,128)S(1)}, f32[128,1024]{1,0:T(8,128)}, u32[]{:S(2)}) copy-start(f32[128,1024]{1,0:T(8,128)} %refs_3_.3) | copy-start | bytes 1572868
  60.9 6.6 %copy-start.9 = (f32[128,1024]{1,0:T(8,128)S(1)}, f32[128,1024]{1,0:T(8,128)}, u32[]{:S(2)}) copy-start(f32[128,1024]{1,0:T(8,128)} %refs_4_.3) | copy-start | bytes 1572868
  60.9 6.6 %copy-start.12 = (f32[128,1024]{1,0:T(8,128)S(1)}, f32[128,1024]{1,0:T(8,128)}, u32[]{:S(2)}) copy-start(f32[128,1024]{1,0:T(8,128)} %refs_5_.1) | copy-start | bytes 1572868
  60.9 2.0 %collective-permute-start.21 = (s16[1056,256]{1,0:T(8,128)(2,1)S(1)}, s16[1056,256]{1,0:T(8,128)(2,1)S(1)}, u32[]{:S(2)}, u32[]{:S(2)}) collective-permute-start(s16[1056,256]{1,0:T(8,128)(2,1)S(1)} %get-tuple-element.77.given), channel_id=1, source_target_pairs={{0,1},{1,0},{2,3},{3,2},{4,5},{5,4},{6,7},{7,6},{8,9},{9,8},{10,11... | collective-permute-start | bytes 1622024 | tf_op jit(solution)/shard_map/ppermute | solution.py:449
  61.0 6.5 %collective-permute-start.17 = (s16[528,128]{1,0:T(8,128)(2,1)S(1)}, s16[528,128]{1,0:T(8,128)(2,1)S(1)}, u32[]{:S(2)}, u32[]{:S(2)}) collective-permute-start(s16[528,128]{1,0:T(8,128)(2,1)S(1)} %get-tuple-element.70), channel_id=1, source_target_pairs={{0,2},{2,0},{4,6},{6,4},{1,3},{3,1},{5,7},{7,5},{8,10},{10,8},{12,... | collective-permute-start | bytes 405512 | tf_op jit(solution)/shard_map/ppermute | solution.py:452
  63.3 13.2 %collective-permute-start.22 = (s16[528,128]{1,0:T(8,128)(2,1)S(1)}, s16[528,128]{1,0:T(8,128)(2,1)S(1)}, u32[]{:S(2)}, u32[]{:S(2)}) collective-permute-start(s16[528,128]{1,0:T(8,128)(2,1)S(1)} %get-tuple-element.80), channel_id=1, source_target_pairs={{0,4},{2,6},{4,0},{6,2},{1,5},{3,7},{5,1},{7,3},{8,12},{10,14},{12... | collective-permute-start | bytes 405512 | tf_op jit(solution)/shard_map/ppermute | solution.py:452
  65.7 10.9 %collective-permute-start.23 = (s16[528,128]{1,0:T(8,128)(2,1)S(1)}, s16[528,128]{1,0:T(8,128)(2,1)S(1)}, u32[]{:S(2)}, u32[]{:S(2)}) collective-permute-start(s16[528,128]{1,0:T(8,128)(2,1)S(1)} %get-tuple-element.81), channel_id=1, source_target_pairs={{0,6},{2,4},{4,2},{6,0},{1,7},{3,5},{5,3},{7,1},{8,14},{10,12},{12... | collective-permute-start | bytes 405512 | tf_op jit(solution)/shard_map/ppermute | solution.py:452
  67.3 9.2 %collective-permute-start.24 = (s16[528,128]{1,0:T(8,128)(2,1)S(1)}, s16[528,128]{1,0:T(8,128)(2,1)S(1)}, u32[]{:S(2)}, u32[]{:S(2)}) collective-permute-start(s16[528,128]{1,0:T(8,128)(2,1)S(1)} %get-tuple-element.82), channel_id=1, source_target_pairs={{0,2},{2,0},{4,6},{6,4},{1,3},{3,1},{5,7},{7,5},{8,10},{10,8},{12,... | collective-permute-start | bytes 405512 | tf_op jit(solution)/shard_map/ppermute | solution.py:452
  70.4 7.9 %copy-start.6 = (bf16[4,1,128,2048]{3,2,1,0:T(8,128)(2,1)S(1)}, bf16[4,1,128,2048]{3,2,1,0:T(8,128)(2,1)}, u32[]{:S(2)}) copy-start(bf16[4,1,128,2048]{3,2,1,0:T(8,128)(2,1)} %param.11) | copy-start | bytes 6291460
